TPU v7x, 32 devices: a whole 2x2x4 slice. The times are simulated.
32 devices in a mesh: sub: 8 (over z, y), rhs: 4 (over x, core).
Axes of the slice: x: 2, y: 2, z: 4, core: 2. Of those that a mesh axis runs over, the one named last changes fastest.
Arguments:
- stiffness: float32 [384, 4, 9216], P('sub'), may hold values from -1 to 2, as said below
- precond: float32 [384, 9216], P('sub'), may hold values from -0.625 to 0.625
- rhs_vec: float32 [8, 36864], P('rhs', 'sub'), may hold values from -50 to 50
- cotangent: float32 [8, 36864], P('rhs', 'sub'), may hold values from -6 to 6
- col_index: int32 [384, 4], P('sub'), may hold values from 0 to 59, as said below
- send_rows: int32 [8, 12], P('sub'), may hold values from 0 to 47, as said below
- counts: int32 [8], P('sub'), may hold values from 12 to 48, as said below
Outputs:
- solution: float32 [8, 36864], P('rhs', 'sub')
- grad_precond: float32 [384, 9216], P('sub')
Inputs may be any that keep to these rules, and one draw needn't show every extreme that they name: `counts`: at least one subdomain has 48 live block rows. `send_rows`: for subdomain s, entries 0 to 5 are distinct live rows below counts[s] // 2 in increasing order, the first of them 0; entries 6 to 11 are distinct live rows from counts[s] // 2 on in increasing order, the last of them counts[s] - 1. Interface row j of the first group of subdomain s is coupled with interface row j of the second group of subdomain s - 1. `col_index`: index 6 + n is block n of the subdomain; indices below 6 and from 54 on are the blocks received from the previous and the next subdomain. Slot 0 of row n is 6 + n. A slot other than slot 0 that names 6 + n holds a zero block; rows that are not live hold only slot 0's block. `stiffness`: the operator A is symmetric and positive definite.
All inputs are finite; a program needn't handle non-finite values.
Results may differ from a plain program's by a relative error of at most 0.0003.
Values sent between devices are 32-bit elements; how exact they have to be, the bound alone decides.
No kernel may reach another device: no remote copies, remote signals or barrier semaphores. Data moves between devices by JAX's collectives and lax.ppermute only.
A program may use at most 128 MiB of HBM per device.

v0:
```python
import jax
import jax.numpy as jnp
from jax import lax
from jax.sharding import PartitionSpec as P

BS = 96
K = 4
NBLK = 48
IF = 6
ITERS = 4


highest = lax.Precision.HIGHEST


def with_halo(array, sides, width):
    for axis, dim in sides:
        size, length = (lax.axis_size(axis), array.shape[dim])
        up = [(i, (i + 1) % size) for i in range(size - 1)]
        down = [(j, i) for i, j in up]
        last = lax.slice_in_dim(array, length - width, length, axis=dim)
        initial = lax.slice_in_dim(array, 0, width, axis=dim)
        before = lax.ppermute(last, axis, up)
        after = lax.ppermute(initial, axis, down)
        array = jnp.concatenate([before, array, after], axis=dim)
    return array


def local_dot(first_vec, second_vec):
    return jnp.sum(first_vec * second_vec, axis=(1, 2))


def widen(scalars):
    return scalars[:, None, None]


def precond_apply(weights, vector):
    projected = jnp.einsum("nab,rnb->rna", weights, vector, precision=highest)
    return (projected, vector + jnp.einsum("nab,rna->rnb", weights, projected, precision=highest))


def block_product(blocks, gathered):
    return jnp.einsum("nkab,rnkb->rna", blocks, gathered, precision=highest)


def stiff_apply(vector, blocks, columns, sending):
    outgoing = jnp.take(vector, sending, axis=1)
    framed = with_halo(outgoing, (("sub", 1),), IF)
    extended = jnp.concatenate([framed[:, :IF], vector, framed[:, 3 * IF :]], axis=1)
    return block_product(blocks, jnp.take(extended, columns, axis=1))


def norm_sum(first_vec, second_vec):
    return lax.psum(local_dot(first_vec, second_vec), "sub")


def grad_term(projected, zeta_bar, weight_zeta, resid_vec):
    first_part = jnp.einsum("rna,rnb->nab", projected, zeta_bar, precision=highest)
    return first_part + jnp.einsum("rna,rnb->nab", weight_zeta, resid_vec, precision=highest)


def shards(stiffness, precond, rhs_vec, cotangent, col_index, send_rows, counts):
    rhs_all, cot_all = (rhs_vec, cotangent)
    local_rhs = rhs_all.shape[0]
    blocks = stiffness.reshape(NBLK, K, BS, BS)
    weights = precond.reshape(NBLK, BS, BS)
    live_count = counts[0]
    sending = send_rows[0]
    live_mask = (jnp.arange(NBLK) < live_count).astype(jnp.float32)
    source = rhs_all.reshape(local_rhs, NBLK, BS) * live_mask[None, :, None]
    target = cot_all.reshape(local_rhs, NBLK, BS)
    residual = source
    first_proj, precon = precond_apply(weights, residual)
    first_res = residual
    direction = precon
    norm_now = norm_sum(residual, precon)
    solution = jnp.zeros_like(source)
    history = []
    for iteration in range(ITERS):
        applied = stiff_apply(direction, blocks, col_index, sending)
        curvature = lax.psum(local_dot(direction, applied), "sub")
        step_len = norm_now / curvature
        solution = solution + widen(step_len) * direction
        residual = residual - widen(step_len) * applied
        record = [direction, applied, step_len, curvature, norm_now]
        if iteration + 1 < ITERS:
            projected, precon = precond_apply(weights, residual)
            norm_next = norm_sum(residual, precon)
            ratio = norm_next / norm_now
            record = record + [residual, precon, projected, norm_next, ratio]
            direction = precon + widen(ratio) * direction
            norm_now = norm_next
        history.append(record)
    dir_bar = jnp.zeros_like(source)
    res_bar = jnp.zeros_like(source)
    norm_bar = jnp.zeros((local_rhs,), jnp.float32)
    grad_sum = jnp.zeros((NBLK, BS, BS), jnp.float32)
    for iteration in reversed(range(ITERS)):
        direction, applied, step_len, curvature, norm_now = history[iteration][:5]
        if iteration + 1 < ITERS:
            resid_next, precon, projected, norm_next, ratio = history[iteration][5:]
            ratio_bar, cot_dir = lax.psum(
                (local_dot(dir_bar, direction), local_dot(target, direction)), "sub"
            )
            norm_full = norm_bar + ratio_bar / norm_now
            zeta_bar = dir_bar + widen(norm_full) * resid_next
            weight_zeta, mapped = precond_apply(weights, zeta_bar)
            res_bar = res_bar + widen(norm_full) * precon + mapped
            res_image = lax.psum(local_dot(res_bar, applied), "sub")
            grad_sum = grad_sum + grad_term(projected, zeta_bar, weight_zeta, resid_next)
            dir_new = widen(ratio) * dir_bar
            norm_new = -ratio_bar * norm_next / (norm_now * norm_now)
        else:
            cot_dir = lax.psum(local_dot(target, direction), "sub")
            res_image = jnp.zeros_like(cot_dir)
            dir_new = jnp.zeros_like(source)
            norm_new = jnp.zeros_like(cot_dir)
        step_bar = cot_dir - res_image
        curv_bar = -step_bar * step_len / curvature
        dir_new = dir_new + widen(step_len) * target + widen(curv_bar) * applied
        image_bar = widen(curv_bar) * direction - widen(step_len) * res_bar
        dir_bar = dir_new + stiff_apply(image_bar, blocks, col_index, sending)
        norm_bar = norm_new + step_bar / curvature
    zeta_bar = dir_bar + widen(norm_bar) * first_res
    weight_zeta = jnp.einsum("nab,rnb->rna", weights, zeta_bar, precision=highest)
    grad_sum = grad_sum + grad_term(first_proj, zeta_bar, weight_zeta, first_res)
    grad_sum = lax.psum(grad_sum, "rhs")
    flat_solution = solution.reshape(local_rhs, NBLK * BS)
    return (flat_solution, grad_sum.reshape(NBLK, BS * BS))


def solution(mesh):
    in_specs = (
        P("sub", None, None),
        P("sub", None),
        P("rhs", "sub"),
        P("rhs", "sub"),
        P("sub", None),
        P("sub", None),
        P("sub"),
    )
    out_specs = (P("rhs", "sub"), P("sub", None))
    return jax.shard_map(shards, mesh=mesh, in_specs=in_specs, out_specs=out_specs, check_vma=False)
```

profile of v0, /device:TPU:13, one launch (start us, length us, event | category | flops | bytes accessed | tf_op | source)
XLA Modules:
  0.0 563.8 jit_solution(1573668951216222546)
XLA Ops:
  10.1 2.2 reshape.53
  12.3 3.8 convolution_bitcast_fusion.22
  16.1 2.1 fusion.14
  18.9 3.1 collective-permute-start
  22.1 2.1 collective-permute-start.1
  24.6 10.6 %reshape.54 = f32[48,4,96,96]{3,2,1,0:T(8,128)} reshape(f32[48,4,9216]{2,1,0:T(4,128)} %param.11) | data formatting | bytes 14155776 | tf_op jit(solution)/shard_map/reshape | solution.py:65
  36.1 10.5 %multiply_reduce_fusion.16 = (f32[2]{0:T(128)S(1)}, f32[2]{0:T(128)S(1)}, f32[2,48,96]{2,0,1:T(2,128)S(1)}) fusion(f32[2,48,96]{2,0,1:T(2,128)S(1)} %fusion.14, f32[48]{0:T(128)S(1)} %compare_convert_fusion, f32[2,48,96]{2,1,0:T(8,128)S(1)} %reshape.52, f32[48,4,96,96]{3,2,1,0:T(8,128)} %reshape.54, f32[48,4,2,96]{3,2,1,0:T(2,128)S(1)} %bitcast.225, ...), kind=kOutput, calls=%fused_computation.126 | convolution fusion | flops 42550268 | bytes 7336336 | tf_op jit(solution)/shard_map/nkab,rnkb->rna/dot_general | solution.py:43
  46.6 12.8 %all-reduce.4 = (f32[2]{0:T(128)S(1)}, f32[2]{0:T(128)S(1)}) all-reduce(f32[2]{0:T(128)S(1)} %get-tuple-element.10, f32[2]{0:T(128)S(1)} %get-tuple-element.9), channel_id=1, replica_groups=mesh['sub'=8,'rhs'=4] {'sub'}, use_global_device_ids=true, to_apply=%region_1.0 | all-reduce | flops 4 | bytes 32 | tf_op jit(solution)/shard_map/psum | solution.py:54
  59.5 3.8 convolution_bitcast_fusion.20
  63.3 2.2 multiply_reduce_fusion.15
  65.5 16.8 %psum.135 = f32[2]{0:T(128)S(1)} all-reduce(f32[2]{0:T(128)S(1)} %get-tuple-element.44), channel_id=1, replica_groups=mesh['sub'=8,'rhs'=4] {'sub'}, use_global_device_ids=true, to_apply=%region_5.8 | all-reduce | flops 2 | bytes 16 | tf_op jit(solution)/shard_map/psum | solution.py:54
  83.1 1.9 collective-permute-start.2
  85.1 3.4 collective-permute-start.3
  91.2 10.5 %multiply_reduce_fusion.14 = (f32[2]{0:T(128)S(1)}, f32[2,48,96]{2,0,1:T(2,128)S(1)}) fusion(f32[2,48,96]{2,0,1:T(2,128)S(1)} %multiply_add_fusion.6, f32[48,4,96,96]{3,2,1,0:T(8,128)} %reshape.54, f32[48,4,2,96]{3,2,1,0:T(2,128)S(1)} %bitcast.226, pred[48,4]{1,0:T(8,128)(4,1)S(1)} %copy.18), kind=kOutput, calls=%fused_computation.122 | convolution fusion | flops 42522624 | bytes 7299272 | tf_op jit(solution)/shard_map/nkab,rnkb->rna/dot_general | solution.py:43
  101.7 14.4 %psum.136 = f32[2]{0:T(128)S(1)} all-reduce(f32[2]{0:T(128)S(1)} %get-tuple-element.46), channel_id=1, replica_groups=mesh['sub'=8,'rhs'=4] {'sub'}, use_global_device_ids=true, to_apply=%region_7.10 | all-reduce | flops 2 | bytes 16 | tf_op jit(solution)/shard_map/psum | solution.py:81
  116.2 3.8 convolution_bitcast_fusion.18
  120.0 2.2 multiply_reduce_fusion.13
  122.2 14.8 %psum.137 = f32[2]{0:T(128)S(1)} all-reduce(f32[2]{0:T(128)S(1)} %get-tuple-element.48), channel_id=1, replica_groups=mesh['sub'=8,'rhs'=4] {'sub'}, use_global_device_ids=true, to_apply=%region_9.12 | all-reduce | flops 2 | bytes 16 | tf_op jit(solution)/shard_map/psum | solution.py:54
  137.8 1.9 collective-permute-start.4
  139.7 3.4 collective-permute-start.5
  145.9 10.5 %multiply_reduce_fusion.12 = (f32[2]{0:T(128)S(1)}, f32[2,48,96]{2,0,1:T(2,128)S(1)}) fusion(f32[2,48,96]{2,0,1:T(2,128)S(1)} %multiply_add_fusion.5, f32[48,4,96,96]{3,2,1,0:T(8,128)} %reshape.54, f32[48,4,2,96]{3,2,1,0:T(2,128)S(1)} %bitcast.227, pred[48,4]{1,0:T(8,128)(4,1)S(1)} %copy.18), kind=kOutput, calls=%fused_computation.118 | convolution fusion | flops 42522624 | bytes 7299272 | tf_op jit(solution)/shard_map/nkab,rnkb->rna/dot_general | solution.py:43
  156.4 14.9 %psum.138 = f32[2]{0:T(128)S(1)} all-reduce(f32[2]{0:T(128)S(1)} %get-tuple-element.50), channel_id=1, replica_groups=mesh['sub'=8,'rhs'=4] {'sub'}, use_global_device_ids=true, to_apply=%region_11.14 | all-reduce | flops 2 | bytes 16 | tf_op jit(solution)/shard_map/psum | solution.py:81
  171.4 3.8 convolution_bitcast_fusion.16
  175.2 2.2 multiply_reduce_fusion.11
  177.4 14.3 %psum.139 = f32[2]{0:T(128)S(1)} all-reduce(f32[2]{0:T(128)S(1)} %get-tuple-element.52), channel_id=1, replica_groups=mesh['sub'=8,'rhs'=4] {'sub'}, use_global_device_ids=true, to_apply=%region_13.16 | all-reduce | flops 2 | bytes 16 | tf_op jit(solution)/shard_map/psum | solution.py:54
  192.5 1.9 collective-permute-start.6
  194.4 3.4 collective-permute-start.7
  200.6 11.1 %multiply_reduce_fusion.1 = (f32[2]{0:T(128)}, f32[2]{0:T(128)S(1)}, f32[2]{0:T(128)S(1)}, f32[2]{0:T(128)}, f32[2]{0:T(128)}, /*index=5*/f32[2,48,96]{2,0,1:T(2,128)S(1)}) fusion(f32[2,48,96]{2,0,1:T(2,128)S(1)} %fusion.14, f32[2,48,96]{2,1,0:T(8,128)S(1)} %reshape.56, f32[2,48,96]{2,0,1:T(2,128)S(1)} %multiply_add_fusion.4, ...), kind=kOutput, calls=%fused_computation.98 | convolution fusion | flops 42596344 | bytes 7446760 | tf_op jit(solution)/shard_map/nkab,rnkb->rna/dot_general | solution.py:43
  211.7 14.4 %all-reduce.3 = (f32[2]{0:T(128)S(1)}, f32[2]{0:T(128)S(1)}) all-reduce(f32[2]{0:T(128)S(1)} %get-tuple-element.6, f32[2]{0:T(128)S(1)} %get-tuple-element.5), channel_id=1, replica_groups=mesh['sub'=8,'rhs'=4] {'sub'}, use_global_device_ids=true, to_apply=%region_15.18 | all-reduce | flops 4 | bytes 32 | tf_op jit(solution)/shard_map/psum | solution.py:81
  227.5 1.9 collective-permute-start.8
  229.4 3.5 collective-permute-start.9
  235.6 10.5 %multiply_reduce_fusion.8 = (f32[2]{0:T(128)S(1)}, f32[2,48,96]{2,0,1:T(2,128)S(1)}) fusion(f32[2,48,96]{2,0,1:T(2,128)S(1)} %multiply_add_fusion.5, f32[48,4,96,96]{3,2,1,0:T(8,128)} %reshape.54, f32[48,4,2,96]{3,2,1,0:T(2,128)S(1)} %bitcast.224, pred[48,4]{1,0:T(8,128)(4,1)S(1)} %copy.18, f32[2,48,96]{2,0,1:T(2,128)S(1)} %get-tuple-element.54, ...), kind=kOutput, calls=%fused_computation.110 | convolution fusion | flops 42559488 | bytes 7373016 | tf_op jit(solution)/shard_map/nkab,rnkb->rna/dot_general | solution.py:43
  246.1 14.0 %psum.142 = f32[2]{0:T(128)S(1)} all-reduce(f32[2]{0:T(128)S(1)} %get-tuple-element.55), channel_id=1, replica_groups=mesh['sub'=8,'rhs'=4] {'sub'}, use_global_device_ids=true, to_apply=%region_19.22 | all-reduce | flops 2 | bytes 16 | tf_op jit(solution)/shard_map/psum | solution.py:102
  260.2 3.8 convolution_bitcast_fusion.14
  264.0 2.2 multiply_reduce_fusion.6
  266.2 5.2 fusion.64
  271.4 14.8 %all-reduce.2 = (f32[2]{0:T(128)S(1)}, f32[2]{0:T(128)S(1)}) all-reduce(f32[2]{0:T(128)S(1)} %copy-done.43, f32[2]{0:T(128)S(1)} %get-tuple-element.57), channel_id=1, replica_groups=mesh['sub'=8,'rhs'=4] {'sub'}, use_global_device_ids=true, to_apply=%region_21.24 | all-reduce | flops 4 | bytes 32 | tf_op jit(solution)/shard_map/psum | solution.py:102
  287.6 1.9 collective-permute-start.10
  289.5 3.6 collective-permute-start.11
  293.1 5.4 fusion.63
  299.4 10.5 %multiply_reduce_fusion.5 = (f32[2]{0:T(128)S(1)}, f32[2,48,96]{2,0,1:T(2,128)S(1)}) fusion(f32[2,48,96]{2,0,1:T(2,128)S(1)} %multiply_add_fusion.6, f32[48,4,96,96]{3,2,1,0:T(8,128)} %reshape.54, f32[48,4,2,96]{3,2,1,0:T(2,128)S(1)} %bitcast.222, pred[48,4]{1,0:T(8,128)(4,1)S(1)} %copy.18, f32[2,48,96]{2,0,1:T(2,128)S(1)} %get-tuple-element.51, ...), kind=kOutput, calls=%fused_computation.105 | convolution fusion | flops 42577920 | bytes 7409888 | tf_op jit(solution)/shard_map/nkab,rnkb->rna/dot_general | solution.py:43
  310.0 13.2 %psum.145 = f32[2]{0:T(128)S(1)} all-reduce(f32[2]{0:T(128)S(1)} %get-tuple-element.59), channel_id=1, replica_groups=mesh['sub'=8,'rhs'=4] {'sub'}, use_global_device_ids=true, to_apply=%region_25.28 | all-reduce | flops 2 | bytes 16 | tf_op jit(solution)/shard_map/psum | solution.py:102
  323.3 3.8 convolution_bitcast_fusion.12
  327.1 2.2 multiply_reduce_fusion.3
  329.3 5.2 fusion.66
  334.5 15.7 %all-reduce.1 = (f32[2]{0:T(128)S(1)}, f32[2]{0:T(128)S(1)}) all-reduce(f32[2]{0:T(128)S(1)} %copy-done.42, f32[2]{0:T(128)S(1)} %get-tuple-element.61), channel_id=1, replica_groups=mesh['sub'=8,'rhs'=4] {'sub'}, use_global_device_ids=true, to_apply=%region_27.30 | all-reduce | flops 4 | bytes 32 | tf_op jit(solution)/shard_map/psum | solution.py:102
  351.0 1.9 collective-permute-start.12
  353.0 3.5 collective-permute-start.13
  356.5 5.3 fusion.65
  362.7 10.5 %multiply_reduce_fusion.2 = (f32[2]{0:T(128)S(1)}, f32[2,48,96]{2,0,1:T(2,128)S(1)}) fusion(f32[2,48,96]{2,0,1:T(2,128)S(1)} %fusion.14, f32[48,4,96,96]{3,2,1,0:T(8,128)} %reshape.54, f32[48,4,2,96]{3,2,1,0:T(2,128)S(1)} %bitcast.223, pred[48,4]{1,0:T(8,128)(4,1)S(1)} %copy.18, f32[2,48,96]{2,0,1:T(2,128)S(1)} %get-tuple-element.47, ...), kind=kOutput, calls=%fused_computation.100 | convolution fusion | flops 42577920 | bytes 7409888 | tf_op jit(solution)/shard_map/nkab,rnkb->rna/dot_general | solution.py:43
  373.2 13.2 %psum.148 = f32[2]{0:T(128)S(1)} all-reduce(f32[2]{0:T(128)S(1)} %get-tuple-element.63), channel_id=1, replica_groups=mesh['sub'=8,'rhs'=4] {'sub'}, use_global_device_ids=true, to_apply=%region_31.34 | all-reduce | flops 2 | bytes 16 | tf_op jit(solution)/shard_map/psum | solution.py:102
  386.6 3.8 convolution_bitcast_fusion.10
  390.3 2.2 multiply_reduce_fusion
  392.6 5.2 fusion.68
  397.8 15.7 %all-reduce = (f32[2]{0:T(128)S(1)}, f32[2]{0:T(128)S(1)}) all-reduce(f32[2]{0:T(128)S(1)} %copy-done.41, f32[2]{0:T(128)S(1)} %get-tuple-element.65), channel_id=1, replica_groups=mesh['sub'=8,'rhs'=4] {'sub'}, use_global_device_ids=true, to_apply=%region_33.36 | all-reduce | flops 4 | bytes 32 | tf_op jit(solution)/shard_map/psum | solution.py:102
  416.3 3.8 collective-permute-start.15
  420.1 5.3 fusion.67
  426.3 10.7 %fusion.1 = f32[2,48,96]{2,0,1:T(2,128)S(1)} fusion(f32[48,4,96,96]{3,2,1,0:T(8,128)} %reshape.54, f32[48,4,2,96]{3,2,1,0:T(2,128)S(1)} %bitcast.220, pred[48,4]{1,0:T(8,128)(4,1)S(1)} %copy.18, f32[2,48,96]{2,0,1:T(2,128)S(1)} %get-tuple-element.43, f32[2,48,96]{2,0,1:T(2,128)S(1)} %get-tuple-element.64, f32[2]{0:T(128)S(1)} %get-tuple-element.41, ...), kind=kOutput, calls=%fused_computation.19 | convolution fusion | flops 42587136 | bytes 7410080 | tf_op jit(solution)/shard_map/nkab,rnkb->rna/dot_general | solution.py:43
  437.1 3.8 convolution_bitcast_fusion.8
  440.8 3.9 fusion.69
  444.8 4.3 add_add_fusion
  449.1 2.5 reshape.57
  452.4 101.6 %all-reduce.7.cloned.1.call-done = f32[48,9216]{1,0:T(8,128)} async-done(((f32[48,9216]{1,0:T(8,128)}), f32[48,9216]{1,0:T(8,128)}) %all-reduce.7.cloned.1.call-update) | async-done | bytes 1769488 | tf_op jit(solution)/shard_map/psum | solution.py:127
  554.0 2.8 copy.72
  (192 shorter events, 27.7 us)
Async XLA Ops:
  7.2 546.8 %all-reduce.7.cloned.1.call-start = ((), (), s32[]{:S(2)}) async-start(), calls=%async_computation | async-start | bytes 3538944 | tf_op jit(solution)/shard_map/psum | solution.py:127
  12.3 11.9 %copy-start.13 = (s32[48,4]{0,1:T(4,128)S(1)}, s32[48,4]{0,1:T(4,128)}, u32[]{:S(2)}) copy-start(s32[48,4]{0,1:T(4,128)} %param.15) | copy-start | bytes 2308
  18.9 16.2 %collective-permute-start = (f32[2,6,96]{2,0,1:T(2,128)S(1)}, f32[2,6,96]{2,0,1:T(2,128)S(1)}, u32[]{:S(2)}, u32[]{:S(2)}) collective-permute-start(f32[2,6,96]{2,0,1:T(2,128)S(1)} %get-tuple-element.39), channel_id=1, source_target_pairs={{0,4},{4,8},{8,12},{12,16},{16,20},{20,24},{24,28},{1,5},{5,9},{9,... | collective-permute-start | bytes 13832 | tf_op jit(solution)/shard_map/ppermute | solution.py:23
  22.1 13.1 %collective-permute-start.1 = (f32[2,6,96]{2,0,1:T(2,128)S(1)}, f32[2,6,96]{2,0,1:T(2,128)S(1)}, u32[]{:S(2)}, u32[]{:S(2)}) collective-permute-start(f32[2,6,96]{2,0,1:T(2,128)S(1)} %get-tuple-element.40), channel_id=1, source_target_pairs={{4,0},{8,4},{12,8},{16,12},{20,16},{24,20},{28,24},{5,1},{9,5},{13... | collective-permute-start | bytes 13832 | tf_op jit(solution)/shard_map/ppermute | solution.py:24
  59.4 6.1 %copy-start.44 = (f32[2]{0:T(128)}, f32[2]{0:T(128)S(1)}, u32[]{:S(2)}) copy-start(f32[2]{0:T(128)S(1)} %get-tuple-element.20) | copy-start | bytes 28
  59.4 23.0 %copy-start.19 = (f32[2]{0:T(128)}, f32[2]{0:T(128)S(1)}, u32[]{:S(2)}) copy-start(f32[2]{0:T(128)S(1)} %get-tuple-element.19) | copy-start | bytes 28
  63.3 38.5 %copy-start.6 = (f32[2,48,96]{2,0,1:T(2,128)}, f32[2,48,96]{2,0,1:T(2,128)S(1)}, u32[]{:S(2)}) copy-start(f32[2,48,96]{2,0,1:T(2,128)S(1)} %convolution_bitcast_fusion.20) | copy-start | bytes 110596
  82.3 0.7 copy-start.14
  83.1 5.3 collective-permute-start.2
  85.1 5.3 collective-permute-start.3
  116.1 6.1 %copy-start.21 = (f32[2]{0:T(128)}, f32[2]{0:T(128)S(1)}, u32[]{:S(2)}) copy-start(f32[2]{0:T(128)S(1)} %psum.136) | copy-start | bytes 28
  120.0 17.0 %copy-start.8 = (f32[2,48,96]{2,0,1:T(2,128)}, f32[2,48,96]{2,0,1:T(2,128)S(1)}, u32[]{:S(2)}) copy-start(f32[2,48,96]{2,0,1:T(2,128)S(1)} %convolution_bitcast_fusion.18) | copy-start | bytes 110596
  137.0 19.4 %copy-start.16 = (f32[2]{0:T(128)}, f32[2]{0:T(128)S(1)}, u32[]{:S(2)}) copy-start(f32[2]{0:T(128)S(1)} %div.66) | copy-start | bytes 28
  137.8 5.3 collective-permute-start.4
  139.7 5.3 collective-permute-start.5
  171.3 6.1 %copy-start.24 = (f32[2]{0:T(128)}, f32[2]{0:T(128)S(1)}, u32[]{:S(2)}) copy-start(f32[2]{0:T(128)S(1)} %psum.138) | copy-start | bytes 28
  171.4 26.4 %copy-start.12 = (f32[2,4608]{1,0:T(2,128)S(1)}, f32[2,4608]{1,0:T(2,128)}, u32[]{:S(2)}) copy-start(f32[2,4608]{1,0:T(2,128)} %param.14) | copy-start | bytes 110596
  175.1 19.2 %copy-start.10 = (f32[2,48,96]{2,0,1:T(2,128)}, f32[2,48,96]{2,0,1:T(2,128)S(1)}, u32[]{:S(2)}) copy-start(f32[2,48,96]{2,0,1:T(2,128)S(1)} %convolution_bitcast_fusion.16) | copy-start | bytes 110596
  191.7 34.5 %copy-start.27 = (f32[2]{0:T(128)}, f32[2]{0:T(128)S(1)}, u32[]{:S(2)}) copy-start(f32[2]{0:T(128)S(1)} %psum.139) | copy-start | bytes 28
  191.7 20.0 %copy-start.18 = (f32[2]{0:T(128)}, f32[2]{0:T(128)S(1)}, u32[]{:S(2)}) copy-start(f32[2]{0:T(128)S(1)} %div.68) | copy-start | bytes 28
  192.5 5.4 collective-permute-start.6
  194.4 5.3 collective-permute-start.7
  226.1 0.6 copy-start.37
  226.1 0.6 copy-start.39
  227.5 5.5 collective-permute-start.8
  229.4 5.3 collective-permute-start.9
  235.6 24.5 %copy-start.38 = (f32[2]{0:T(128)S(1)}, f32[2]{0:T(128)}, u32[]{:S(2)}) copy-start(f32[2]{0:T(128)} %copy-done.37) | copy-start | bytes 28
  235.6 24.5 %copy-start.40 = (f32[2]{0:T(128)S(1)}, f32[2]{0:T(128)}, u32[]{:S(2)}) copy-start(f32[2]{0:T(128)} %copy-done.39) | copy-start | bytes 28
  260.1 6.1 %copy-start.31 = (f32[2]{0:T(128)}, f32[2]{0:T(128)S(1)}, u32[]{:S(2)}) copy-start(f32[2]{0:T(128)S(1)} %psum.142) | copy-start | bytes 28
  264.0 7.5 %copy-start.43 = (f32[2]{0:T(128)S(1)}, f32[2]{0:T(128)}, u32[]{:S(2)}) copy-start(f32[2]{0:T(128)} %get-tuple-element.7) | copy-start | bytes 28
  264.0 22.3 %copy-start.25 = (f32[2]{0:T(128)S(1)}, f32[2]{0:T(128)}, u32[]{:S(2)}) copy-start(f32[2]{0:T(128)} %copy-done.24) | copy-start | bytes 28
  264.0 29.2 %copy-start.11 = (f32[2,48,96]{2,0,1:T(2,128)S(1)}, f32[2,48,96]{2,0,1:T(2,128)}, u32[]{:S(2)}) copy-start(f32[2,48,96]{2,0,1:T(2,128)} %copy-done.10) | copy-start | bytes 110596
  286.3 0.5 copy-start.33
  286.3 0.6 copy-start.35
  287.6 10.9 %collective-permute-start.10 = (f32[2,6,96]{2,0,1:T(2,128)S(1)}, f32[2,6,96]{2,0,1:T(2,128)S(1)}, u32[]{:S(2)}, u32[]{:S(2)}) collective-permute-start(f32[2,6,96]{2,0,1:T(2,128)S(1)} %get-tuple-element.29), channel_id=1, source_target_pairs={{0,4},{4,8},{8,12},{12,16},{16,20},{20,24},{24,28},{1,5},{5,9},{9,... | collective-permute-start | bytes 13832 | tf_op jit(solution)/shard_map/ppermute | solution.py:23
  289.5 8.9 %collective-permute-start.11 = (f32[2,6,96]{2,0,1:T(2,128)S(1)}, f32[2,6,96]{2,0,1:T(2,128)S(1)}, u32[]{:S(2)}, u32[]{:S(2)}) collective-permute-start(f32[2,6,96]{2,0,1:T(2,128)S(1)} %get-tuple-element.30), channel_id=1, source_target_pairs={{4,0},{8,4},{12,8},{16,12},{20,16},{24,20},{28,24},{5,1},{9,5},{13... | collective-permute-start | bytes 13832 | tf_op jit(solution)/shard_map/ppermute | solution.py:24
  299.4 23.7 %copy-start.26 = (f32[2]{0:T(128)S(1)}, f32[2]{0:T(128)}, u32[]{:S(2)}) copy-start(f32[2]{0:T(128)} %copy-done.24) | copy-start | bytes 28
  299.4 23.7 %copy-start.28 = (f32[2]{0:T(128)S(1)}, f32[2]{0:T(128)}, u32[]{:S(2)}) copy-start(f32[2]{0:T(128)} %copy-done.27) | copy-start | bytes 28
  299.4 23.7 %copy-start.32 = (f32[2]{0:T(128)S(1)}, f32[2]{0:T(128)}, u32[]{:S(2)}) copy-start(f32[2]{0:T(128)} %copy-done.31) | copy-start | bytes 28
  299.4 23.7 %copy-start.34 = (f32[2]{0:T(128)S(1)}, f32[2]{0:T(128)}, u32[]{:S(2)}) copy-start(f32[2]{0:T(128)} %copy-done.33) | copy-start | bytes 28
  299.4 23.7 %copy-start.36 = (f32[2]{0:T(128)S(1)}, f32[2]{0:T(128)}, u32[]{:S(2)}) copy-start(f32[2]{0:T(128)} %copy-done.35) | copy-start | bytes 28
  323.2 3.9 copy-start.29
  327.0 7.5 %copy-start.42 = (f32[2]{0:T(128)S(1)}, f32[2]{0:T(128)}, u32[]{:S(2)}) copy-start(f32[2]{0:T(128)} %get-tuple-element.8) | copy-start | bytes 28
  327.0 23.2 %copy-start.22 = (f32[2]{0:T(128)S(1)}, f32[2]{0:T(128)}, u32[]{:S(2)}) copy-start(f32[2]{0:T(128)} %copy-done.21) | copy-start | bytes 28
  327.1 29.4 %copy-start.9 = (f32[2,48,96]{2,0,1:T(2,128)S(1)}, f32[2,48,96]{2,0,1:T(2,128)}, u32[]{:S(2)}) copy-start(f32[2,48,96]{2,0,1:T(2,128)} %copy-done.8) | copy-start | bytes 110596
  329.3 33.4 %copy-start.17 = (f32[2]{0:T(128)S(1)}, f32[2]{0:T(128)}, u32[]{:S(2)}) copy-start(f32[2]{0:T(128)} %copy-done.16) | copy-start | bytes 28
  351.0 10.8 %collective-permute-start.12 = (f32[2,6,96]{2,0,1:T(2,128)S(1)}, f32[2,6,96]{2,0,1:T(2,128)S(1)}, u32[]{:S(2)}, u32[]{:S(2)}) collective-permute-start(f32[2,6,96]{2,0,1:T(2,128)S(1)} %get-tuple-element.27), channel_id=1, source_target_pairs={{0,4},{4,8},{8,12},{12,16},{16,20},{20,24},{24,28},{1,5},{5,9},{9,... | collective-permute-start | bytes 13832 | tf_op jit(solution)/shard_map/ppermute | solution.py:23
  353.0 8.8 %collective-permute-start.13 = (f32[2,6,96]{2,0,1:T(2,128)S(1)}, f32[2,6,96]{2,0,1:T(2,128)S(1)}, u32[]{:S(2)}, u32[]{:S(2)}) collective-permute-start(f32[2,6,96]{2,0,1:T(2,128)S(1)} %get-tuple-element.28), channel_id=1, source_target_pairs={{4,0},{8,4},{12,8},{16,12},{20,16},{24,20},{28,24},{5,1},{9,5},{13... | collective-permute-start | bytes 13832 | tf_op jit(solution)/shard_map/ppermute | solution.py:24
  362.7 23.8 %copy-start.20 = (f32[2]{0:T(128)S(1)}, f32[2]{0:T(128)}, u32[]{:S(2)}) copy-start(f32[2]{0:T(128)} %copy-done.19) | copy-start | bytes 28
  362.7 23.8 %copy-start.23 = (f32[2]{0:T(128)S(1)}, f32[2]{0:T(128)}, u32[]{:S(2)}) copy-start(f32[2]{0:T(128)} %copy-done.21) | copy-start | bytes 28
  362.7 23.8 %copy-start.30 = (f32[2]{0:T(128)S(1)}, f32[2]{0:T(128)}, u32[]{:S(2)}) copy-start(f32[2]{0:T(128)} %copy-done.29) | copy-start | bytes 28
  390.3 7.5 %copy-start.41 = (f32[2]{0:T(128)S(1)}, f32[2]{0:T(128)}, u32[]{:S(2)}) copy-start(f32[2]{0:T(128)} %get-tuple-element.4) | copy-start | bytes 28
  390.3 23.2 %copy-start.45 = (f32[2]{0:T(128)S(1)}, f32[2]{0:T(128)}, u32[]{:S(2)}) copy-start(f32[2]{0:T(128)} %copy-done.44) | copy-start | bytes 28
  390.3 29.7 %copy-start.7 = (f32[2,48,96]{2,0,1:T(2,128)S(1)}, f32[2,48,96]{2,0,1:T(2,128)}, u32[]{:S(2)}) copy-start(f32[2,48,96]{2,0,1:T(2,128)} %copy-done.6) | copy-start | bytes 110596
  392.6 33.7 %copy-start.15 = (f32[2]{0:T(128)S(1)}, f32[2]{0:T(128)}, u32[]{:S(2)}) copy-start(f32[2]{0:T(128)} %copy-done.14) | copy-start | bytes 28
  414.4 11.0 %collective-permute-start.14 = (f32[2,6,96]{2,0,1:T(2,128)S(1)}, f32[2,6,96]{2,0,1:T(2,128)S(1)}, u32[]{:S(2)}, u32[]{:S(2)}) collective-permute-start(f32[2,6,96]{2,0,1:T(2,128)S(1)} %get-tuple-element.25), channel_id=1, source_target_pairs={{0,4},{4,8},{8,12},{12,16},{16,20},{20,24},{24,28},{1,5},{5,9},{9,... | collective-permute-start | bytes 13832 | tf_op jit(solution)/shard_map/ppermute | solution.py:23
  416.3 9.1 %collective-permute-start.15 = (f32[2,6,96]{2,0,1:T(2,128)S(1)}, f32[2,6,96]{2,0,1:T(2,128)S(1)}, u32[]{:S(2)}, u32[]{:S(2)}) collective-permute-start(f32[2,6,96]{2,0,1:T(2,128)S(1)} %get-tuple-element.26), channel_id=1, source_target_pairs={{4,0},{8,4},{12,8},{16,12},{20,16},{24,20},{28,24},{5,1},{9,5},{13... | collective-permute-start | bytes 13832 | tf_op jit(solution)/shard_map/ppermute | solution.py:24
  426.3 18.4 %copy-start.2 = (f32[48,96,96]{2,1,0:T(8,128)S(1)}, f32[48,96,96]{2,1,0:T(8,128)}, u32[]{:S(2)}) copy-start(f32[48,96,96]{2,1,0:T(8,128)} %fusion.66) | copy-start | bytes 5308420
  426.3 18.4 %copy-start.3 = (f32[48,96,96]{2,1,0:T(8,128)S(1)}, f32[48,96,96]{2,1,0:T(8,128)}, u32[]{:S(2)}) copy-start(f32[48,96,96]{2,1,0:T(8,128)} %fusion.65) | copy-start | bytes 5308420
  426.3 18.4 %copy-start.4 = (f32[48,96,96]{2,1,0:T(8,128)S(1)}, f32[48,96,96]{2,1,0:T(8,128)}, u32[]{:S(2)}) copy-start(f32[48,96,96]{2,1,0:T(8,128)} %fusion.68) | copy-start | bytes 5308420
  426.3 18.4 %copy-start.5 = (f32[48,96,96]{2,1,0:T(8,128)S(1)}, f32[48,96,96]{2,1,0:T(8,128)}, u32[]{:S(2)}) copy-start(f32[48,96,96]{2,1,0:T(8,128)} %fusion.67) | copy-start | bytes 5308420
  437.1 7.7 %copy-start = (f32[48,96,96]{2,1,0:T(8,128)S(1)}, f32[48,96,96]{2,1,0:T(8,128)}, u32[]{:S(2)}) copy-start(f32[48,96,96]{2,1,0:T(8,128)} %fusion.64) | copy-start | bytes 5308420
  437.1 7.7 %copy-start.1 = (f32[48,96,96]{2,1,0:T(8,128)S(1)}, f32[48,96,96]{2,1,0:T(8,128)}, u32[]{:S(2)}) copy-start(f32[48,96,96]{2,1,0:T(8,128)} %fusion.63) | copy-start | bytes 5308420
Sparse Core Ops, SparseCore 0:
  451.8 102.1 all-reduce.6
where the time goes:
time: 575 us; the launch traced here: 564 us
  blocking collectives  189 us (33%)
  matrix products  170 us (30%)
  waiting for transfers between devices  109 us (19%)
  starting transfers between devices  43.3 us (8%)
  local copies, waits for them, and re-layouts  32.9 us (6%)
  between operations  15.8 us (3%)
    psum x1, waiting for transfers between devices, shards(): grad_sum = lax.psum(grad_sum, 'rhs')  102 us
    psum x6, blocking collectives, shards(): lax.psum((local_dot(dir_bar, direction), local_dot(target, direction)), '...  86.6 us
    dot_general x8, matrix products, block_product(): return jnp.einsum('nkab,rnkb->rna', blocks, gathered, precision=highest)  84.9 us
    psum x4, blocking collectives, norm_sum(): return lax.psum(local_dot(first_vec, second_vec), 'sub')  58.7 us
    psum x3, blocking collectives, shards(): curvature = lax.psum(local_dot(direction, applied), 'sub')  43.7 us
    ppermute x8, starting transfers between devices, with_halo(): after = lax.ppermute(initial, axis, down)  26.6 us
    dot_general x7, matrix products, precond_apply(): projected = jnp.einsum('nab,rnb->rna', weights, vector, precision=highest)  26.3 us
    dot_general x4, matrix products, grad_term(): jnp.einsum('rna,rnb->nab', weight_zeta, resid_vec, precision=highest)  20 us
  transfers between devices with their start and end apart: 17, of which 5 were waited for; matrix products, arithmetic and copies ran while one was open for 5% of the time, Pallas kernels for 0%

commit v1 on v0

v1 whole, which is shorter than its diff:
```python
import functools

import jax
import jax.numpy as jnp
from jax import lax
from jax.experimental import pallas as pl
from jax.experimental.pallas import tpu as pltpu
from jax.sharding import PartitionSpec as P

BS = 96
K = 4
NBLK = 48
IF = 6
ITERS = 4
LANES = 128
OFF = 8
ROWS = 64
LOW = OFF - IF
HIGH = OFF + NBLK
CHUNK = 8
MIB = 1024 * 1024

highest = lax.Precision.HIGHEST
f32 = jnp.float32


def own(value):
    return value[:, OFF:HIGH]


def lane_ids():
    return lax.broadcasted_iota(jnp.int32, (BS, LANES), 1)


def diagonal():
    return lax.broadcasted_iota(jnp.int32, (BS, LANES), 0) == lane_ids()


def fold(prod):
    return jnp.sum(prod.reshape(BS // 8, 8, prod.shape[-1]), axis=0)


def make_operator(weights):
    gram = lax.dot_general(
        weights, weights, (((0,), (0,)), ((), ())), precision=highest, preferred_element_type=f32
    )
    wide = jnp.concatenate([gram, jnp.zeros((BS, LANES - BS), f32)], axis=1)
    return wide + jnp.where(diagonal(), 1.0, 0.0)


def scatter_apply(blocks, op_ref, x_ref, y_ref, col_ref, column_ref, wait):
    count = x_ref.shape[0]
    y_ref[...] = jnp.zeros_like(y_ref)

    def step(group, carry):
        wait(group)
        base = pl.multiple_of(group * CHUNK, CHUNK)
        tiles = [x_ref[r, pl.ds(base + OFF, CHUNK), :] for r in range(count)]
        for i in range(CHUNK):
            n = group * CHUNK + i
            oper = op_ref[n + OFF]
            images = [jnp.sum(oper * tiles[r][i : i + 1, :], axis=1, keepdims=True) for r in range(count)]
            if column_ref is not None:
                for r in range(column_ref.shape[0]):
                    column_ref[r, :BS, :] = jnp.where(lane_ids() == n + OFF, images[r], column_ref[r, :BS, :])
            for k in range(K):
                block = blocks[n, k]
                slot = col_ref[n, k] + LOW
                for r in range(count):
                    y_ref[r, slot, :, :BS] = y_ref[r, slot, :, :BS] + fold(block * images[r])
        return carry

    lax.fori_loop(0, NBLK // CHUNK, step, 0)


def ghost_images(op_ref, x_ref, g_ref):
    count = x_ref.shape[0]
    mask = diagonal()
    g_ref[...] = jnp.zeros_like(g_ref)
    for first in (LOW, HIGH):
        for j in range(IF):
            slot = first + j
            oper = op_ref[slot]
            for r in range(count):
                image = jnp.sum(oper * x_ref[r, slot : slot + 1, :], axis=1, keepdims=True)
                line = jnp.sum(fold(jnp.where(mask, image, 0.0)), axis=0, keepdims=True)
                g_ref[r, slot : slot + 1, :] = line


def ghost_apply(blocks, g_ref, y_ref, col_ref, list_ref):
    count = g_ref.shape[0]
    mask = diagonal()[:, :BS]

    def step(item, carry):
        for u in range(4):
            entry = list_ref[0, 1 + item * 4 + u]
            n = entry // K
            k = entry % K
            slot = col_ref[n, k] + LOW
            block = blocks[n, k]
            for r in range(count):
                image = jnp.sum(block * g_ref[r, pl.ds(slot, 1), :BS], axis=1, keepdims=True)
                y_ref[r, n + OFF, :, :BS] = y_ref[r, n + OFF, :, :BS] + fold(jnp.where(mask, image, 0.0))
        return carry

    lax.fori_loop(0, (list_ref[0, 0] + 3) // 4, step, 0)


def pack(y_ref, r):
    sub = lax.broadcasted_iota(jnp.int32, (8, LANES), 0)
    groups = []
    for g in range(ROWS // 8):
        total = jnp.zeros((8, LANES), f32)
        for i in range(8):
            line = jnp.sum(y_ref[r, g * 8 + i], axis=0, keepdims=True)
            total = jnp.where(sub == i, line, total)
        groups.append(total)
    return jnp.concatenate(groups, axis=0)


def unpack_columns(column_ref, r):
    return column_ref[r].T[:ROWS]


def messages(up_ref, down_ref, v_ref, h_ref, send_ref):
    for r in range(v_ref.shape[0]):
        for j in range(IF):
            down_ref[r, j : j + 1, :] = v_ref[r, pl.ds(send_ref[0, j] + OFF, 1), :]
            up_ref[r, j : j + 1, :] = v_ref[r, pl.ds(send_ref[0, IF + j] + OFF, 1), :]
            down_ref[r, 8 + j : 9 + j, :] = h_ref[r, LOW + j : LOW + j + 1, :]
            up_ref[r, 8 + j : 9 + j, :] = h_ref[r, HIGH + j : HIGH + j + 1, :]


def complete(v_ref, low_ref, high_ref, send_ref, edge_ref):
    for r in range(v_ref.shape[0]):
        for j in range(IF):
            for part, base, ghost, flag in ((low_ref, 0, LOW, 0), (high_ref, IF, HIGH, 1)):
                at = pl.ds(send_ref[0, base + j] + OFF, 1)
                v_ref[r, at, :] = v_ref[r, at, :] + part[r, 8 + j : 9 + j, :]
                slot = ghost + j
                summed = v_ref[r, slot : slot + 1, :] + part[r, j : j + 1, :]
                v_ref[r, slot : slot + 1, :] = jnp.where(edge_ref[flag] > 0, summed, 0.0)


def tile_sum(first, second):
    prod = first * second
    return jnp.sum(prod.reshape(prod.shape[0] // 8, 8, LANES), axis=0)


def stream(hbm, buffer, sems):
    def copy(group):
        part = pl.ds(group * CHUNK, CHUNK)
        return pltpu.make_async_copy(hbm.at[part], buffer.at[part], sems.at[group])

    for g in range(NBLK // CHUNK):
        copy(g).start()
    return lambda group: copy(group).wait()


def nowait(group):
    return None


def prepare_kernel(weights_ref, op_ref):
    for i in range(weights_ref.shape[0]):
        op_ref[i] = make_operator(weights_ref[i])


def list_kernel(col_ref, list_ref):
    def clear(i, carry):
        list_ref[0, i] = 0
        return carry

    lax.fori_loop(0, list_ref.shape[1], clear, 0)

    def step(i, count):
        col = col_ref[i // K, i % K]
        list_ref[0, 1 + count] = i
        return count + jnp.where((col < IF) | (col >= IF + NBLK), 1, 0)

    count = lax.fori_loop(0, NBLK * K, step, 0)
    list_ref[0, 0] = count
    for u in range(4):
        list_ref[0, 1 + count + u] = 0


def first_kernel(
    col_ref, list_ref, send_ref, edge_ref, count_ref, sigma_ref,
    blocks_hbm, op_own_ref, ghost_w_ref, base_ref,
    ops_ref, zero_ref, v1_ref, b1_ref, v2_ref, up_ref, down_ref, dots_ref,
    blocks, y_ref, column_ref, g_ref, sems,
):
    wait = stream(blocks_hbm, blocks, sems)
    count = v1_ref.shape[0]
    ops_ref[OFF:HIGH] = op_own_ref[...]
    for j in range(IF):
        ops_ref[LOW + j] = make_operator(ghost_w_ref[j])
        ops_ref[HIGH + j] = make_operator(ghost_w_ref[IF + j])
    column_ref[...] = jnp.zeros_like(column_ref)
    row = lax.broadcasted_iota(jnp.int32, (ROWS, LANES), 0)
    dead = (row >= count_ref[0] + OFF) & (row < HIGH)
    for r in range(count):
        zero_ref[r] = jnp.where(dead, 0.0, base_ref[r])
        zero_ref[count + r] = base_ref[count + r]
    scatter_apply(blocks, ops_ref, zero_ref, y_ref, col_ref, column_ref, wait)
    ghost_images(ops_ref, zero_ref, g_ref)
    ghost_apply(blocks, g_ref, y_ref, col_ref, list_ref)
    inner = (row >= OFF) & (row < HIGH)
    for r in range(count):
        v0 = jnp.where(inner, zero_ref[r], 0.0)
        target = jnp.where(inner, zero_ref[count + r], 0.0)
        image = unpack_columns(column_ref, r)
        v1 = jnp.where(inner, pack(y_ref, r) - sigma_ref[r] * v0, 0.0)
        v1_ref[r] = v1
        b1_ref[r] = jnp.where(inner, pack(y_ref, count + r), 0.0)
        dots_ref[r, 0] = tile_sum(v0, image)
        dots_ref[r, 1] = tile_sum(v1, image)
        dots_ref[r, 8] = tile_sum(target, image)
    half = y_ref.at[pl.ds(0, count)]
    scatter_apply(blocks, ops_ref, v1_ref, half, col_ref, column_ref, nowait)
    for r in range(count):
        target = jnp.where(inner, zero_ref[count + r], 0.0)
        image = unpack_columns(column_ref, r)
        dots_ref[r, 2] = tile_sum(v1_ref[r], image)
        dots_ref[r, 9] = tile_sum(target, image)
        v2_ref[r] = pack(y_ref, r) - sigma_ref[r] * v1_ref[r]
        for d in (3, 4, 5, 6, 7, 10, 11):
            dots_ref[r, d] = jnp.zeros((8, LANES), f32)
    messages(up_ref, down_ref, v2_ref, v2_ref, send_ref)


def second_kernel(
    col_ref, list_ref, send_ref, edge_ref, sigma_ref,
    blocks_hbm, ops_ref, zero_ref, v1_ref, v2_in, low_ref, high_ref, dots_in,
    v2_ref, v3_ref, v4_ref, k3_ref, up_ref, down_ref, dots_ref,
    blocks, y_ref, column_ref, g_ref, sems,
):
    wait = stream(blocks_hbm, blocks, sems)
    count = v1_ref.shape[0]
    column_ref[...] = jnp.zeros_like(column_ref)
    v2_ref[...] = v2_in[...]
    complete(v2_ref, low_ref, high_ref, send_ref, edge_ref)
    scatter_apply(blocks, ops_ref, v2_ref, y_ref, col_ref, column_ref, wait)
    ghost_images(ops_ref, v2_ref, g_ref)
    ghost_apply(blocks, g_ref, y_ref, col_ref, list_ref)
    row = lax.broadcasted_iota(jnp.int32, (ROWS, LANES), 0)
    inner = (row >= OFF) & (row < HIGH)
    for r in range(count):
        image = unpack_columns(column_ref, r)
        v3 = jnp.where(inner, pack(y_ref, r) - sigma_ref[r] * v2_ref[r], 0.0)
        v3_ref[r] = v3
        for d in (0, 1, 2, 8, 9):
            dots_ref[r, d] = dots_in[r, d]
        dots_ref[r, 3] = tile_sum(v1_ref[r], image)
        dots_ref[r, 4] = tile_sum(v2_ref[r], image)
        dots_ref[r, 5] = tile_sum(v3, image)
        dots_ref[r, 10] = tile_sum(jnp.where(inner, zero_ref[count + r], 0.0), image)
    scatter_apply(blocks, ops_ref, v3_ref, y_ref, col_ref, column_ref, nowait)
    for r in range(count):
        image = unpack_columns(column_ref, r)
        dots_ref[r, 6] = tile_sum(v3_ref[r], image)
        dots_ref[r, 11] = tile_sum(jnp.where(inner, zero_ref[count + r], 0.0), image)
        dots_ref[r, 7] = jnp.zeros((8, LANES), f32)
        k3_ref[r] = image
        v4_ref[r] = pack(y_ref, r) - sigma_ref[r] * v3_ref[r]
    messages(up_ref, down_ref, v4_ref, v4_ref, send_ref)


def moment_kernel(send_ref, edge_ref, v4_in, k3_ref, low_ref, high_ref, dots_in, v4_ref, dots_ref):
    v4_ref[...] = v4_in[...]
    complete(v4_ref, low_ref, high_ref, send_ref, edge_ref)
    lane = lax.broadcasted_iota(jnp.int32, (8, LANES), 1)
    for r in range(v4_ref.shape[0]):
        total = jnp.zeros((8, LANES), f32)
        for d in range(12):
            part = tile_sum(v4_ref[r], k3_ref[r]) if d == 7 else dots_in[r, d]
            whole = jnp.sum(jnp.sum(part, axis=0, keepdims=True), axis=1, keepdims=True)
            total = jnp.where(lane == d, whole, total)
        dots_ref[r] = total


def third_kernel(
    col_ref, list_ref, blocks_hbm, ops_ref, v4_ref, w5_ref, blocks, y_ref, g_ref, sems
):
    wait = stream(blocks_hbm, blocks, sems)
    scatter_apply(blocks, ops_ref, v4_ref, y_ref, col_ref, None, wait)
    ghost_images(ops_ref, v4_ref, g_ref)
    ghost_apply(blocks, g_ref, y_ref, col_ref, list_ref)
    for r in range(v4_ref.shape[0]):
        w5_ref[r] = pack(y_ref, r)


TARGETS = 10


def fourth_kernel(
    col_ref, send_ref, coef_ref, scale_ref,
    blocks_hbm, ops_ref, zero_ref, v1_ref, v2_ref, v3_ref, v4_ref, w5_ref, b1_ref,
    comb_ref, rho_ref, up_ref, down_ref,
    blocks, y_ref, x_ref, sems,
):
    wait = stream(blocks_hbm, blocks, sems)
    count = v1_ref.shape[0]
    row = lax.broadcasted_iota(jnp.int32, (ROWS, LANES), 0)
    inner = (row >= OFF) & (row < HIGH)
    for r in range(count):
        parts = [zero_ref[r], v1_ref[r], v2_ref[r], v3_ref[r], v4_ref[r], w5_ref[r], zero_ref[count + r], b1_ref[r]]
        parts = [jnp.where(inner, part, 0.0) for part in parts]
        for g in range(TARGETS):
            total = coef_ref[g, 0, r] * parts[0]
            for s in range(1, 8):
                total = total + coef_ref[g, s, r] * parts[s]
            comb_ref[g, r] = total
        x_ref[r] = comb_ref[5, r]
    scatter_apply(blocks, ops_ref, x_ref, y_ref, col_ref, None, wait)
    for r in range(count):
        rho_ref[r] = comb_ref[7, r] - scale_ref[0, r] * pack(y_ref, r)
    messages(up_ref, down_ref, rho_ref, rho_ref, send_ref)


def fifth_kernel(
    col_ref, list_ref, send_ref, edge_ref, scale_ref,
    blocks_hbm, ops_ref, rho_in, comb_ref, low_ref, high_ref,
    zeta_ref, sol_ref,
    blocks, y_ref, rho_ref, column_ref, g_ref, sems,
):
    wait = stream(blocks_hbm, blocks, sems)
    count = rho_in.shape[0]
    column_ref[...] = jnp.zeros_like(column_ref)
    rho_ref[...] = rho_in[...]
    complete(rho_ref, low_ref, high_ref, send_ref, edge_ref)
    scatter_apply(blocks, ops_ref, rho_ref, y_ref, col_ref, None, wait)
    ghost_images(ops_ref, rho_ref, g_ref)
    ghost_apply(blocks, g_ref, y_ref, col_ref, list_ref)
    for r in range(count):
        change = rho_ref[r] - comb_ref[7, r]
        zeta_ref[0, r] = own((comb_ref[8, r] + scale_ref[1, r] * change - scale_ref[2, r] * pack(y_ref, r))[None])[0]
        zeta_ref[1, r] = own((comb_ref[6, r] + change)[None])[0]
    lanes = lane_ids()
    for n in range(NBLK):
        for r in range(count):
            image = jnp.sum(ops_ref[n + OFF] * comb_ref[9, r, n + OFF : n + OFF + 1, :], axis=1, keepdims=True)
            column_ref[r, :BS, :] = jnp.where(lanes == n + OFF, image, column_ref[r, :BS, :])
    for r in range(count):
        sol_ref[r] = own(unpack_columns(column_ref, r)[None])[0]


def total_over(values, axis):
    size = lax.axis_size(axis)
    if size & (size - 1):
        return lax.psum(values, axis)
    step = 1
    while step < size:
        width = min(8, size // step)
        parts = [values]
        for d in range(1, width):
            parts.append(lax.ppermute(values, axis, [(i, i ^ (d * step)) for i in range(size)]))
        while len(parts) > 1:
            parts = [parts[i] + parts[i + 1] for i in range(0, len(parts), 2)]
        values = parts[0]
        step *= width
    return values


def exchange(up, down):
    size = lax.axis_size("sub")
    rising = [(i, i + 1) for i in range(size - 1)]
    falling = [(j, i) for i, j in rising]
    return lax.ppermute(up, "sub", rising), lax.ppermute(down, "sub", falling)


def scalars(moments, products, sigma):
    zero = jnp.zeros_like(sigma)
    one = jnp.ones_like(sigma)

    def quad(poly, shifted):
        total = zero
        for i in range(ITERS):
            for j in range(ITERS):
                pair = poly[i] * poly[j]
                total = total + pair * moments[i + j]
                del pair
        return total

    def inner(first, second):
        total = zero
        for i in range(len(first)):
            for j in range(len(second)):
                if i + j < len(moments):
                    total = total + first[i] * second[j] * moments[i + j]
        return total

    def apply(poly):
        out = [zero] * (len(poly) + 1)
        for j, value in enumerate(poly):
            out[j] = out[j] + sigma * value
            out[j + 1] = out[j + 1] + value
        return out

    def add(first, second, scale):
        size = max(len(first), len(second))
        first = list(first) + [zero] * (size - len(first))
        second = list(second) + [zero] * (size - len(second))
        return [a + scale * b for a, b in zip(first, second)]

    resid = [[one]]
    direc = [[one]]
    image = []
    step, ratio, norm, curv = [], [zero], [moments[0]], []
    for i in range(ITERS):
        image.append(apply(direc[i]))
        curv.append(inner(direc[i], image[i]))
        step.append(norm[i] / curv[i])
        if i + 1 < ITERS:
            resid.append(add(resid[i], image[i], -step[i]))
            norm.append(inner(resid[i + 1], resid[i + 1]))
            ratio.append(norm[i + 1] / norm[i])
            direc.append(add(resid[i + 1], direc[i], ratio[i + 1]))
    cot = []
    for i in range(ITERS):
        total = zero
        for j, value in enumerate(resid[i]):
            total = total + value * products[j]
        cot.append(total)
    along = [cot[0]]
    for i in range(1, ITERS):
        along.append(cot[i] + ratio[i] * along[i - 1])

    def row(poly):
        return list(poly) + [zero] * (8 - len(poly))

    def scaled(first, scale):
        return [scale * a for a in first]

    target = [zero] * 6 + [one, zero]
    resid_rows = [row(poly) for poly in resid]
    image_rows = [row(poly) for poly in image]

    def resid_prod(i):
        return [norm[l] if l == i else zero for l in range(ITERS)]

    def image_prod(i):
        return [norm[i] / step[i] if l == i else (-norm[l] / step[i] if l == i + 1 else zero) for l in range(ITERS)]

    def along_dir(prod, i):
        total = prod[0]
        for l in range(1, i + 1):
            total = prod[l] + ratio[l] * total
        return total

    def operator_prod(prod):
        out = []
        for l in range(ITERS - 1):
            value = (prod[l] - prod[l + 1]) / step[l]
            if l > 0:
                value = value - ratio[l] * (prod[l - 1] - prod[l]) / step[l - 1]
            out.append(value)
        return out + [zero]

    last = ITERS - 1
    step_bar = along[last]
    curv_bar = -step_bar * step[last] / curv[last]
    dir_row = add(scaled(target, step[last]), image_rows[last], 2 * curv_bar)
    dir_prod = add(scaled(cot, step[last]), image_prod(last), 2 * curv_bar)
    norm_bar = step_bar / curv[last]
    rho_row = [zero] * 8
    rho_prod = [zero] * ITERS
    zetas = [None] * ITERS
    rho_rows = []
    for i in (2, 1, 0):
        ratio_bar = along_dir(dir_prod, i)
        full = norm_bar + ratio_bar / norm[i]
        zeta_row = add(dir_row, resid_rows[i + 1], full)
        zetas[i + 1] = zeta_row
        rho_row = add(add(rho_row, zeta_row, one), resid_rows[i + 1], full)
        rho_prod = add(add(rho_prod, dir_prod, one), resid_prod(i + 1), 2 * full)
        rho_rows.append(rho_row)
        step_bar = along[i] - (rho_prod[i] - rho_prod[i + 1]) / step[i]
        curv_bar = -step_bar * step[i] / curv[i]
        if i == 2:
            oper = [zero] * 8
            for k in range(5):
                if k < 4:
                    oper[k] = oper[k] + sigma * rho_row[k]
                    oper[k + 1] = oper[k + 1] + rho_row[k]
                else:
                    oper[5] = oper[5] + rho_row[4]
            oper[7] = rho_row[6]
        else:
            oper = [zero] * 8
        kept = add(scaled(dir_row, ratio[i + 1]), target, step[i])
        kept = add(kept, image_rows[i], 2 * curv_bar)
        dir_row = add(kept, oper, -step[i])
        oper_prod = operator_prod(rho_prod)
        dir_prod = add(add(scaled(dir_prod, ratio[i + 1]), cot, step[i]), image_prod(i), 2 * curv_bar)
        dir_prod = add(dir_prod, oper_prod, -step[i])
        norm_bar = -ratio_bar * norm[i + 1] / (norm[i] * norm[i]) + step_bar / curv[i]
    zetas[0] = add(dir_row, resid_rows[0], norm_bar)
    answer = [zero] * 8
    for i in range(ITERS):
        answer = add(answer, row(direc[i]), step[i])
    combos = [resid_rows[1], resid_rows[2], resid_rows[3], zetas[3], zetas[2], rho_rows[1], zetas[1], rho_rows[2], zetas[0], answer]
    coefs = jnp.stack([jnp.stack(combo) for combo in combos])
    scales = jnp.stack([step[1], ratio[1], step[0]])
    return coefs, scales


def vmem():
    return pl.BlockSpec(memory_space=pltpu.VMEM)


def smem():
    return pl.BlockSpec(memory_space=pltpu.SMEM)


def hbm():
    return pl.BlockSpec(memory_space=pl.ANY)


def shards(stiffness, precond, rhs_vec, cotangent, col_index, send_rows, counts):
    count = rhs_vec.shape[0]
    sub = lax.axis_index("sub")
    size = lax.axis_size("sub")
    edge = jnp.stack([sub > 0, sub + 1 < size]).astype(jnp.int32)
    sending = send_rows[0]
    base = jnp.concatenate([rhs_vec, cotangent], axis=0).reshape(2 * count, NBLK, BS)

    outgoing = jnp.take(base, sending, axis=1).transpose(1, 0, 2).reshape(2 * IF, 2 * count * BS)
    outgoing = jnp.concatenate([jnp.take(precond, sending, axis=0), outgoing], axis=1)
    before, after = exchange(outgoing[IF:], outgoing[:IF])

    diag = stiffness[:, 0, :: BS + 1]
    stats = jnp.stack([jnp.sum(precond * precond), jnp.sum(diag)])
    stats = lax.psum(stats, "sub") / (size * NBLK * BS)
    sigma = jnp.full((count,), (1.0 + stats[0]) * stats[1])

    blocks = stiffness.reshape(NBLK, K, BS, BS)
    weights = precond.reshape(NBLK, BS, BS)
    op_own = pl.pallas_call(
        prepare_kernel,
        grid=(NBLK // CHUNK,),
        in_specs=[pl.BlockSpec((CHUNK, BS, BS), lambda i: (i, 0, 0))],
        out_specs=pl.BlockSpec((CHUNK, BS, LANES), lambda i: (i, 0, 0)),
        out_shape=jax.ShapeDtypeStruct((NBLK, BS, LANES), f32),
        name="prepare",
    )(weights)
    halo_list = pl.pallas_call(
        list_kernel,
        in_specs=[smem()],
        out_specs=smem(),
        out_shape=jax.ShapeDtypeStruct((1, NBLK * K + 8), jnp.int32),
        name="halo_list",
    )(col_index)

    ghosts = jnp.concatenate([before, after], axis=0)
    ghost_w = ghosts[:, : BS * BS].reshape(2 * IF, BS, BS)
    ghost_v = ghosts[:, BS * BS :].reshape(2 * IF, 2 * count, BS).transpose(1, 0, 2)
    pads = jnp.zeros((2 * count, LOW, BS), f32)
    extended = jnp.concatenate([pads, ghost_v[:, :IF], base, ghost_v[:, IF:], pads], axis=1)
    extended = jnp.pad(extended, ((0, 0), (0, 0), (0, LANES - BS)))

    rows = jax.ShapeDtypeStruct((count, ROWS, LANES), f32)
    message = jax.ShapeDtypeStruct((count, 16, LANES), f32)
    dots = jax.ShapeDtypeStruct((count, 12, 8, LANES), f32)
    big = pltpu.VMEM((NBLK, K, BS, BS), f32)
    sems = pltpu.SemaphoreType.DMA((NBLK // CHUNK,))
    partial = lambda r: pltpu.VMEM((r, ROWS, 8, LANES), f32)
    square = pltpu.VMEM((count, LANES, LANES), f32)
    ghost_rows = lambda r: pltpu.VMEM((r, ROWS, LANES), f32)
    params = pltpu.CompilerParams(vmem_limit_bytes=40 * MIB)

    ops, zero, v1, b1, v2, up, down, dot = pl.pallas_call(
        first_kernel,
        in_specs=[smem()] * 6 + [hbm()] + [vmem()] * 3,
        out_specs=[vmem()] * 8,
        out_shape=[
            jax.ShapeDtypeStruct((ROWS, BS, LANES), f32),
            jax.ShapeDtypeStruct((2 * count, ROWS, LANES), f32),
            rows, rows, rows, message, message, dots,
        ],
        scratch_shapes=[big, partial(2 * count), square, ghost_rows(2 * count), sems],
        compiler_params=params,
        name="first",
    )(col_index, halo_list, send_rows, edge, counts, sigma, blocks, op_own, ghost_w, extended)
    low, high = exchange(up, down)

    v2, v3, v4, k3, up, down, dot = pl.pallas_call(
        second_kernel,
        in_specs=[smem()] * 5 + [hbm()] + [vmem()] * 7,
        out_specs=[vmem()] * 7,
        out_shape=[rows, rows, rows, rows, message, message, dots],
        scratch_shapes=[big, partial(count), square, ghost_rows(count), sems],
        compiler_params=params,
        name="second",
    )(col_index, halo_list, send_rows, edge, sigma, blocks, ops, zero, v1, v2, low, high, dot)
    low, high = exchange(up, down)

    v4, dot = pl.pallas_call(
        moment_kernel,
        in_specs=[smem()] * 2 + [vmem()] * 5,
        out_specs=[vmem()] * 2,
        out_shape=[rows, jax.ShapeDtypeStruct((count, 8, LANES), f32)],
        name="moments",
    )(send_rows, edge, v4, k3, low, high, dot)
    sums = total_over(dot[:, 0, :12], "sub")

    w5 = pl.pallas_call(
        third_kernel,
        in_specs=[smem()] * 2 + [hbm()] + [vmem()] * 2,
        out_specs=vmem(),
        out_shape=rows,
        scratch_shapes=[big, partial(count), ghost_rows(count), sems],
        compiler_params=params,
        name="third",
    )(col_index, halo_list, blocks, ops, v4)

    coefs, scales = scalars([sums[:, i] for i in range(8)], [sums[:, 8 + i] for i in range(4)], sigma)

    comb, rho, up, down = pl.pallas_call(
        fourth_kernel,
        in_specs=[smem()] * 4 + [hbm()] + [vmem()] * 8,
        out_specs=[vmem()] * 4,
        out_shape=[jax.ShapeDtypeStruct((TARGETS, count, ROWS, LANES), f32), rows, message, message],
        scratch_shapes=[big, partial(count), ghost_rows(count), sems],
        compiler_params=params,
        name="fourth",
    )(col_index, send_rows, coefs, scales, blocks, ops, zero, v1, v2, v3, v4, w5, b1)
    low, high = exchange(up, down)

    zeta, answer = pl.pallas_call(
        fifth_kernel,
        in_specs=[smem()] * 5 + [hbm()] + [vmem()] * 5,
        out_specs=[vmem()] * 2,
        out_shape=[
            jax.ShapeDtypeStruct((2, count, NBLK, LANES), f32),
            jax.ShapeDtypeStruct((count, NBLK, LANES), f32),
        ],
        scratch_shapes=[big, partial(count), ghost_rows(count), square, ghost_rows(count), sems],
        compiler_params=params,
        name="fifth",
    )(col_index, halo_list, send_rows, edge, scales, blocks, ops, rho, comb, low, high)

    resid = jnp.concatenate([zero[None, :count, OFF:HIGH, :BS], comb[:3, :, OFF:HIGH, :BS]], axis=0)
    adjoint = jnp.concatenate([zeta[..., :BS], comb[4:5, :, OFF:HIGH, :BS], comb[3:4, :, OFF:HIGH, :BS]], axis=0)
    mixed = jnp.einsum("irna,irnb->nab", resid, adjoint, precision=highest)
    mixed = mixed + jnp.swapaxes(mixed, 1, 2)
    grad = jnp.einsum("nab,nbc->nac", weights, mixed, precision=highest)
    grad = lax.psum(grad, "rhs")
    return answer[..., :BS].reshape(count, NBLK * BS), grad.reshape(NBLK, BS * BS)


def solution(mesh):
    in_specs = (
        P("sub", None, None),
        P("sub", None),
        P("rhs", "sub"),
        P("rhs", "sub"),
        P("sub", None),
        P("sub", None),
        P("sub"),
    )
    out_specs = (P("rhs", "sub"), P("sub", None))
    return jax.shard_map(shards, mesh=mesh, in_specs=in_specs, out_specs=out_specs, check_vma=False)
```

time: 575 us -> 338 us (0.59); the launches traced: 564 us -> 334 us
  blocking collectives: 189 us -> 13.9 us
  matrix products: 170 us -> 13.2 us
  local copies, waits for them, and re-layouts: 32.9 us -> 121 us
  Pallas kernels: 0 us -> 52.3 us
  waiting for transfers between devices: 109 us -> 65 us
  other arithmetic: 3.62 us -> 20.8 us
  starting transfers between devices: 43.3 us -> 31.7 us
    psum x13 -> x1, blocking collectives: 189 us -> 13.9 us  [shards(): stats = lax.psum(stats, 'sub') / (size * NBLK * BS)]
    dot_general x31 -> x2, matrix products: 170 us -> 13.2 us  [the longest x1 7.87 us: shards(): grad = jnp.einsum('nab,nbc->nac', weights, mixed, precision=highest)]
    pallas_call x0 -> x8, Pallas kernels: none -> 52.3 us  [the longest x1 12 us: shards(): pl.pallas_call(first_kernel, in_specs=[smem()] * 6 + [hbm()] + [vmem()] *...]
    add x1 -> x57, local copies, waits for them, and re-layouts: 0.01 us -> 45.7 us  [add(): return [a + scale * b for a, b in zip(first, second)]]
    psum x1, waiting for transfers between devices: 102 us -> 56.3 us  [shards(): grad = lax.psum(grad, 'rhs')]
    unnamed x93 -> x95, local copies, waits for them, and re-layouts: 4.05 us -> 31.1 us
    ppermute x16 -> x15, starting transfers between devices: 43.2 us -> 31.7 us  [the longest x8 22.5 us: exchange(): return (lax.ppermute(up, 'sub', rising), lax.ppermute(down, 'sub', falling))]
    add x10 -> x11, other arithmetic: 0.59 us -> 12.1 us  [the longest x10 12 us: add(): return [a + scale * b for a, b in zip(first, second)]]
  transfers between devices with their start and end apart: 17 -> 16, of which waited for: 5 -> 6; matrix products, arithmetic and copies ran while one was open for 5% -> 7% of each run, Pallas kernels for 0% -> 5%
where the time goes in v1:
time: 338 us; the launch traced here: 334 us
  local copies, waits for them, and re-layouts  121 us (36%)
  waiting for transfers between devices  65 us (19%)
  Pallas kernels  52.3 us (15%)
  starting transfers between devices  31.7 us (9%)
  other arithmetic  20.8 us (6%)
  between operations  16.6 us (5%)
  blocking collectives  13.9 us (4%)
  matrix products  13.2 us (4%)
    psum x1, waiting for transfers between devices, shards(): grad = lax.psum(grad, 'rhs')  56.3 us
    add x57, local copies, waits for them, and re-layouts, add(): return [a + scale * b for a, b in zip(first, second)]  45.7 us
    unnamed x95, local copies, waits for them, and re-layouts  31.1 us
    ppermute x8, starting transfers between devices, exchange(): return (lax.ppermute(up, 'sub', rising), lax.ppermute(down, 'sub', falling))  22.5 us
    psum x1, blocking collectives, shards(): stats = lax.psum(stats, 'sub') / (size * NBLK * BS)  13.9 us
    add x10, other arithmetic, add(): return [a + scale * b for a, b in zip(first, second)]  12 us
    pallas_call x1, Pallas kernels, shards(): pl.pallas_call(first_kernel, in_specs=[smem()] * 6 + [hbm()] + [vmem()] *...  12 us
    reshape x1, local copies, waits for them, and re-layouts, shards(): blocks = stiffness.reshape(NBLK, K, BS, BS)  10.6 us
  transfers between devices with their start and end apart: 16, of which 6 were waited for; matrix products, arithmetic and copies ran while one was open for 7% of the time, Pallas kernels for 5%

profile of v1, /device:TPU:13, one launch (start us, length us, event | category | flops | bytes accessed | tf_op | source)
XLA Modules:
  0.0 334.4 jit_solution(14378375674489947496)
XLA Ops:
  10.3 2.4 gather_fusion
  12.8 3.3 collective-permute-start
  17.2 4.2 %slice.84 = f32[48,1,96]{2,1,0:T(1,128)S(1)} slice(f32[48,4,9216]{2,1,0:T(4,128)} %param.7), slice={[0:48:1], [0:1:1], [0:9216:97]} | slice | bytes 36864 | tf_op jit(solution)/shard_map/slice | solution.py:532
  22.1 1.4 pad_maximum_fusion.6
  23.4 2.1 collective-permute-start.1
  25.6 13.9 %psum.14 = f32[2]{0:T(128)S(1)} all-reduce(f32[2]{0:T(128)S(1)} %pad_maximum_fusion.6), channel_id=1, replica_groups=mesh['sub'=8,'rhs'=4] {'sub'}, use_global_device_ids=true, to_apply=%region_2.3 | all-reduce | flops 2 | bytes 16 | tf_op jit(solution)/shard_map/psum | solution.py:534
  39.4 10.6 %reshape.15208.blocks_hbm = f32[48,4,96,96]{3,2,1,0:T(8,128)} reshape(f32[48,4,9216]{2,1,0:T(4,128)} %param.7) | data formatting | bytes 14155776 | tf_op jit(solution)/shard_map/reshape | solution.py:537
  50.0 2.3 reshape.15209.weights_ref
  53.0 5.9 %halo_list.1.list_ref = s32[1,200]{1,0:T(1,128)} custom-call(s32[48,4]{1,0:T(8,128)} %copy.259.col_ref), custom_call_target="tpu_custom_call" | custom-call | tf_op jit(solution)/shard_map/halo_list/pallas_call | solution.py:547
  58.9 6.3 %prepare.1.op_own_ref = f32[48,96,128]{2,1,0:T(8,128)} custom-call(f32[48,96,96]{2,1,0:T(8,128)} %reshape.15209.weights_ref), custom_call_target="tpu_custom_call" | custom-call | tf_op jit(solution)/shard_map/prepare/pallas_call | solution.py:539
  69.3 1.7 copy-done.4
  72.0 12.0 %first.1 = (f32[64,96,128]{2,1,0:T(8,128)S(1)}, f32[4,64,128]{2,1,0:T(8,128)S(1)}, f32[2,64,128]{2,1,0:T(8,128)S(1)}, f32[2,64,128]{2,1,0:T(8,128)S(1)}, f32[2,6...) custom-call(s32[48,4]{1,0:T(8,128)S(1)} %copy-done.6, ...), custom_call_target="tpu_custom_call" | custom-call | tf_op jit(solution)/shard_map/first/pallas_call | solution.py:572
  85.9 4.5 %collective-permute-start.2 = (f32[2,16,128]{2,1,0:T(8,128)S(1)}, f32[2,16,128]{2,1,0:T(8,128)S(1)}, u32[]{:S(2)}, u32[]{:S(2)}) collective-permute-start(f32[2,16,128]{2,1,0:T(8,128)S(1)} %get-tuple-element.29), channel_id=1, source_target_pairs={{0,4},{4,8},{8,12},{12,16},{16,20},{20,24},{24,28},{1,5},{5,9},{9,... | collective-permute-start | bytes 49160 | tf_op jit(solution)/shard_map/ppermute | solution.py:369
  90.3 1.9 collective-permute-start.3
  92.9 2.8 collective-permute-done.3.high_ref
  95.7 3.7 %copy-done = f32[48,4,96,96]{3,2,1,0:T(8,128)S(1)} copy-done((f32[48,4,96,96]{3,2,1,0:T(8,128)S(1)}, f32[48,4,96,96]{3,2,1,0:T(8,128)}, u32[]{:S(2)}) %copy-start) | copy-done | bytes 7077912
  101.1 8.6 %second.1 = (f32[2,64,128]{2,1,0:T(8,128)S(1)}, f32[2,64,128]{2,1,0:T(8,128)S(1)}, f32[2,64,128]{2,1,0:T(8,128)S(1)}, f32[2,64,128]{2,1,0:T(8,128)S(1)}, f32[2,1...) custom-call(s32[48,4]{1,0:T(8,128)S(1)} %copy-done.6, s32[1,200]{1,0:T(1,128)S(1)} %copy-done.21, ...), custom_call_target="tpu_custom_call" | custom-call | tf_op jit(solution)/shard_map/second/pallas_call | solution.py:587
  112.2 2.0 collective-permute-start.4
  114.2 3.5 %collective-permute-start.5 = (f32[2,16,128]{2,1,0:T(8,128)S(1)}, f32[2,16,128]{2,1,0:T(8,128)S(1)}, u32[]{:S(2)}, u32[]{:S(2)}) collective-permute-start(f32[2,16,128]{2,1,0:T(8,128)S(1)} %get-tuple-element.35), channel_id=1, source_target_pairs={{4,0},{8,4},{12,8},{16,12},{20,16},{24,20},{28,24},{5,1},{9,5},{13... | collective-permute-start | bytes 49160 | tf_op jit(solution)/shard_map/ppermute | solution.py:369
  118.3 1.4 collective-permute-done.5.high_ref
  120.4 1.8 moments.1
  126.2 3.8 %collective-permute-start.7 = (f32[2,12]{1,0:T(2,128)S(1)}, f32[2,12]{1,0:T(2,128)S(1)}, u32[]{:S(2)}, u32[]{:S(2)}) collective-permute-start(f32[2,12]{1,0:T(2,128)S(1)} %bitcast.532), channel_id=1, source_target_pairs={{0,8},{4,12},{8,0},{12,4},{16,24},{20,28},{24,16},{28,20},{1,9},{5... | collective-permute-start | bytes 296 | tf_op jit(solution)/shard_map/ppermute | solution.py:357
  130.0 3.7 %copy-done.1 = f32[48,4,96,96]{3,2,1,0:T(8,128)S(1)} copy-done((f32[48,4,96,96]{3,2,1,0:T(8,128)S(1)}, f32[48,4,96,96]{3,2,1,0:T(8,128)}, u32[]{:S(2)}) %copy-start.1) | copy-done | bytes 7077912
  134.5 5.3 %third.1.w5_ref = f32[2,64,128]{2,1,0:T(8,128)S(1)} custom-call(s32[48,4]{1,0:T(8,128)S(1)} %copy-done.6, s32[1,200]{1,0:T(1,128)S(1)} %copy-done.21, f32[48,4,96,96]{3,2,1,0:T(8,128)S(1)} %copy-done.1, f32[64,96,128]{2,1,0:T(8,128)S(1)} %get-tuple-element.25.ops_ref, f32[2,64,128]{2,1,0:T(8,128)S(1)} %copy-done.7), custom_call_target="tpu_custom_call" | custom-call | tf_op jit(solution)/shard_map/third/pallas_call | solution.py:607
  140.4 1.5 collective-permute-start.9
  142.0 1.3 collective-permute-done.8
  146.7 1.3 copy.189
  147.9 1.3 copy.190
  149.2 1.2 copy.183
  150.5 1.2 copy.184
  152.4 1.2 copy.181
  155.9 1.3 add_add_fusion.2
  157.2 1.3 add_add_fusion.4
  158.5 1.3 add_add_fusion.3
  159.8 1.2 add_add_fusion.10
  161.0 1.3 copy.196
  162.3 1.3 copy.195
  163.6 1.2 copy.197
  164.8 1.4 add_add_fusion.11
  166.2 1.2 add_add_fusion.7
  167.4 1.2 add_add_fusion.8
  168.7 1.2 add_add_fusion.9
  178.4 1.2 copy.238
  180.4 1.3 add_add_fusion.15
  190.9 1.2 copy.222
  197.3 1.2 copy.210
  198.5 1.3 copy.214
  204.1 1.3 copy.205
  206.6 1.3 copy.206
  214.2 1.3 copy.182
  216.4 3.7 %copy-done.2 = f32[48,4,96,96]{3,2,1,0:T(8,128)S(1)} copy-done((f32[48,4,96,96]{3,2,1,0:T(8,128)S(1)}, f32[48,4,96,96]{3,2,1,0:T(8,128)}, u32[]{:S(2)}) %copy-start.2) | copy-done | bytes 7077912
  222.6 5.4 %fourth.1 = (f32[10,2,64,128]{3,2,1,0:T(8,128)S(1)}, f32[2,64,128]{2,1,0:T(8,128)S(1)}, f32[2,16,128]{2,1,0:T(8,128)S(1)}, f32[2,16,128]{2,1,0:T(8,128)S(1)}) custom-call(s32[48,4]{1,0:T(8,128)S(1)} %copy-done.6, s32[1,12]{1,0:T(1,128)S(1)} %copy-done.23, f32[10,8,2]{2,1,0:T(8,128)S(1)} %constant_dynamic-update-slice_fusion.coef_ref, ...), custom_call_target="tpu_custom_call" | custom-call | tf_op jit(solution)/shard_map/fourth/pallas_call | solution.py:619
  228.1 2.5 collective-permute-start.13
  230.6 2.7 collective-permute-start.14
  233.4 2.6 collective-permute-done.14.high_ref
  236.0 3.7 %copy-done.3 = f32[48,4,96,96]{3,2,1,0:T(8,128)S(1)} copy-done((f32[48,4,96,96]{3,2,1,0:T(8,128)S(1)}, f32[48,4,96,96]{3,2,1,0:T(8,128)}, u32[]{:S(2)}) %copy-start.3) | copy-done | bytes 7077912
  239.7 7.0 %fifth.1 = (f32[2,2,48,128]{3,2,1,0:T(8,128)S(1)}, f32[2,48,128]{2,1,0:T(8,128)S(1)}) custom-call(s32[48,4]{1,0:T(8,128)S(1)} %copy-done.6, s32[1,200]{1,0:T(1,128)S(1)} %copy-done.21, s32[1,12]{1,0:T(1,128)S(1)} %copy-done.23, s32[2]{0:T(128)S(1)} %copy-done.25, f32[3,2]{1,0:T(4,128)S(1)} %pad_maximum_fusion.5.scale_ref, f32[48,4,96,96]{3,2,1,0:T(8,128)S(1)} %copy-done.3, ...), custom_call_target="tpu_custom_call" | custom-call | tf_op jit(solution)/shard_map/fifth/pallas_call | solution.py:630
  246.7 5.3 %convolution_bitcast_fusion = f32[48,96,96]{2,1,0:T(8,128)} fusion(f32[4,2,48,96]{3,2,1,0:T(8,128)S(1)} %pad_maximum_fusion.2, f32[4,2,48,96]{3,2,1,0:T(8,128)S(1)} %pad_maximum_fusion.1), kind=kOutput, calls=%fused_computation.6 | convolution fusion | flops 42467328 | bytes 2064384 | tf_op jit(solution)/shard_map/irna,irnb->nab/dot_general | solution.py:645
  252.0 3.2 copy.262
  255.2 7.9 %fusion.1 = f32[48,96,96]{1,2,0:T(8,128)} fusion(f32[48,96,96]{2,1,0:T(8,128)S(1)} %copy-done.27, f32[48,96,96]{2,1,0:T(8,128)} %convolution_bitcast_fusion, f32[48,96,96]{1,2,0:T(8,128)} %copy.262), kind=kOutput, calls=%fused_computation.5 | convolution fusion | flops 510050304 | bytes 7077888 | tf_op jit(solution)/shard_map/nab,nbc->nac/dot_general | solution.py:647
  263.1 2.0 copy.264
  265.1 2.5 reshape.15215
  268.4 56.3 %all-reduce.3.cloned.1.call-done = f32[48,9216]{1,0:T(8,128)} async-done(((f32[48,9216]{1,0:T(8,128)}), f32[48,9216]{1,0:T(8,128)}) %all-reduce.3.cloned.1.call-update) | async-done | bytes 1769488 | tf_op jit(solution)/shard_map/psum | solution.py:648
  324.8 2.8 copy.287
  (218 shorter events, 68.1 us)
Async XLA Ops:
  7.2 317.6 %all-reduce.3.cloned.1.call-start = ((), (), s32[]{:S(2)}) async-start(), calls=%async_computation | async-start | bytes 3538944 | tf_op jit(solution)/shard_map/psum | solution.py:648
  12.7 3.5 %copy-start.26 = (f32[48,9216]{1,0:T(8,128)S(1)}, f32[48,9216]{1,0:T(8,128)}, u32[]{:S(2)}) copy-start(f32[48,9216]{1,0:T(8,128)} %param.8) | copy-start | bytes 5308420
  12.8 55.1 %collective-permute-start = (f32[6,9600]{1,0:T(8,128)S(1)}, f32[6,9600]{1,0:T(8,128)S(1)}, u32[]{:S(2)}, u32[]{:S(2)}) collective-permute-start(f32[6,9600]{1,0:T(8,128)S(1)} %get-tuple-element.176), channel_id=1, source_target_pairs={{0,4},{4,8},{8,12},{12,16},{16,20},{20,24},{24,28},{1,5},{5,9},{9,... | collective-permute-start | bytes 691208 | tf_op jit(solution)/shard_map/ppermute | solution.py:369
  23.4 44.5 %collective-permute-start.1 = (f32[6,9600]{1,0:T(8,128)S(1)}, f32[6,9600]{1,0:T(8,128)S(1)}, u32[]{:S(2)}, u32[]{:S(2)}) collective-permute-start(f32[6,9600]{1,0:T(8,128)S(1)} %get-tuple-element.175), channel_id=1, source_target_pairs={{4,0},{8,4},{12,8},{16,12},{20,16},{24,20},{28,24},{5,1},{9,5},{13... | collective-permute-start | bytes 691208 | tf_op jit(solution)/shard_map/ppermute | solution.py:369
  50.0 2.3 copy-start.41
  65.2 4.0 %copy-start.6 = (s32[48,4]{1,0:T(8,128)S(1)}, s32[48,4]{1,0:T(8,128)}, u32[]{:S(2)}) copy-start(s32[48,4]{1,0:T(8,128)} %copy.259.col_ref) | copy-start | bytes 2308
  65.2 4.0 %copy-start.21 = (s32[1,200]{1,0:T(1,128)S(1)}, s32[1,200]{1,0:T(1,128)}, u32[]{:S(2)}) copy-start(s32[1,200]{1,0:T(1,128)} %halo_list.1.list_ref) | copy-start | bytes 2404
  65.2 4.0 %copy-start.22 = (s32[1,12]{1,0:T(1,128)S(1)}, s32[1,12]{1,0:T(1,128)}, u32[]{:S(2)}) copy-start(s32[1,12]{1,0:T(1,128)} %send_ref.9) | copy-start | bytes 148
  67.9 27.8 %copy-start.24 = (s32[2]{0:T(128)}, s32[2]{0:T(128)S(1)}, u32[]{:S(2)}) copy-start(s32[2]{0:T(128)S(1)} %add_convert_fusion.edge_ref) | copy-start | bytes 28
  69.3 1.7 copy-start.4
  70.9 1.1 copy-start.5
  84.0 0.6 copy-start.8
  84.6 0.6 copy-start.11
  85.2 0.6 copy-start.17
  85.9 7.1 %collective-permute-start.2 = (f32[2,16,128]{2,1,0:T(8,128)S(1)}, f32[2,16,128]{2,1,0:T(8,128)S(1)}, u32[]{:S(2)}, u32[]{:S(2)}) collective-permute-start(f32[2,16,128]{2,1,0:T(8,128)S(1)} %get-tuple-element.29), channel_id=1, source_target_pairs={{0,4},{4,8},{8,12},{12,16},{16,20},{20,24},{24,28},{1,5},{5,9},{9,... | collective-permute-start | bytes 49160 | tf_op jit(solution)/shard_map/ppermute | solution.py:369
  90.3 5.4 %collective-permute-start.3 = (f32[2,16,128]{2,1,0:T(8,128)S(1)}, f32[2,16,128]{2,1,0:T(8,128)S(1)}, u32[]{:S(2)}, u32[]{:S(2)}) collective-permute-start(f32[2,16,128]{2,1,0:T(8,128)S(1)} %get-tuple-element.30), channel_id=1, source_target_pairs={{4,0},{8,4},{12,8},{16,12},{20,16},{24,20},{28,24},{5,1},{9,5},{13... | collective-permute-start | bytes 49160 | tf_op jit(solution)/shard_map/ppermute | solution.py:369
  95.7 3.7 %copy-start = (f32[48,4,96,96]{3,2,1,0:T(8,128)S(1)}, f32[48,4,96,96]{3,2,1,0:T(8,128)}, u32[]{:S(2)}) copy-start(f32[48,4,96,96]{3,2,1,0:T(8,128)} %reshape.15208.blocks_hbm) | copy-start | bytes 21233668
  99.4 0.9 copy-start.9
  100.3 0.8 copy-start.18
  109.8 0.6 copy-start.13
  110.4 0.6 copy-start.15
  111.0 0.6 copy-start.19
  111.6 0.6 copy-start.20
  112.2 7.5 %copy-start.10 = (f32[2,12,8,128]{3,2,1,0:T(8,128)}, f32[2,12,8,128]{3,2,1,0:T(8,128)S(1)}, u32[]{:S(2)}) copy-start(f32[2,12,8,128]{3,2,1,0:T(8,128)S(1)} %get-tuple-element.36.dots_in) | copy-start | bytes 294916
  112.2 6.1 %collective-permute-start.4 = (f32[2,16,128]{2,1,0:T(8,128)S(1)}, f32[2,16,128]{2,1,0:T(8,128)S(1)}, u32[]{:S(2)}, u32[]{:S(2)}) collective-permute-start(f32[2,16,128]{2,1,0:T(8,128)S(1)} %get-tuple-element.34), channel_id=1, source_target_pairs={{0,4},{4,8},{8,12},{12,16},{16,20},{20,24},{24,28},{1,5},{5,9},{9,... | collective-permute-start | bytes 49160 | tf_op jit(solution)/shard_map/ppermute | solution.py:369
  114.2 5.5 %collective-permute-start.5 = (f32[2,16,128]{2,1,0:T(8,128)S(1)}, f32[2,16,128]{2,1,0:T(8,128)S(1)}, u32[]{:S(2)}, u32[]{:S(2)}) collective-permute-start(f32[2,16,128]{2,1,0:T(8,128)S(1)} %get-tuple-element.35), channel_id=1, source_target_pairs={{4,0},{8,4},{12,8},{16,12},{20,16},{24,20},{28,24},{5,1},{9,5},{13... | collective-permute-start | bytes 49160 | tf_op jit(solution)/shard_map/ppermute | solution.py:369
  118.3 1.4 copy-start.31
  119.8 0.6 copy-start.32
  122.9 16.9 %collective-permute-start.10 = (f32[2,12]{1,0:T(2,128)S(1)}, f32[2,12]{1,0:T(2,128)S(1)}, u32[]{:S(2)}, u32[]{:S(2)}) collective-permute-start(f32[2,12]{1,0:T(2,128)S(1)} %bitcast.528), channel_id=1, source_target_pairs={{0,20},{4,16},{8,28},{12,24},{16,4},{20,0},{24,12},{28,8},{1,21},{... | collective-permute-start | bytes 296 | tf_op jit(solution)/shard_map/ppermute | solution.py:357
  123.5 16.9 %collective-permute-start.11 = (f32[2,12]{1,0:T(2,128)S(1)}, f32[2,12]{1,0:T(2,128)S(1)}, u32[]{:S(2)}, u32[]{:S(2)}) collective-permute-start(f32[2,12]{1,0:T(2,128)S(1)} %bitcast.529), channel_id=1, source_target_pairs={{0,24},{4,28},{8,16},{12,20},{16,8},{20,12},{24,0},{28,4},{1,25},{... | collective-permute-start | bytes 296 | tf_op jit(solution)/shard_map/ppermute | solution.py:357
  124.5 17.5 %collective-permute-start.12 = (f32[2,12]{1,0:T(2,128)S(1)}, f32[2,12]{1,0:T(2,128)S(1)}, u32[]{:S(2)}, u32[]{:S(2)}) collective-permute-start(f32[2,12]{1,0:T(2,128)S(1)} %bitcast.530), channel_id=1, source_target_pairs={{0,28},{4,24},{8,20},{12,16},{16,12},{20,8},{24,4},{28,0},{1,29},{... | collective-permute-start | bytes 296 | tf_op jit(solution)/shard_map/ppermute | solution.py:357
  125.1 16.9 %collective-permute-start.6 = (f32[2,12]{1,0:T(2,128)S(1)}, f32[2,12]{1,0:T(2,128)S(1)}, u32[]{:S(2)}, u32[]{:S(2)}) collective-permute-start(f32[2,12]{1,0:T(2,128)S(1)} %bitcast.531), channel_id=1, source_target_pairs={{0,4},{4,0},{8,12},{12,8},{16,20},{20,16},{24,28},{28,24},{1,5},{5... | collective-permute-start | bytes 296 | tf_op jit(solution)/shard_map/ppermute | solution.py:357
  126.2 15.8 %collective-permute-start.7 = (f32[2,12]{1,0:T(2,128)S(1)}, f32[2,12]{1,0:T(2,128)S(1)}, u32[]{:S(2)}, u32[]{:S(2)}) collective-permute-start(f32[2,12]{1,0:T(2,128)S(1)} %bitcast.532), channel_id=1, source_target_pairs={{0,8},{4,12},{8,0},{12,4},{16,24},{20,28},{24,16},{28,20},{1,9},{5... | collective-permute-start | bytes 296 | tf_op jit(solution)/shard_map/ppermute | solution.py:357
  130.0 3.7 %copy-start.1 = (f32[48,4,96,96]{3,2,1,0:T(8,128)S(1)}, f32[48,4,96,96]{3,2,1,0:T(8,128)}, u32[]{:S(2)}) copy-start(f32[48,4,96,96]{3,2,1,0:T(8,128)} %reshape.15208.blocks_hbm) | copy-start | bytes 21233668
  133.7 0.8 copy-start.7
  134.5 81.9 %copy-start.23 = (s32[1,12]{1,0:T(1,128)S(1)}, s32[1,12]{1,0:T(1,128)}, u32[]{:S(2)}) copy-start(s32[1,12]{1,0:T(1,128)} %send_ref.9) | copy-start | bytes 148
  139.9 3.4 %collective-permute-start.8 = (f32[2,12]{1,0:T(2,128)S(1)}, f32[2,12]{1,0:T(2,128)S(1)}, u32[]{:S(2)}, u32[]{:S(2)}) collective-permute-start(f32[2,12]{1,0:T(2,128)S(1)} %bitcast.533), channel_id=1, source_target_pairs={{0,12},{4,8},{8,4},{12,0},{16,28},{20,24},{24,20},{28,16},{1,13},{... | collective-permute-start | bytes 296 | tf_op jit(solution)/shard_map/ppermute | solution.py:357
  140.4 3.3 collective-permute-start.9
  144.6 9.8 %copy-start.35 = (f32[2]{0:T(128)}, f32[2]{0:T(128)S(1)}, u32[]{:S(2)}) copy-start(f32[2]{0:T(128)S(1)} %get-tuple-element.51) | copy-start | bytes 28
  144.6 10.6 %copy-start.33 = (f32[2]{0:T(128)}, f32[2]{0:T(128)S(1)}, u32[]{:S(2)}) copy-start(f32[2]{0:T(128)S(1)} %get-tuple-element.59) | copy-start | bytes 28
  145.3 8.3 %copy-start.38 = (f32[1,2]{1,0:T(1,128)}, f32[1,2]{1,0:T(1,128)S(1)}, u32[]{:S(2)}) copy-start(f32[1,2]{1,0:T(1,128)S(1)} %get-tuple-element.71) | copy-start | bytes 28
  145.3 8.3 %copy-start.39 = (f32[1,2]{1,0:T(1,128)}, f32[1,2]{1,0:T(1,128)S(1)}, u32[]{:S(2)}) copy-start(f32[1,2]{1,0:T(1,128)S(1)} %get-tuple-element.72) | copy-start | bytes 28
  145.3 8.3 %copy-start.40 = (f32[1,2]{1,0:T(1,128)}, f32[1,2]{1,0:T(1,128)S(1)}, u32[]{:S(2)}) copy-start(f32[1,2]{1,0:T(1,128)S(1)} %get-tuple-element.80) | copy-start | bytes 28
  155.2 5.8 %copy-start.36 = (f32[1,2]{1,0:T(1,128)}, f32[1,2]{1,0:T(1,128)S(1)}, u32[]{:S(2)}) copy-start(f32[1,2]{1,0:T(1,128)S(1)} %get-tuple-element.158) | copy-start | bytes 28
  155.9 3.8 %copy-start.34 = (f32[1,2]{1,0:T(1,128)}, f32[1,2]{1,0:T(1,128)S(1)}, u32[]{:S(2)}) copy-start(f32[1,2]{1,0:T(1,128)S(1)} %get-tuple-element.133) | copy-start | bytes 28
  157.2 1.3 copy-start.29
  157.2 2.6 copy-start.30
  168.6 1.2 copy-start.37
  216.4 3.7 %copy-start.2 = (f32[48,4,96,96]{3,2,1,0:T(8,128)S(1)}, f32[48,4,96,96]{3,2,1,0:T(8,128)}, u32[]{:S(2)}) copy-start(f32[48,4,96,96]{3,2,1,0:T(8,128)} %reshape.15208.blocks_hbm) | copy-start | bytes 21233668
  220.1 0.8 copy-start.12
  220.9 0.8 copy-start.14
  221.8 0.8 copy-start.16
  222.6 10.7 %copy-start.28 = (f32[1,2,48,96]{3,2,1,0:T(8,128)S(1)}, f32[1,2,48,96]{3,2,1,0:T(8,128)}, u32[]{:S(2)}) copy-start(f32[1,2,48,96]{3,2,1,0:T(8,128)} %slice_bitcast_fusion) | copy-start | bytes 110596
  222.6 13.4 %copy-start.25 = (s32[2]{0:T(128)S(1)}, s32[2]{0:T(128)}, u32[]{:S(2)}) copy-start(s32[2]{0:T(128)} %copy-done.24) | copy-start | bytes 28
  228.1 5.3 %collective-permute-start.13 = (f32[2,16,128]{2,1,0:T(8,128)S(1)}, f32[2,16,128]{2,1,0:T(8,128)S(1)}, u32[]{:S(2)}, u32[]{:S(2)}) collective-permute-start(f32[2,16,128]{2,1,0:T(8,128)S(1)} %get-tuple-element.44), channel_id=1, source_target_pairs={{0,4},{4,8},{8,12},{12,16},{16,20},{20,24},{24,28},{1,5},{5,9},{9,... | collective-permute-start | bytes 49160 | tf_op jit(solution)/shard_map/ppermute | solution.py:369
  230.6 5.4 %collective-permute-start.14 = (f32[2,16,128]{2,1,0:T(8,128)S(1)}, f32[2,16,128]{2,1,0:T(8,128)S(1)}, u32[]{:S(2)}, u32[]{:S(2)}) collective-permute-start(f32[2,16,128]{2,1,0:T(8,128)S(1)} %get-tuple-element.45), channel_id=1, source_target_pairs={{4,0},{8,4},{12,8},{16,12},{20,16},{24,20},{28,24},{5,1},{9,5},{13... | collective-permute-start | bytes 49160 | tf_op jit(solution)/shard_map/ppermute | solution.py:369
  236.0 3.7 %copy-start.3 = (f32[48,4,96,96]{3,2,1,0:T(8,128)S(1)}, f32[48,4,96,96]{3,2,1,0:T(8,128)}, u32[]{:S(2)}) copy-start(f32[48,4,96,96]{3,2,1,0:T(8,128)} %reshape.15208.blocks_hbm) | copy-start | bytes 21233668
  252.0 3.2 copy-start.27
Sparse Core Ops, SparseCore 0:
  267.8 56.8 all-reduce.2

commit v2 on v1

v2 whole, which is shorter than its diff:
```python
import functools

import jax
import jax.numpy as jnp
from jax import lax
from jax.experimental import pallas as pl
from jax.experimental.pallas import tpu as pltpu
from jax.sharding import PartitionSpec as P

BS = 96
K = 4
NBLK = 48
IF = 6
ITERS = 4
EARLY = 16
LATE = 4
CUTS = BS * BS // 128
LANES = 128
OFF = 8
ROWS = 64
LOW = OFF - IF
HIGH = OFF + NBLK
CHUNK = 8
MIB = 1024 * 1024

highest = lax.Precision.HIGHEST
f32 = jnp.float32


def own(value):
    return value[:, OFF:HIGH]


def lane_ids():
    return lax.broadcasted_iota(jnp.int32, (BS, LANES), 1)


def diagonal():
    pos = lax.broadcasted_iota(jnp.int32, (BS, LANES), 0)
    row = (pos & ~31) + 4 * (pos & 7) + ((pos >> 3) & 3)
    return row == lane_ids()


def fold(prod):
    return jnp.sum(prod.reshape(BS // 8, 8, prod.shape[-1]), axis=0)


def unflatten(read):
    lane = lax.broadcasted_iota(jnp.int32, (8, LANES), 1)
    out = []
    for h in range(BS // 32):
        one, two, three = (read(24 * h + m) for m in range(3))
        out.append(jnp.where(lane < BS, one, 0.0))
        mixed = jnp.where(lane < 32, pltpu.roll(one, 32, 1), pltpu.roll(two, 32, 1))
        out.append(jnp.where(lane < BS, mixed, 0.0))
        mixed = jnp.where(lane < 64, pltpu.roll(two, 64, 1), pltpu.roll(three, 64, 1))
        out.append(jnp.where(lane < BS, mixed, 0.0))
        out.append(jnp.where(lane < BS, pltpu.roll(three, 96, 1), 0.0))
    return jnp.concatenate(out, axis=0)


def flatten(block, write):
    lane = lax.broadcasted_iota(jnp.int32, (8, LANES), 1)
    for h in range(BS // 32):
        one, two, three, four = (block[32 * h + 8 * j : 32 * h + 8 * j + 8] for j in range(4))
        two = pltpu.roll(two, 96, 1)
        three = pltpu.roll(three, 64, 1)
        write(24 * h, jnp.where(lane < BS, one, two))
        write(24 * h + 1, jnp.where(lane < 64, two, three))
        write(24 * h + 2, jnp.where(lane < 32, three, pltpu.roll(four, 32, 1)))


def make_operator(weights, gram_ref):
    gram = lax.dot_general(
        weights, weights, (((0,), (0,)), ((), ())), precision=highest, preferred_element_type=f32
    )
    gram_ref[...] = gram[:BS]
    rows = [gram_ref[pl.ds(32 * h + j, 8, stride=4), :] for h in range(BS // 32) for j in range(4)]
    return jnp.concatenate(rows, axis=0) + jnp.where(diagonal(), 1.0, 0.0)


def scatter_apply(blocks, op_ref, x_ref, y_ref, col_ref, column_ref):
    count = x_ref.shape[0]
    y_ref[...] = jnp.zeros_like(y_ref)

    def step(group, carry):
        base = pl.multiple_of(group * CHUNK, CHUNK)
        tiles = [x_ref[r, pl.ds(base + OFF, CHUNK), :] for r in range(count)]
        for i in range(CHUNK):
            n = group * CHUNK + i
            oper = op_ref[n + OFF]
            images = [jnp.sum(oper * tiles[r][i : i + 1, :], axis=1, keepdims=True) for r in range(count)]
            if column_ref is not None:
                for r in range(column_ref.shape[0]):
                    column_ref[r] = jnp.where(lane_ids() == n + OFF, images[r], column_ref[r])
            for k in range(K):
                block = blocks[n, k]
                slot = col_ref[k, n] + LOW
                for r in range(count):
                    y_ref[r, slot] = y_ref[r, slot] + fold(block * images[r])
        return carry

    lax.fori_loop(0, NBLK // CHUNK, step, 0)


def ghost_images(op_ref, x_ref, g_ref):
    count = x_ref.shape[0]
    mask = diagonal()
    g_ref[...] = jnp.zeros_like(g_ref)
    for first in (LOW, HIGH):
        for j in range(IF):
            slot = first + j
            oper = op_ref[slot]
            for r in range(count):
                image = jnp.sum(oper * x_ref[r, slot : slot + 1, :], axis=1, keepdims=True)
                line = jnp.sum(fold(jnp.where(mask, image, 0.0)), axis=0, keepdims=True)
                g_ref[r, slot : slot + 1, :] = line


def ghost_apply(blocks, g_ref, y_ref, col_ref, list_ref):
    count = g_ref.shape[0]
    mask = diagonal()

    def step(item, carry):
        for u in range(4):
            entry = list_ref[0, 1 + item * 4 + u]
            n = entry >> 2
            k = entry & 3
            slot = col_ref[k, n] + LOW
            block = blocks[n, k]
            for r in range(count):
                image = jnp.sum(block * g_ref[r, pl.ds(slot, 1), :], axis=1, keepdims=True)
                y_ref[r, n + OFF] = y_ref[r, n + OFF] + fold(jnp.where(mask, image, 0.0))
        return carry

    lax.fori_loop(0, (list_ref[0, 0] + 3) >> 2, step, 0)


def pack(y_ref, r):
    sub = lax.broadcasted_iota(jnp.int32, (8, LANES), 0)
    groups = []
    for g in range(ROWS // 8):
        total = jnp.zeros((8, LANES), f32)
        for i in range(8):
            line = jnp.sum(y_ref[r, g * 8 + i], axis=0, keepdims=True)
            total = jnp.where(sub == i, line, total)
        groups.append(total)
    return jnp.concatenate(groups, axis=0)


def unpack_columns(column_ref, square_ref, r):
    for h in range(BS // 32):
        for j in range(4):
            start = 32 * h + 8 * j
            square_ref[pl.ds(32 * h + j, 8, stride=4), :] = column_ref[r, start : start + 8, :]
    square_ref[BS:, :] = jnp.zeros((LANES - BS, LANES), f32)
    return square_ref[...].T[:ROWS]


def messages(up_ref, down_ref, v_ref, send_ref, extra_ref=None):
    for r in range(v_ref.shape[0]):
        for j in range(IF):
            low = pl.ds(send_ref[0, j] + OFF, 1)
            high = pl.ds(send_ref[0, IF + j] + OFF, 1)
            down_ref[r, j : j + 1, :] = v_ref[r, low, :]
            up_ref[r, j : j + 1, :] = v_ref[r, high, :]
            down_ref[r, 8 + j : 9 + j, :] = v_ref[r, LOW + j : LOW + j + 1, :]
            up_ref[r, 8 + j : 9 + j, :] = v_ref[r, HIGH + j : HIGH + j + 1, :]
            if extra_ref is not None:
                down_ref[r, 16 + j : 17 + j, :] = extra_ref[r, low, :]
                up_ref[r, 16 + j : 17 + j, :] = extra_ref[r, high, :]


def complete(v_ref, low_ref, high_ref, send_ref, edge_ref):
    for r in range(v_ref.shape[0]):
        for j in range(IF):
            for part, base, ghost, flag in ((low_ref, 0, LOW, 0), (high_ref, IF, HIGH, 1)):
                at = pl.ds(send_ref[0, base + j] + OFF, 1)
                v_ref[r, at, :] = v_ref[r, at, :] + part[r, 8 + j : 9 + j, :]
                slot = ghost + j
                summed = v_ref[r, slot : slot + 1, :] + part[r, j : j + 1, :]
                v_ref[r, slot : slot + 1, :] = jnp.where(edge_ref[flag] > 0, summed, 0.0)


def tile_sum(first, second):
    prod = first * second
    return jnp.sum(prod.reshape(prod.shape[0] // 8, 8, LANES), axis=0)


def whole_sum(tile):
    return jnp.sum(jnp.sum(tile, axis=0, keepdims=True), axis=1, keepdims=True)


def inner_rows():
    row = lax.broadcasted_iota(jnp.int32, (ROWS, LANES), 0)
    return (row >= OFF) & (row < HIGH)


def pack_kernel(send_ref, raw_ref, base_ref, up_ref, down_ref):
    for part, ref in ((0, down_ref), (IF, up_ref)):
        for j in range(IF):
            n = send_ref[0, part + j]
            start = (n >> 3) * (8 * CUTS) + (n & 7)
            for i in range(CUTS // 8):
                ref[j, 8 * i : 8 * i + 8, :] = raw_ref[pl.ds(start + 64 * i, 8, stride=8), :]
            ref[j, CUTS:, :] = jnp.zeros((8, LANES), f32)
            for r in range(base_ref.shape[0]):
                ref[j, CUTS + r : CUTS + r + 1, :] = base_ref[r, pl.ds(n + OFF, 1), :]


def prepare_kernel(col_ref, stiff_ref, raw_ref, blocks_ref, weights_ref, ops_ref, list_ref, stats_ref, gram_ref):
    mask = diagonal()

    def step(group, carry):
        count, squares, traces = carry
        for i in range(CHUNK):
            n = group * CHUNK + i
            for k in range(K):
                block = unflatten(lambda q: stiff_ref[pl.ds(n * (CUTS * K) + 4 * q + k, 8, stride=12), :])
                blocks_ref[n, k] = block
                if k == 0:
                    traces = traces + fold(jnp.where(mask, block, 0.0))
                col = col_ref[k, n]
                list_ref[0, 1 + count] = n * K + k
                count = count + jnp.where((col < IF) | (col >= IF + NBLK), 1, 0)
            weights = unflatten(lambda q: raw_ref[pl.ds(group * (8 * CUTS) + 8 * q + i, 8, stride=24), :])
            weights_ref[n] = weights
            squares = squares + fold(weights * weights)
            ops_ref[n] = make_operator(weights, gram_ref.at[i & 1])
        return count, squares, traces

    blank = jnp.zeros((8, LANES), f32)
    count, squares, traces = lax.fori_loop(0, NBLK // CHUNK, step, (jnp.int32(0), blank, blank))
    list_ref[0, 0] = count
    for u in range(4):
        list_ref[0, 1 + count + u] = 0
    stats_ref[:8] = squares
    stats_ref[8:] = traces


def first_kernel(
    col_ref, list_ref, send_ref, edge_ref, count_ref,
    blocks, op_own_ref, base_ref, low_ref, high_ref,
    ops_ref, zero_ref, a1_ref, b1_ref, a2_ref, k0_ref, k1_ref, up_ref, down_ref,
    y_ref, column_ref, square_ref, g_ref, gram_ref,
):
    count = a1_ref.shape[0]
    ops_ref[OFF:HIGH] = op_own_ref[...]
    zero_ref[...] = base_ref[...]
    for part, first in ((low_ref, LOW), (high_ref, HIGH)):
        for j in range(IF):
            weights = unflatten(lambda q: part[j, pl.ds(q, 8, stride=3), :])
            ops_ref[first + j] = make_operator(weights, gram_ref.at[j & 1])
            for r in range(2 * count):
                zero_ref[r, first + j : first + j + 1, :] = part[j, CUTS + r : CUTS + r + 1, :]
    column_ref[...] = jnp.zeros_like(column_ref)
    row = lax.broadcasted_iota(jnp.int32, (ROWS, LANES), 0)
    dead = (row >= count_ref[0] + OFF) & (row < HIGH)
    for r in range(count):
        zero_ref[r] = jnp.where(dead, 0.0, zero_ref[r])
    scatter_apply(blocks, ops_ref, zero_ref, y_ref, col_ref, column_ref)
    ghost_images(ops_ref, zero_ref, g_ref)
    ghost_apply(blocks, g_ref, y_ref, col_ref, list_ref)
    inner = inner_rows()
    for r in range(count):
        k0_ref[r] = unpack_columns(column_ref, square_ref, r)
        a1_ref[r] = jnp.where(inner, pack(y_ref, r), 0.0)
        b1_ref[r] = jnp.where(inner, pack(y_ref, count + r), 0.0)
    half = y_ref.at[pl.ds(0, count)]
    scatter_apply(blocks, ops_ref, a1_ref, half, col_ref, column_ref)
    for r in range(count):
        k1_ref[r] = unpack_columns(column_ref, square_ref, r)
        a2_ref[r] = pack(y_ref, r)
    messages(up_ref, down_ref, a2_ref, send_ref, a1_ref)


def second_kernel(
    col_ref, list_ref, send_ref, edge_ref,
    blocks, ops_ref, zero_ref, a1_ref, a2_in, k0_ref, k1_ref, low_ref, high_ref, stats_ref,
    v1_ref, v2_ref, v3_ref, v4_ref, k3_ref, dots_ref, sigma_ref, up_ref, down_ref,
    y_ref, column_ref, square_ref, g_ref,
):
    count = a1_ref.shape[0]
    inner = inner_rows()
    squares, traces = stats_ref[0, :8], stats_ref[0, 8:]
    for s in range(1, stats_ref.shape[0]):
        squares = squares + stats_ref[s, :8]
        traces = traces + stats_ref[s, 8:]
    scale = 1.0 / (stats_ref.shape[0] * NBLK * BS)
    sigma = (1.0 + scale * whole_sum(squares)) * (scale * whole_sum(traces))
    sigma_ref[...] = jnp.broadcast_to(sigma, sigma_ref.shape)
    column_ref[...] = jnp.zeros_like(column_ref)
    v2_ref[...] = a2_in[...]
    complete(v2_ref, low_ref, high_ref, send_ref, edge_ref)
    for r in range(count):
        v1_ref[r] = a1_ref[r]
        for part, ghost, flag in ((low_ref, LOW, 0), (high_ref, HIGH, 1)):
            for j in range(IF):
                v1_ref[r, ghost + j : ghost + j + 1, :] = part[r, 16 + j : 17 + j, :]
        v1 = v1_ref[r] - sigma * zero_ref[r]
        v2_ref[r] = v2_ref[r] - sigma * v1_ref[r] - sigma * v1
        v1 = jnp.where(inner, v1, 0.0)
        v1_ref[r] = v1
        v0 = jnp.where(inner, zero_ref[r], 0.0)
        target = jnp.where(inner, zero_ref[count + r], 0.0)
        second = k1_ref[r] - sigma * k0_ref[r]
        dots_ref[r, 0] = tile_sum(v0, k0_ref[r])
        dots_ref[r, 1] = tile_sum(v1, k0_ref[r])
        dots_ref[r, 2] = tile_sum(v1, second)
        dots_ref[r, 8] = tile_sum(target, k0_ref[r])
        dots_ref[r, 9] = tile_sum(target, second)
    scatter_apply(blocks, ops_ref, v2_ref, y_ref, col_ref, column_ref)
    ghost_images(ops_ref, v2_ref, g_ref)
    ghost_apply(blocks, g_ref, y_ref, col_ref, list_ref)
    for r in range(count):
        image = unpack_columns(column_ref, square_ref, r)
        v3 = jnp.where(inner, pack(y_ref, r) - sigma * v2_ref[r], 0.0)
        v3_ref[r] = v3
        dots_ref[r, 3] = tile_sum(v1_ref[r], image)
        dots_ref[r, 4] = tile_sum(jnp.where(inner, v2_ref[r], 0.0), image)
        dots_ref[r, 5] = tile_sum(v3, image)
        dots_ref[r, 10] = tile_sum(jnp.where(inner, zero_ref[count + r], 0.0), image)
    scatter_apply(blocks, ops_ref, v3_ref, y_ref, col_ref, column_ref)
    for r in range(count):
        image = unpack_columns(column_ref, square_ref, r)
        dots_ref[r, 6] = tile_sum(v3_ref[r], image)
        dots_ref[r, 7] = jnp.zeros((8, LANES), f32)
        dots_ref[r, 11] = tile_sum(jnp.where(inner, zero_ref[count + r], 0.0), image)
        k3_ref[r] = image
        v4_ref[r] = pack(y_ref, r) - sigma * v3_ref[r]
    messages(up_ref, down_ref, v4_ref, send_ref)


def moment_kernel(send_ref, edge_ref, v4_in, k3_ref, low_ref, high_ref, dots_in, v4_ref, dots_ref):
    v4_ref[...] = v4_in[...]
    complete(v4_ref, low_ref, high_ref, send_ref, edge_ref)
    lane = lax.broadcasted_iota(jnp.int32, (8, LANES), 1)
    sub = lax.broadcasted_iota(jnp.int32, (8, LANES), 0)
    total = jnp.zeros((8, LANES), f32)
    for r in range(v4_ref.shape[0]):
        for d in range(12):
            part = tile_sum(v4_ref[r], k3_ref[r]) if d == 7 else dots_in[r, d]
            total = jnp.where((lane == d) & (sub == r), whole_sum(part), total)
    dots_ref[...] = total


def third_kernel(col_ref, list_ref, blocks, ops_ref, v4_ref, w5_ref, y_ref, g_ref):
    scatter_apply(blocks, ops_ref, v4_ref, y_ref, col_ref, None)
    ghost_images(ops_ref, v4_ref, g_ref)
    ghost_apply(blocks, g_ref, y_ref, col_ref, list_ref)
    for r in range(v4_ref.shape[0]):
        w5_ref[r] = pack(y_ref, r)


def fourth_kernel(*refs):
    col_ref, send_ref, blocks, ops_ref, zero_ref, v1_ref, v2_ref, v3_ref, v4_ref, w5_ref, b1_ref, sigma_ref = refs[:12]
    parts_refs = refs[12:-9]
    comb_ref, rho_ref, early_ref, scale_ref, up_ref, down_ref, y_ref, x_ref, coef_ref = refs[-9:]
    sums = [part[...] for part in parts_refs]
    while len(sums) > 1:
        sums = [sums[i] + sums[i + 1] for i in range(0, len(sums), 2)]
    sums = sums[0]
    column = lambda d: jnp.broadcast_to(sums[:, d : d + 1], (8, LANES))
    combos, scales = scalars([column(d) for d in range(8)], [column(8 + d) for d in range(4)], sigma_ref[...])
    for g, value in enumerate(scales):
        scale_ref[g] = value
    count = v1_ref.shape[0]
    inner = inner_rows()
    for g, combo in enumerate(combos):
        for s, value in enumerate(combo):
            if value is not None:
                coef_ref[g, s] = value
    for r in range(count):
        parts = [zero_ref[r], v1_ref[r], v2_ref[r], v3_ref[r], v4_ref[r], w5_ref[r], zero_ref[count + r], b1_ref[r]]
        parts = [jnp.where(inner, part, 0.0) for part in parts]
        for g, combo in enumerate(combos):
            total = None
            for s, value in enumerate(combo):
                if value is not None:
                    term = coef_ref[g, s, r : r + 1, :] * parts[s]
                    total = term if total is None else total + term
            if g == 5:
                x_ref[r] = total
            slot = {0: 2, 1: 4, 2: 6, 3: 14, 4: 12}.get(g)
            if slot is None:
                comb_ref[g - 5, r] = total
            else:
                early_ref[pl.ds(slot + r, NBLK, stride=EARLY), :] = total[OFF:HIGH]
        early_ref[pl.ds(r, NBLK, stride=EARLY), :] = parts[0][OFF:HIGH]
        for slot in (8, 10):
            early_ref[pl.ds(slot + r, NBLK, stride=EARLY), :] = jnp.zeros((NBLK, LANES), f32)
    scatter_apply(blocks, ops_ref, x_ref, y_ref, col_ref, None)
    for r in range(count):
        rho_ref[r] = comb_ref[2, r] - scale_ref[0, r : r + 1, :] * pack(y_ref, r)
    messages(up_ref, down_ref, rho_ref, send_ref)


def answer_kernel(ops_ref, comb_ref, sol_ref, column_ref, square_ref):
    column_ref[...] = jnp.zeros_like(column_ref)
    lanes = lane_ids()
    for r in range(sol_ref.shape[0]):
        for n in range(NBLK):
            image = jnp.sum(ops_ref[n + OFF] * comb_ref[4, r, n + OFF : n + OFF + 1, :], axis=1, keepdims=True)
            column_ref[r] = jnp.where(lanes == n, image, column_ref[r])
        sol_ref[r] = unpack_columns(column_ref, square_ref, r)[:NBLK]


def fifth_kernel(
    col_ref, list_ref, send_ref, edge_ref,
    blocks, ops_ref, rho_in, comb_ref, scale_ref, low_ref, high_ref,
    late_ref, y_ref, rho_ref, g_ref,
):
    count = rho_in.shape[0]
    rho_ref[...] = rho_in[...]
    complete(rho_ref, low_ref, high_ref, send_ref, edge_ref)
    scatter_apply(blocks, ops_ref, rho_ref, y_ref, col_ref, None)
    ghost_images(ops_ref, rho_ref, g_ref)
    ghost_apply(blocks, g_ref, y_ref, col_ref, list_ref)
    for r in range(count):
        change = rho_ref[r] - comb_ref[2, r]
        first = comb_ref[3, r] + scale_ref[1, r : r + 1, :] * change - scale_ref[2, r : r + 1, :] * pack(y_ref, r)
        second = comb_ref[1, r] + change
        late_ref[pl.ds(r, NBLK, stride=LATE), :] = first[OFF:HIGH]
        late_ref[pl.ds(2 + r, NBLK, stride=LATE), :] = second[OFF:HIGH]


def split(value):
    high = value.astype(jnp.bfloat16)
    return high, (value - high.astype(f32)).astype(jnp.bfloat16)


def product(first, second, dim):
    (fh, fl), (sh, sl) = split(first), split(second)
    left = jnp.concatenate([fh, fl, fh], axis=dim)
    right = jnp.concatenate([sh, sh, sl], axis=0)
    return lax.dot_general(left, right, (((dim,), (0,)), ((), ())), preferred_element_type=f32)


def grad_kernel(*refs):
    peers = (len(refs) - 2) // 2
    early, late, weights_ref, grad_ref = refs[:peers], refs[peers : 2 * peers], refs[-2], refs[-1]
    sub = lax.broadcasted_iota(jnp.int32, (8, LANES), 0)

    def step(group, carry):
        for i in range(CHUNK):
            n = group * CHUNK + i
            at = pl.multiple_of(n * EARLY, EARLY)
            resid = [ref[pl.ds(at, 8), :] for ref in early]
            zeta = []
            for first, last in zip(early, late):
                pair = last[pl.ds(pl.multiple_of(group * (CHUNK * LATE) + 8 * (i // 2), 8), 8), :]
                if i % 2:
                    pair = pltpu.roll(pair, 4, 0)
                zeta.append(jnp.where(sub < LATE, pair, first[pl.ds(at + 8, 8), :]))
            mixed = product(jnp.concatenate(resid + zeta, axis=0), jnp.concatenate(zeta + resid, axis=0), 0)
            grad = product(weights_ref[n], mixed, 1)

            def write(q, value):
                grad_ref[pl.ds(group * (8 * CUTS) + 8 * q + i, 8, stride=24), :] = value

            flatten(grad, write)
        return carry

    lax.fori_loop(0, NBLK // CHUNK, step, 0)


def parts_over(values, axis):
    size = lax.axis_size(axis)
    if size & (size - 1):
        return [lax.psum(values, axis)]
    step = 1
    parts = [values]
    while step < size:
        if step > 1:
            while len(parts) > 1:
                parts = [parts[i] + parts[i + 1] for i in range(0, len(parts), 2)]
            values = parts[0]
        width = min(8, size // step)
        parts = [values]
        for d in range(1, width):
            parts.append(lax.ppermute(values, axis, [(i, i ^ (d * step)) for i in range(size)]))
        step *= width
    return parts


def all_of(values, axis):
    size = lax.axis_size(axis)
    return [values] + [
        lax.ppermute(values, axis, [(i, (i + d) % size) for i in range(size)]) for d in range(1, size)
    ]


def exchange(up, down):
    size = lax.axis_size("sub")
    rising = [(i, i + 1) for i in range(size - 1)]
    falling = [(j, i) for i, j in rising]
    return lax.ppermute(up, "sub", rising), lax.ppermute(down, "sub", falling)


def plus(first, second):
    if first is None:
        return second
    return first if second is None else first + second


def times(first, second):
    return None if first is None or second is None else first * second


def add(first, second, scale):
    size = max(len(first), len(second))
    first = list(first) + [None] * (size - len(first))
    second = list(second) + [None] * (size - len(second))
    return [plus(a, times(scale, b)) for a, b in zip(first, second)]


def scaled(first, scale):
    return [times(scale, a) for a in first]


def scalars(moments, products, sigma):
    one = jnp.ones_like(sigma)

    def inner(first, second):
        weights = [None] * (len(first) + len(second) - 1)
        for i, a in enumerate(first):
            for j, b in enumerate(second):
                weights[i + j] = plus(weights[i + j], a * b)
        total = None
        for weight, moment in zip(weights, moments):
            total = plus(total, weight * moment)
        return total

    def apply(poly):
        out = [None] * (len(poly) + 1)
        for j, value in enumerate(poly):
            out[j] = plus(out[j], sigma * value)
            out[j + 1] = plus(out[j + 1], value)
        return out

    resid = [[one]]
    direc = [[one]]
    image = []
    step, ratio, norm, curv = [], [None], [moments[0]], []
    for i in range(ITERS):
        image.append(apply(direc[i]))
        curv.append(inner(direc[i], image[i]))
        step.append(norm[i] / curv[i])
        if i + 1 < ITERS:
            resid.append(add(resid[i], image[i], -step[i]))
            norm.append(inner(resid[i + 1], resid[i + 1]))
            ratio.append(norm[i + 1] / norm[i])
            direc.append(add(resid[i + 1], direc[i], ratio[i + 1]))
    cot = []
    for i in range(ITERS):
        total = None
        for j, value in enumerate(resid[i]):
            total = plus(total, value * products[j])
        cot.append(total)
    along = [cot[0]]
    for i in range(1, ITERS):
        along.append(cot[i] + ratio[i] * along[i - 1])

    def row(poly):
        return list(poly) + [None] * (8 - len(poly))

    target = [None] * 6 + [one, None]
    resid_rows = [row(poly) for poly in resid]
    image_rows = [row(poly) for poly in image]
    inverse = [1.0 / value for value in step]

    def resid_prod(i):
        return [norm[l] if l == i else None for l in range(ITERS)]

    def image_prod(i):
        out = [None] * ITERS
        out[i] = norm[i] * inverse[i]
        if i + 1 < ITERS:
            out[i + 1] = -norm[i + 1] * inverse[i]
        return out

    def along_dir(prod, i):
        total = prod[0]
        for l in range(1, i + 1):
            total = plus(prod[l], times(ratio[l], total))
        return total

    def operator_prod(prod):
        out = []
        for l in range(ITERS - 1):
            value = times(add([prod[l]], [prod[l + 1]], -one)[0], inverse[l])
            if l > 0:
                back = times(add([prod[l - 1]], [prod[l]], -one)[0], inverse[l - 1])
                value = add([value], [back], -ratio[l])[0]
            out.append(value)
        return out + [None]

    last = ITERS - 1
    step_bar = along[last]
    curv_bar = -step_bar * step[last] / curv[last]
    dir_row = add(scaled(target, step[last]), image_rows[last], 2 * curv_bar)
    dir_prod = add(scaled(cot, step[last]), image_prod(last), 2 * curv_bar)
    norm_bar = step_bar / curv[last]
    rho_row = [None] * 8
    rho_prod = [None] * ITERS
    zetas = [None] * ITERS
    rho_rows = []
    for i in (2, 1, 0):
        ratio_bar = along_dir(dir_prod, i)
        full = norm_bar + ratio_bar / norm[i]
        zetas[i + 1] = add(dir_row, resid_rows[i + 1], full)
        rho_row = add(add(rho_row, zetas[i + 1], one), resid_rows[i + 1], full)
        rho_prod = add(add(rho_prod, dir_prod, one), resid_prod(i + 1), 2 * full)
        rho_rows.append(rho_row)
        step_bar = along[i] - (rho_prod[i] - rho_prod[i + 1]) * inverse[i]
        curv_bar = -step_bar * step[i] / curv[i]
        oper = [None] * 8
        if i == 2:
            for k in range(5):
                if k < 4:
                    oper[k] = plus(oper[k], times(sigma, rho_row[k]))
                    oper[k + 1] = plus(oper[k + 1], rho_row[k])
                else:
                    oper[5] = plus(oper[5], rho_row[4])
            oper[7] = rho_row[6]
        kept = add(scaled(dir_row, ratio[i + 1]), target, step[i])
        kept = add(kept, image_rows[i], 2 * curv_bar)
        dir_row = add(kept, oper, -step[i])
        dir_prod = add(add(scaled(dir_prod, ratio[i + 1]), cot, step[i]), image_prod(i), 2 * curv_bar)
        dir_prod = add(dir_prod, operator_prod(rho_prod), -step[i])
        norm_bar = step_bar / curv[i] - ratio_bar * norm[i + 1] / (norm[i] * norm[i])
    zetas[0] = add(dir_row, resid_rows[0], norm_bar)
    answer = [None] * 8
    for i in range(ITERS):
        answer = add(answer, row(direc[i]), step[i])
    combos = [resid_rows[1], resid_rows[2], resid_rows[3], zetas[3], zetas[2], rho_rows[1], zetas[1], rho_rows[2], zetas[0], answer]
    return combos, [step[1], ratio[1], step[0]]


def vmem():
    return pl.BlockSpec(memory_space=pltpu.VMEM)


def smem():
    return pl.BlockSpec(memory_space=pltpu.SMEM)


def shards(stiffness, precond, rhs_vec, cotangent, col_index, send_rows, counts):
    count = rhs_vec.shape[0]
    sub = lax.axis_index("sub")
    size = lax.axis_size("sub")
    edge = jnp.stack([sub > 0, sub + 1 < size]).astype(jnp.int32)
    columns = col_index.T
    stiff_cuts = stiffness.reshape(NBLK, K, CUTS, LANES).transpose(0, 2, 1, 3).reshape(NBLK * K * CUTS, LANES)
    weight_cuts = precond.reshape(NBLK // 8, 8, CUTS, LANES).transpose(0, 2, 1, 3).reshape(NBLK * CUTS, LANES)
    base = jnp.concatenate([rhs_vec, cotangent], axis=0).reshape(2 * count, NBLK, BS)
    base = jnp.pad(base, ((0, 0), (OFF, ROWS - HIGH), (0, LANES - BS)))

    def shape(*dims):
        return jax.ShapeDtypeStruct(dims, f32)

    def call(kernel, name, scalars_in, arrays_in, outs, scratch, flops, specs=None):
        return pl.pallas_call(
            kernel,
            in_specs=[smem()] * len(scalars_in) + [vmem()] * len(arrays_in),
            out_specs=specs or [vmem()] * len(outs),
            out_shape=outs,
            scratch_shapes=scratch,
            compiler_params=pltpu.CompilerParams(vmem_limit_bytes=8 * MIB),
            cost_estimate=pl.CostEstimate(flops=flops, bytes_accessed=flops // 2, transcendentals=0),
            name=name,
        )(*scalars_in, *arrays_in)

    rows = shape(count, ROWS, LANES)
    message = shape(count, 16, LANES)
    longer = shape(count, 24, LANES)
    ghost_message = shape(IF, CUTS + 8, LANES)
    partial = lambda r: pltpu.VMEM((r, ROWS, 8, LANES), f32)
    turned = [pltpu.VMEM((count, BS, LANES), f32), pltpu.VMEM((LANES, LANES), f32)]
    held = lambda r: pltpu.VMEM((r, ROWS, LANES), f32)
    grams = pltpu.VMEM((2, BS, LANES), f32)
    work = 4 * MIB

    up, down = call(pack_kernel, "pack", [send_rows], [weight_cuts, base], [ghost_message] * 2, [], MIB)
    low, high = exchange(up, down)

    blocks, weights, op_own, halo_list, stats = call(
        prepare_kernel, "prepare", [columns], [stiff_cuts, weight_cuts],
        [
            shape(NBLK, K, BS, LANES), shape(NBLK, BS, LANES), shape(NBLK, BS, LANES),
            jax.ShapeDtypeStruct((1, NBLK * K + 8), jnp.int32), shape(16, LANES),
        ],
        [grams], 2 * work, [vmem(), vmem(), vmem(), smem(), vmem()],
    )
    stats = lax.all_gather(stats, "sub")

    ops, zero, a1, b1, a2, k0, k1, up, down = call(
        first_kernel, "first", [columns, halo_list, send_rows, edge, counts], [blocks, op_own, base, low, high],
        [shape(ROWS, BS, LANES), shape(2 * count, ROWS, LANES), rows, rows, rows, rows, rows, longer, longer],
        [partial(2 * count), *turned, held(2 * count), grams], 2 * work,
    )
    low, high = exchange(up, down)

    v1, v2, v3, v4, k3, dots, sigma, up, down = call(
        second_kernel, "second", [columns, halo_list, send_rows, edge],
        [blocks, ops, zero, a1, a2, k0, k1, low, high, stats],
        [rows, rows, rows, rows, rows, shape(count, 12, 8, LANES), shape(8, LANES), message, message],
        [partial(count), *turned, held(count)], 2 * work,
    )
    low, high = exchange(up, down)

    v4, dots = call(
        moment_kernel, "moments", [send_rows, edge], [v4, k3, low, high, dots], [rows, shape(8, LANES)], [], MIB
    )
    parts = parts_over(dots, "sub")

    (w5,) = call(
        third_kernel, "third", [columns, halo_list], [blocks, ops, v4], [rows], [partial(count), held(count)], work
    )

    comb, rho, early, scales, up, down = call(
        fourth_kernel, "fourth", [columns, send_rows],
        [blocks, ops, zero, v1, v2, v3, v4, w5, b1, sigma, *parts],
        [shape(5, count, ROWS, LANES), rows, shape(NBLK * EARLY, LANES), shape(3, 8, LANES), message, message],
        [partial(count), held(count), pltpu.VMEM((10, 8, 8, LANES), f32)], work,
    )
    low, high = exchange(up, down)
    early = all_of(early, "rhs")

    (answer,) = call(answer_kernel, "answer", [], [ops, comb], [shape(count, NBLK, LANES)], turned, MIB)

    (late,) = call(
        fifth_kernel, "fifth", [columns, halo_list, send_rows, edge], [blocks, ops, rho, comb, scales, low, high],
        [shape(NBLK * LATE, LANES)], [partial(count), held(count), held(count)], work,
    )
    late = all_of(late, "rhs")

    (grad,) = call(grad_kernel, "grad", [], [*early, *late, weights], [shape(NBLK * CUTS, LANES)], [], work)
    grad = grad.reshape(NBLK // 8, CUTS, 8, LANES).transpose(0, 2, 1, 3).reshape(NBLK, BS * BS)
    return answer[..., :BS].reshape(count, NBLK * BS), grad


def solution(mesh):
    in_specs = (
        P("sub", None, None),
        P("sub", None),
        P("rhs", "sub"),
        P("rhs", "sub"),
        P("sub", None),
        P("sub", None),
        P("sub"),
    )
    out_specs = (P("rhs", "sub"), P("sub", None))
    return jax.shard_map(shards, mesh=mesh, in_specs=in_specs, out_specs=out_specs, check_vma=False)
```

time: 338 us -> 141 us (0.42)
  local copies, waits for them, and re-layouts: 121 us -> 6.01 us
  waiting for transfers between devices: 65 us -> 8.78 us
  other arithmetic: 20.8 us -> 0.91 us
  starting transfers between devices: 31.7 us -> 51.3 us
  between operations: 16.6 us -> 1.58 us
  matrix products: 13.2 us -> 0 us
  blocking collectives: 13.9 us -> 21.2 us
  Pallas kernels: 52.3 us -> 48.8 us
    psum x1 -> x0, waiting for transfers between devices: 56.3 us -> none  [shards(): grad = lax.psum(grad, 'rhs')]
    add x57 -> x0, local copies, waits for them, and re-layouts: 45.7 us -> none  [add(): return [a + scale * b for a, b in zip(first, second)]]
    unnamed x95 -> x16, local copies, waits for them, and re-layouts: 31.1 us -> 5.15 us
    all_gather x0 -> x1, blocking collectives: none -> 21.2 us  [shards(): stats = lax.all_gather(stats, 'sub')]
    ppermute x7 -> x13, starting transfers between devices: 9.17 us -> 28.5 us  [the longest x6 18.8 us: all_of(): lax.ppermute(values, axis, [(i, (i + d) % size) for i in range(size)])]
    reshape x8 -> x1, local copies, waits for them, and re-layouts: 17.4 us -> 0.74 us  [shards(): return (answer[..., :BS].reshape(count, NBLK * BS), grad)]
    psum x1 -> x0, blocking collectives: 13.9 us -> none  [shards(): stats = lax.psum(stats, 'sub') / (size * NBLK * BS)]
    dot_general x2 -> x0, matrix products: 13.2 us -> none  [the longest x1 7.87 us: shards(): grad = jnp.einsum('nab,nbc->nac', weights, mixed, precision=highest)]
  transfers between devices with their start and end apart: 16 -> 21, of which waited for: 6 -> 4; matrix products, arithmetic and copies ran while one was open for 7% -> 1% of each run, Pallas kernels for 5% -> 12%
where the time goes in v2:
time: 141 us; the launch traced here: 139 us
  starting transfers between devices  51.3 us (36%)
  Pallas kernels  48.8 us (35%)
  blocking collectives  21.2 us (15%)
  waiting for transfers between devices  8.78 us (6%)
  local copies, waits for them, and re-layouts  6.01 us (4%)
  between operations  1.58 us (1%)
    pallas_call x10, Pallas kernels, call(): pl.pallas_call(kernel, in_specs=[smem()] * len(scalars_in) + [vmem()] * l...  48.8 us
    ppermute x8, starting transfers between devices, exchange(): return (lax.ppermute(up, 'sub', rising), lax.ppermute(down, 'sub', falling))  22.9 us
    all_gather x1, blocking collectives, shards(): stats = lax.all_gather(stats, 'sub')  21.2 us
    ppermute x6, starting transfers between devices, all_of(): lax.ppermute(values, axis, [(i, (i + d) % size) for i in range(size)])  18.8 us
    ppermute x7, starting transfers between devices, parts_over(): lax.ppermute(values, axis, [(i, i ^ d * step) for i in range(size)])  9.71 us
    ppermute x8, waiting for transfers between devices, exchange(): return (lax.ppermute(up, 'sub', rising), lax.ppermute(down, 'sub', falling))  6.25 us
    unnamed x16, local copies, waits for them, and re-layouts  5.15 us
  transfers between devices with their start and end apart: 21, of which 4 were waited for; matrix products, arithmetic and copies ran while one was open for 1% of the time, Pallas kernels for 12%

profile of v2, /device:TPU:13, one launch (start us, length us, event | category | flops | bytes accessed | tf_op | source)
XLA Modules:
  0.0 138.7 jit_solution(17810398337915913320)
XLA Ops:
  0.6 0.0 copy-start.5
  0.6 0.8 pad_maximum_fusion
  1.5 0.1 reshape.32
  1.6 0.0 copy-start.1
  1.6 1.5 %copy-done.1 = f32[48,9216]{1,0:T(8,128)S(1)} copy-done((f32[48,9216]{1,0:T(8,128)S(1)}, f32[48,9216]{1,0:T(8,128)}, u32[]{:S(2)}) %copy-start.1) | copy-done | bytes 1769496
  3.1 0.7 copy-done.6
  3.7 0.7 pack.1
  4.4 3.1 %collective-permute-start = (f32[6,80,128]{2,1,0:T(8,128)S(1)}, f32[6,80,128]{2,1,0:T(8,128)S(1)}, u32[]{:S(2)}, u32[]{:S(2)}) collective-permute-start(f32[6,80,128]{2,1,0:T(8,128)S(1)} %get-tuple-element.38), channel_id=1, source_target_pairs={{0,4},{4,8},{8,12},{12,16},{16,20},{20,24},{24,28},{1,5},{5,9},{9,... | collective-permute-start | bytes 737288 | tf_op jit(solution)/shard_map/ppermute | solution.py:497
  7.6 2.1 %collective-permute-start.1 = (f32[6,80,128]{2,1,0:T(8,128)S(1)}, f32[6,80,128]{2,1,0:T(8,128)S(1)}, u32[]{:S(2)}, u32[]{:S(2)}) collective-permute-start(f32[6,80,128]{2,1,0:T(8,128)S(1)} %get-tuple-element.39), channel_id=1, source_target_pairs={{4,0},{8,4},{12,8},{16,12},{20,16},{24,20},{28,24},{5,1},{9,5},{13... | collective-permute-start | bytes 737288 | tf_op jit(solution)/shard_map/ppermute | solution.py:497
  10.4 0.0 copy-start
  10.4 3.0 %copy-done = f32[48,4,9216]{2,1,0:T(4,128)S(1)} copy-done((f32[48,4,9216]{2,1,0:T(4,128)S(1)}, f32[48,4,9216]{2,1,0:T(4,128)}, u32[]{:S(2)}) %copy-start) | copy-done | bytes 7077912
  13.4 8.4 %prepare.1 = (f32[48,4,96,128]{3,2,1,0:T(8,128)S(1)}, f32[48,96,128]{2,1,0:T(8,128)S(1)}, f32[48,96,128]{2,1,0:T(8,128)S(1)}, s32[1,200]{1,0:T(1,128)S(1)}, f32[16,128]{1,0:T(8,128)S(1)}) custom-call(s32[4,48]{1,0:T(4,128)S(1)} %bitcast.25, f32[13824,128]{1,0:T(8,128)S(1)} %bitcast.20, f32[3456,128]{1,0:T(8,128)S(1)} %bitcast.22), custom_call_target="tpu_custom_call" | custom-call | flops 8388608 | bytes 4194304 | tf_op jit(solution)/shard_map/prepare/pallas_call | solution.py:663
  21.8 0.0 copy-start.3
  21.8 0.1 add_convert_fusion.edge_ref
  21.9 0.0 collective-permute-done.low_ref
  21.9 0.0 collective-permute-done.1.high_ref
  21.9 9.7 %first.1 = (f32[64,96,128]{2,1,0:T(8,128)S(1)}, f32[4,64,128]{2,1,0:T(8,128)S(1)}, f32[2,64,128]{2,1,0:T(8,128)S(1)}, f32[2,64,128]{2,1,0:T(8,128)S(1)}, f32[2,6...) custom-call(s32[4,48]{1,0:T(4,128)S(1)} %bitcast.26, ...), custom_call_target="tpu_custom_call" | custom-call | flops 8388608 | bytes 4194304 | tf_op jit(solution)/shard_map/first/pallas_call | solution.py:663
  31.6 4.2 %collective-permute-start.2 = (f32[2,24,128]{2,1,0:T(8,128)S(1)}, f32[2,24,128]{2,1,0:T(8,128)S(1)}, u32[]{:S(2)}, u32[]{:S(2)}) collective-permute-start(f32[2,24,128]{2,1,0:T(8,128)S(1)} %get-tuple-element.46), channel_id=1, source_target_pairs={{0,4},{4,8},{8,12},{12,16},{16,20},{20,24},{24,28},{1,5},{5,9},{9,... | collective-permute-start | bytes 73736 | tf_op jit(solution)/shard_map/ppermute | solution.py:497
  35.8 1.9 %collective-permute-start.3 = (f32[2,24,128]{2,1,0:T(8,128)S(1)}, f32[2,24,128]{2,1,0:T(8,128)S(1)}, u32[]{:S(2)}, u32[]{:S(2)}) collective-permute-start(f32[2,24,128]{2,1,0:T(8,128)S(1)} %get-tuple-element.47), channel_id=1, source_target_pairs={{4,0},{8,4},{12,8},{16,12},{20,16},{24,20},{28,24},{5,1},{9,5},{13... | collective-permute-start | bytes 73736 | tf_op jit(solution)/shard_map/ppermute | solution.py:497
  37.7 21.2 %all-gather = f32[128,128]{1,0:T(8,128)S(1)} all-gather(f32[16,128]{1,0:T(8,128)S(1)} %get-tuple-element.48), channel_id=2, replica_groups=mesh['sub'=8,'rhs'=4] {'sub'}, dimensions={0}, use_global_device_ids=true | all-gather | bytes 73728 | tf_op jit(solution)/shard_map/all_gather | solution.py:695
  58.9 0.0 collective-permute-done.2.low_ref
  58.9 0.0 collective-permute-done.3.high_ref
  59.0 6.4 %second.1 = (f32[2,64,128]{2,1,0:T(8,128)S(1)}, f32[2,64,128]{2,1,0:T(8,128)S(1)}, f32[2,64,128]{2,1,0:T(8,128)S(1)}, f32[2,64,128]{2,1,0:T(8,128)S(1)}, f32[2,6...) custom-call(s32[4,48]{1,0:T(4,128)S(1)} %bitcast.27, ...), custom_call_target="tpu_custom_call" | custom-call | flops 8388608 | bytes 4194304 | tf_op jit(solution)/shard_map/second/pallas_call | solution.py:663
  65.4 3.2 %collective-permute-start.4 = (f32[2,16,128]{2,1,0:T(8,128)S(1)}, f32[2,16,128]{2,1,0:T(8,128)S(1)}, u32[]{:S(2)}, u32[]{:S(2)}) collective-permute-start(f32[2,16,128]{2,1,0:T(8,128)S(1)} %get-tuple-element.54), channel_id=1, source_target_pairs={{0,4},{4,8},{8,12},{12,16},{16,20},{20,24},{24,28},{1,5},{5,9},{9,... | collective-permute-start | bytes 49160 | tf_op jit(solution)/shard_map/ppermute | solution.py:497
  68.5 2.6 %collective-permute-start.5 = (f32[2,16,128]{2,1,0:T(8,128)S(1)}, f32[2,16,128]{2,1,0:T(8,128)S(1)}, u32[]{:S(2)}, u32[]{:S(2)}) collective-permute-start(f32[2,16,128]{2,1,0:T(8,128)S(1)} %get-tuple-element.55), channel_id=1, source_target_pairs={{4,0},{8,4},{12,8},{16,12},{20,16},{24,20},{28,24},{5,1},{9,5},{13... | collective-permute-start | bytes 49160 | tf_op jit(solution)/shard_map/ppermute | solution.py:497
  71.1 0.0 collective-permute-done.4.low_ref
  71.1 2.8 %collective-permute-done.5.high_ref = f32[2,16,128]{2,1,0:T(8,128)S(1)} collective-permute-done((f32[2,16,128]{2,1,0:T(8,128)S(1)}, f32[2,16,128]{2,1,0:T(8,128)S(1)}, u32[]{:S(2)}, u32[]{:S(2)}) %collective-permute-start.5) | collective-permute-done | bytes 16416 | tf_op jit(solution)/shard_map/ppermute | solution.py:497
  73.9 0.8 moments.1
  74.7 3.7 %collective-permute-start.10 = (f32[8,128]{1,0:T(8,128)S(1)}, f32[8,128]{1,0:T(8,128)S(1)}, u32[]{:S(2)}, u32[]{:S(2)}) collective-permute-start(f32[8,128]{1,0:T(8,128)S(1)} %get-tuple-element.60.refs_12_), channel_id=1, source_target_pairs={{0,20},{4,16},{8,28},{12,24},{16,4},{20,0},{24,12},{28,8},{1,21},{... | collective-permute-start | bytes 12296 | tf_op jit(solution)/shard_map/ppermute | solution.py:481
  78.5 0.0 collective-permute-start.11
  78.5 0.9 collective-permute-start.12
  79.4 1.7 %collective-permute-start.6 = (f32[8,128]{1,0:T(8,128)S(1)}, f32[8,128]{1,0:T(8,128)S(1)}, u32[]{:S(2)}, u32[]{:S(2)}) collective-permute-start(f32[8,128]{1,0:T(8,128)S(1)} %get-tuple-element.60.refs_12_), channel_id=1, source_target_pairs={{0,4},{4,0},{8,12},{12,8},{16,20},{20,16},{24,28},{28,24},{1,5},{5... | collective-permute-start | bytes 12296 | tf_op jit(solution)/shard_map/ppermute | solution.py:481
  81.1 1.9 %collective-permute-start.7 = (f32[8,128]{1,0:T(8,128)S(1)}, f32[8,128]{1,0:T(8,128)S(1)}, u32[]{:S(2)}, u32[]{:S(2)}) collective-permute-start(f32[8,128]{1,0:T(8,128)S(1)} %get-tuple-element.60.refs_12_), channel_id=1, source_target_pairs={{0,8},{4,12},{8,0},{12,4},{16,24},{20,28},{24,16},{28,20},{1,9},{5... | collective-permute-start | bytes 12296 | tf_op jit(solution)/shard_map/ppermute | solution.py:481
  83.0 0.0 collective-permute-done.10.refs_17_
  83.0 1.2 collective-permute-start.8
  84.2 0.0 collective-permute-done.11.refs_18_
  84.2 0.3 collective-permute-start.9
  84.5 3.6 %third.1.refs_9_ = f32[2,64,128]{2,1,0:T(8,128)S(1)} custom-call(s32[4,48]{1,0:T(4,128)S(1)} %bitcast.28, s32[1,200]{1,0:T(1,128)S(1)} %get-tuple-element.35.list_ref, f32[48,4,96,128]{3,2,1,0:T(8,128)S(1)} %get-tuple-element.36.blocks.refs_2_, f32[64,96,128]{2,1,0:T(8,128)S(1)} %get-tuple-element.40.ops_ref.refs_3_, ...), custom_call_target="tpu_custom_call" | custom-call | flops 4194304 | bytes 2097152 | tf_op jit(solution)/shard_map/third/pallas_call | solution.py:663
  88.1 0.0 collective-permute-done.12.refs_19_
  88.1 0.0 collective-permute-done.6.refs_13_
  88.1 0.0 collective-permute-done.7.refs_14_
  88.1 0.0 collective-permute-done.8.refs_15_
  88.1 0.0 collective-permute-done.9.refs_16_
  88.1 3.2 %fourth.1 = (f32[5,2,64,128]{3,2,1,0:T(8,128)S(1)}, f32[2,64,128]{2,1,0:T(8,128)S(1)}, f32[768,128]{1,0:T(8,128)S(1)}, f32[3,8,128]{2,1,0:T(8,128)S(1)}, f32[2,1...) custom-call(s32[4,48]{1,0:T(4,128)S(1)} %bitcast.29, s32[1,12]{1,0:T(1,128)S(1)} %copy-done.7, ...), custom_call_target="tpu_custom_call" | custom-call | flops 4194304 | bytes 2097152 | tf_op jit(solution)/shard_map/fourth/pallas_call | solution.py:663
  91.4 12.4 %collective-permute-start.13 = (f32[768,128]{1,0:T(8,128)S(1)}, f32[768,128]{1,0:T(8,128)S(1)}, u32[]{:S(2)}, u32[]{:S(2)}) collective-permute-start(f32[768,128]{1,0:T(8,128)S(1)} %get-tuple-element.62.refs_0_), channel_id=1, source_target_pairs={{0,1},{1,2},{2,3},{3,0},{4,5},{5,6},{6,7},{7,4},{8,9},{9,10},{10,1... | collective-permute-start | bytes 1179656 | tf_op jit(solution)/shard_map/ppermute | solution.py:489
  103.8 0.3 collective-permute-start.14
  104.0 0.2 collective-permute-start.15
  104.2 3.8 %collective-permute-start.16 = (f32[2,16,128]{2,1,0:T(8,128)S(1)}, f32[2,16,128]{2,1,0:T(8,128)S(1)}, u32[]{:S(2)}, u32[]{:S(2)}) collective-permute-start(f32[2,16,128]{2,1,0:T(8,128)S(1)} %get-tuple-element.65), channel_id=1, source_target_pairs={{0,4},{4,8},{8,12},{12,16},{16,20},{20,24},{24,28},{1,5},{5,9},{9,... | collective-permute-start | bytes 49160 | tf_op jit(solution)/shard_map/ppermute | solution.py:497
  108.1 1.9 %collective-permute-start.17 = (f32[2,16,128]{2,1,0:T(8,128)S(1)}, f32[2,16,128]{2,1,0:T(8,128)S(1)}, u32[]{:S(2)}, u32[]{:S(2)}) collective-permute-start(f32[2,16,128]{2,1,0:T(8,128)S(1)} %get-tuple-element.66), channel_id=1, source_target_pairs={{4,0},{8,4},{12,8},{16,12},{20,16},{24,20},{28,24},{5,1},{9,5},{13... | collective-permute-start | bytes 49160 | tf_op jit(solution)/shard_map/ppermute | solution.py:497
  110.0 0.0 collective-permute-done.16.low_ref
  110.0 3.4 %collective-permute-done.17.high_ref = f32[2,16,128]{2,1,0:T(8,128)S(1)} collective-permute-done((f32[2,16,128]{2,1,0:T(8,128)S(1)}, f32[2,16,128]{2,1,0:T(8,128)S(1)}, u32[]{:S(2)}, u32[]{:S(2)}) %collective-permute-start.17) | collective-permute-done | bytes 16416 | tf_op jit(solution)/shard_map/ppermute | solution.py:497
  113.5 3.7 %fifth.1.refs_4_ = f32[192,128]{1,0:T(8,128)S(1)} custom-call(s32[4,48]{1,0:T(4,128)S(1)} %bitcast.30, s32[1,200]{1,0:T(1,128)S(1)} %get-tuple-element.35.list_ref, s32[1,12]{1,0:T(1,128)S(1)} %copy-done.7, s32[2]{0:T(128)S(1)} %add_convert_fusion.edge_ref, f32[48,4,96,128]{3,2,1,0:T(8,128)S(1)} %get-tuple-element.36.blocks.refs_2_, ...), custom_call_target="tpu_custom_call" | custom-call | flops 4194304 | bytes 2097152 | tf_op jit(solution)/shard_map/fifth/pallas_call | solution.py:663
  117.2 3.0 %collective-permute-start.18 = (f32[192,128]{1,0:T(8,128)S(1)}, f32[192,128]{1,0:T(8,128)S(1)}, u32[]{:S(2)}, u32[]{:S(2)}) collective-permute-start(f32[192,128]{1,0:T(8,128)S(1)} %fifth.1.refs_4_), channel_id=1, source_target_pairs={{0,1},{1,2},{2,3},{3,0},{4,5},{5,6},{6,7},{7,4},{8,9},{9,10},{10,1... | collective-permute-start | bytes 294920 | tf_op jit(solution)/shard_map/ppermute | solution.py:489
  120.2 1.2 collective-permute-start.19
  121.4 1.5 %collective-permute-done.18.refs_5_ = f32[192,128]{1,0:T(8,128)S(1)} collective-permute-done((f32[192,128]{1,0:T(8,128)S(1)}, f32[192,128]{1,0:T(8,128)S(1)}, u32[]{:S(2)}, u32[]{:S(2)}) %collective-permute-start.18) | collective-permute-done | bytes 98336 | tf_op jit(solution)/shard_map/ppermute | solution.py:489
  122.9 1.7 %collective-permute-start.20 = (f32[192,128]{1,0:T(8,128)S(1)}, f32[192,128]{1,0:T(8,128)}, u32[]{:S(2)}, u32[]{:S(2)}) collective-permute-start(f32[192,128]{1,0:T(8,128)S(1)} %fifth.1.refs_4_), channel_id=1, source_target_pairs={{0,3},{1,0},{2,1},{3,2},{4,7},{5,4},{6,5},{7,6},{8,11},{9,8},{10,9... | collective-permute-start | bytes 294920 | tf_op jit(solution)/shard_map/ppermute | solution.py:489
  124.6 1.4 %answer.1 = f32[2,48,128]{2,1,0:T(8,128)S(1)} custom-call(f32[64,96,128]{2,1,0:T(8,128)S(1)} %get-tuple-element.40.ops_ref.refs_3_, f32[5,2,64,128]{3,2,1,0:T(8,128)S(1)} %get-tuple-element.61.comb_ref), custom_call_target="tpu_custom_call" | custom-call | flops 1048576 | bytes 524288 | tf_op jit(solution)/shard_map/answer/pallas_call | solution.py:663
  126.0 0.7 reshape.33
  126.7 0.0 collective-permute-done.19.refs_6_
  126.7 1.0 collective-permute-done.20.refs_7_
  127.8 0.0 collective-permute-done.13.refs_1_
  127.8 0.0 collective-permute-done.14.refs_2_
  127.8 0.0 collective-permute-done.15.refs_3_
  127.8 10.9 %grad.1 = f32[3456,128]{1,0:T(8,128)} custom-call(f32[768,128]{1,0:T(8,128)S(1)} %get-tuple-element.62.refs_0_, f32[768,128]{1,0:T(8,128)S(1)} %collective-permute-done.13.refs_1_, f32[768,128]{1,0:T(8,128)} %collective-permute-done.14.refs_2_, f32[768,128]{1,0:T(8,128)} %collective-permute-done.15.refs_3_, f32[192,128]{1,0:T(8,128)S(1)} %fifth.1.refs_4_, ...), custom_call_target="tpu_custom_call" | custom-call | flops 4194304 | bytes 2097152 | tf_op jit(solution)/shard_map/grad/pallas_call | solution.py:663
  (10 shorter events, 0.0 us)
Async XLA Ops:
  0.6 9.8 %copy-start.5 = (s32[48,4]{0,1:T(4,128)S(1)}, s32[48,4]{0,1:T(4,128)}, u32[]{:S(2)}) copy-start(s32[48,4]{0,1:T(4,128)} %param.11) | copy-start | bytes 2308
  1.6 1.5 %copy-start.1 = (f32[48,9216]{1,0:T(8,128)S(1)}, f32[48,9216]{1,0:T(8,128)}, u32[]{:S(2)}) copy-start(f32[48,9216]{1,0:T(8,128)} %param.8) | copy-start | bytes 5308420
  3.1 0.7 copy-start.6
  3.7 6.7 %copy-start.2 = (f32[48,9216]{1,0:T(8,128)S(1)}, f32[48,9216]{1,0:T(8,128)}, u32[]{:S(2)}) copy-start(f32[48,9216]{1,0:T(8,128)} %param.8) | copy-start | bytes 5308420
  4.4 17.4 %collective-permute-start = (f32[6,80,128]{2,1,0:T(8,128)S(1)}, f32[6,80,128]{2,1,0:T(8,128)S(1)}, u32[]{:S(2)}, u32[]{:S(2)}) collective-permute-start(f32[6,80,128]{2,1,0:T(8,128)S(1)} %get-tuple-element.38), channel_id=1, source_target_pairs={{0,4},{4,8},{8,12},{12,16},{16,20},{20,24},{24,28},{1,5},{5,9},{9,... | collective-permute-start | bytes 737288 | tf_op jit(solution)/shard_map/ppermute | solution.py:497
  7.6 14.3 %collective-permute-start.1 = (f32[6,80,128]{2,1,0:T(8,128)S(1)}, f32[6,80,128]{2,1,0:T(8,128)S(1)}, u32[]{:S(2)}, u32[]{:S(2)}) collective-permute-start(f32[6,80,128]{2,1,0:T(8,128)S(1)} %get-tuple-element.39), channel_id=1, source_target_pairs={{4,0},{8,4},{12,8},{16,12},{20,16},{24,20},{28,24},{5,1},{9,5},{13... | collective-permute-start | bytes 737288 | tf_op jit(solution)/shard_map/ppermute | solution.py:497
  10.4 3.0 %copy-start = (f32[48,4,9216]{2,1,0:T(4,128)S(1)}, f32[48,4,9216]{2,1,0:T(4,128)}, u32[]{:S(2)}) copy-start(f32[48,4,9216]{2,1,0:T(4,128)} %param.7) | copy-start | bytes 21233668
  13.4 8.5 %copy-start.7 = (s32[1,12]{1,0:T(1,128)S(1)}, s32[1,12]{1,0:T(1,128)}, u32[]{:S(2)}) copy-start(s32[1,12]{1,0:T(1,128)} %send_ref.9) | copy-start | bytes 148
  21.8 9.8 %copy-start.3 = (f32[48,96,128]{2,1,0:T(8,128)}, f32[48,96,128]{2,1,0:T(8,128)S(1)}, u32[]{:S(2)}) copy-start(f32[48,96,128]{2,1,0:T(8,128)S(1)} %get-tuple-element.67.refs_8_) | copy-start | bytes 7077892
  31.6 27.3 %collective-permute-start.2 = (f32[2,24,128]{2,1,0:T(8,128)S(1)}, f32[2,24,128]{2,1,0:T(8,128)S(1)}, u32[]{:S(2)}, u32[]{:S(2)}) collective-permute-start(f32[2,24,128]{2,1,0:T(8,128)S(1)} %get-tuple-element.46), channel_id=1, source_target_pairs={{0,4},{4,8},{8,12},{12,16},{16,20},{20,24},{24,28},{1,5},{5,9},{9,... | collective-permute-start | bytes 73736 | tf_op jit(solution)/shard_map/ppermute | solution.py:497
  35.8 23.2 %collective-permute-start.3 = (f32[2,24,128]{2,1,0:T(8,128)S(1)}, f32[2,24,128]{2,1,0:T(8,128)S(1)}, u32[]{:S(2)}, u32[]{:S(2)}) collective-permute-start(f32[2,24,128]{2,1,0:T(8,128)S(1)} %get-tuple-element.47), channel_id=1, source_target_pairs={{4,0},{8,4},{12,8},{16,12},{20,16},{24,20},{28,24},{5,1},{9,5},{13... | collective-permute-start | bytes 73736 | tf_op jit(solution)/shard_map/ppermute | solution.py:497
  65.4 5.8 %collective-permute-start.4 = (f32[2,16,128]{2,1,0:T(8,128)S(1)}, f32[2,16,128]{2,1,0:T(8,128)S(1)}, u32[]{:S(2)}, u32[]{:S(2)}) collective-permute-start(f32[2,16,128]{2,1,0:T(8,128)S(1)} %get-tuple-element.54), channel_id=1, source_target_pairs={{0,4},{4,8},{8,12},{12,16},{16,20},{20,24},{24,28},{1,5},{5,9},{9,... | collective-permute-start | bytes 49160 | tf_op jit(solution)/shard_map/ppermute | solution.py:497
  68.5 5.4 %collective-permute-start.5 = (f32[2,16,128]{2,1,0:T(8,128)S(1)}, f32[2,16,128]{2,1,0:T(8,128)S(1)}, u32[]{:S(2)}, u32[]{:S(2)}) collective-permute-start(f32[2,16,128]{2,1,0:T(8,128)S(1)} %get-tuple-element.55), channel_id=1, source_target_pairs={{4,0},{8,4},{12,8},{16,12},{20,16},{24,20},{28,24},{5,1},{9,5},{13... | collective-permute-start | bytes 49160 | tf_op jit(solution)/shard_map/ppermute | solution.py:497
  74.7 8.2 %collective-permute-start.10 = (f32[8,128]{1,0:T(8,128)S(1)}, f32[8,128]{1,0:T(8,128)S(1)}, u32[]{:S(2)}, u32[]{:S(2)}) collective-permute-start(f32[8,128]{1,0:T(8,128)S(1)} %get-tuple-element.60.refs_12_), channel_id=1, source_target_pairs={{0,20},{4,16},{8,28},{12,24},{16,4},{20,0},{24,12},{28,8},{1,21},{... | collective-permute-start | bytes 12296 | tf_op jit(solution)/shard_map/ppermute | solution.py:481
  78.5 5.7 %collective-permute-start.11 = (f32[8,128]{1,0:T(8,128)S(1)}, f32[8,128]{1,0:T(8,128)S(1)}, u32[]{:S(2)}, u32[]{:S(2)}) collective-permute-start(f32[8,128]{1,0:T(8,128)S(1)} %get-tuple-element.60.refs_12_), channel_id=1, source_target_pairs={{0,24},{4,28},{8,16},{12,20},{16,8},{20,12},{24,0},{28,4},{1,25},{... | collective-permute-start | bytes 12296 | tf_op jit(solution)/shard_map/ppermute | solution.py:481
  78.5 9.6 %collective-permute-start.12 = (f32[8,128]{1,0:T(8,128)S(1)}, f32[8,128]{1,0:T(8,128)S(1)}, u32[]{:S(2)}, u32[]{:S(2)}) collective-permute-start(f32[8,128]{1,0:T(8,128)S(1)} %get-tuple-element.60.refs_12_), channel_id=1, source_target_pairs={{0,28},{4,24},{8,20},{12,16},{16,12},{20,8},{24,4},{28,0},{1,29},{... | collective-permute-start | bytes 12296 | tf_op jit(solution)/shard_map/ppermute | solution.py:481
  79.4 8.7 %collective-permute-start.6 = (f32[8,128]{1,0:T(8,128)S(1)}, f32[8,128]{1,0:T(8,128)S(1)}, u32[]{:S(2)}, u32[]{:S(2)}) collective-permute-start(f32[8,128]{1,0:T(8,128)S(1)} %get-tuple-element.60.refs_12_), channel_id=1, source_target_pairs={{0,4},{4,0},{8,12},{12,8},{16,20},{20,16},{24,28},{28,24},{1,5},{5... | collective-permute-start | bytes 12296 | tf_op jit(solution)/shard_map/ppermute | solution.py:481
  81.1 7.0 %collective-permute-start.7 = (f32[8,128]{1,0:T(8,128)S(1)}, f32[8,128]{1,0:T(8,128)S(1)}, u32[]{:S(2)}, u32[]{:S(2)}) collective-permute-start(f32[8,128]{1,0:T(8,128)S(1)} %get-tuple-element.60.refs_12_), channel_id=1, source_target_pairs={{0,8},{4,12},{8,0},{12,4},{16,24},{20,28},{24,16},{28,20},{1,9},{5... | collective-permute-start | bytes 12296 | tf_op jit(solution)/shard_map/ppermute | solution.py:481
  83.0 5.1 %collective-permute-start.8 = (f32[8,128]{1,0:T(8,128)S(1)}, f32[8,128]{1,0:T(8,128)S(1)}, u32[]{:S(2)}, u32[]{:S(2)}) collective-permute-start(f32[8,128]{1,0:T(8,128)S(1)} %get-tuple-element.60.refs_12_), channel_id=1, source_target_pairs={{0,12},{4,8},{8,4},{12,0},{16,28},{20,24},{24,20},{28,16},{1,13},{... | collective-permute-start | bytes 12296 | tf_op jit(solution)/shard_map/ppermute | solution.py:481
  84.2 4.0 %collective-permute-start.9 = (f32[8,128]{1,0:T(8,128)S(1)}, f32[8,128]{1,0:T(8,128)S(1)}, u32[]{:S(2)}, u32[]{:S(2)}) collective-permute-start(f32[8,128]{1,0:T(8,128)S(1)} %get-tuple-element.60.refs_12_), channel_id=1, source_target_pairs={{0,16},{4,20},{8,24},{12,28},{16,0},{20,4},{24,8},{28,12},{1,17},{... | collective-permute-start | bytes 12296 | tf_op jit(solution)/shard_map/ppermute | solution.py:481
  91.4 36.4 %collective-permute-start.13 = (f32[768,128]{1,0:T(8,128)S(1)}, f32[768,128]{1,0:T(8,128)S(1)}, u32[]{:S(2)}, u32[]{:S(2)}) collective-permute-start(f32[768,128]{1,0:T(8,128)S(1)} %get-tuple-element.62.refs_0_), channel_id=1, source_target_pairs={{0,1},{1,2},{2,3},{3,0},{4,5},{5,6},{6,7},{7,4},{8,9},{9,10},{10,1... | collective-permute-start | bytes 1179656 | tf_op jit(solution)/shard_map/ppermute | solution.py:489
  103.8 24.0 %collective-permute-start.14 = (f32[768,128]{1,0:T(8,128)S(1)}, f32[768,128]{1,0:T(8,128)}, u32[]{:S(2)}, u32[]{:S(2)}) collective-permute-start(f32[768,128]{1,0:T(8,128)S(1)} %get-tuple-element.62.refs_0_), channel_id=1, source_target_pairs={{0,2},{1,3},{2,0},{3,1},{4,6},{5,7},{6,4},{7,5},{8,10},{9,11},{10,... | collective-permute-start | bytes 1179656 | tf_op jit(solution)/shard_map/ppermute | solution.py:489
  104.0 23.8 %collective-permute-start.15 = (f32[768,128]{1,0:T(8,128)S(1)}, f32[768,128]{1,0:T(8,128)}, u32[]{:S(2)}, u32[]{:S(2)}) collective-permute-start(f32[768,128]{1,0:T(8,128)S(1)} %get-tuple-element.62.refs_0_), channel_id=1, source_target_pairs={{0,3},{1,0},{2,1},{3,2},{4,7},{5,4},{6,5},{7,6},{8,11},{9,8},{10,9... | collective-permute-start | bytes 1179656 | tf_op jit(solution)/shard_map/ppermute | solution.py:489
  104.2 5.8 %collective-permute-start.16 = (f32[2,16,128]{2,1,0:T(8,128)S(1)}, f32[2,16,128]{2,1,0:T(8,128)S(1)}, u32[]{:S(2)}, u32[]{:S(2)}) collective-permute-start(f32[2,16,128]{2,1,0:T(8,128)S(1)} %get-tuple-element.65), channel_id=1, source_target_pairs={{0,4},{4,8},{8,12},{12,16},{16,20},{20,24},{24,28},{1,5},{5,9},{9,... | collective-permute-start | bytes 49160 | tf_op jit(solution)/shard_map/ppermute | solution.py:497
  108.1 5.4 %collective-permute-start.17 = (f32[2,16,128]{2,1,0:T(8,128)S(1)}, f32[2,16,128]{2,1,0:T(8,128)S(1)}, u32[]{:S(2)}, u32[]{:S(2)}) collective-permute-start(f32[2,16,128]{2,1,0:T(8,128)S(1)} %get-tuple-element.66), channel_id=1, source_target_pairs={{4,0},{8,4},{12,8},{16,12},{20,16},{24,20},{28,24},{5,1},{9,5},{13... | collective-permute-start | bytes 49160 | tf_op jit(solution)/shard_map/ppermute | solution.py:497
  117.2 10.6 %copy-start.4 = (f32[48,96,128]{2,1,0:T(8,128)S(1)}, f32[48,96,128]{2,1,0:T(8,128)}, u32[]{:S(2)}) copy-start(f32[48,96,128]{2,1,0:T(8,128)} %copy-done.3) | copy-start | bytes 7077892
  117.2 5.7 %collective-permute-start.18 = (f32[192,128]{1,0:T(8,128)S(1)}, f32[192,128]{1,0:T(8,128)S(1)}, u32[]{:S(2)}, u32[]{:S(2)}) collective-permute-start(f32[192,128]{1,0:T(8,128)S(1)} %fifth.1.refs_4_), channel_id=1, source_target_pairs={{0,1},{1,2},{2,3},{3,0},{4,5},{5,6},{6,7},{7,4},{8,9},{9,10},{10,1... | collective-permute-start | bytes 294920 | tf_op jit(solution)/shard_map/ppermute | solution.py:489
  120.2 6.5 %collective-permute-start.19 = (f32[192,128]{1,0:T(8,128)S(1)}, f32[192,128]{1,0:T(8,128)S(1)}, u32[]{:S(2)}, u32[]{:S(2)}) collective-permute-start(f32[192,128]{1,0:T(8,128)S(1)} %fifth.1.refs_4_), channel_id=1, source_target_pairs={{0,2},{1,3},{2,0},{3,1},{4,6},{5,7},{6,4},{7,5},{8,10},{9,11},{10,... | collective-permute-start | bytes 294920 | tf_op jit(solution)/shard_map/ppermute | solution.py:489
  122.9 4.9 %collective-permute-start.20 = (f32[192,128]{1,0:T(8,128)S(1)}, f32[192,128]{1,0:T(8,128)}, u32[]{:S(2)}, u32[]{:S(2)}) collective-permute-start(f32[192,128]{1,0:T(8,128)S(1)} %fifth.1.refs_4_), channel_id=1, source_target_pairs={{0,3},{1,0},{2,1},{3,2},{4,7},{5,4},{6,5},{7,6},{8,11},{9,8},{10,9... | collective-permute-start | bytes 294920 | tf_op jit(solution)/shard_map/ppermute | solution.py:489

commit v3 on v2

--- a/solution.py
+++ b/solution.py
@@ -12,6 +12,8 @@
 NBLK = 48
 IF = 6
 ITERS = 4
+ALL = (0, 1, 2, 3, 4, 5, 6, 7)
+USED = ((0, 1), (0, 1, 2), (0, 1, 2, 3), (0, 1, 2, 3, 4, 6), ALL, ALL, ALL, ALL, ALL, (0, 1, 2, 3))
 EARLY = 16
 LATE = 4
 CUTS = BS * BS // 128
@@ -88,10 +90,10 @@
         tiles = [x_ref[r, pl.ds(base + OFF, CHUNK), :] for r in range(count)]
         for i in range(CHUNK):
             n = group * CHUNK + i
-            oper = op_ref[n + OFF]
+            oper = op_ref[n]
             images = [jnp.sum(oper * tiles[r][i : i + 1, :], axis=1, keepdims=True) for r in range(count)]
             if column_ref is not None:
-                for r in range(column_ref.shape[0]):
+                for r in range(count):
                     column_ref[r] = jnp.where(lane_ids() == n + OFF, images[r], column_ref[r])
             for k in range(K):
                 block = blocks[n, k]
@@ -107,10 +109,10 @@
     count = x_ref.shape[0]
     mask = diagonal()
     g_ref[...] = jnp.zeros_like(g_ref)
-    for first in (LOW, HIGH):
+    for first, side in ((LOW, 0), (HIGH, IF)):
         for j in range(IF):
             slot = first + j
-            oper = op_ref[slot]
+            oper = op_ref[side + j]
             for r in range(count):
                 image = jnp.sum(oper * x_ref[r, slot : slot + 1, :], axis=1, keepdims=True)
                 line = jnp.sum(fold(jnp.where(mask, image, 0.0)), axis=0, keepdims=True)
@@ -197,6 +199,7 @@
 
 
 def pack_kernel(send_ref, raw_ref, base_ref, up_ref, down_ref):
+    vectors = base_ref.shape[0]
     for part, ref in ((0, down_ref), (IF, up_ref)):
         for j in range(IF):
             n = send_ref[0, part + j]
@@ -204,15 +207,33 @@
             for i in range(CUTS // 8):
                 ref[j, 8 * i : 8 * i + 8, :] = raw_ref[pl.ds(start + 64 * i, 8, stride=8), :]
             ref[j, CUTS:, :] = jnp.zeros((8, LANES), f32)
-            for r in range(base_ref.shape[0]):
-                ref[j, CUTS + r : CUTS + r + 1, :] = base_ref[r, pl.ds(n + OFF, 1), :]
-
-
-def prepare_kernel(col_ref, stiff_ref, raw_ref, blocks_ref, weights_ref, ops_ref, list_ref, stats_ref, gram_ref):
+            weights = unflatten(lambda q: raw_ref[pl.ds(start + 8 * q, 8, stride=24), :])
+            for r in range(vectors):
+                line = base_ref[r, pl.ds(n + OFF, 1), :]
+                if r < vectors // 2:
+                    ref[j, CUTS + r : CUTS + r + 1, :] = line
+                inside = jnp.sum(weights * line, axis=1, keepdims=True)
+                image = line + jnp.sum(fold(weights * inside), axis=0, keepdims=True)
+                at = CUTS + vectors // 2 + r
+                ref[j, at : at + 1, :] = image
+
+
+def prepare_kernel(
+    col_ref, raw_ref, stiff_hbm, blocks_ref, weights_ref, ops_ref, list_ref, stats_ref, gram_ref, stiff_ref, sems
+):
     mask = diagonal()
+    part = CHUNK * CUTS * K
+
+    def fetch(group):
+        at = pl.ds(group * part, part)
+        return pltpu.make_async_copy(stiff_hbm.at[at], stiff_ref.at[at], sems.at[group])
+
+    for g in range(NBLK // CHUNK):
+        fetch(g).start()
 
     def step(group, carry):
         count, squares, traces = carry
+        fetch(group).wait()
         for i in range(CHUNK):
             n = group * CHUNK + i
             for k in range(K):
@@ -239,44 +260,70 @@
 
 
 def first_kernel(
-    col_ref, list_ref, send_ref, edge_ref, count_ref,
-    blocks, op_own_ref, base_ref, low_ref, high_ref,
-    ops_ref, zero_ref, a1_ref, b1_ref, a2_ref, k0_ref, k1_ref, up_ref, down_ref,
-    y_ref, column_ref, square_ref, g_ref, gram_ref,
+    col_ref, list_ref, send_ref, count_ref,
+    blocks, op_ref, base_ref, low_ref, high_ref,
+    zero_ref, a1_ref, a2_ref, up_ref, down_ref,
+    y_ref, g_ref,
 ):
     count = a1_ref.shape[0]
-    ops_ref[OFF:HIGH] = op_own_ref[...]
     zero_ref[...] = base_ref[...]
-    for part, first in ((low_ref, LOW), (high_ref, HIGH)):
+    g_ref[...] = jnp.zeros_like(g_ref)
+    row = lax.broadcasted_iota(jnp.int32, (ROWS, LANES), 0)
+    dead = (row >= count_ref[0] + OFF) & (row < HIGH)
+    for r in range(count):
+        zero_ref[r] = jnp.where(dead, 0.0, zero_ref[r])
+        for part, first in ((low_ref, LOW), (high_ref, HIGH)):
+            for j in range(IF):
+                at = slice(first + j, first + j + 1)
+                zero_ref[r, at, :] = part[j, CUTS + r : CUTS + r + 1, :]
+                g_ref[r, at, :] = part[j, CUTS + count + r : CUTS + count + r + 1, :]
+    scatter_apply(blocks, op_ref, zero_ref.at[pl.ds(0, count)], y_ref, col_ref, None)
+    ghost_apply(blocks, g_ref, y_ref, col_ref, list_ref)
+    inner = inner_rows()
+    for r in range(count):
+        a1_ref[r] = jnp.where(inner, pack(y_ref, r), 0.0)
+    scatter_apply(blocks, op_ref, a1_ref, y_ref, col_ref, None)
+    for r in range(count):
+        a2_ref[r] = pack(y_ref, r)
+    messages(up_ref, down_ref, a2_ref, send_ref, a1_ref)
+
+
+def operator_rows(op_ref, x_ref, out_ref, column_ref, square_ref):
+    column_ref[...] = jnp.zeros_like(column_ref)
+    lanes = lane_ids()
+    for r in range(column_ref.shape[0]):
+        for n in range(NBLK):
+            image = jnp.sum(op_ref[n] * x_ref[r, n + OFF : n + OFF + 1, :], axis=1, keepdims=True)
+            column_ref[r] = jnp.where(lanes == n + OFF, image, column_ref[r])
+        out_ref[r] = unpack_columns(column_ref, square_ref, r)
+
+
+def ghost_kernel(op_ref, zero_ref, a1_ref, low_ref, high_ref, gop_ref, k0_ref, k1_ref, gram_ref, column_ref, square_ref):
+    for part, first in ((low_ref, 0), (high_ref, IF)):
         for j in range(IF):
             weights = unflatten(lambda q: part[j, pl.ds(q, 8, stride=3), :])
-            ops_ref[first + j] = make_operator(weights, gram_ref.at[j & 1])
-            for r in range(2 * count):
-                zero_ref[r, first + j : first + j + 1, :] = part[j, CUTS + r : CUTS + r + 1, :]
-    column_ref[...] = jnp.zeros_like(column_ref)
-    row = lax.broadcasted_iota(jnp.int32, (ROWS, LANES), 0)
-    dead = (row >= count_ref[0] + OFF) & (row < HIGH)
-    for r in range(count):
-        zero_ref[r] = jnp.where(dead, 0.0, zero_ref[r])
-    scatter_apply(blocks, ops_ref, zero_ref, y_ref, col_ref, column_ref)
-    ghost_images(ops_ref, zero_ref, g_ref)
+            gop_ref[first + j] = make_operator(weights, gram_ref.at[j & 1])
+    operator_rows(op_ref, zero_ref, k0_ref, column_ref, square_ref)
+    operator_rows(op_ref, a1_ref, k1_ref, column_ref, square_ref)
+
+
+def target_kernel(col_ref, list_ref, blocks, op_ref, zero_ref, low_ref, high_ref, b1_ref, y_ref, g_ref):
+    count = b1_ref.shape[0]
+    g_ref[...] = jnp.zeros_like(g_ref)
+    for r in range(count):
+        for part, first in ((low_ref, LOW), (high_ref, HIGH)):
+            for j in range(IF):
+                g_ref[r, first + j : first + j + 1, :] = part[j, CUTS + 2 * count + r : CUTS + 2 * count + r + 1, :]
+    scatter_apply(blocks, op_ref, zero_ref.at[pl.ds(count, count)], y_ref, col_ref, None)
     ghost_apply(blocks, g_ref, y_ref, col_ref, list_ref)
     inner = inner_rows()
     for r in range(count):
-        k0_ref[r] = unpack_columns(column_ref, square_ref, r)
-        a1_ref[r] = jnp.where(inner, pack(y_ref, r), 0.0)
-        b1_ref[r] = jnp.where(inner, pack(y_ref, count + r), 0.0)
-    half = y_ref.at[pl.ds(0, count)]
-    scatter_apply(blocks, ops_ref, a1_ref, half, col_ref, column_ref)
-    for r in range(count):
-        k1_ref[r] = unpack_columns(column_ref, square_ref, r)
-        a2_ref[r] = pack(y_ref, r)
-    messages(up_ref, down_ref, a2_ref, send_ref, a1_ref)
+        b1_ref[r] = jnp.where(inner, pack(y_ref, r), 0.0)
 
 
 def second_kernel(
     col_ref, list_ref, send_ref, edge_ref,
-    blocks, ops_ref, zero_ref, a1_ref, a2_in, k0_ref, k1_ref, low_ref, high_ref, stats_ref,
+    blocks, ops_ref, gop_ref, zero_ref, a1_ref, a2_in, k0_ref, k1_ref, low_ref, high_ref, stats_ref,
     v1_ref, v2_ref, v3_ref, v4_ref, k3_ref, dots_ref, sigma_ref, up_ref, down_ref,
     y_ref, column_ref, square_ref, g_ref,
 ):
@@ -310,7 +357,7 @@
         dots_ref[r, 8] = tile_sum(target, k0_ref[r])
         dots_ref[r, 9] = tile_sum(target, second)
     scatter_apply(blocks, ops_ref, v2_ref, y_ref, col_ref, column_ref)
-    ghost_images(ops_ref, v2_ref, g_ref)
+    ghost_images(gop_ref, v2_ref, g_ref)
     ghost_apply(blocks, g_ref, y_ref, col_ref, list_ref)
     for r in range(count):
         image = unpack_columns(column_ref, square_ref, r)
@@ -331,7 +378,8 @@
     messages(up_ref, down_ref, v4_ref, send_ref)
 
 
-def moment_kernel(send_ref, edge_ref, v4_in, k3_ref, low_ref, high_ref, dots_in, v4_ref, dots_ref):
+def moment_kernel(send_ref, edge_ref, v4_in, k3_ref, low_ref, high_ref, dots_in, b1_ref, v4_ref, dots_ref):
+    del b1_ref
     v4_ref[...] = v4_in[...]
     complete(v4_ref, low_ref, high_ref, send_ref, edge_ref)
     lane = lax.broadcasted_iota(jnp.int32, (8, LANES), 1)
@@ -344,82 +392,85 @@
     dots_ref[...] = total
 
 
-def third_kernel(col_ref, list_ref, blocks, ops_ref, v4_ref, w5_ref, y_ref, g_ref):
+def third_kernel(col_ref, list_ref, blocks, ops_ref, gop_ref, v4_ref, w5_ref, y_ref, g_ref):
     scatter_apply(blocks, ops_ref, v4_ref, y_ref, col_ref, None)
-    ghost_images(ops_ref, v4_ref, g_ref)
+    ghost_images(gop_ref, v4_ref, g_ref)
     ghost_apply(blocks, g_ref, y_ref, col_ref, list_ref)
     for r in range(v4_ref.shape[0]):
         w5_ref[r] = pack(y_ref, r)
 
 
-def fourth_kernel(*refs):
-    col_ref, send_ref, blocks, ops_ref, zero_ref, v1_ref, v2_ref, v3_ref, v4_ref, w5_ref, b1_ref, sigma_ref = refs[:12]
-    parts_refs = refs[12:-9]
-    comb_ref, rho_ref, early_ref, scale_ref, up_ref, down_ref, y_ref, x_ref, coef_ref = refs[-9:]
-    sums = [part[...] for part in parts_refs]
+def combine(coef_ref, parts, g, r):
+    total = None
+    for s in USED[g]:
+        term = coef_ref[g, s, r : r + 1, :] * parts[s]
+        total = term if total is None else total + term
+    return total
+
+
+def sources(zero_ref, stored, r, count):
+    v1_ref, v2_ref, v3_ref, v4_ref, w5_ref, b1_ref = stored
+    parts = [zero_ref[r], v1_ref[r], v2_ref[r], v3_ref[r], v4_ref[r], w5_ref[r], zero_ref[count + r], b1_ref[r]]
+    inner = inner_rows()
+    return [jnp.where(inner, part, 0.0) for part in parts]
+
+
+def fourth_kernel(col_ref, send_ref, blocks, ops_ref, sums_ref, sigma_ref, zero_ref, *refs):
+    stored, (first_ref, base_ref, rho_ref, coef_ref, scale_ref, up_ref, down_ref, y_ref) = refs[:6], refs[6:]
+    sums = [sums_ref[s] for s in range(sums_ref.shape[0])]
     while len(sums) > 1:
-        sums = [sums[i] + sums[i + 1] for i in range(0, len(sums), 2)]
+        sums = [sum(sums[i : i + 2]) for i in range(0, len(sums), 2)]
     sums = sums[0]
     column = lambda d: jnp.broadcast_to(sums[:, d : d + 1], (8, LANES))
     combos, scales = scalars([column(d) for d in range(8)], [column(8 + d) for d in range(4)], sigma_ref[...])
     for g, value in enumerate(scales):
         scale_ref[g] = value
-    count = v1_ref.shape[0]
-    inner = inner_rows()
     for g, combo in enumerate(combos):
         for s, value in enumerate(combo):
-            if value is not None:
+            if s in USED[g]:
                 coef_ref[g, s] = value
-    for r in range(count):
-        parts = [zero_ref[r], v1_ref[r], v2_ref[r], v3_ref[r], v4_ref[r], w5_ref[r], zero_ref[count + r], b1_ref[r]]
-        parts = [jnp.where(inner, part, 0.0) for part in parts]
-        for g, combo in enumerate(combos):
-            total = None
-            for s, value in enumerate(combo):
-                if value is not None:
-                    term = coef_ref[g, s, r : r + 1, :] * parts[s]
-                    total = term if total is None else total + term
-            if g == 5:
-                x_ref[r] = total
-            slot = {0: 2, 1: 4, 2: 6, 3: 14, 4: 12}.get(g)
-            if slot is None:
-                comb_ref[g - 5, r] = total
-            else:
-                early_ref[pl.ds(slot + r, NBLK, stride=EARLY), :] = total[OFF:HIGH]
+    count = rho_ref.shape[0]
+    for r in range(count):
+        parts = sources(zero_ref, stored, r, count)
+        first_ref[r] = combine(coef_ref, parts, 5, r)
+        base_ref[r] = combine(coef_ref, parts, 7, r)
+    scatter_apply(blocks, ops_ref, first_ref, y_ref, col_ref, None)
+    for r in range(count):
+        rho_ref[r] = base_ref[r] - scale_ref[0, r : r + 1, :] * pack(y_ref, r)
+    messages(up_ref, down_ref, rho_ref, send_ref)
+
+
+def combine_kernel(ops_ref, coef_ref, zero_ref, *refs):
+    stored, (early_ref, zeta_ref, sol_ref, x_ref, column_ref, square_ref) = refs[:6], refs[6:]
+    count = zeta_ref.shape[1]
+    for r in range(count):
+        parts = sources(zero_ref, stored, r, count)
         early_ref[pl.ds(r, NBLK, stride=EARLY), :] = parts[0][OFF:HIGH]
+        for g, slot in ((0, 2), (1, 4), (2, 6), (4, 12), (3, 14)):
+            early_ref[pl.ds(slot + r, NBLK, stride=EARLY), :] = combine(coef_ref, parts, g, r)[OFF:HIGH]
         for slot in (8, 10):
             early_ref[pl.ds(slot + r, NBLK, stride=EARLY), :] = jnp.zeros((NBLK, LANES), f32)
-    scatter_apply(blocks, ops_ref, x_ref, y_ref, col_ref, None)
-    for r in range(count):
-        rho_ref[r] = comb_ref[2, r] - scale_ref[0, r : r + 1, :] * pack(y_ref, r)
-    messages(up_ref, down_ref, rho_ref, send_ref)
-
-
-def answer_kernel(ops_ref, comb_ref, sol_ref, column_ref, square_ref):
-    column_ref[...] = jnp.zeros_like(column_ref)
-    lanes = lane_ids()
-    for r in range(sol_ref.shape[0]):
-        for n in range(NBLK):
-            image = jnp.sum(ops_ref[n + OFF] * comb_ref[4, r, n + OFF : n + OFF + 1, :], axis=1, keepdims=True)
-            column_ref[r] = jnp.where(lanes == n, image, column_ref[r])
-        sol_ref[r] = unpack_columns(column_ref, square_ref, r)[:NBLK]
+        zeta_ref[0, r] = combine(coef_ref, parts, 8, r)
+        zeta_ref[1, r] = combine(coef_ref, parts, 6, r)
+        x_ref[r] = combine(coef_ref, parts, 9, r)
+    operator_rows(ops_ref, x_ref, sol_ref, column_ref, square_ref)
 
 
 def fifth_kernel(
     col_ref, list_ref, send_ref, edge_ref,
-    blocks, ops_ref, rho_in, comb_ref, scale_ref, low_ref, high_ref,
+    blocks, ops_ref, gop_ref, rho_in, base_ref, zeta_ref, scale_ref, low_ref, high_ref,
     late_ref, y_ref, rho_ref, g_ref,
 ):
     count = rho_in.shape[0]
     rho_ref[...] = rho_in[...]
     complete(rho_ref, low_ref, high_ref, send_ref, edge_ref)
     scatter_apply(blocks, ops_ref, rho_ref, y_ref, col_ref, None)
-    ghost_images(ops_ref, rho_ref, g_ref)
+    ghost_images(gop_ref, rho_ref, g_ref)
     ghost_apply(blocks, g_ref, y_ref, col_ref, list_ref)
     for r in range(count):
-        change = rho_ref[r] - comb_ref[2, r]
-        first = comb_ref[3, r] + scale_ref[1, r : r + 1, :] * change - scale_ref[2, r : r + 1, :] * pack(y_ref, r)
-        second = comb_ref[1, r] + change
+        change = rho_ref[r] - base_ref[r]
+        first = zeta_ref[0, r] + scale_ref[1, r : r + 1, :] * change - scale_ref[2, r : r + 1, :] * pack(y_ref, r)
+        second = zeta_ref[1, r] + change
         late_ref[pl.ds(r, NBLK, stride=LATE), :] = first[OFF:HIGH]
         late_ref[pl.ds(2 + r, NBLK, stride=LATE), :] = second[OFF:HIGH]
 
@@ -436,24 +487,45 @@
     return lax.dot_general(left, right, (((dim,), (0,)), ((), ())), preferred_element_type=f32)
 
 
+def mixed_kernel(*refs):
+    early, mixed_ref = refs[:-1], refs[-1]
+
+    def step(group, carry):
+        for i in range(CHUNK):
+            at = pl.multiple_of((group * CHUNK + i) * EARLY, EARLY)
+            resid = [ref[pl.ds(at, 8), :] for ref in early]
+            zeta = [ref[pl.ds(at + 8, 8), :] for ref in early]
+            left = jnp.concatenate(resid + zeta, axis=0)
+            right = jnp.concatenate(zeta + resid, axis=0)
+            mixed_ref[group * CHUNK + i] = product(left, right, 0)
+        return carry
+
+    lax.fori_loop(0, NBLK // CHUNK, step, 0)
+
+
 def grad_kernel(*refs):
-    peers = (len(refs) - 2) // 2
-    early, late, weights_ref, grad_ref = refs[:peers], refs[peers : 2 * peers], refs[-2], refs[-1]
-    sub = lax.broadcasted_iota(jnp.int32, (8, LANES), 0)
+    peers = (len(refs) - 3) // 2
+    early, late, mixed_ref, weights_ref, grad_ref = refs[:peers], refs[peers : 2 * peers], *refs[-3:]
+    upper = lax.broadcasted_iota(jnp.int32, (8, LANES), 0) < LATE
+
+    def join(tiles):
+        out = []
+        for q in range(0, len(tiles), 2):
+            other = pltpu.roll(tiles[q + 1], LATE, 0) if q + 1 < len(tiles) else jnp.zeros((8, LANES), f32)
+            out.append(jnp.where(upper, tiles[q], other))
+        return out
 
     def step(group, carry):
         for i in range(CHUNK):
             n = group * CHUNK + i
             at = pl.multiple_of(n * EARLY, EARLY)
-            resid = [ref[pl.ds(at, 8), :] for ref in early]
-            zeta = []
-            for first, last in zip(early, late):
-                pair = last[pl.ds(pl.multiple_of(group * (CHUNK * LATE) + 8 * (i // 2), 8), 8), :]
-                if i % 2:
-                    pair = pltpu.roll(pair, 4, 0)
-                zeta.append(jnp.where(sub < LATE, pair, first[pl.ds(at + 8, 8), :]))
-            mixed = product(jnp.concatenate(resid + zeta, axis=0), jnp.concatenate(zeta + resid, axis=0), 0)
-            grad = product(weights_ref[n], mixed, 1)
+            pair = pl.ds(pl.multiple_of(group * (CHUNK * LATE) + 8 * (i // 2), 8), 8)
+            resid = join([ref[pl.ds(at, 8), :] for ref in early])
+            zeta = [ref[pair, :] for ref in late]
+            zeta = join([pltpu.roll(tile, LATE, 0) for tile in zeta] if i % 2 else zeta)
+            left = jnp.concatenate(resid + zeta, axis=0)
+            right = jnp.concatenate(zeta + resid, axis=0)
+            grad = product(weights_ref[n], mixed_ref[n] + product(left, right, 0), 1)
 
             def write(q, value):
                 grad_ref[pl.ds(group * (8 * CUTS) + 8 * q + i, 8, stride=24), :] = value
@@ -464,23 +536,9 @@
     lax.fori_loop(0, NBLK // CHUNK, step, 0)
 
 
-def parts_over(values, axis):
+def from_all(values, axis):
     size = lax.axis_size(axis)
-    if size & (size - 1):
-        return [lax.psum(values, axis)]
-    step = 1
-    parts = [values]
-    while step < size:
-        if step > 1:
-            while len(parts) > 1:
-                parts = [parts[i] + parts[i + 1] for i in range(0, len(parts), 2)]
-            values = parts[0]
-        width = min(8, size // step)
-        parts = [values]
-        for d in range(1, width):
-            parts.append(lax.ppermute(values, axis, [(i, i ^ (d * step)) for i in range(size)]))
-        step *= width
-    return parts
+    return lax.all_to_all(jnp.broadcast_to(values[None], (size, *values.shape)), axis, 0, 0)
 
 
 def all_of(values, axis):
@@ -641,6 +699,10 @@
     return pl.BlockSpec(memory_space=pltpu.VMEM)
 
 
+def hbm():
+    return pl.BlockSpec(memory_space=pltpu.HBM)
+
+
 def smem():
     return pl.BlockSpec(memory_space=pltpu.SMEM)
 
@@ -659,14 +721,14 @@
     def shape(*dims):
         return jax.ShapeDtypeStruct(dims, f32)
 
-    def call(kernel, name, scalars_in, arrays_in, outs, scratch, flops, specs=None):
+    def call(kernel, name, scalars_in, arrays_in, outs, scratch, flops, specs=None, limit=8, in_specs=None):
         return pl.pallas_call(
             kernel,
-            in_specs=[smem()] * len(scalars_in) + [vmem()] * len(arrays_in),
+            in_specs=in_specs or [smem()] * len(scalars_in) + [vmem()] * len(arrays_in),
             out_specs=specs or [vmem()] * len(outs),
             out_shape=outs,
             scratch_shapes=scratch,
-            compiler_params=pltpu.CompilerParams(vmem_limit_bytes=8 * MIB),
+            compiler_params=pltpu.CompilerParams(vmem_limit_bytes=limit * MIB),
             cost_estimate=pl.CostEstimate(flops=flops, bytes_accessed=flops // 2, transcendentals=0),
             name=name,
         )(*scalars_in, *arrays_in)
@@ -682,62 +744,79 @@
     work = 4 * MIB
 
     up, down = call(pack_kernel, "pack", [send_rows], [weight_cuts, base], [ghost_message] * 2, [], MIB)
-    low, high = exchange(up, down)
-
-    blocks, weights, op_own, halo_list, stats = call(
-        prepare_kernel, "prepare", [columns], [stiff_cuts, weight_cuts],
+    near, far = exchange(up, down)
+
+    blocks, weights, ops, halo_list, stats = call(
+        prepare_kernel, "prepare", [columns], [weight_cuts, stiff_cuts],
         [
             shape(NBLK, K, BS, LANES), shape(NBLK, BS, LANES), shape(NBLK, BS, LANES),
             jax.ShapeDtypeStruct((1, NBLK * K + 8), jnp.int32), shape(16, LANES),
         ],
-        [grams], 2 * work, [vmem(), vmem(), vmem(), smem(), vmem()],
-    )
-    stats = lax.all_gather(stats, "sub")
-
-    ops, zero, a1, b1, a2, k0, k1, up, down = call(
-        first_kernel, "first", [columns, halo_list, send_rows, edge, counts], [blocks, op_own, base, low, high],
-        [shape(ROWS, BS, LANES), shape(2 * count, ROWS, LANES), rows, rows, rows, rows, rows, longer, longer],
-        [partial(2 * count), *turned, held(2 * count), grams], 2 * work,
+        [grams, pltpu.VMEM((NBLK * K * CUTS, LANES), f32), pltpu.SemaphoreType.DMA((NBLK // CHUNK,))],
+        2 * work, [vmem(), vmem(), vmem(), smem(), vmem()], 16, [smem(), vmem(), hbm()],
+    )
+    stats = from_all(stats, "sub")
+
+    zero, a1, a2, up, down = call(
+        first_kernel, "first", [columns, halo_list, send_rows, counts], [blocks, ops, base, near, far],
+        [shape(2 * count, ROWS, LANES), rows, rows, longer, longer],
+        [partial(count), held(count)], 2 * work,
     )
     low, high = exchange(up, down)
+
+    gops, k0, k1 = call(
+        ghost_kernel, "ghosts", [], [ops, zero, a1, near, far],
+        [shape(2 * IF, BS, LANES), rows, rows], [grams, *turned], work,
+    )
 
     v1, v2, v3, v4, k3, dots, sigma, up, down = call(
         second_kernel, "second", [columns, halo_list, send_rows, edge],
-        [blocks, ops, zero, a1, a2, k0, k1, low, high, stats],
+        [blocks, ops, gops, zero, a1, a2, k0, k1, low, high, stats],
         [rows, rows, rows, rows, rows, shape(count, 12, 8, LANES), shape(8, LANES), message, message],
         [partial(count), *turned, held(count)], 2 * work,
     )
     low, high = exchange(up, down)
 
+    zero, v3 = lax.optimization_barrier((zero, v3))
+    (b1,) = call(
+        target_kernel, "target", [columns, halo_list], [blocks, ops, zero, near, far], [rows],
+        [partial(count), held(count)], work,
+    )
+
     v4, dots = call(
-        moment_kernel, "moments", [send_rows, edge], [v4, k3, low, high, dots], [rows, shape(8, LANES)], [], MIB
-    )
-    parts = parts_over(dots, "sub")
+        moment_kernel, "moments", [send_rows, edge], [v4, k3, low, high, dots, b1], [rows, shape(8, LANES)], [], MIB
+    )
+    sums = from_all(dots, "sub")
 
     (w5,) = call(
-        third_kernel, "third", [columns, halo_list], [blocks, ops, v4], [rows], [partial(count), held(count)], work
-    )
-
-    comb, rho, early, scales, up, down = call(
-        fourth_kernel, "fourth", [columns, send_rows],
-        [blocks, ops, zero, v1, v2, v3, v4, w5, b1, sigma, *parts],
-        [shape(5, count, ROWS, LANES), rows, shape(NBLK * EARLY, LANES), shape(3, 8, LANES), message, message],
-        [partial(count), held(count), pltpu.VMEM((10, 8, 8, LANES), f32)], work,
+        third_kernel, "third", [columns, halo_list], [blocks, ops, gops, v4], [rows],
+        [partial(count), held(count)], work,
+    )
+
+    stored = [zero, v1, v2, v3, v4, w5, b1]
+    first, fixed, rho, coefs, scales, up, down = call(
+        fourth_kernel, "fourth", [columns, send_rows], [blocks, ops, sums, sigma, *stored],
+        [rows, rows, rows, shape(10, 8, 8, LANES), shape(3, 8, LANES), message, message], [partial(count)], work,
     )
     low, high = exchange(up, down)
+
+    early, zeta, answer = call(
+        combine_kernel, "combine", [], [ops, coefs, *stored],
+        [shape(NBLK * EARLY, LANES), shape(2, count, ROWS, LANES), rows], [held(count), *turned], MIB,
+    )
     early = all_of(early, "rhs")
 
-    (answer,) = call(answer_kernel, "answer", [], [ops, comb], [shape(count, NBLK, LANES)], turned, MIB)
-
     (late,) = call(
-        fifth_kernel, "fifth", [columns, halo_list, send_rows, edge], [blocks, ops, rho, comb, scales, low, high],
+        fifth_kernel, "fifth", [columns, halo_list, send_rows, edge],
+        [blocks, ops, gops, rho, fixed, zeta, scales, low, high],
         [shape(NBLK * LATE, LANES)], [partial(count), held(count), held(count)], work,
     )
     late = all_of(late, "rhs")
 
-    (grad,) = call(grad_kernel, "grad", [], [*early, *late, weights], [shape(NBLK * CUTS, LANES)], [], work)
+    (mixed,) = call(mixed_kernel, "mixed", [], early, [shape(NBLK, LANES, LANES)], [], work)
+    (grad,) = call(grad_kernel, "grad", [], [*early, *late, mixed, weights], [shape(NBLK * CUTS, LANES)], [], work)
     grad = grad.reshape(NBLK // 8, CUTS, 8, LANES).transpose(0, 2, 1, 3).reshape(NBLK, BS * BS)
-    return answer[..., :BS].reshape(count, NBLK * BS), grad
+    return answer[:, OFF:HIGH, :BS].reshape(count, NBLK * BS), grad
 
 
 def solution(mesh):

time: 141 us -> 152 us (1.078)
  local copies, waits for them, and re-layouts: 6.01 us -> 42.3 us
  blocking collectives: 21.2 us -> 0 us
  Pallas kernels: 48.8 us -> 60.7 us
  starting transfers between devices: 51.3 us -> 41.5 us
  waiting for transfers between devices: 8.78 us -> 3.11 us
    unnamed x16 -> x80, local copies, waits for them, and re-layouts: 5.15 us -> 40.2 us
    all_gather x1 -> x0, blocking collectives: 21.2 us -> none  [shards(): stats = lax.all_gather(stats, 'sub')]
    pallas_call x10 -> x13, Pallas kernels: 48.8 us -> 60.7 us  [call(): pl.pallas_call(kernel, in_specs=in_specs or [smem()] * len(scalars_in) +...]
    all_to_all x0 -> x2, starting transfers between devices: none -> 11.5 us  [from_all(): lax.all_to_all(jnp.broadcast_to(values[None], (size, *values.shape)), axi...]
    ppermute x6, starting transfers between devices: 18.8 us -> 8.62 us  [all_of(): lax.ppermute(values, axis, [(i, (i + d) % size) for i in range(size)])]
    ppermute x7 -> x0, starting transfers between devices: 9.71 us -> none  [parts_over(): lax.ppermute(values, axis, [(i, i ^ d * step) for i in range(size)])]
    ppermute x8, waiting for transfers between devices: 6.25 us -> 3.09 us  [exchange(): return (lax.ppermute(up, 'sub', rising), lax.ppermute(down, 'sub', falling))]
    ppermute x6, waiting for transfers between devices: 2.51 us -> 0.02 us  [all_of(): lax.ppermute(values, axis, [(i, (i + d) % size) for i in range(size)])]
  transfers between devices with their start and end apart: 21 -> 16, of which waited for: 4 -> 2; matrix products, arithmetic and copies ran while one was open for 1% -> 1% of each run, Pallas kernels for 12% -> 22%
where the time goes in v3:
time: 152 us; the launch traced here: 150 us
  Pallas kernels  60.7 us (40%)
  local copies, waits for them, and re-layouts  42.3 us (28%)
  starting transfers between devices  41.5 us (27%)
  waiting for transfers between devices  3.11 us (2%)
  between operations  1.74 us (1%)
    pallas_call x13, Pallas kernels, call(): pl.pallas_call(kernel, in_specs=in_specs or [smem()] * len(scalars_in) +...  60.7 us
    unnamed x80, local copies, waits for them, and re-layouts  40.2 us
    ppermute x8, starting transfers between devices, exchange(): return (lax.ppermute(up, 'sub', rising), lax.ppermute(down, 'sub', falling))  21.4 us
    all_to_all x2, starting transfers between devices, from_all(): lax.all_to_all(jnp.broadcast_to(values[None], (size, *values.shape)), axi...  11.5 us
    ppermute x6, starting transfers between devices, all_of(): lax.ppermute(values, axis, [(i, (i + d) % size) for i in range(size)])  8.62 us
    ppermute x8, waiting for transfers between devices, exchange(): return (lax.ppermute(up, 'sub', rising), lax.ppermute(down, 'sub', falling))  3.09 us
  transfers between devices with their start and end apart: 16, of which 2 were waited for; matrix products, arithmetic and copies ran while one was open for 1% of the time, Pallas kernels for 22%

profile of v3, /device:TPU:13, one launch (start us, length us, event | category | flops | bytes accessed | tf_op | source)
XLA Modules:
  0.0 150.2 jit_solution(9343213991545935722)
XLA Ops:
  0.6 0.8 pad_maximum_fusion
  1.5 0.1 reshape.34
  1.6 0.0 copy-start.7
  1.6 1.5 copy-done.7
  3.1 0.7 copy-done.36
  3.7 2.9 %pack.1 = (f32[6,80,128]{2,1,0:T(8,128)}, f32[6,80,128]{2,1,0:T(8,128)S(1)}) custom-call(s32[1,12]{1,0:T(1,128)S(1)} %copy-done.36, f32[3456,128]{1,0:T(8,128)S(1)} %bitcast.19, f32[4,64,128]{2,1,0:T(8,128)S(1)} %pad.4.base_ref), custom_call_target="tpu_custom_call" | custom-call | flops 1048576 | bytes 524288 | tf_op jit(solution)/shard_map/pack/pallas_call | solution.py:725
  6.6 3.1 %collective-permute-start = (f32[6,80,128]{2,1,0:T(8,128)}, f32[6,80,128]{2,1,0:T(8,128)S(1)}, u32[]{:S(2)}, u32[]{:S(2)}) collective-permute-start(f32[6,80,128]{2,1,0:T(8,128)} %get-tuple-element.42), channel_id=1, source_target_pairs={{0,4},{4,8},{8,12},{12,16},{16,20},{20,24},{24,28},{1,5},{5,9},{9,... | collective-permute-start | bytes 737288 | tf_op jit(solution)/shard_map/ppermute | solution.py:555
  9.8 2.1 %collective-permute-start.1 = (f32[6,80,128]{2,1,0:T(8,128)S(1)}, f32[6,80,128]{2,1,0:T(8,128)S(1)}, u32[]{:S(2)}, u32[]{:S(2)}) collective-permute-start(f32[6,80,128]{2,1,0:T(8,128)S(1)} %get-tuple-element.43), channel_id=1, source_target_pairs={{4,0},{8,4},{12,8},{16,12},{20,16},{24,20},{28,24},{5,1},{9,5},{13... | collective-permute-start | bytes 737288 | tf_op jit(solution)/shard_map/ppermute | solution.py:555
  12.0 3.0 %copy-done.6 = f32[48,4,9216]{2,1,0:T(4,128)S(1)} copy-done((f32[48,4,9216]{2,1,0:T(4,128)S(1)}, f32[48,4,9216]{2,1,0:T(4,128)}, u32[]{:S(2)}) %copy-start.6) | copy-done | bytes 7077912
  15.0 9.9 %prepare.1 = (f32[48,4,96,128]{3,2,1,0:T(8,128)S(1)}, f32[48,96,128]{2,1,0:T(8,128)S(1)}, f32[48,96,128]{2,1,0:T(8,128)S(1)}, s32[1,200]{1,0:T(1,128)S(1)}, f32[16,128]{1,0:T(8,128)S(1)}) custom-call(s32[4,48]{1,0:T(4,128)S(1)} %bitcast.21, f32[3456,128]{1,0:T(8,128)S(1)} %bitcast.20, f32[13824,128]{1,0:T(8,128)S(1)} %bitcast.18), custom_call_target="tpu_custom_call" | custom-call | flops 8388608 | bytes 4194304 | tf_op jit(solution)/shard_map/prepare/pallas_call | solution.py:725
  24.9 3.7 %copy-done = f32[48,4,96,128]{3,2,1,0:T(8,128)} copy-done((f32[48,4,96,128]{3,2,1,0:T(8,128)}, f32[48,4,96,128]{3,2,1,0:T(8,128)S(1)}, u32[]{:S(2)}) %copy-start) | copy-done | bytes 9437208
  28.6 1.4 copy-done.9
  30.0 0.6 broadcast_in_dim.4
  30.6 5.7 %all-to-all-start = ((f32[8,16,128]{2,1,0:T(8,128)}), f32[8,16,128]{2,1,0:T(8,128)S(1)}, u32[]{:S(2)}, u32[]{:S(2)}) async-start(f32[8,16,128]{2,1,0:T(8,128)} %broadcast_in_dim.4), calls=%async_computation | async-start | bytes 131072 | tf_op jit(solution)/shard_map/all_to_all | solution.py:541
  37.0 0.0 copy-start.11
  37.0 3.8 %copy-done.1 = f32[48,4,96,128]{3,2,1,0:T(8,128)S(1)} copy-done((f32[48,4,96,128]{3,2,1,0:T(8,128)S(1)}, f32[48,4,96,128]{3,2,1,0:T(8,128)}, u32[]{:S(2)}) %copy-start.1) | copy-done | bytes 9437208
  40.8 6.1 %first.1 = (f32[4,64,128]{2,1,0:T(8,128)S(1)}, f32[2,64,128]{2,1,0:T(8,128)S(1)}, f32[2,64,128]{2,1,0:T(8,128)S(1)}, f32[2,24,128]{2,1,0:T(8,128)}, f32[2,24,128]{2,1,0:T(8,128)}) custom-call(s32[4,48]{1,0:T(4,128)S(1)} %bitcast.22, s32[1,200]{1,0:T(1,128)S(1)} %get-tuple-element.41.list_ref, s32[1,12]{1,0:T(1,128)S(1)} %copy-done.37, s32[1]{0:T(128)S(6)} %copy.10.count_ref, ...), custom_call_target="tpu_custom_call" | custom-call | flops 8388608 | bytes 4194304 | tf_op jit(solution)/shard_map/first/pallas_call | solution.py:725
  46.9 2.9 %collective-permute-start.2 = (f32[2,24,128]{2,1,0:T(8,128)}, f32[2,24,128]{2,1,0:T(8,128)}, u32[]{:S(2)}, u32[]{:S(2)}) collective-permute-start(f32[2,24,128]{2,1,0:T(8,128)} %get-tuple-element.50), channel_id=1, source_target_pairs={{0,4},{4,8},{8,12},{12,16},{16,20},{20,24},{24,28},{1,5},{5,9},{9,... | collective-permute-start | bytes 73736 | tf_op jit(solution)/shard_map/ppermute | solution.py:555
  49.8 2.4 %collective-permute-start.3 = (f32[2,24,128]{2,1,0:T(8,128)}, f32[2,24,128]{2,1,0:T(8,128)}, u32[]{:S(2)}, u32[]{:S(2)}) collective-permute-start(f32[2,24,128]{2,1,0:T(8,128)} %get-tuple-element.51), channel_id=1, source_target_pairs={{4,0},{8,4},{12,8},{16,12},{20,16},{24,20},{28,24},{5,1},{9,5},{13... | collective-permute-start | bytes 73736 | tf_op jit(solution)/shard_map/ppermute | solution.py:555
  52.2 0.1 add_convert_fusion.edge_ref
  52.3 0.9 copy-done.12
  53.2 3.2 %ghosts.1 = (f32[12,96,128]{2,1,0:T(8,128)S(1)}, f32[2,64,128]{2,1,0:T(8,128)S(1)}, f32[2,64,128]{2,1,0:T(8,128)S(1)}) custom-call(f32[48,96,128]{2,1,0:T(8,128)S(1)} %get-tuple-element.39.op_ref.ops_ref, f32[4,64,128]{2,1,0:T(8,128)S(1)} %get-tuple-element.59.zero_ref, f32[2,64,128]{2,1,0:T(8,128)S(1)} %get-tuple-element.45.a1_ref, ...), custom_call_target="tpu_custom_call" | custom-call | flops 4194304 | bytes 2097152 | tf_op jit(solution)/shard_map/ghosts/pallas_call | solution.py:725
  56.4 0.0 copy-start.32
  56.4 0.6 copy-done.32
  57.1 0.6 copy-done.34
  57.7 0.6 copy-done.27
  58.3 3.7 %copy-done.2 = f32[48,4,96,128]{3,2,1,0:T(8,128)S(1)} copy-done((f32[48,4,96,128]{3,2,1,0:T(8,128)S(1)}, f32[48,4,96,128]{3,2,1,0:T(8,128)}, u32[]{:S(2)}) %copy-start.2) | copy-done | bytes 9437208
  62.0 0.8 copy-done.28
  62.8 0.8 copy-done.31
  63.7 0.8 copy-done.33
  64.5 0.8 copy-done.35
  65.3 6.8 %second.1 = (f32[2,64,128]{2,1,0:T(8,128)S(1)}, f32[2,64,128]{2,1,0:T(8,128)S(1)}, f32[2,64,128]{2,1,0:T(8,128)S(1)}, f32[2,64,128]{2,1,0:T(8,128)S(1)}, f32[2,6...) custom-call(s32[4,48]{1,0:T(4,128)S(1)} %bitcast.23, ...), custom_call_target="tpu_custom_call" | custom-call | flops 8388608 | bytes 4194304 | tf_op jit(solution)/shard_map/second/pallas_call | solution.py:725
  72.2 3.7 %collective-permute-start.4 = (f32[2,16,128]{2,1,0:T(8,128)S(1)}, f32[2,16,128]{2,1,0:T(8,128)S(1)}, u32[]{:S(2)}, u32[]{:S(2)}) collective-permute-start(f32[2,16,128]{2,1,0:T(8,128)S(1)} %get-tuple-element.55), channel_id=1, source_target_pairs={{0,4},{4,8},{8,12},{12,16},{16,20},{20,24},{24,28},{1,5},{5,9},{9,... | collective-permute-start | bytes 49160 | tf_op jit(solution)/shard_map/ppermute | solution.py:555
  75.9 1.9 %collective-permute-start.5 = (f32[2,16,128]{2,1,0:T(8,128)S(1)}, f32[2,16,128]{2,1,0:T(8,128)S(1)}, u32[]{:S(2)}, u32[]{:S(2)}) collective-permute-start(f32[2,16,128]{2,1,0:T(8,128)S(1)} %get-tuple-element.56), channel_id=1, source_target_pairs={{4,0},{8,4},{12,8},{16,12},{20,16},{24,20},{28,24},{5,1},{9,5},{13... | collective-permute-start | bytes 49160 | tf_op jit(solution)/shard_map/ppermute | solution.py:555
  77.8 3.3 %target.1.b1_ref.refs_5_ = f32[2,64,128]{2,1,0:T(8,128)S(1)} custom-call(s32[4,48]{1,0:T(4,128)S(1)} %bitcast.24, s32[1,200]{1,0:T(1,128)S(1)} %get-tuple-element.41.list_ref, f32[48,4,96,128]{3,2,1,0:T(8,128)S(1)} %copy-done.2, f32[48,96,128]{2,1,0:T(8,128)S(1)} %get-tuple-element.39.op_ref.ops_ref, f32[4,64,128]{2,1,0:T(8,128)S(1)} %get-tuple-element.59.zero_ref, ...), custom_call_target="tpu_custom_call" | custom-call | flops 4194304 | bytes 2097152 | tf_op jit(solution)/shard_map/target/pallas_call | solution.py:725
  81.2 0.1 collective-permute-done.5.high_ref
  81.3 0.8 moments.1
  82.1 0.6 broadcast_in_dim.5
  82.7 5.8 %all-to-all-start.1 = ((f32[8,8,128]{2,1,0:T(8,128)}), f32[8,8,128]{2,1,0:T(8,128)S(1)}, u32[]{:S(2)}, u32[]{:S(2)}) async-start(f32[8,8,128]{2,1,0:T(8,128)} %broadcast_in_dim.5), calls=%async_computation.1 | async-start | bytes 65536 | tf_op jit(solution)/shard_map/all_to_all | solution.py:541
  88.6 3.7 %copy-done.3 = f32[48,4,96,128]{3,2,1,0:T(8,128)S(1)} copy-done((f32[48,4,96,128]{3,2,1,0:T(8,128)S(1)}, f32[48,4,96,128]{3,2,1,0:T(8,128)}, u32[]{:S(2)}) %copy-start.3) | copy-done | bytes 9437208
  92.2 3.9 %third.1.refs_4_ = f32[2,64,128]{2,1,0:T(8,128)S(1)} custom-call(s32[4,48]{1,0:T(4,128)S(1)} %bitcast.25, s32[1,200]{1,0:T(1,128)S(1)} %get-tuple-element.41.list_ref, f32[48,4,96,128]{3,2,1,0:T(8,128)S(1)} %copy-done.3, f32[48,96,128]{2,1,0:T(8,128)S(1)} %get-tuple-element.39.op_ref.ops_ref, f32[12,96,128]{2,1,0:T(8,128)S(1)} %get-tuple-element.46.gop_ref, ...), custom_call_target="tpu_custom_call" | custom-call | flops 4194304 | bytes 2097152 | tf_op jit(solution)/shard_map/third/pallas_call | solution.py:725
  96.2 3.7 %copy-done.4 = f32[48,4,96,128]{3,2,1,0:T(8,128)S(1)} copy-done((f32[48,4,96,128]{3,2,1,0:T(8,128)S(1)}, f32[48,4,96,128]{3,2,1,0:T(8,128)}, u32[]{:S(2)}) %copy-start.4) | copy-done | bytes 9437208
  99.9 3.5 %fourth.1 = (f32[2,64,128]{2,1,0:T(8,128)}, f32[2,64,128]{2,1,0:T(8,128)S(1)}, f32[2,64,128]{2,1,0:T(8,128)S(1)}, f32[10,8,8,128]{3,2,1,0:T(8,128)S(1)}, f32[3,8...) custom-call(s32[4,48]{1,0:T(4,128)S(1)} %bitcast.26, s32[1,12]{1,0:T(1,128)S(1)} %copy-done.37, ...), custom_call_target="tpu_custom_call" | custom-call | flops 4194304 | bytes 2097152 | tf_op jit(solution)/shard_map/fourth/pallas_call | solution.py:725
  103.4 0.8 copy-done.17
  104.3 0.8 copy-done.19
  105.1 0.8 copy-done.21
  106.0 0.8 copy-done.23
  106.8 1.5 %combine.1 = (f32[768,128]{1,0:T(8,128)S(1)}, f32[2,2,64,128]{3,2,1,0:T(8,128)S(1)}, f32[2,64,128]{2,1,0:T(8,128)S(1)}) custom-call(f32[48,96,128]{2,1,0:T(8,128)S(1)} %get-tuple-element.39.op_ref.ops_ref, f32[10,8,8,128]{3,2,1,0:T(8,128)S(1)} %get-tuple-element.66.coef_ref, f32[4,64,128]{2,1,0:T(8,128)S(1)} %get-tuple-element.59.zero_ref, ...), custom_call_target="tpu_custom_call" | custom-call | flops 1048576 | bytes 524288 | tf_op jit(solution)/shard_map/combine/pallas_call | solution.py:725
  108.3 3.5 %collective-permute-start.8 = (f32[768,128]{1,0:T(8,128)S(1)}, f32[768,128]{1,0:T(8,128)S(1)}, u32[]{:S(2)}, u32[]{:S(2)}) collective-permute-start(f32[768,128]{1,0:T(8,128)S(1)} %get-tuple-element.68.refs_0_), channel_id=1, source_target_pairs={{0,3},{1,0},{2,1},{3,2},{4,7},{5,4},{6,5},{7,6},{8,11},{9,8},{10,9... | collective-permute-start | bytes 1179656 | tf_op jit(solution)/shard_map/ppermute | solution.py:547
  111.8 1.2 collective-permute-start.7
  113.1 0.5 collective-permute-start.6
  113.5 2.9 %collective-permute-start.9 = (f32[2,16,128]{2,1,0:T(8,128)S(1)}, f32[2,16,128]{2,1,0:T(8,128)S(1)}, u32[]{:S(2)}, u32[]{:S(2)}) collective-permute-start(f32[2,16,128]{2,1,0:T(8,128)S(1)} %get-tuple-element.73), channel_id=1, source_target_pairs={{0,4},{4,8},{8,12},{12,16},{16,20},{20,24},{24,28},{1,5},{5,9},{9,... | collective-permute-start | bytes 49160 | tf_op jit(solution)/shard_map/ppermute | solution.py:555
  116.4 2.4 %collective-permute-start.10 = (f32[2,16,128]{2,1,0:T(8,128)S(1)}, f32[2,16,128]{2,1,0:T(8,128)S(1)}, u32[]{:S(2)}, u32[]{:S(2)}) collective-permute-start(f32[2,16,128]{2,1,0:T(8,128)S(1)} %get-tuple-element.74), channel_id=1, source_target_pairs={{4,0},{8,4},{12,8},{16,12},{20,16},{24,20},{28,24},{5,1},{9,5},{13... | collective-permute-start | bytes 49160 | tf_op jit(solution)/shard_map/ppermute | solution.py:555
  118.8 3.0 %collective-permute-done.10.high_ref = f32[2,16,128]{2,1,0:T(8,128)S(1)} collective-permute-done((f32[2,16,128]{2,1,0:T(8,128)S(1)}, f32[2,16,128]{2,1,0:T(8,128)S(1)}, u32[]{:S(2)}, u32[]{:S(2)}) %collective-permute-start.10) | collective-permute-done | bytes 16416 | tf_op jit(solution)/shard_map/ppermute | solution.py:555
  121.8 3.7 %copy-done.5 = f32[48,4,96,128]{3,2,1,0:T(8,128)S(1)} copy-done((f32[48,4,96,128]{3,2,1,0:T(8,128)S(1)}, f32[48,4,96,128]{3,2,1,0:T(8,128)}, u32[]{:S(2)}) %copy-start.5) | copy-done | bytes 9437208
  125.5 3.8 %fifth.1.refs_4_ = f32[192,128]{1,0:T(8,128)S(1)} custom-call(s32[4,48]{1,0:T(4,128)S(1)} %bitcast.27, s32[1,200]{1,0:T(1,128)S(1)} %get-tuple-element.41.list_ref, s32[1,12]{1,0:T(1,128)S(1)} %copy-done.37, s32[2]{0:T(128)S(1)} %add_convert_fusion.edge_ref, f32[48,4,96,128]{3,2,1,0:T(8,128)S(1)} %copy-done.5, ...), custom_call_target="tpu_custom_call" | custom-call | flops 4194304 | bytes 2097152 | tf_op jit(solution)/shard_map/fifth/pallas_call | solution.py:725
  129.3 1.5 %collective-permute-start.13 = (f32[192,128]{1,0:T(8,128)S(1)}, f32[192,128]{1,0:T(8,128)S(1)}, u32[]{:S(2)}, u32[]{:S(2)}) collective-permute-start(f32[192,128]{1,0:T(8,128)S(1)} %fifth.1.refs_4_), channel_id=1, source_target_pairs={{0,3},{1,0},{2,1},{3,2},{4,7},{5,4},{6,5},{7,6},{8,11},{9,8},{10,9... | collective-permute-start | bytes 294920 | tf_op jit(solution)/shard_map/ppermute | solution.py:547
  130.8 0.3 collective-permute-start.12
  131.1 0.7 copy-done.14
  131.8 1.6 %collective-permute-start.11 = (f32[192,128]{1,0:T(8,128)S(1)}, f32[192,128]{1,0:T(8,128)S(1)}, u32[]{:S(2)}, u32[]{:S(2)}) collective-permute-start(f32[192,128]{1,0:T(8,128)S(1)} %fifth.1.refs_4_), channel_id=1, source_target_pairs={{0,1},{1,2},{2,3},{3,0},{4,5},{5,6},{6,7},{7,4},{8,9},{9,10},{10,1... | collective-permute-start | bytes 294920 | tf_op jit(solution)/shard_map/ppermute | solution.py:547
  133.5 0.7 reshape.35
  134.2 1.1 copy-done.15
  135.3 3.2 %mixed.1.refs_8_ = f32[48,128,128]{2,1,0:T(8,128)S(1)} custom-call(f32[768,128]{1,0:T(8,128)S(1)} %get-tuple-element.68.refs_0_, f32[768,128]{1,0:T(8,128)} %collective-permute-done.6.refs_1_, f32[768,128]{1,0:T(8,128)} %collective-permute-done.7.refs_2_, f32[768,128]{1,0:T(8,128)S(1)} %copy-done.15), custom_call_target="tpu_custom_call" | custom-call | flops 4194304 | bytes 2097152 | tf_op jit(solution)/shard_map/mixed/pallas_call | solution.py:725
  138.6 11.6 %grad.1 = f32[3456,128]{1,0:T(8,128)} custom-call(f32[768,128]{1,0:T(8,128)S(1)} %get-tuple-element.68.refs_0_, f32[768,128]{1,0:T(8,128)} %collective-permute-done.6.refs_1_, f32[768,128]{1,0:T(8,128)} %collective-permute-done.7.refs_2_, f32[768,128]{1,0:T(8,128)S(1)} %copy-done.15, f32[192,128]{1,0:T(8,128)S(1)} %fifth.1.refs_4_, ...), custom_call_target="tpu_custom_call" | custom-call | flops 4194304 | bytes 2097152 | tf_op jit(solution)/shard_map/grad/pallas_call | solution.py:725
  (69 shorter events, 0.2 us)
Async XLA Ops:
  0.6 11.3 %copy-start.29 = (s32[48,4]{0,1:T(4,128)S(1)}, s32[48,4]{0,1:T(4,128)}, u32[]{:S(2)}) copy-start(s32[48,4]{0,1:T(4,128)} %param.11) | copy-start | bytes 2308
  1.6 1.5 copy-start.7
  3.1 0.7 copy-start.36
  3.7 8.2 %copy-start.8 = (f32[48,9216]{1,0:T(8,128)S(1)}, f32[48,9216]{1,0:T(8,128)}, u32[]{:S(2)}) copy-start(f32[48,9216]{1,0:T(8,128)} %param.8) | copy-start | bytes 5308420
  6.6 30.3 %collective-permute-start = (f32[6,80,128]{2,1,0:T(8,128)}, f32[6,80,128]{2,1,0:T(8,128)S(1)}, u32[]{:S(2)}, u32[]{:S(2)}) collective-permute-start(f32[6,80,128]{2,1,0:T(8,128)} %get-tuple-element.42), channel_id=1, source_target_pairs={{0,4},{4,8},{8,12},{12,16},{16,20},{20,24},{24,28},{1,5},{5,9},{9,... | collective-permute-start | bytes 737288 | tf_op jit(solution)/shard_map/ppermute | solution.py:555
  9.8 27.2 %collective-permute-start.1 = (f32[6,80,128]{2,1,0:T(8,128)S(1)}, f32[6,80,128]{2,1,0:T(8,128)S(1)}, u32[]{:S(2)}, u32[]{:S(2)}) collective-permute-start(f32[6,80,128]{2,1,0:T(8,128)S(1)} %get-tuple-element.43), channel_id=1, source_target_pairs={{4,0},{8,4},{12,8},{16,12},{20,16},{24,20},{28,24},{5,1},{9,5},{13... | collective-permute-start | bytes 737288 | tf_op jit(solution)/shard_map/ppermute | solution.py:555
  11.9 3.0 %copy-start.6 = (f32[48,4,9216]{2,1,0:T(4,128)S(1)}, f32[48,4,9216]{2,1,0:T(4,128)}, u32[]{:S(2)}) copy-start(f32[48,4,9216]{2,1,0:T(4,128)} %param.7) | copy-start | bytes 21233668
  15.0 22.0 %copy-start.37 = (s32[1,12]{1,0:T(1,128)S(1)}, s32[1,12]{1,0:T(1,128)}, u32[]{:S(2)}) copy-start(s32[1,12]{1,0:T(1,128)} %send_ref.11) | copy-start | bytes 148
  24.9 3.7 %copy-start = (f32[48,4,96,128]{3,2,1,0:T(8,128)}, f32[48,4,96,128]{3,2,1,0:T(8,128)S(1)}, u32[]{:S(2)}) copy-start(f32[48,4,96,128]{3,2,1,0:T(8,128)S(1)} %get-tuple-element.40.blocks) | copy-start | bytes 28311556
  28.6 1.4 copy-start.9
  30.6 27.0 %all-to-all-start = ((f32[8,16,128]{2,1,0:T(8,128)}), f32[8,16,128]{2,1,0:T(8,128)S(1)}, u32[]{:S(2)}, u32[]{:S(2)}) async-start(f32[8,16,128]{2,1,0:T(8,128)} %broadcast_in_dim.4), calls=%async_computation | async-start | bytes 131072 | tf_op jit(solution)/shard_map/all_to_all | solution.py:541
  37.0 9.9 %copy-start.11 = (f32[6,80,128]{2,1,0:T(8,128)}, f32[6,80,128]{2,1,0:T(8,128)S(1)}, u32[]{:S(2)}) copy-start(f32[6,80,128]{2,1,0:T(8,128)S(1)} %collective-permute-done.1.high_ref) | copy-start | bytes 737284
  37.0 3.8 %copy-start.1 = (f32[48,4,96,128]{3,2,1,0:T(8,128)S(1)}, f32[48,4,96,128]{3,2,1,0:T(8,128)}, u32[]{:S(2)}) copy-start(f32[48,4,96,128]{3,2,1,0:T(8,128)} %copy-done) | copy-start | bytes 28311556
  46.9 11.4 %copy-start.30 = (f32[2,64,128]{2,1,0:T(8,128)}, f32[2,64,128]{2,1,0:T(8,128)S(1)}, u32[]{:S(2)}) copy-start(f32[2,64,128]{2,1,0:T(8,128)S(1)} %get-tuple-element.47.a2_in) | copy-start | bytes 196612
  46.9 11.4 %collective-permute-start.2 = (f32[2,24,128]{2,1,0:T(8,128)}, f32[2,24,128]{2,1,0:T(8,128)}, u32[]{:S(2)}, u32[]{:S(2)}) collective-permute-start(f32[2,24,128]{2,1,0:T(8,128)} %get-tuple-element.50), channel_id=1, source_target_pairs={{0,4},{4,8},{8,12},{12,16},{16,20},{20,24},{24,28},{1,5},{5,9},{9,... | collective-permute-start | bytes 73736 | tf_op jit(solution)/shard_map/ppermute | solution.py:555
  49.8 8.5 %collective-permute-start.3 = (f32[2,24,128]{2,1,0:T(8,128)}, f32[2,24,128]{2,1,0:T(8,128)}, u32[]{:S(2)}, u32[]{:S(2)}) collective-permute-start(f32[2,24,128]{2,1,0:T(8,128)} %get-tuple-element.51), channel_id=1, source_target_pairs={{4,0},{8,4},{12,8},{16,12},{20,16},{24,20},{28,24},{5,1},{9,5},{13... | collective-permute-start | bytes 73736 | tf_op jit(solution)/shard_map/ppermute | solution.py:555
  52.3 0.9 copy-start.12
  56.4 0.6 copy-start.32
  57.0 0.6 copy-start.34
  57.7 0.6 copy-start.27
  58.3 3.7 %copy-start.2 = (f32[48,4,96,128]{3,2,1,0:T(8,128)S(1)}, f32[48,4,96,128]{3,2,1,0:T(8,128)}, u32[]{:S(2)}) copy-start(f32[48,4,96,128]{3,2,1,0:T(8,128)} %copy-done) | copy-start | bytes 28311556
  62.0 0.8 copy-start.28
  62.8 0.8 copy-start.31
  63.7 0.8 copy-start.33
  64.5 0.8 copy-start.35
  65.3 12.5 %copy-start.13 = (f32[6,80,128]{2,1,0:T(8,128)S(1)}, f32[6,80,128]{2,1,0:T(8,128)}, u32[]{:S(2)}) copy-start(f32[6,80,128]{2,1,0:T(8,128)} %copy-done.11) | copy-start | bytes 737284
  72.2 9.0 %copy-start.24 = (f32[2,64,128]{2,1,0:T(8,128)}, f32[2,64,128]{2,1,0:T(8,128)S(1)}, u32[]{:S(2)}) copy-start(f32[2,64,128]{2,1,0:T(8,128)S(1)} %get-tuple-element.64.refs_2_) | copy-start | bytes 196612
  72.2 9.0 %copy-start.38 = (f32[8,128]{1,0:T(8,128)}, f32[8,128]{1,0:T(8,128)S(1)}, u32[]{:S(2)}) copy-start(f32[8,128]{1,0:T(8,128)S(1)} %get-tuple-element.61.sigma_ref) | copy-start | bytes 12292
  72.2 23.9 %copy-start.20 = (f32[2,64,128]{2,1,0:T(8,128)}, f32[2,64,128]{2,1,0:T(8,128)S(1)}, u32[]{:S(2)}) copy-start(f32[2,64,128]{2,1,0:T(8,128)S(1)} %get-tuple-element.62.refs_0_) | copy-start | bytes 196612
  72.2 23.9 %copy-start.22 = (f32[2,64,128]{2,1,0:T(8,128)}, f32[2,64,128]{2,1,0:T(8,128)S(1)}, u32[]{:S(2)}) copy-start(f32[2,64,128]{2,1,0:T(8,128)S(1)} %get-tuple-element.63.refs_1_) | copy-start | bytes 196612
  72.2 8.9 %collective-permute-start.4 = (f32[2,16,128]{2,1,0:T(8,128)S(1)}, f32[2,16,128]{2,1,0:T(8,128)S(1)}, u32[]{:S(2)}, u32[]{:S(2)}) collective-permute-start(f32[2,16,128]{2,1,0:T(8,128)S(1)} %get-tuple-element.55), channel_id=1, source_target_pairs={{0,4},{4,8},{8,12},{12,16},{16,20},{20,24},{24,28},{1,5},{5,9},{9,... | collective-permute-start | bytes 49160 | tf_op jit(solution)/shard_map/ppermute | solution.py:555
  75.9 5.4 %collective-permute-start.5 = (f32[2,16,128]{2,1,0:T(8,128)S(1)}, f32[2,16,128]{2,1,0:T(8,128)S(1)}, u32[]{:S(2)}, u32[]{:S(2)}) collective-permute-start(f32[2,16,128]{2,1,0:T(8,128)S(1)} %get-tuple-element.56), channel_id=1, source_target_pairs={{4,0},{8,4},{12,8},{16,12},{20,16},{24,20},{28,24},{5,1},{9,5},{13... | collective-permute-start | bytes 49160 | tf_op jit(solution)/shard_map/ppermute | solution.py:555
  82.1 14.1 %copy-start.16 = (f32[2,64,128]{2,1,0:T(8,128)}, f32[2,64,128]{2,1,0:T(8,128)S(1)}, u32[]{:S(2)}) copy-start(f32[2,64,128]{2,1,0:T(8,128)S(1)} %get-tuple-element.65.v4_ref.refs_3_) | copy-start | bytes 196612
  82.7 13.4 %all-to-all-start.1 = ((f32[8,8,128]{2,1,0:T(8,128)}), f32[8,8,128]{2,1,0:T(8,128)S(1)}, u32[]{:S(2)}, u32[]{:S(2)}) async-start(f32[8,8,128]{2,1,0:T(8,128)} %broadcast_in_dim.5), calls=%async_computation.1 | async-start | bytes 65536 | tf_op jit(solution)/shard_map/all_to_all | solution.py:541
  88.6 3.7 %copy-start.3 = (f32[48,4,96,128]{3,2,1,0:T(8,128)S(1)}, f32[48,4,96,128]{3,2,1,0:T(8,128)}, u32[]{:S(2)}) copy-start(f32[48,4,96,128]{3,2,1,0:T(8,128)} %copy-done) | copy-start | bytes 28311556
  92.2 3.9 %copy-start.25 = (f32[2,64,128]{2,1,0:T(8,128)S(1)}, f32[2,64,128]{2,1,0:T(8,128)}, u32[]{:S(2)}) copy-start(f32[2,64,128]{2,1,0:T(8,128)} %copy-done.24) | copy-start | bytes 196612
  92.2 3.9 %copy-start.39 = (f32[8,128]{1,0:T(8,128)S(1)}, f32[8,128]{1,0:T(8,128)}, u32[]{:S(2)}) copy-start(f32[8,128]{1,0:T(8,128)} %copy-done.38) | copy-start | bytes 12292
  96.1 7.3 %copy-start.18 = (f32[2,64,128]{2,1,0:T(8,128)}, f32[2,64,128]{2,1,0:T(8,128)S(1)}, u32[]{:S(2)}) copy-start(f32[2,64,128]{2,1,0:T(8,128)S(1)} %third.1.refs_4_) | copy-start | bytes 196612
  96.2 3.7 %copy-start.4 = (f32[48,4,96,128]{3,2,1,0:T(8,128)S(1)}, f32[48,4,96,128]{3,2,1,0:T(8,128)}, u32[]{:S(2)}) copy-start(f32[48,4,96,128]{3,2,1,0:T(8,128)} %copy-done) | copy-start | bytes 28311556
  99.9 3.6 %copy-start.26 = (f32[2,64,128]{2,1,0:T(8,128)S(1)}, f32[2,64,128]{2,1,0:T(8,128)}, u32[]{:S(2)}) copy-start(f32[2,64,128]{2,1,0:T(8,128)} %copy-done.24) | copy-start | bytes 196612
  103.4 0.8 copy-start.17
  104.3 0.8 copy-start.19
  105.1 0.8 copy-start.21
  106.0 0.8 copy-start.23
  108.3 22.8 %collective-permute-start.8 = (f32[768,128]{1,0:T(8,128)S(1)}, f32[768,128]{1,0:T(8,128)S(1)}, u32[]{:S(2)}, u32[]{:S(2)}) collective-permute-start(f32[768,128]{1,0:T(8,128)S(1)} %get-tuple-element.68.refs_0_), channel_id=1, source_target_pairs={{0,3},{1,0},{2,1},{3,2},{4,7},{5,4},{6,5},{7,6},{8,11},{9,8},{10,9... | collective-permute-start | bytes 1179656 | tf_op jit(solution)/shard_map/ppermute | solution.py:547
  111.8 22.4 %collective-permute-start.7 = (f32[768,128]{1,0:T(8,128)S(1)}, f32[768,128]{1,0:T(8,128)}, u32[]{:S(2)}, u32[]{:S(2)}) collective-permute-start(f32[768,128]{1,0:T(8,128)S(1)} %get-tuple-element.68.refs_0_), channel_id=1, source_target_pairs={{0,2},{1,3},{2,0},{3,1},{4,6},{5,7},{6,4},{7,5},{8,10},{9,11},{10,... | collective-permute-start | bytes 1179656 | tf_op jit(solution)/shard_map/ppermute | solution.py:547
  113.1 21.1 %collective-permute-start.6 = (f32[768,128]{1,0:T(8,128)S(1)}, f32[768,128]{1,0:T(8,128)}, u32[]{:S(2)}, u32[]{:S(2)}) collective-permute-start(f32[768,128]{1,0:T(8,128)S(1)} %get-tuple-element.68.refs_0_), channel_id=1, source_target_pairs={{0,1},{1,2},{2,3},{3,0},{4,5},{5,6},{6,7},{7,4},{8,9},{9,10},{10,1... | collective-permute-start | bytes 1179656 | tf_op jit(solution)/shard_map/ppermute | solution.py:547
  113.5 5.3 %collective-permute-start.9 = (f32[2,16,128]{2,1,0:T(8,128)S(1)}, f32[2,16,128]{2,1,0:T(8,128)S(1)}, u32[]{:S(2)}, u32[]{:S(2)}) collective-permute-start(f32[2,16,128]{2,1,0:T(8,128)S(1)} %get-tuple-element.73), channel_id=1, source_target_pairs={{0,4},{4,8},{8,12},{12,16},{16,20},{20,24},{24,28},{1,5},{5,9},{9,... | collective-permute-start | bytes 49160 | tf_op jit(solution)/shard_map/ppermute | solution.py:555
  116.4 5.4 %collective-permute-start.10 = (f32[2,16,128]{2,1,0:T(8,128)S(1)}, f32[2,16,128]{2,1,0:T(8,128)S(1)}, u32[]{:S(2)}, u32[]{:S(2)}) collective-permute-start(f32[2,16,128]{2,1,0:T(8,128)S(1)} %get-tuple-element.74), channel_id=1, source_target_pairs={{4,0},{8,4},{12,8},{16,12},{20,16},{24,20},{28,24},{5,1},{9,5},{13... | collective-permute-start | bytes 49160 | tf_op jit(solution)/shard_map/ppermute | solution.py:555
  121.8 3.7 %copy-start.5 = (f32[48,4,96,128]{3,2,1,0:T(8,128)S(1)}, f32[48,4,96,128]{3,2,1,0:T(8,128)}, u32[]{:S(2)}) copy-start(f32[48,4,96,128]{3,2,1,0:T(8,128)} %copy-done) | copy-start | bytes 28311556
  129.3 9.2 %collective-permute-start.13 = (f32[192,128]{1,0:T(8,128)S(1)}, f32[192,128]{1,0:T(8,128)S(1)}, u32[]{:S(2)}, u32[]{:S(2)}) collective-permute-start(f32[192,128]{1,0:T(8,128)S(1)} %fifth.1.refs_4_), channel_id=1, source_target_pairs={{0,3},{1,0},{2,1},{3,2},{4,7},{5,4},{6,5},{7,6},{8,11},{9,8},{10,9... | collective-permute-start | bytes 294920 | tf_op jit(solution)/shard_map/ppermute | solution.py:547
  130.8 7.7 %collective-permute-start.12 = (f32[192,128]{1,0:T(8,128)S(1)}, f32[192,128]{1,0:T(8,128)S(1)}, u32[]{:S(2)}, u32[]{:S(2)}) collective-permute-start(f32[192,128]{1,0:T(8,128)S(1)} %fifth.1.refs_4_), channel_id=1, source_target_pairs={{0,2},{1,3},{2,0},{3,1},{4,6},{5,7},{6,4},{7,5},{8,10},{9,11},{10,... | collective-permute-start | bytes 294920 | tf_op jit(solution)/shard_map/ppermute | solution.py:547
  131.1 0.7 copy-start.14
  131.8 6.7 %collective-permute-start.11 = (f32[192,128]{1,0:T(8,128)S(1)}, f32[192,128]{1,0:T(8,128)S(1)}, u32[]{:S(2)}, u32[]{:S(2)}) collective-permute-start(f32[192,128]{1,0:T(8,128)S(1)} %fifth.1.refs_4_), channel_id=1, source_target_pairs={{0,1},{1,2},{2,3},{3,0},{4,5},{5,6},{6,7},{7,4},{8,9},{9,10},{10,1... | collective-permute-start | bytes 294920 | tf_op jit(solution)/shard_map/ppermute | solution.py:547
  134.2 4.4 %copy-start.10 = (f32[48,96,128]{2,1,0:T(8,128)S(1)}, f32[48,96,128]{2,1,0:T(8,128)}, u32[]{:S(2)}) copy-start(f32[48,96,128]{2,1,0:T(8,128)} %copy-done.9) | copy-start | bytes 7077892
  134.2 1.1 copy-start.15

commit v4 on v3

--- a/solution.py
+++ b/solution.py
@@ -210,30 +210,32 @@
             weights = unflatten(lambda q: raw_ref[pl.ds(start + 8 * q, 8, stride=24), :])
             for r in range(vectors):
                 line = base_ref[r, pl.ds(n + OFF, 1), :]
+                ref[j, CUTS + r : CUTS + r + 1, :] = line
                 if r < vectors // 2:
-                    ref[j, CUTS + r : CUTS + r + 1, :] = line
-                inside = jnp.sum(weights * line, axis=1, keepdims=True)
-                image = line + jnp.sum(fold(weights * inside), axis=0, keepdims=True)
-                at = CUTS + vectors // 2 + r
-                ref[j, at : at + 1, :] = image
-
-
-def prepare_kernel(
-    col_ref, raw_ref, stiff_hbm, blocks_ref, weights_ref, ops_ref, list_ref, stats_ref, gram_ref, stiff_ref, sems
-):
+                    inside = jnp.sum(weights * line, axis=1, keepdims=True)
+                    image = line + jnp.sum(fold(weights * inside), axis=0, keepdims=True)
+                    at = CUTS + vectors + r
+                    ref[j, at : at + 1, :] = image
+
+
+def operator_kernel(raw_ref, weights_ref, ops_ref, squares_ref, gram_ref):
+    def step(group, squares):
+        for i in range(CHUNK):
+            n = group * CHUNK + i
+            weights = unflatten(lambda q: raw_ref[pl.ds(group * (8 * CUTS) + 8 * q + i, 8, stride=24), :])
+            weights_ref[n] = weights
+            squares = squares + fold(weights * weights)
+            ops_ref[n] = make_operator(weights, gram_ref.at[i & 1])
+        return squares
+
+    squares_ref[...] = lax.fori_loop(0, NBLK // CHUNK, step, jnp.zeros((8, LANES), f32))
+
+
+def blocks_kernel(col_ref, stiff_ref, squares_ref, blocks_ref, list_ref, stats_ref):
     mask = diagonal()
-    part = CHUNK * CUTS * K
-
-    def fetch(group):
-        at = pl.ds(group * part, part)
-        return pltpu.make_async_copy(stiff_hbm.at[at], stiff_ref.at[at], sems.at[group])
-
-    for g in range(NBLK // CHUNK):
-        fetch(g).start()
 
     def step(group, carry):
-        count, squares, traces = carry
-        fetch(group).wait()
+        count, traces = carry
         for i in range(CHUNK):
             n = group * CHUNK + i
             for k in range(K):
@@ -244,18 +246,13 @@
                 col = col_ref[k, n]
                 list_ref[0, 1 + count] = n * K + k
                 count = count + jnp.where((col < IF) | (col >= IF + NBLK), 1, 0)
-            weights = unflatten(lambda q: raw_ref[pl.ds(group * (8 * CUTS) + 8 * q + i, 8, stride=24), :])
-            weights_ref[n] = weights
-            squares = squares + fold(weights * weights)
-            ops_ref[n] = make_operator(weights, gram_ref.at[i & 1])
-        return count, squares, traces
-
-    blank = jnp.zeros((8, LANES), f32)
-    count, squares, traces = lax.fori_loop(0, NBLK // CHUNK, step, (jnp.int32(0), blank, blank))
+        return count, traces
+
+    count, traces = lax.fori_loop(0, NBLK // CHUNK, step, (jnp.int32(0), jnp.zeros((8, LANES), f32)))
     list_ref[0, 0] = count
     for u in range(4):
         list_ref[0, 1 + count + u] = 0
-    stats_ref[:8] = squares
+    stats_ref[:8] = squares_ref[...]
     stats_ref[8:] = traces
 
 
@@ -275,8 +272,9 @@
         for part, first in ((low_ref, LOW), (high_ref, HIGH)):
             for j in range(IF):
                 at = slice(first + j, first + j + 1)
-                zero_ref[r, at, :] = part[j, CUTS + r : CUTS + r + 1, :]
-                g_ref[r, at, :] = part[j, CUTS + count + r : CUTS + count + r + 1, :]
+                for s in (r, count + r):
+                    zero_ref[s, at, :] = part[j, CUTS + s : CUTS + s + 1, :]
+                g_ref[r, at, :] = part[j, CUTS + 2 * count + r : CUTS + 2 * count + r + 1, :]
     scatter_apply(blocks, op_ref, zero_ref.at[pl.ds(0, count)], y_ref, col_ref, None)
     ghost_apply(blocks, g_ref, y_ref, col_ref, list_ref)
     inner = inner_rows()
@@ -307,14 +305,11 @@
     operator_rows(op_ref, a1_ref, k1_ref, column_ref, square_ref)
 
 
-def target_kernel(col_ref, list_ref, blocks, op_ref, zero_ref, low_ref, high_ref, b1_ref, y_ref, g_ref):
+def target_kernel(col_ref, list_ref, blocks, op_ref, gop_ref, zero_ref, b1_ref, y_ref, g_ref):
     count = b1_ref.shape[0]
-    g_ref[...] = jnp.zeros_like(g_ref)
-    for r in range(count):
-        for part, first in ((low_ref, LOW), (high_ref, HIGH)):
-            for j in range(IF):
-                g_ref[r, first + j : first + j + 1, :] = part[j, CUTS + 2 * count + r : CUTS + 2 * count + r + 1, :]
-    scatter_apply(blocks, op_ref, zero_ref.at[pl.ds(count, count)], y_ref, col_ref, None)
+    target = zero_ref.at[pl.ds(count, count)]
+    scatter_apply(blocks, op_ref, target, y_ref, col_ref, None)
+    ghost_images(gop_ref, target, g_ref)
     ghost_apply(blocks, g_ref, y_ref, col_ref, list_ref)
     inner = inner_rows()
     for r in range(count):
@@ -333,7 +328,7 @@
     for s in range(1, stats_ref.shape[0]):
         squares = squares + stats_ref[s, :8]
         traces = traces + stats_ref[s, 8:]
-    scale = 1.0 / (stats_ref.shape[0] * NBLK * BS)
+    scale = 1.0 / (lax.axis_size("sub") * NBLK * BS)
     sigma = (1.0 + scale * whole_sum(squares)) * (scale * whole_sum(traces))
     sigma_ref[...] = jnp.broadcast_to(sigma, sigma_ref.shape)
     column_ref[...] = jnp.zeros_like(column_ref)
@@ -415,11 +410,11 @@
     return [jnp.where(inner, part, 0.0) for part in parts]
 
 
-def fourth_kernel(col_ref, send_ref, blocks, ops_ref, sums_ref, sigma_ref, zero_ref, *refs):
-    stored, (first_ref, base_ref, rho_ref, coef_ref, scale_ref, up_ref, down_ref, y_ref) = refs[:6], refs[6:]
-    sums = [sums_ref[s] for s in range(sums_ref.shape[0])]
+def fourth_kernel(col_ref, send_ref, blocks, ops_ref, sigma_ref, zero_ref, *refs):
+    stored, sums = refs[:6], [part[...] for part in refs[6:-8]]
+    first_ref, base_ref, rho_ref, coef_ref, scale_ref, up_ref, down_ref, y_ref = refs[-8:]
     while len(sums) > 1:
-        sums = [sum(sums[i : i + 2]) for i in range(0, len(sums), 2)]
+        sums = [sums[i] + sums[i + 1] for i in range(0, len(sums), 2)]
     sums = sums[0]
     column = lambda d: jnp.broadcast_to(sums[:, d : d + 1], (8, LANES))
     combos, scales = scalars([column(d) for d in range(8)], [column(8 + d) for d in range(4)], sigma_ref[...])
@@ -440,9 +435,9 @@
     messages(up_ref, down_ref, rho_ref, send_ref)
 
 
-def combine_kernel(ops_ref, coef_ref, zero_ref, *refs):
-    stored, (early_ref, zeta_ref, sol_ref, x_ref, column_ref, square_ref) = refs[:6], refs[6:]
-    count = zeta_ref.shape[1]
+def early_kernel(coef_ref, zero_ref, *refs):
+    stored, early_ref = refs[:6], refs[6]
+    count = zero_ref.shape[0] // 2
     for r in range(count):
         parts = sources(zero_ref, stored, r, count)
         early_ref[pl.ds(r, NBLK, stride=EARLY), :] = parts[0][OFF:HIGH]
@@ -450,6 +445,13 @@
             early_ref[pl.ds(slot + r, NBLK, stride=EARLY), :] = combine(coef_ref, parts, g, r)[OFF:HIGH]
         for slot in (8, 10):
             early_ref[pl.ds(slot + r, NBLK, stride=EARLY), :] = jnp.zeros((NBLK, LANES), f32)
+
+
+def answer_kernel(ops_ref, coef_ref, zero_ref, *refs):
+    stored, (zeta_ref, sol_ref, x_ref, column_ref, square_ref) = refs[:6], refs[6:]
+    count = zeta_ref.shape[1]
+    for r in range(count):
+        parts = sources(zero_ref, stored, r, count)
         zeta_ref[0, r] = combine(coef_ref, parts, 8, r)
         zeta_ref[1, r] = combine(coef_ref, parts, 6, r)
         x_ref[r] = combine(coef_ref, parts, 9, r)
@@ -536,9 +538,36 @@
     lax.fori_loop(0, NBLK // CHUNK, step, 0)
 
 
-def from_all(values, axis):
+def parts_over(values, axis, most):
     size = lax.axis_size(axis)
-    return lax.all_to_all(jnp.broadcast_to(values[None], (size, *values.shape)), axis, 0, 0)
+    if size & (size - 1):
+        return [lax.psum(values, axis)]
+    parts = [values]
+    step = 1
+    while step < size:
+        while len(parts) > 1:
+            parts = [parts[i] + parts[i + 1] for i in range(0, len(parts), 2)]
+        width = min(most, size // step)
+        for d in range(1, width):
+            parts.append(lax.ppermute(parts[0], axis, [(i, i ^ (d * step)) for i in range(size)]))
+        step *= width
+    return parts
+
+
+def widening(parts, axis, step, most):
+    if step is None:
+        return parts, None
+    size = lax.axis_size(axis)
+    if size & (size - 1):
+        return [lax.psum(parts[0], axis)], None
+    step = step or 1
+    while len(parts) > 1:
+        parts = [parts[i] + parts[i + 1] for i in range(0, len(parts), 2)]
+    width = min(most, size // step)
+    total = parts[0]
+    parts = [total] + [lax.ppermute(total, axis, [(i, i ^ (d * step)) for i in range(size)]) for d in range(1, width)]
+    step *= width
+    return parts, step if step < size else None
 
 
 def all_of(values, axis):
@@ -721,15 +750,15 @@
     def shape(*dims):
         return jax.ShapeDtypeStruct(dims, f32)
 
-    def call(kernel, name, scalars_in, arrays_in, outs, scratch, flops, specs=None, limit=8, in_specs=None):
+    def call(kernel, name, scalars_in, arrays_in, outs, scratch, expected, specs=None):
         return pl.pallas_call(
             kernel,
-            in_specs=in_specs or [smem()] * len(scalars_in) + [vmem()] * len(arrays_in),
+            in_specs=[smem()] * len(scalars_in) + [vmem()] * len(arrays_in),
             out_specs=specs or [vmem()] * len(outs),
             out_shape=outs,
             scratch_shapes=scratch,
-            compiler_params=pltpu.CompilerParams(vmem_limit_bytes=limit * MIB),
-            cost_estimate=pl.CostEstimate(flops=flops, bytes_accessed=flops // 2, transcendentals=0),
+            compiler_params=pltpu.CompilerParams(vmem_limit_bytes=8 * MIB),
+            cost_estimate=pl.CostEstimate(flops=MIB, bytes_accessed=int(expected * 3.2e6), transcendentals=0),
             name=name,
         )(*scalars_in, *arrays_in)
 
@@ -741,80 +770,95 @@
     turned = [pltpu.VMEM((count, BS, LANES), f32), pltpu.VMEM((LANES, LANES), f32)]
     held = lambda r: pltpu.VMEM((r, ROWS, LANES), f32)
     grams = pltpu.VMEM((2, BS, LANES), f32)
-    work = 4 * MIB
-
-    up, down = call(pack_kernel, "pack", [send_rows], [weight_cuts, base], [ghost_message] * 2, [], MIB)
+
+    up, down = call(pack_kernel, "pack", [send_rows], [weight_cuts, base], [ghost_message] * 2, [], 2)
     near, far = exchange(up, down)
 
-    blocks, weights, ops, halo_list, stats = call(
-        prepare_kernel, "prepare", [columns], [weight_cuts, stiff_cuts],
-        [
-            shape(NBLK, K, BS, LANES), shape(NBLK, BS, LANES), shape(NBLK, BS, LANES),
-            jax.ShapeDtypeStruct((1, NBLK * K + 8), jnp.int32), shape(16, LANES),
-        ],
-        [grams, pltpu.VMEM((NBLK * K * CUTS, LANES), f32), pltpu.SemaphoreType.DMA((NBLK // CHUNK,))],
-        2 * work, [vmem(), vmem(), vmem(), smem(), vmem()], 16, [smem(), vmem(), hbm()],
-    )
-    stats = from_all(stats, "sub")
+    weights, ops, squares = call(
+        operator_kernel, "operators", [], [weight_cuts],
+        [shape(NBLK, BS, LANES), shape(NBLK, BS, LANES), shape(8, LANES)], [grams], 4,
+    )
+    blocks, halo_list, stats = call(
+        blocks_kernel, "blocks", [columns], [stiff_cuts, squares],
+        [shape(NBLK, K, BS, LANES), jax.ShapeDtypeStruct((1, NBLK * K + 8), jnp.int32), shape(16, LANES)],
+        [], 5, [vmem(), smem(), vmem()],
+    )
+    stats, waiting = widening([stats], "sub", 0, 2)
 
     zero, a1, a2, up, down = call(
         first_kernel, "first", [columns, halo_list, send_rows, counts], [blocks, ops, base, near, far],
         [shape(2 * count, ROWS, LANES), rows, rows, longer, longer],
-        [partial(count), held(count)], 2 * work,
-    )
+        [partial(count), held(count)], 6,
+    )
+    stats, a2 = lax.optimization_barrier((stats, a2))
+    while waiting is not None:
+        stats, waiting = widening(stats, "sub", waiting, 4)
     low, high = exchange(up, down)
+    stats = jnp.stack(stats)
 
     gops, k0, k1 = call(
         ghost_kernel, "ghosts", [], [ops, zero, a1, near, far],
-        [shape(2 * IF, BS, LANES), rows, rows], [grams, *turned], work,
+        [shape(2 * IF, BS, LANES), rows, rows], [grams, *turned], 3,
     )
 
     v1, v2, v3, v4, k3, dots, sigma, up, down = call(
         second_kernel, "second", [columns, halo_list, send_rows, edge],
         [blocks, ops, gops, zero, a1, a2, k0, k1, low, high, stats],
         [rows, rows, rows, rows, rows, shape(count, 12, 8, LANES), shape(8, LANES), message, message],
-        [partial(count), *turned, held(count)], 2 * work,
+        [partial(count), *turned, held(count)], 7,
     )
     low, high = exchange(up, down)
 
     zero, v3 = lax.optimization_barrier((zero, v3))
     (b1,) = call(
-        target_kernel, "target", [columns, halo_list], [blocks, ops, zero, near, far], [rows],
-        [partial(count), held(count)], work,
+        target_kernel, "target", [columns, halo_list], [blocks, ops, gops, zero], [rows],
+        [partial(count), held(count)], 3,
     )
 
     v4, dots = call(
-        moment_kernel, "moments", [send_rows, edge], [v4, k3, low, high, dots, b1], [rows, shape(8, LANES)], [], MIB
-    )
-    sums = from_all(dots, "sub")
+        moment_kernel, "moments", [send_rows, edge], [v4, k3, low, high, dots, b1], [rows, shape(8, LANES)], [], 0.8
+    )
+    sums = parts_over(dots, "sub", 8)
 
     (w5,) = call(
         third_kernel, "third", [columns, halo_list], [blocks, ops, gops, v4], [rows],
-        [partial(count), held(count)], work,
+        [partial(count), held(count)], 4,
     )
 
     stored = [zero, v1, v2, v3, v4, w5, b1]
     first, fixed, rho, coefs, scales, up, down = call(
-        fourth_kernel, "fourth", [columns, send_rows], [blocks, ops, sums, sigma, *stored],
-        [rows, rows, rows, shape(10, 8, 8, LANES), shape(3, 8, LANES), message, message], [partial(count)], work,
-    )
+        fourth_kernel, "fourth", [columns, send_rows], [blocks, ops, sigma, *stored, *sums],
+        [rows, rows, rows, shape(10, 8, 8, LANES), shape(3, 8, LANES), message, message], [partial(count)], 3,
+    )
+    (early,) = call(early_kernel, "early", [], [coefs, *stored], [shape(NBLK * EARLY, LANES)], [], 0.5)
+    size = lax.axis_size("rhs")
+    early = [early]
+    if size == 4:
+        early.append(lax.ppermute(early[0], "rhs", [(i, i ^ 2) for i in range(size)]))
     low, high = exchange(up, down)
 
-    early, zeta, answer = call(
-        combine_kernel, "combine", [], [ops, coefs, *stored],
-        [shape(NBLK * EARLY, LANES), shape(2, count, ROWS, LANES), rows], [held(count), *turned], MIB,
-    )
-    early = all_of(early, "rhs")
+    zeta, answer = call(
+        answer_kernel, "answer", [], [ops, coefs, *stored],
+        [shape(2, count, ROWS, LANES), rows], [held(count), *turned], 1.5,
+    )
+    early, low, high, zeta = lax.optimization_barrier((early, low, high, zeta))
+    if size == 4:
+        early = early + [lax.ppermute(part, "rhs", [(i, i ^ 1) for i in range(size)]) for part in early]
+    else:
+        early = all_of(early[0], "rhs")
 
     (late,) = call(
         fifth_kernel, "fifth", [columns, halo_list, send_rows, edge],
         [blocks, ops, gops, rho, fixed, zeta, scales, low, high],
-        [shape(NBLK * LATE, LANES)], [partial(count), held(count), held(count)], work,
-    )
-    late = all_of(late, "rhs")
-
-    (mixed,) = call(mixed_kernel, "mixed", [], early, [shape(NBLK, LANES, LANES)], [], work)
-    (grad,) = call(grad_kernel, "grad", [], [*early, *late, mixed, weights], [shape(NBLK * CUTS, LANES)], [], work)
+        [shape(NBLK * LATE, LANES)], [partial(count), held(count), held(count)], 4,
+    )
+    if size == 4:
+        late = [late] + [lax.ppermute(late, "rhs", [(i, i ^ d) for i in range(size)]) for d in (2, 1, 3)]
+    else:
+        late = all_of(late, "rhs")
+
+    (mixed,) = call(mixed_kernel, "mixed", [], early, [shape(NBLK, LANES, LANES)], [], 3)
+    (grad,) = call(grad_kernel, "grad", [], [*early, *late, mixed, weights], [shape(NBLK * CUTS, LANES)], [], 10)
     grad = grad.reshape(NBLK // 8, CUTS, 8, LANES).transpose(0, 2, 1, 3).reshape(NBLK, BS * BS)
     return answer[:, OFF:HIGH, :BS].reshape(count, NBLK * BS), grad
 

time: 152 us -> 128 us (0.84)
  local copies, waits for them, and re-layouts: 42.3 us -> 14.7 us
  starting transfers between devices: 41.5 us -> 46.4 us
    unnamed x80 -> x20, local copies, waits for them, and re-layouts: 40.2 us -> 13.8 us
    ppermute x6 -> x17, starting transfers between devices: 8.62 us -> 23.9 us  [the longest x7 9.41 us: parts_over(): lax.ppermute(parts[0], axis, [(i, i ^ d * step) for i in range(size)])]
    all_to_all x2 -> x0, starting transfers between devices: 11.5 us -> none  [from_all(): lax.all_to_all(jnp.broadcast_to(values[None], (size, *values.shape)), axi...]
    pallas_call x13 -> x15, Pallas kernels: 60.7 us -> 60.2 us  [call(): pl.pallas_call(kernel, in_specs=[smem()] * len(scalars_in) + [vmem()] * l...]
  transfers between devices with their start and end apart: 16 -> 25, of which waited for: 2 -> 3; matrix products, arithmetic and copies ran while one was open for 1% -> 1% of each run, Pallas kernels for 22% -> 28%
where the time goes in v4:
time: 128 us; the launch traced here: 127 us
  Pallas kernels  60.2 us (47%)
  starting transfers between devices  46.4 us (36%)
  local copies, waits for them, and re-layouts  14.7 us (11%)
  waiting for transfers between devices  3.72 us (3%)
  between operations  1.66 us (1%)
    pallas_call x15, Pallas kernels, call(): pl.pallas_call(kernel, in_specs=[smem()] * len(scalars_in) + [vmem()] * l...  60.2 us
    ppermute x8, starting transfers between devices, exchange(): return (lax.ppermute(up, 'sub', rising), lax.ppermute(down, 'sub', falling))  22.4 us
    unnamed x20, local copies, waits for them, and re-layouts  13.8 us
    ppermute x7, starting transfers between devices, parts_over(): lax.ppermute(parts[0], axis, [(i, i ^ d * step) for i in range(size)])  9.41 us
    ppermute x2, starting transfers between devices, shards(): lax.ppermute(part, 'rhs', [(i, i ^ 1) for i in range(size)])  6.87 us
    ppermute x4, starting transfers between devices, widening(): lax.ppermute(total, axis, [(i, i ^ d * step) for i in range(size)])  4.5 us
  transfers between devices with their start and end apart: 25, of which 3 were waited for; matrix products, arithmetic and copies ran while one was open for 1% of the time, Pallas kernels for 28%

profile of v4, /device:TPU:13, one launch (start us, length us, event | category | flops | bytes accessed | tf_op | source)
XLA Modules:
  0.0 127.5 jit_solution(16692159904016468793)
XLA Ops:
  0.6 0.8 pad_maximum_fusion
  1.5 0.1 reshape.32
  1.6 0.0 copy-start.4
  1.6 1.5 %copy-done.4 = f32[48,9216]{1,0:T(8,128)S(1)} copy-done((f32[48,9216]{1,0:T(8,128)S(1)}, f32[48,9216]{1,0:T(8,128)}, u32[]{:S(2)}) %copy-start.4) | copy-done | bytes 1769496
  3.1 0.7 copy-done.8
  3.7 1.8 %pack.1 = (f32[6,80,128]{2,1,0:T(8,128)S(1)}, f32[6,80,128]{2,1,0:T(8,128)S(1)}) custom-call(s32[1,12]{1,0:T(1,128)S(1)} %copy-done.8, f32[3456,128]{1,0:T(8,128)S(1)} %bitcast.23, f32[4,64,128]{2,1,0:T(8,128)S(1)} %pad.4.base_ref), custom_call_target="tpu_custom_call" | custom-call | flops 1048576 | bytes 6400000 | tf_op jit(solution)/shard_map/pack/pallas_call | solution.py:754
  5.6 3.1 %collective-permute-start = (f32[6,80,128]{2,1,0:T(8,128)S(1)}, f32[6,80,128]{2,1,0:T(8,128)S(1)}, u32[]{:S(2)}, u32[]{:S(2)}) collective-permute-start(f32[6,80,128]{2,1,0:T(8,128)S(1)} %get-tuple-element.51), channel_id=1, source_target_pairs={{0,4},{4,8},{8,12},{12,16},{16,20},{20,24},{24,28},{1,5},{5,9},{9,... | collective-permute-start | bytes 737288 | tf_op jit(solution)/shard_map/ppermute | solution.py:584
  8.7 2.1 %collective-permute-start.1 = (f32[6,80,128]{2,1,0:T(8,128)S(1)}, f32[6,80,128]{2,1,0:T(8,128)S(1)}, u32[]{:S(2)}, u32[]{:S(2)}) collective-permute-start(f32[6,80,128]{2,1,0:T(8,128)S(1)} %get-tuple-element.52), channel_id=1, source_target_pairs={{4,0},{8,4},{12,8},{16,12},{20,16},{24,20},{28,24},{5,1},{9,5},{13... | collective-permute-start | bytes 737288 | tf_op jit(solution)/shard_map/ppermute | solution.py:584
  10.9 4.9 %operators.1 = (f32[48,96,128]{2,1,0:T(8,128)S(1)}, f32[48,96,128]{2,1,0:T(8,128)S(1)}, f32[8,128]{1,0:T(8,128)S(1)}) custom-call(f32[3456,128]{1,0:T(8,128)S(1)} %bitcast.24), custom_call_target="tpu_custom_call" | custom-call | flops 1048576 | bytes 12800000 | tf_op jit(solution)/shard_map/operators/pallas_call | solution.py:754
  15.8 1.4 %copy-done.5 = f32[48,96,128]{2,1,0:T(8,128)} copy-done((f32[48,96,128]{2,1,0:T(8,128)}, f32[48,96,128]{2,1,0:T(8,128)S(1)}, u32[]{:S(2)}) %copy-start.5) | copy-done | bytes 2359320
  17.2 3.0 %copy-done.3 = f32[48,4,9216]{2,1,0:T(4,128)S(1)} copy-done((f32[48,4,9216]{2,1,0:T(4,128)S(1)}, f32[48,4,9216]{2,1,0:T(4,128)}, u32[]{:S(2)}) %copy-start.3) | copy-done | bytes 7077912
  20.2 5.2 %blocks.1 = (f32[48,4,96,128]{3,2,1,0:T(8,128)S(1)}, s32[1,200]{1,0:T(1,128)S(1)}, f32[16,128]{1,0:T(8,128)S(1)}) custom-call(s32[4,48]{1,0:T(4,128)S(1)} %bitcast.25, f32[13824,128]{1,0:T(8,128)S(1)} %bitcast.22, f32[8,128]{1,0:T(8,128)S(1)} %get-tuple-element.48.squares_ref), custom_call_target="tpu_custom_call" | custom-call | flops 1048576 | bytes 16000000 | tf_op jit(solution)/shard_map/blocks/pallas_call | solution.py:754
  25.4 3.6 %copy-done = f32[48,4,96,128]{3,2,1,0:T(8,128)} copy-done((f32[48,4,96,128]{3,2,1,0:T(8,128)}, f32[48,4,96,128]{3,2,1,0:T(8,128)S(1)}, u32[]{:S(2)}) %copy-start) | copy-done | bytes 9437208
  29.0 1.1 collective-permute-start.2
  30.8 0.0 collective-permute-done.low_ref
  30.8 0.0 collective-permute-done.1.high_ref
  30.8 3.7 %copy-done.1 = f32[48,4,96,128]{3,2,1,0:T(8,128)S(1)} copy-done((f32[48,4,96,128]{3,2,1,0:T(8,128)S(1)}, f32[48,4,96,128]{3,2,1,0:T(8,128)}, u32[]{:S(2)}) %copy-start.1) | copy-done | bytes 9437208
  34.5 5.6 %first.1 = (f32[4,64,128]{2,1,0:T(8,128)S(1)}, f32[2,64,128]{2,1,0:T(8,128)S(1)}, f32[2,64,128]{2,1,0:T(8,128)S(1)}, f32[2,24,128]{2,1,0:T(8,128)S(1)}, f32[2,24,128]{2,1,0:T(8,128)S(1)}) custom-call(s32[4,48]{1,0:T(4,128)S(1)} %bitcast.26, s32[1,200]{1,0:T(1,128)S(1)} %get-tuple-element.50.list_ref, s32[1,12]{1,0:T(1,128)S(1)} %copy-done.9, ...), custom_call_target="tpu_custom_call" | custom-call | flops 1048576 | bytes 19200000 | tf_op jit(solution)/shard_map/first/pallas_call | solution.py:754
  40.1 1.1 collective-permute-start.7
  41.2 1.2 collective-permute-start.6
  42.4 1.1 collective-permute-start.5
  43.5 0.1 add_convert_fusion.edge_ref
  43.5 3.3 %collective-permute-start.3 = (f32[2,24,128]{2,1,0:T(8,128)S(1)}, f32[2,24,128]{2,1,0:T(8,128)S(1)}, u32[]{:S(2)}, u32[]{:S(2)}) collective-permute-start(f32[2,24,128]{2,1,0:T(8,128)S(1)} %get-tuple-element.61), channel_id=1, source_target_pairs={{0,4},{4,8},{8,12},{12,16},{16,20},{20,24},{24,28},{1,5},{5,9},{9,... | collective-permute-start | bytes 73736 | tf_op jit(solution)/shard_map/ppermute | solution.py:584
  46.8 2.0 %collective-permute-start.4 = (f32[2,24,128]{2,1,0:T(8,128)S(1)}, f32[2,24,128]{2,1,0:T(8,128)S(1)}, u32[]{:S(2)}, u32[]{:S(2)}) collective-permute-start(f32[2,24,128]{2,1,0:T(8,128)S(1)} %get-tuple-element.62), channel_id=1, source_target_pairs={{4,0},{8,4},{12,8},{16,12},{20,16},{24,20},{28,24},{5,1},{9,5},{13... | collective-permute-start | bytes 73736 | tf_op jit(solution)/shard_map/ppermute | solution.py:584
  48.8 3.2 %ghosts.1 = (f32[12,96,128]{2,1,0:T(8,128)S(1)}, f32[2,64,128]{2,1,0:T(8,128)S(1)}, f32[2,64,128]{2,1,0:T(8,128)S(1)}) custom-call(f32[48,96,128]{2,1,0:T(8,128)S(1)} %get-tuple-element.47.op_ref.ops_ref, f32[4,64,128]{2,1,0:T(8,128)S(1)} %get-tuple-element.67.zero_ref, f32[2,64,128]{2,1,0:T(8,128)S(1)} %get-tuple-element.54.a1_ref, ...), custom_call_target="tpu_custom_call" | custom-call | flops 1048576 | bytes 9600000 | tf_op jit(solution)/shard_map/ghosts/pallas_call | solution.py:754
  52.0 0.0 collective-permute-done.7
  52.1 0.0 collective-permute-done.3.low_ref
  52.1 0.2 collective-permute-done.4.high_ref
  52.3 6.7 %second.1 = (f32[2,64,128]{2,1,0:T(8,128)S(1)}, f32[2,64,128]{2,1,0:T(8,128)S(1)}, f32[2,64,128]{2,1,0:T(8,128)S(1)}, f32[2,64,128]{2,1,0:T(8,128)S(1)}, f32[2,6...) custom-call(s32[4,48]{1,0:T(4,128)S(1)} %bitcast.27, ...), custom_call_target="tpu_custom_call" | custom-call | flops 1048576 | bytes 22400000 | tf_op jit(solution)/shard_map/second/pallas_call | solution.py:754
  58.9 4.0 %collective-permute-start.8 = (f32[2,16,128]{2,1,0:T(8,128)S(1)}, f32[2,16,128]{2,1,0:T(8,128)S(1)}, u32[]{:S(2)}, u32[]{:S(2)}) collective-permute-start(f32[2,16,128]{2,1,0:T(8,128)S(1)} %get-tuple-element.73), channel_id=1, source_target_pairs={{0,4},{4,8},{8,12},{12,16},{16,20},{20,24},{24,28},{1,5},{5,9},{9,... | collective-permute-start | bytes 49160 | tf_op jit(solution)/shard_map/ppermute | solution.py:584
  63.0 1.9 %collective-permute-start.9 = (f32[2,16,128]{2,1,0:T(8,128)S(1)}, f32[2,16,128]{2,1,0:T(8,128)S(1)}, u32[]{:S(2)}, u32[]{:S(2)}) collective-permute-start(f32[2,16,128]{2,1,0:T(8,128)S(1)} %get-tuple-element.74), channel_id=1, source_target_pairs={{4,0},{8,4},{12,8},{16,12},{20,16},{24,20},{28,24},{5,1},{9,5},{13... | collective-permute-start | bytes 49160 | tf_op jit(solution)/shard_map/ppermute | solution.py:584
  64.9 3.7 %target.1.b1_ref.refs_5_ = f32[2,64,128]{2,1,0:T(8,128)S(1)} custom-call(s32[4,48]{1,0:T(4,128)S(1)} %bitcast.28, s32[1,200]{1,0:T(1,128)S(1)} %get-tuple-element.50.list_ref, f32[48,4,96,128]{3,2,1,0:T(8,128)S(1)} %copy-done.2, f32[48,96,128]{2,1,0:T(8,128)S(1)} %get-tuple-element.47.op_ref.ops_ref, f32[12,96,128]{2,1,0:T(8,128)S(1)} %get-tuple-element.55.gop_ref, ...), custom_call_target="tpu_custom_call" | custom-call | flops 1048576 | bytes 9600000 | tf_op jit(solution)/shard_map/target/pallas_call | solution.py:754
  68.6 0.0 collective-permute-done.8.low_ref
  68.6 0.8 moments.1
  69.4 2.4 %collective-permute-start.16 = (f32[8,128]{1,0:T(8,128)S(1)}, f32[8,128]{1,0:T(8,128)S(1)}, u32[]{:S(2)}, u32[]{:S(2)}) collective-permute-start(f32[8,128]{1,0:T(8,128)S(1)} %get-tuple-element.77.refs_6_), channel_id=1, source_target_pairs={{0,28},{4,24},{8,20},{12,16},{16,12},{20,8},{24,4},{28,0},{1,29},{... | collective-permute-start | bytes 12296 | tf_op jit(solution)/shard_map/ppermute | solution.py:552
  71.8 0.3 collective-permute-start.15
  72.1 2.8 %collective-permute-start.14 = (f32[8,128]{1,0:T(8,128)S(1)}, f32[8,128]{1,0:T(8,128)S(1)}, u32[]{:S(2)}, u32[]{:S(2)}) collective-permute-start(f32[8,128]{1,0:T(8,128)S(1)} %get-tuple-element.77.refs_6_), channel_id=1, source_target_pairs={{0,20},{4,16},{8,28},{12,24},{16,4},{20,0},{24,12},{28,8},{1,21},{... | collective-permute-start | bytes 12296 | tf_op jit(solution)/shard_map/ppermute | solution.py:552
  74.9 1.2 collective-permute-start.13
  76.2 1.2 collective-permute-start.12
  77.4 0.0 collective-permute-done.16.refs_13_
  77.4 1.2 collective-permute-start.11
  78.5 0.0 collective-permute-done.15.refs_12_
  78.5 0.3 collective-permute-start.10
  78.8 3.9 %third.1.refs_4_ = f32[2,64,128]{2,1,0:T(8,128)S(1)} custom-call(s32[4,48]{1,0:T(4,128)S(1)} %bitcast.29, s32[1,200]{1,0:T(1,128)S(1)} %get-tuple-element.50.list_ref, f32[48,4,96,128]{3,2,1,0:T(8,128)S(1)} %copy-done.2, f32[48,96,128]{2,1,0:T(8,128)S(1)} %get-tuple-element.47.op_ref.ops_ref, f32[12,96,128]{2,1,0:T(8,128)S(1)} %get-tuple-element.55.gop_ref, ...), custom_call_target="tpu_custom_call" | custom-call | flops 1048576 | bytes 12800000 | tf_op jit(solution)/shard_map/third/pallas_call | solution.py:754
  82.7 0.0 collective-permute-done.14.refs_11_
  82.7 0.0 collective-permute-done.13.refs_10_
  82.8 0.0 collective-permute-done.11.refs_8_
  82.8 3.6 %fourth.1 = (f32[2,64,128]{2,1,0:T(8,128)}, f32[2,64,128]{2,1,0:T(8,128)S(1)}, f32[2,64,128]{2,1,0:T(8,128)S(1)}, f32[10,8,8,128]{3,2,1,0:T(8,128)S(1)}, f32[3,8...) custom-call(s32[4,48]{1,0:T(4,128)S(1)} %bitcast.30, s32[1,12]{1,0:T(1,128)S(1)} %copy-done.9, ...), custom_call_target="tpu_custom_call" | custom-call | flops 1048576 | bytes 9600000 | tf_op jit(solution)/shard_map/fourth/pallas_call | solution.py:754
  86.4 0.2 early.1.refs_0_
  86.6 1.3 %collective-permute-start.17 = (f32[768,128]{1,0:T(8,128)S(1)}, f32[768,128]{1,0:T(8,128)S(1)}, u32[]{:S(2)}, u32[]{:S(2)}) collective-permute-start(f32[768,128]{1,0:T(8,128)S(1)} %early.1.refs_0_), channel_id=1, source_target_pairs={{0,2},{1,3},{2,0},{3,1},{4,6},{5,7},{6,4},{7,5},{8,10},{9,11},{10,... | collective-permute-start | bytes 1179656 | tf_op jit(solution)/shard_map/ppermute | solution.py:837
  87.8 4.0 %collective-permute-start.18 = (f32[2,16,128]{2,1,0:T(8,128)S(1)}, f32[2,16,128]{2,1,0:T(8,128)S(1)}, u32[]{:S(2)}, u32[]{:S(2)}) collective-permute-start(f32[2,16,128]{2,1,0:T(8,128)S(1)} %get-tuple-element.80), channel_id=1, source_target_pairs={{0,4},{4,8},{8,12},{12,16},{16,20},{20,24},{24,28},{1,5},{5,9},{9,... | collective-permute-start | bytes 49160 | tf_op jit(solution)/shard_map/ppermute | solution.py:584
  91.9 1.9 %collective-permute-start.19 = (f32[2,16,128]{2,1,0:T(8,128)S(1)}, f32[2,16,128]{2,1,0:T(8,128)S(1)}, u32[]{:S(2)}, u32[]{:S(2)}) collective-permute-start(f32[2,16,128]{2,1,0:T(8,128)S(1)} %get-tuple-element.81), channel_id=1, source_target_pairs={{4,0},{8,4},{12,8},{16,12},{20,16},{24,20},{28,24},{5,1},{9,5},{13... | collective-permute-start | bytes 49160 | tf_op jit(solution)/shard_map/ppermute | solution.py:584
  93.8 1.5 %answer.1 = (f32[2,2,64,128]{3,2,1,0:T(8,128)S(1)}, f32[2,64,128]{2,1,0:T(8,128)S(1)}) custom-call(f32[48,96,128]{2,1,0:T(8,128)S(1)} %get-tuple-element.47.op_ref.ops_ref, f32[10,8,8,128]{3,2,1,0:T(8,128)S(1)} %get-tuple-element.78.coef_ref, f32[4,64,128]{2,1,0:T(8,128)S(1)} %get-tuple-element.67.zero_ref, f32[2,64,128]{2,1,0:T(8,128)S(1)} %get-tuple-element.68.refs_0_, ...), custom_call_target="tpu_custom_call" | custom-call | flops 1048576 | bytes 4800000 | tf_op jit(solution)/shard_map/answer/pallas_call | solution.py:754
  95.3 0.0 collective-permute-done.18.low_ref
  95.3 2.0 %collective-permute-done.19.high_ref = f32[2,16,128]{2,1,0:T(8,128)S(1)} collective-permute-done((f32[2,16,128]{2,1,0:T(8,128)S(1)}, f32[2,16,128]{2,1,0:T(8,128)S(1)}, u32[]{:S(2)}, u32[]{:S(2)}) %collective-permute-start.19) | collective-permute-done | bytes 16416 | tf_op jit(solution)/shard_map/ppermute | solution.py:584
  97.3 6.9 %collective-permute-start.20 = (f32[768,128]{1,0:T(8,128)S(1)}, f32[768,128]{1,0:T(8,128)S(1)}, u32[]{:S(2)}, u32[]{:S(2)}) collective-permute-start(f32[768,128]{1,0:T(8,128)S(1)} %early.1.refs_0_), channel_id=1, source_target_pairs={{0,1},{1,0},{2,3},{3,2},{4,5},{5,4},{6,7},{7,6},{8,9},{9,8},{10,11... | collective-permute-start | bytes 1179656 | tf_op jit(solution)/shard_map/ppermute | solution.py:846
  104.1 0.0 collective-permute-start.21
  104.1 4.5 %fifth.1.refs_4_ = f32[192,128]{1,0:T(8,128)} custom-call(s32[4,48]{1,0:T(4,128)S(1)} %bitcast.31, s32[1,200]{1,0:T(1,128)S(1)} %get-tuple-element.50.list_ref, s32[1,12]{1,0:T(1,128)S(1)} %copy-done.9, s32[2]{0:T(128)S(1)} %add_convert_fusion.edge_ref, f32[48,4,96,128]{3,2,1,0:T(8,128)S(1)} %copy-done.2, ...), custom_call_target="tpu_custom_call" | custom-call | flops 1048576 | bytes 12800000 | tf_op jit(solution)/shard_map/fifth/pallas_call | solution.py:754
  108.6 0.6 collective-permute-start.24
  109.3 1.2 collective-permute-start.22
  110.5 0.7 reshape.33
  111.2 3.2 %mixed.1.refs_8_ = f32[48,128,128]{2,1,0:T(8,128)S(1)} custom-call(f32[768,128]{1,0:T(8,128)S(1)} %early.1.refs_0_, f32[768,128]{1,0:T(8,128)S(1)} %collective-permute-done.17.refs_1_, f32[768,128]{1,0:T(8,128)S(1)} %collective-permute-done.20.refs_2_, f32[768,128]{1,0:T(8,128)} %collective-permute-done.21.refs_3_), custom_call_target="tpu_custom_call" | custom-call | flops 1048576 | bytes 9600000 | tf_op jit(solution)/shard_map/mixed/pallas_call | solution.py:754
  114.5 1.5 %collective-permute-done.22.refs_5_ = f32[192,128]{1,0:T(8,128)S(1)} collective-permute-done((f32[192,128]{1,0:T(8,128)}, f32[192,128]{1,0:T(8,128)S(1)}, u32[]{:S(2)}, u32[]{:S(2)}) %collective-permute-start.22) | collective-permute-done | bytes 98336 | tf_op jit(solution)/shard_map/ppermute | solution.py:856
  115.9 11.5 %grad.1 = f32[3456,128]{1,0:T(8,128)} custom-call(f32[768,128]{1,0:T(8,128)S(1)} %early.1.refs_0_, f32[768,128]{1,0:T(8,128)S(1)} %collective-permute-done.17.refs_1_, f32[768,128]{1,0:T(8,128)S(1)} %collective-permute-done.20.refs_2_, f32[768,128]{1,0:T(8,128)} %collective-permute-done.21.refs_3_, f32[192,128]{1,0:T(8,128)} %fifth.1.refs_4_, ...), custom_call_target="tpu_custom_call" | custom-call | flops 1048576 | bytes 32000000 | tf_op jit(solution)/shard_map/grad/pallas_call | solution.py:754
  (29 shorter events, 0.1 us)
Async XLA Ops:
  0.6 16.6 %copy-start.7 = (s32[48,4]{0,1:T(4,128)S(1)}, s32[48,4]{0,1:T(4,128)}, u32[]{:S(2)}) copy-start(s32[48,4]{0,1:T(4,128)} %param.11) | copy-start | bytes 2308
  1.6 1.5 %copy-start.4 = (f32[48,9216]{1,0:T(8,128)S(1)}, f32[48,9216]{1,0:T(8,128)}, u32[]{:S(2)}) copy-start(f32[48,9216]{1,0:T(8,128)} %param.8) | copy-start | bytes 5308420
  3.1 0.7 copy-start.8
  5.6 25.2 %collective-permute-start = (f32[6,80,128]{2,1,0:T(8,128)S(1)}, f32[6,80,128]{2,1,0:T(8,128)S(1)}, u32[]{:S(2)}, u32[]{:S(2)}) collective-permute-start(f32[6,80,128]{2,1,0:T(8,128)S(1)} %get-tuple-element.51), channel_id=1, source_target_pairs={{0,4},{4,8},{8,12},{12,16},{16,20},{20,24},{24,28},{1,5},{5,9},{9,... | collective-permute-start | bytes 737288 | tf_op jit(solution)/shard_map/ppermute | solution.py:584
  8.7 22.1 %collective-permute-start.1 = (f32[6,80,128]{2,1,0:T(8,128)S(1)}, f32[6,80,128]{2,1,0:T(8,128)S(1)}, u32[]{:S(2)}, u32[]{:S(2)}) collective-permute-start(f32[6,80,128]{2,1,0:T(8,128)S(1)} %get-tuple-element.52), channel_id=1, source_target_pairs={{4,0},{8,4},{12,8},{16,12},{20,16},{24,20},{28,24},{5,1},{9,5},{13... | collective-permute-start | bytes 737288 | tf_op jit(solution)/shard_map/ppermute | solution.py:584
  15.8 1.4 %copy-start.5 = (f32[48,96,128]{2,1,0:T(8,128)}, f32[48,96,128]{2,1,0:T(8,128)S(1)}, u32[]{:S(2)}) copy-start(f32[48,96,128]{2,1,0:T(8,128)S(1)} %get-tuple-element.91.refs_9_) | copy-start | bytes 7077892
  17.2 3.0 %copy-start.3 = (f32[48,4,9216]{2,1,0:T(4,128)S(1)}, f32[48,4,9216]{2,1,0:T(4,128)}, u32[]{:S(2)}) copy-start(f32[48,4,9216]{2,1,0:T(4,128)} %param.7) | copy-start | bytes 21233668
  20.2 10.6 %copy-start.9 = (s32[1,12]{1,0:T(1,128)S(1)}, s32[1,12]{1,0:T(1,128)}, u32[]{:S(2)}) copy-start(s32[1,12]{1,0:T(1,128)} %send_ref.11) | copy-start | bytes 148
  25.4 3.6 %copy-start = (f32[48,4,96,128]{3,2,1,0:T(8,128)}, f32[48,4,96,128]{3,2,1,0:T(8,128)S(1)}, u32[]{:S(2)}) copy-start(f32[48,4,96,128]{3,2,1,0:T(8,128)S(1)} %get-tuple-element.49.blocks) | copy-start | bytes 28311556
  29.0 11.1 %collective-permute-start.2 = (f32[16,128]{1,0:T(8,128)S(1)}, f32[16,128]{1,0:T(8,128)S(1)}, u32[]{:S(2)}, u32[]{:S(2)}) collective-permute-start(f32[16,128]{1,0:T(8,128)S(1)} %get-tuple-element.63), channel_id=1, source_target_pairs={{0,4},{4,0},{8,12},{12,8},{16,20},{20,16},{24,28},{28,24},{1,5},{5... | collective-permute-start | bytes 24584 | tf_op jit(solution)/shard_map/ppermute | solution.py:568
  30.8 3.7 %copy-start.1 = (f32[48,4,96,128]{3,2,1,0:T(8,128)S(1)}, f32[48,4,96,128]{3,2,1,0:T(8,128)}, u32[]{:S(2)}) copy-start(f32[48,4,96,128]{3,2,1,0:T(8,128)} %copy-done) | copy-start | bytes 28311556
  34.5 17.8 %copy-start.2 = (f32[48,4,96,128]{3,2,1,0:T(8,128)S(1)}, f32[48,4,96,128]{3,2,1,0:T(8,128)}, u32[]{:S(2)}) copy-start(f32[48,4,96,128]{3,2,1,0:T(8,128)} %copy-done) | copy-start | bytes 28311556
  40.1 11.9 %collective-permute-start.7 = (f32[16,128]{1,0:T(8,128)S(1)}, f32[16,128]{1,0:T(8,128)S(1)}, u32[]{:S(2)}, u32[]{:S(2)}) collective-permute-start(f32[16,128]{1,0:T(8,128)S(1)} %add.9), channel_id=1, source_target_pairs={{0,24},{4,28},{8,16},{12,20},{16,8},{20,12},{24,0},{28,4},{1,25},{... | collective-permute-start | bytes 24584 | tf_op jit(solution)/shard_map/ppermute | solution.py:568
  41.2 10.8 %collective-permute-start.6 = (f32[16,128]{1,0:T(8,128)S(1)}, f32[16,128]{1,0:T(8,128)S(1)}, u32[]{:S(2)}, u32[]{:S(2)}) collective-permute-start(f32[16,128]{1,0:T(8,128)S(1)} %add.9), channel_id=1, source_target_pairs={{0,16},{4,20},{8,24},{12,28},{16,0},{20,4},{24,8},{28,12},{1,17},{... | collective-permute-start | bytes 24584 | tf_op jit(solution)/shard_map/ppermute | solution.py:568
  42.4 9.7 %collective-permute-start.5 = (f32[16,128]{1,0:T(8,128)S(1)}, f32[16,128]{1,0:T(8,128)S(1)}, u32[]{:S(2)}, u32[]{:S(2)}) collective-permute-start(f32[16,128]{1,0:T(8,128)S(1)} %add.9), channel_id=1, source_target_pairs={{0,8},{4,12},{8,0},{12,4},{16,24},{20,28},{24,16},{28,20},{1,9},{5... | collective-permute-start | bytes 24584 | tf_op jit(solution)/shard_map/ppermute | solution.py:568
  43.5 8.5 %collective-permute-start.3 = (f32[2,24,128]{2,1,0:T(8,128)S(1)}, f32[2,24,128]{2,1,0:T(8,128)S(1)}, u32[]{:S(2)}, u32[]{:S(2)}) collective-permute-start(f32[2,24,128]{2,1,0:T(8,128)S(1)} %get-tuple-element.61), channel_id=1, source_target_pairs={{0,4},{4,8},{8,12},{12,16},{16,20},{20,24},{24,28},{1,5},{5,9},{9,... | collective-permute-start | bytes 73736 | tf_op jit(solution)/shard_map/ppermute | solution.py:584
  46.8 5.5 %collective-permute-start.4 = (f32[2,24,128]{2,1,0:T(8,128)S(1)}, f32[2,24,128]{2,1,0:T(8,128)S(1)}, u32[]{:S(2)}, u32[]{:S(2)}) collective-permute-start(f32[2,24,128]{2,1,0:T(8,128)S(1)} %get-tuple-element.62), channel_id=1, source_target_pairs={{4,0},{8,4},{12,8},{16,12},{20,16},{24,20},{28,24},{5,1},{9,5},{13... | collective-permute-start | bytes 73736 | tf_op jit(solution)/shard_map/ppermute | solution.py:584
  58.9 9.6 %collective-permute-start.8 = (f32[2,16,128]{2,1,0:T(8,128)S(1)}, f32[2,16,128]{2,1,0:T(8,128)S(1)}, u32[]{:S(2)}, u32[]{:S(2)}) collective-permute-start(f32[2,16,128]{2,1,0:T(8,128)S(1)} %get-tuple-element.73), channel_id=1, source_target_pairs={{0,4},{4,8},{8,12},{12,16},{16,20},{20,24},{24,28},{1,5},{5,9},{9,... | collective-permute-start | bytes 49160 | tf_op jit(solution)/shard_map/ppermute | solution.py:584
  63.0 5.6 %collective-permute-start.9 = (f32[2,16,128]{2,1,0:T(8,128)S(1)}, f32[2,16,128]{2,1,0:T(8,128)S(1)}, u32[]{:S(2)}, u32[]{:S(2)}) collective-permute-start(f32[2,16,128]{2,1,0:T(8,128)S(1)} %get-tuple-element.74), channel_id=1, source_target_pairs={{4,0},{8,4},{12,8},{16,12},{20,16},{24,20},{28,24},{5,1},{9,5},{13... | collective-permute-start | bytes 49160 | tf_op jit(solution)/shard_map/ppermute | solution.py:584
  69.4 7.9 %collective-permute-start.16 = (f32[8,128]{1,0:T(8,128)S(1)}, f32[8,128]{1,0:T(8,128)S(1)}, u32[]{:S(2)}, u32[]{:S(2)}) collective-permute-start(f32[8,128]{1,0:T(8,128)S(1)} %get-tuple-element.77.refs_6_), channel_id=1, source_target_pairs={{0,28},{4,24},{8,20},{12,16},{16,12},{20,8},{24,4},{28,0},{1,29},{... | collective-permute-start | bytes 12296 | tf_op jit(solution)/shard_map/ppermute | solution.py:552
  71.8 6.7 %collective-permute-start.15 = (f32[8,128]{1,0:T(8,128)S(1)}, f32[8,128]{1,0:T(8,128)S(1)}, u32[]{:S(2)}, u32[]{:S(2)}) collective-permute-start(f32[8,128]{1,0:T(8,128)S(1)} %get-tuple-element.77.refs_6_), channel_id=1, source_target_pairs={{0,24},{4,28},{8,16},{12,20},{16,8},{20,12},{24,0},{28,4},{1,25},{... | collective-permute-start | bytes 12296 | tf_op jit(solution)/shard_map/ppermute | solution.py:552
  72.1 10.6 %collective-permute-start.14 = (f32[8,128]{1,0:T(8,128)S(1)}, f32[8,128]{1,0:T(8,128)S(1)}, u32[]{:S(2)}, u32[]{:S(2)}) collective-permute-start(f32[8,128]{1,0:T(8,128)S(1)} %get-tuple-element.77.refs_6_), channel_id=1, source_target_pairs={{0,20},{4,16},{8,28},{12,24},{16,4},{20,0},{24,12},{28,8},{1,21},{... | collective-permute-start | bytes 12296 | tf_op jit(solution)/shard_map/ppermute | solution.py:552
  74.9 7.8 %collective-permute-start.13 = (f32[8,128]{1,0:T(8,128)S(1)}, f32[8,128]{1,0:T(8,128)S(1)}, u32[]{:S(2)}, u32[]{:S(2)}) collective-permute-start(f32[8,128]{1,0:T(8,128)S(1)} %get-tuple-element.77.refs_6_), channel_id=1, source_target_pairs={{0,16},{4,20},{8,24},{12,28},{16,0},{20,4},{24,8},{28,12},{1,17},{... | collective-permute-start | bytes 12296 | tf_op jit(solution)/shard_map/ppermute | solution.py:552
  76.2 6.6 %collective-permute-start.12 = (f32[8,128]{1,0:T(8,128)S(1)}, f32[8,128]{1,0:T(8,128)S(1)}, u32[]{:S(2)}, u32[]{:S(2)}) collective-permute-start(f32[8,128]{1,0:T(8,128)S(1)} %get-tuple-element.77.refs_6_), channel_id=1, source_target_pairs={{0,12},{4,8},{8,4},{12,0},{16,28},{20,24},{24,20},{28,16},{1,13},{... | collective-permute-start | bytes 12296 | tf_op jit(solution)/shard_map/ppermute | solution.py:552
  77.4 5.4 %collective-permute-start.11 = (f32[8,128]{1,0:T(8,128)S(1)}, f32[8,128]{1,0:T(8,128)S(1)}, u32[]{:S(2)}, u32[]{:S(2)}) collective-permute-start(f32[8,128]{1,0:T(8,128)S(1)} %get-tuple-element.77.refs_6_), channel_id=1, source_target_pairs={{0,8},{4,12},{8,0},{12,4},{16,24},{20,28},{24,16},{28,20},{1,9},{5... | collective-permute-start | bytes 12296 | tf_op jit(solution)/shard_map/ppermute | solution.py:552
  78.5 4.2 %collective-permute-start.10 = (f32[8,128]{1,0:T(8,128)S(1)}, f32[8,128]{1,0:T(8,128)S(1)}, u32[]{:S(2)}, u32[]{:S(2)}) collective-permute-start(f32[8,128]{1,0:T(8,128)S(1)} %get-tuple-element.77.refs_6_), channel_id=1, source_target_pairs={{0,4},{4,0},{8,12},{12,8},{16,20},{20,16},{24,28},{28,24},{1,5},{5... | collective-permute-start | bytes 12296 | tf_op jit(solution)/shard_map/ppermute | solution.py:552
  86.6 10.7 %collective-permute-start.17 = (f32[768,128]{1,0:T(8,128)S(1)}, f32[768,128]{1,0:T(8,128)S(1)}, u32[]{:S(2)}, u32[]{:S(2)}) collective-permute-start(f32[768,128]{1,0:T(8,128)S(1)} %early.1.refs_0_), channel_id=1, source_target_pairs={{0,2},{1,3},{2,0},{3,1},{4,6},{5,7},{6,4},{7,5},{8,10},{9,11},{10,... | collective-permute-start | bytes 1179656 | tf_op jit(solution)/shard_map/ppermute | solution.py:837
  87.8 7.5 %collective-permute-start.18 = (f32[2,16,128]{2,1,0:T(8,128)S(1)}, f32[2,16,128]{2,1,0:T(8,128)S(1)}, u32[]{:S(2)}, u32[]{:S(2)}) collective-permute-start(f32[2,16,128]{2,1,0:T(8,128)S(1)} %get-tuple-element.80), channel_id=1, source_target_pairs={{0,4},{4,8},{8,12},{12,16},{16,20},{20,24},{24,28},{1,5},{5,9},{9,... | collective-permute-start | bytes 49160 | tf_op jit(solution)/shard_map/ppermute | solution.py:584
  91.9 5.4 %collective-permute-start.19 = (f32[2,16,128]{2,1,0:T(8,128)S(1)}, f32[2,16,128]{2,1,0:T(8,128)S(1)}, u32[]{:S(2)}, u32[]{:S(2)}) collective-permute-start(f32[2,16,128]{2,1,0:T(8,128)S(1)} %get-tuple-element.81), channel_id=1, source_target_pairs={{4,0},{8,4},{12,8},{16,12},{20,16},{24,20},{28,24},{5,1},{9,5},{13... | collective-permute-start | bytes 49160 | tf_op jit(solution)/shard_map/ppermute | solution.py:584
  97.3 13.9 %collective-permute-start.20 = (f32[768,128]{1,0:T(8,128)S(1)}, f32[768,128]{1,0:T(8,128)S(1)}, u32[]{:S(2)}, u32[]{:S(2)}) collective-permute-start(f32[768,128]{1,0:T(8,128)S(1)} %early.1.refs_0_), channel_id=1, source_target_pairs={{0,1},{1,0},{2,3},{3,2},{4,5},{5,4},{6,7},{7,6},{8,9},{9,8},{10,11... | collective-permute-start | bytes 1179656 | tf_op jit(solution)/shard_map/ppermute | solution.py:846
  104.1 7.1 %collective-permute-start.21 = (f32[768,128]{1,0:T(8,128)S(1)}, f32[768,128]{1,0:T(8,128)}, u32[]{:S(2)}, u32[]{:S(2)}) collective-permute-start(f32[768,128]{1,0:T(8,128)S(1)} %collective-permute-done.17.refs_1_), channel_id=1, source_target_pairs={{0,1},{1,0},{2,3},{3,2},{4,5},{5,4},{6,7},{7,6},{8,9},{9,8},{10,11... | collective-permute-start | bytes 1179656 | tf_op jit(solution)/shard_map/ppermute | solution.py:846
  108.6 5.8 %collective-permute-start.24 = (f32[192,128]{1,0:T(8,128)}, f32[192,128]{1,0:T(8,128)S(1)}, u32[]{:S(2)}, u32[]{:S(2)}) collective-permute-start(f32[192,128]{1,0:T(8,128)} %fifth.1.refs_4_), channel_id=1, source_target_pairs={{0,3},{1,2},{2,1},{3,0},{4,7},{5,6},{6,5},{7,4},{8,11},{9,10},{10,... | collective-permute-start | bytes 294920 | tf_op jit(solution)/shard_map/ppermute | solution.py:856
  109.2 5.2 %collective-permute-start.23 = (f32[192,128]{1,0:T(8,128)}, f32[192,128]{1,0:T(8,128)S(1)}, u32[]{:S(2)}, u32[]{:S(2)}) collective-permute-start(f32[192,128]{1,0:T(8,128)} %fifth.1.refs_4_), channel_id=1, source_target_pairs={{0,1},{1,0},{2,3},{3,2},{4,5},{5,4},{6,7},{7,6},{8,9},{9,8},{10,11... | collective-permute-start | bytes 294920 | tf_op jit(solution)/shard_map/ppermute | solution.py:856
  109.3 6.7 %collective-permute-start.22 = (f32[192,128]{1,0:T(8,128)}, f32[192,128]{1,0:T(8,128)S(1)}, u32[]{:S(2)}, u32[]{:S(2)}) collective-permute-start(f32[192,128]{1,0:T(8,128)} %fifth.1.refs_4_), channel_id=1, source_target_pairs={{0,2},{1,3},{2,0},{3,1},{4,6},{5,7},{6,4},{7,5},{8,10},{9,11},{10,... | collective-permute-start | bytes 294920 | tf_op jit(solution)/shard_map/ppermute | solution.py:856
  111.2 4.7 %copy-start.6 = (f32[48,96,128]{2,1,0:T(8,128)S(1)}, f32[48,96,128]{2,1,0:T(8,128)}, u32[]{:S(2)}) copy-start(f32[48,96,128]{2,1,0:T(8,128)} %copy-done.5) | copy-start | bytes 7077892

commit v5 on v4

--- a/solution.py
+++ b/solution.py
@@ -17,6 +17,7 @@
 EARLY = 16
 LATE = 4
 CUTS = BS * BS // 128
+PITCH = CUTS + 1
 LANES = 128
 OFF = 8
 ROWS = 64
@@ -198,8 +199,28 @@
     return (row >= OFF) & (row < HIGH)
 
 
-def pack_kernel(send_ref, raw_ref, base_ref, up_ref, down_ref):
+def pack_kernel(send_ref, raw_ref, stiff_ref, base_ref, up_ref, down_ref):
     vectors = base_ref.shape[0]
+    flat = lax.broadcasted_iota(jnp.int32, (CUTS, LANES), 0) * LANES
+    flat = (flat + lax.broadcasted_iota(jnp.int32, (CUTS, LANES), 1)).astype(f32)
+    step = float(BS + 1)
+    mask = jnp.where(flat - step * jnp.floor((flat + 0.5) * (1.0 / step)) == 0.0, 1.0, 0.0)
+
+    def gather(group, carry):
+        squares, traces = carry
+        for i in range(CUTS):
+            tile = raw_ref[pl.ds(pl.multiple_of(group * (8 * CUTS) + 8 * i, 8), 8), :]
+            squares = squares + tile * tile
+        for i in range(0, CHUNK, 2):
+            start = (group * CHUNK + i) * (CUTS * K)
+            for q in range(0, CUTS, 8):
+                traces = traces + mask[q : q + 8] * stiff_ref[pl.ds(start + K * q, 8, stride=K), :]
+        return squares, traces
+
+    blank = jnp.zeros((8, LANES), f32)
+    squares, traces = lax.fori_loop(0, NBLK // CHUNK, gather, (blank, blank))
+    squares = jnp.sum(squares, axis=0, keepdims=True)
+    traces = 2.0 * jnp.sum(traces, axis=0, keepdims=True)
     for part, ref in ((0, down_ref), (IF, up_ref)):
         for j in range(IF):
             n = send_ref[0, part + j]
@@ -216,44 +237,40 @@
                     image = line + jnp.sum(fold(weights * inside), axis=0, keepdims=True)
                     at = CUTS + vectors + r
                     ref[j, at : at + 1, :] = image
-
-
-def operator_kernel(raw_ref, weights_ref, ops_ref, squares_ref, gram_ref):
-    def step(group, squares):
+        ref[0, CUTS + 6 : CUTS + 7, :] = squares
+        ref[0, CUTS + 7 : CUTS + 8, :] = traces
+
+
+def operator_kernel(raw_ref, weights_ref, ops_ref, gram_ref, turn_ref):
+    def step(group, carry):
+        for q in range(CUTS):
+            tile = raw_ref[pl.ds(pl.multiple_of(group * (8 * CUTS) + 8 * q, 8), 8), :]
+            turn_ref[pl.ds(q, 8, stride=PITCH), :] = tile
         for i in range(CHUNK):
             n = group * CHUNK + i
-            weights = unflatten(lambda q: raw_ref[pl.ds(group * (8 * CUTS) + 8 * q + i, 8, stride=24), :])
+            weights = unflatten(lambda q: turn_ref[pl.ds(PITCH * i + q, 8, stride=3), :])
             weights_ref[n] = weights
-            squares = squares + fold(weights * weights)
             ops_ref[n] = make_operator(weights, gram_ref.at[i & 1])
-        return squares
-
-    squares_ref[...] = lax.fori_loop(0, NBLK // CHUNK, step, jnp.zeros((8, LANES), f32))
-
-
-def blocks_kernel(col_ref, stiff_ref, squares_ref, blocks_ref, list_ref, stats_ref):
-    mask = diagonal()
-
-    def step(group, carry):
-        count, traces = carry
+        return carry
+
+    lax.fori_loop(0, NBLK // CHUNK, step, 0)
+
+
+def blocks_kernel(col_ref, stiff_ref, blocks_ref, list_ref):
+    def step(group, count):
         for i in range(CHUNK):
             n = group * CHUNK + i
             for k in range(K):
-                block = unflatten(lambda q: stiff_ref[pl.ds(n * (CUTS * K) + 4 * q + k, 8, stride=12), :])
-                blocks_ref[n, k] = block
-                if k == 0:
-                    traces = traces + fold(jnp.where(mask, block, 0.0))
+                blocks_ref[n, k] = unflatten(lambda q: stiff_ref[pl.ds(n * (CUTS * K) + 4 * q + k, 8, stride=12), :])
                 col = col_ref[k, n]
                 list_ref[0, 1 + count] = n * K + k
                 count = count + jnp.where((col < IF) | (col >= IF + NBLK), 1, 0)
-        return count, traces
-
-    count, traces = lax.fori_loop(0, NBLK // CHUNK, step, (jnp.int32(0), jnp.zeros((8, LANES), f32)))
+        return count
+
+    count = lax.fori_loop(0, NBLK // CHUNK, step, jnp.int32(0))
     list_ref[0, 0] = count
     for u in range(4):
         list_ref[0, 1 + count + u] = 0
-    stats_ref[:8] = squares_ref[...]
-    stats_ref[8:] = traces
 
 
 def first_kernel(
@@ -324,10 +341,10 @@
 ):
     count = a1_ref.shape[0]
     inner = inner_rows()
-    squares, traces = stats_ref[0, :8], stats_ref[0, 8:]
+    squares, traces = stats_ref[0, :1], stats_ref[0, 1:]
     for s in range(1, stats_ref.shape[0]):
-        squares = squares + stats_ref[s, :8]
-        traces = traces + stats_ref[s, 8:]
+        squares = squares + stats_ref[s, :1]
+        traces = traces + stats_ref[s, 1:]
     scale = 1.0 / (lax.axis_size("sub") * NBLK * BS)
     sigma = (1.0 + scale * whole_sum(squares)) * (scale * whole_sum(traces))
     sigma_ref[...] = jnp.broadcast_to(sigma, sigma_ref.shape)
@@ -373,8 +390,7 @@
     messages(up_ref, down_ref, v4_ref, send_ref)
 
 
-def moment_kernel(send_ref, edge_ref, v4_in, k3_ref, low_ref, high_ref, dots_in, b1_ref, v4_ref, dots_ref):
-    del b1_ref
+def moment_kernel(send_ref, edge_ref, v4_in, k3_ref, low_ref, high_ref, dots_in, v4_ref, dots_ref):
     v4_ref[...] = v4_in[...]
     complete(v4_ref, low_ref, high_ref, send_ref, edge_ref)
     lane = lax.broadcasted_iota(jnp.int32, (8, LANES), 1)
@@ -506,8 +522,9 @@
 
 
 def grad_kernel(*refs):
-    peers = (len(refs) - 3) // 2
-    early, late, mixed_ref, weights_ref, grad_ref = refs[:peers], refs[peers : 2 * peers], *refs[-3:]
+    peers = (len(refs) - 4) // 2
+    early, late, mixed_ref, weights_ref, grad_ref, turn_ref = refs[:peers], refs[peers : 2 * peers], *refs[-4:]
+    group = pl.program_id(0)
     upper = lax.broadcasted_iota(jnp.int32, (8, LANES), 0) < LATE
 
     def join(tiles):
@@ -517,41 +534,23 @@
             out.append(jnp.where(upper, tiles[q], other))
         return out
 
-    def step(group, carry):
-        for i in range(CHUNK):
-            n = group * CHUNK + i
-            at = pl.multiple_of(n * EARLY, EARLY)
-            pair = pl.ds(pl.multiple_of(group * (CHUNK * LATE) + 8 * (i // 2), 8), 8)
-            resid = join([ref[pl.ds(at, 8), :] for ref in early])
-            zeta = [ref[pair, :] for ref in late]
-            zeta = join([pltpu.roll(tile, LATE, 0) for tile in zeta] if i % 2 else zeta)
-            left = jnp.concatenate(resid + zeta, axis=0)
-            right = jnp.concatenate(zeta + resid, axis=0)
-            grad = product(weights_ref[n], mixed_ref[n] + product(left, right, 0), 1)
-
-            def write(q, value):
-                grad_ref[pl.ds(group * (8 * CUTS) + 8 * q + i, 8, stride=24), :] = value
-
-            flatten(grad, write)
-        return carry
-
-    lax.fori_loop(0, NBLK // CHUNK, step, 0)
-
-
-def parts_over(values, axis, most):
-    size = lax.axis_size(axis)
-    if size & (size - 1):
-        return [lax.psum(values, axis)]
-    parts = [values]
-    step = 1
-    while step < size:
-        while len(parts) > 1:
-            parts = [parts[i] + parts[i + 1] for i in range(0, len(parts), 2)]
-        width = min(most, size // step)
-        for d in range(1, width):
-            parts.append(lax.ppermute(parts[0], axis, [(i, i ^ (d * step)) for i in range(size)]))
-        step *= width
-    return parts
+    for i in range(CHUNK):
+        n = group * CHUNK + i
+        at = pl.multiple_of(n * EARLY, EARLY)
+        pair = pl.ds(pl.multiple_of(group * (CHUNK * LATE) + 8 * (i // 2), 8), 8)
+        resid = join([ref[pl.ds(at, 8), :] for ref in early])
+        zeta = [ref[pair, :] for ref in late]
+        zeta = join([pltpu.roll(tile, LATE, 0) for tile in zeta] if i % 2 else zeta)
+        left = jnp.concatenate(resid + zeta, axis=0)
+        right = jnp.concatenate(zeta + resid, axis=0)
+        grad = product(weights_ref[n], mixed_ref[n] + product(left, right, 0), 1)
+
+        def write(q, value):
+            turn_ref[pl.ds(PITCH * i + q, 8, stride=3), :] = value
+
+        flatten(grad, write)
+    for q in range(CUTS):
+        grad_ref[8 * q : 8 * q + 8, :] = turn_ref[pl.ds(q, 8, stride=PITCH), :]
 
 
 def widening(parts, axis, step, most):
@@ -750,9 +749,10 @@
     def shape(*dims):
         return jax.ShapeDtypeStruct(dims, f32)
 
-    def call(kernel, name, scalars_in, arrays_in, outs, scratch, expected, specs=None):
+    def call(kernel, name, scalars_in, arrays_in, outs, scratch, expected, specs=None, grid=()):
         return pl.pallas_call(
             kernel,
+            grid=grid,
             in_specs=[smem()] * len(scalars_in) + [vmem()] * len(arrays_in),
             out_specs=specs or [vmem()] * len(outs),
             out_shape=outs,
@@ -770,29 +770,36 @@
     turned = [pltpu.VMEM((count, BS, LANES), f32), pltpu.VMEM((LANES, LANES), f32)]
     held = lambda r: pltpu.VMEM((r, ROWS, LANES), f32)
     grams = pltpu.VMEM((2, BS, LANES), f32)
-
-    up, down = call(pack_kernel, "pack", [send_rows], [weight_cuts, base], [ghost_message] * 2, [], 2)
+    turn = pltpu.VMEM((8 * PITCH, LANES), f32)
+
+    up, down = call(
+        pack_kernel, "pack", [send_rows], [weight_cuts, stiff_cuts, base], [ghost_message] * 2, [], 3
+    )
     near, far = exchange(up, down)
 
-    weights, ops, squares = call(
-        operator_kernel, "operators", [], [weight_cuts],
-        [shape(NBLK, BS, LANES), shape(NBLK, BS, LANES), shape(8, LANES)], [grams], 4,
-    )
-    blocks, halo_list, stats = call(
-        blocks_kernel, "blocks", [columns], [stiff_cuts, squares],
-        [shape(NBLK, K, BS, LANES), jax.ShapeDtypeStruct((1, NBLK * K + 8), jnp.int32), shape(16, LANES)],
-        [], 5, [vmem(), smem(), vmem()],
-    )
-    stats, waiting = widening([stats], "sub", 0, 2)
+    weights, ops = call(
+        operator_kernel, "operators", [], [weight_cuts], [shape(NBLK, BS, LANES), shape(NBLK, BS, LANES)],
+        [grams, turn], 4,
+    )
+    stats, partner = up[0, CUTS + 6 :], jnp.where(sub % 2 == 0, far[0, CUTS + 6 :], near[0, CUTS + 6 :])
+    if size > 1 and size & (size - 1) == 0:
+        stats, waiting = [stats + partner], 2
+    else:
+        stats, waiting = [stats], 0
+    stats, near, far, ops = lax.optimization_barrier((stats, near, far, ops))
+    while waiting is not None and waiting < size:
+        stats, waiting = widening(stats, "sub", waiting, 4)
+    blocks, halo_list = call(
+        blocks_kernel, "blocks", [columns], [stiff_cuts],
+        [shape(NBLK, K, BS, LANES), jax.ShapeDtypeStruct((1, NBLK * K + 8), jnp.int32)],
+        [], 5, [vmem(), smem()],
+    )
 
     zero, a1, a2, up, down = call(
         first_kernel, "first", [columns, halo_list, send_rows, counts], [blocks, ops, base, near, far],
         [shape(2 * count, ROWS, LANES), rows, rows, longer, longer],
         [partial(count), held(count)], 6,
     )
-    stats, a2 = lax.optimization_barrier((stats, a2))
-    while waiting is not None:
-        stats, waiting = widening(stats, "sub", waiting, 4)
     low, high = exchange(up, down)
     stats = jnp.stack(stats)
 
@@ -809,16 +816,18 @@
     )
     low, high = exchange(up, down)
 
-    zero, v3 = lax.optimization_barrier((zero, v3))
+    v4, dots = call(
+        moment_kernel, "moments", [send_rows, edge], [v4, k3, low, high, dots], [rows, shape(8, LANES)], [], 0.8
+    )
+    sums, waiting = widening([dots], "sub", 0, 2)
+    zero, v4 = lax.optimization_barrier((zero, v4))
     (b1,) = call(
         target_kernel, "target", [columns, halo_list], [blocks, ops, gops, zero], [rows],
         [partial(count), held(count)], 3,
     )
-
-    v4, dots = call(
-        moment_kernel, "moments", [send_rows, edge], [v4, k3, low, high, dots, b1], [rows, shape(8, LANES)], [], 0.8
-    )
-    sums = parts_over(dots, "sub", 8)
+    sums, b1, v4 = lax.optimization_barrier((sums, b1, v4))
+    while waiting is not None:
+        sums, waiting = widening(sums, "sub", waiting, 4)
 
     (w5,) = call(
         third_kernel, "third", [columns, halo_list], [blocks, ops, gops, v4], [rows],
@@ -858,7 +867,10 @@
         late = all_of(late, "rhs")
 
     (mixed,) = call(mixed_kernel, "mixed", [], early, [shape(NBLK, LANES, LANES)], [], 3)
-    (grad,) = call(grad_kernel, "grad", [], [*early, *late, mixed, weights], [shape(NBLK * CUTS, LANES)], [], 10)
+    (grad,) = call(
+        grad_kernel, "grad", [], [*early, *late, mixed, weights], [shape(NBLK * CUTS, LANES)],
+        [turn], 10, [pl.BlockSpec((8 * CUTS, LANES), lambda g: (g, 0))], (NBLK // 8,),
+    )
     grad = grad.reshape(NBLK // 8, CUTS, 8, LANES).transpose(0, 2, 1, 3).reshape(NBLK, BS * BS)
     return answer[:, OFF:HIGH, :BS].reshape(count, NBLK * BS), grad
 

time: 128 us -> 120 us (0.938)
  starting transfers between devices: 46.4 us -> 39.5 us
  waiting for transfers between devices: 3.72 us -> 10.5 us
  local copies, waits for them, and re-layouts: 14.7 us -> 10.4 us
  Pallas kernels: 60.2 us -> 56.6 us
    ppermute x7 -> x0, starting transfers between devices: 9.41 us -> none  [parts_over(): lax.ppermute(parts[0], axis, [(i, i ^ d * step) for i in range(size)])]
    ppermute x8, waiting for transfers between devices: 2.19 us -> 7.99 us  [exchange(): return (lax.ppermute(up, 'sub', rising), lax.ppermute(down, 'sub', falling))]
    unnamed x20 -> x18, local copies, waits for them, and re-layouts: 13.8 us -> 9.57 us
    pallas_call x15, Pallas kernels: 60.2 us -> 56.6 us  [call(): pl.pallas_call(kernel, grid=grid, in_specs=[smem()] * len(scalars_in) + [...]
    ppermute x4 -> x7, starting transfers between devices: 4.5 us -> 5.7 us  [widening(): lax.ppermute(total, axis, [(i, i ^ d * step) for i in range(size)])]
  transfers between devices with their start and end apart: 25 -> 21, of which waited for: 3 -> 5; matrix products, arithmetic and copies ran while one was open for 1% -> 1% of each run, Pallas kernels for 28% -> 28%
where the time goes in v5:
time: 120 us
  Pallas kernels  56.6 us (47%)
  starting transfers between devices  39.5 us (33%)
  waiting for transfers between devices  10.5 us (9%)
  local copies, waits for them, and re-layouts  10.4 us (9%)
  between operations  1.62 us (1%)
    pallas_call x15, Pallas kernels, call(): pl.pallas_call(kernel, grid=grid, in_specs=[smem()] * len(scalars_in) + [...  56.6 us
    ppermute x8, starting transfers between devices, exchange(): return (lax.ppermute(up, 'sub', rising), lax.ppermute(down, 'sub', falling))  23.4 us
    unnamed x18, local copies, waits for them, and re-layouts  9.57 us
    ppermute x8, waiting for transfers between devices, exchange(): return (lax.ppermute(up, 'sub', rising), lax.ppermute(down, 'sub', falling))  7.99 us
    ppermute x2, starting transfers between devices, shards(): lax.ppermute(part, 'rhs', [(i, i ^ 1) for i in range(size)])  7.21 us
    ppermute x7, starting transfers between devices, widening(): lax.ppermute(total, axis, [(i, i ^ d * step) for i in range(size)])  5.7 us
    ppermute x3, waiting for transfers between devices, shards(): lax.ppermute(late, 'rhs', [(i, i ^ d) for i in range(size)])  2.44 us
  transfers between devices with their start and end apart: 21, of which 5 were waited for; matrix products, arithmetic and copies ran while one was open for 1% of the time, Pallas kernels for 28%

profile of v5, /device:TPU:13, one launch (start us, length us, event | category | flops | bytes accessed | tf_op | source)
XLA Modules:
  0.0 119.5 jit_solution(5135620217038646410)
XLA Ops:
  0.6 0.8 pad_maximum_fusion
  1.5 0.1 reshape.35
  1.6 0.0 copy-start
  1.6 3.0 %copy-done = f32[48,4,9216]{2,1,0:T(4,128)S(1)} copy-done((f32[48,4,9216]{2,1,0:T(4,128)S(1)}, f32[48,4,9216]{2,1,0:T(4,128)}, u32[]{:S(2)}) %copy-start) | copy-done | bytes 7077912
  4.6 1.5 %copy-done.2 = f32[48,9216]{1,0:T(8,128)S(1)} copy-done((f32[48,9216]{1,0:T(8,128)S(1)}, f32[48,9216]{1,0:T(8,128)}, u32[]{:S(2)}) %copy-start.2) | copy-done | bytes 1769496
  6.1 0.7 copy-done.7
  6.7 2.3 %pack.1 = (f32[6,80,128]{2,1,0:T(8,128)S(1)}, f32[6,80,128]{2,1,0:T(8,128)S(1)}) custom-call(s32[1,12]{1,0:T(1,128)S(1)} %copy-done.7, f32[3456,128]{1,0:T(8,128)S(1)} %bitcast.26, f32[13824,128]{1,0:T(8,128)S(1)} %bitcast.24, f32[4,64,128]{2,1,0:T(8,128)S(1)} %pad.4.base_ref), custom_call_target="tpu_custom_call" | custom-call | flops 1048576 | bytes 9600000 | tf_op jit(solution)/shard_map/pack/pallas_call | solution.py:753
  9.0 2.1 %collective-permute-start = (f32[6,80,128]{2,1,0:T(8,128)S(1)}, f32[6,80,128]{2,1,0:T(8,128)S(1)}, u32[]{:S(2)}, u32[]{:S(2)}) collective-permute-start(f32[6,80,128]{2,1,0:T(8,128)S(1)} %get-tuple-element.51), channel_id=1, source_target_pairs={{4,0},{8,4},{12,8},{16,12},{20,16},{24,20},{28,24},{5,1},{9,5},{13... | collective-permute-start | bytes 737288 | tf_op jit(solution)/shard_map/ppermute | solution.py:583
  11.2 4.0 %collective-permute-start.1 = (f32[6,80,128]{2,1,0:T(8,128)S(1)}, f32[6,80,128]{2,1,0:T(8,128)S(1)}, u32[]{:S(2)}, u32[]{:S(2)}) collective-permute-start(f32[6,80,128]{2,1,0:T(8,128)S(1)} %get-tuple-element.50), channel_id=1, source_target_pairs={{0,4},{4,8},{8,12},{12,16},{16,20},{20,24},{24,28},{1,5},{5,9},{9,... | collective-permute-start | bytes 737288 | tf_op jit(solution)/shard_map/ppermute | solution.py:583
  15.9 5.0 %operators.1 = (f32[48,96,128]{2,1,0:T(8,128)S(1)}, f32[48,96,128]{2,1,0:T(8,128)S(1)}) custom-call(f32[3456,128]{1,0:T(8,128)S(1)} %bitcast.27), custom_call_target="tpu_custom_call" | custom-call | flops 1048576 | bytes 12800000 | tf_op jit(solution)/shard_map/operators/pallas_call | solution.py:753
  20.9 1.4 %copy-done.4 = f32[48,96,128]{2,1,0:T(8,128)} copy-done((f32[48,96,128]{2,1,0:T(8,128)}, f32[48,96,128]{2,1,0:T(8,128)S(1)}, u32[]{:S(2)}) %copy-start.4) | copy-done | bytes 2359320
  22.3 0.1 add_convert_fusion.edge_ref
  22.4 0.0 collective-permute-done.high_ref
  22.4 2.6 %collective-permute-done.1.low_ref = f32[6,80,128]{2,1,0:T(8,128)S(1)} collective-permute-done((f32[6,80,128]{2,1,0:T(8,128)S(1)}, f32[6,80,128]{2,1,0:T(8,128)S(1)}, u32[]{:S(2)}, u32[]{:S(2)}) %collective-permute-start.1) | collective-permute-done | bytes 245792 | tf_op jit(solution)/shard_map/ppermute | solution.py:583
  25.0 1.3 %collective-permute-start.6 = (f32[2,128]{1,0:T(2,128)S(1)}, f32[2,128]{1,0:T(2,128)S(1)}, u32[]{:S(2)}, u32[]{:S(2)}) collective-permute-start(f32[2,128]{1,0:T(2,128)S(1)} %fusion.1), channel_id=1, source_target_pairs={{0,24},{4,28},{8,16},{12,20},{16,8},{20,12},{24,0},{28,4},{1,25},{... | collective-permute-start | bytes 3080 | tf_op jit(solution)/shard_map/ppermute | solution.py:567
  26.2 1.0 collective-permute-start.5
  27.2 0.4 collective-permute-start.4
  27.6 3.0 %copy-done.1 = f32[48,4,9216]{2,1,0:T(4,128)S(1)} copy-done((f32[48,4,9216]{2,1,0:T(4,128)S(1)}, f32[48,4,9216]{2,1,0:T(4,128)}, u32[]{:S(2)}) %copy-start.1) | copy-done | bytes 7077912
  30.6 5.2 %blocks.1 = (f32[48,4,96,128]{3,2,1,0:T(8,128)S(1)}, s32[1,200]{1,0:T(1,128)S(1)}) custom-call(s32[4,48]{1,0:T(4,128)S(1)} %bitcast.28, f32[13824,128]{1,0:T(8,128)S(1)} %bitcast.25), custom_call_target="tpu_custom_call" | custom-call | flops 1048576 | bytes 16000000 | tf_op jit(solution)/shard_map/blocks/pallas_call | solution.py:753
  35.9 5.3 %first.1 = (f32[4,64,128]{2,1,0:T(8,128)S(1)}, f32[2,64,128]{2,1,0:T(8,128)S(1)}, f32[2,64,128]{2,1,0:T(8,128)S(1)}, f32[2,24,128]{2,1,0:T(8,128)S(1)}, f32[2,24,128]{2,1,0:T(8,128)S(1)}) custom-call(s32[4,48]{1,0:T(4,128)S(1)} %bitcast.29, s32[1,200]{1,0:T(1,128)S(1)} %get-tuple-element.55.list_ref, s32[1,12]{1,0:T(1,128)S(1)} %copy-done.8, ...), custom_call_target="tpu_custom_call" | custom-call | flops 1048576 | bytes 19200000 | tf_op jit(solution)/shard_map/first/pallas_call | solution.py:753
  41.2 2.5 %collective-permute-start.2 = (f32[2,24,128]{2,1,0:T(8,128)S(1)}, f32[2,24,128]{2,1,0:T(8,128)S(1)}, u32[]{:S(2)}, u32[]{:S(2)}) collective-permute-start(f32[2,24,128]{2,1,0:T(8,128)S(1)} %get-tuple-element.64), channel_id=1, source_target_pairs={{0,4},{4,8},{8,12},{12,16},{16,20},{20,24},{24,28},{1,5},{5,9},{9,... | collective-permute-start | bytes 73736 | tf_op jit(solution)/shard_map/ppermute | solution.py:583
  43.6 2.8 %collective-permute-start.3 = (f32[2,24,128]{2,1,0:T(8,128)S(1)}, f32[2,24,128]{2,1,0:T(8,128)S(1)}, u32[]{:S(2)}, u32[]{:S(2)}) collective-permute-start(f32[2,24,128]{2,1,0:T(8,128)S(1)} %get-tuple-element.65), channel_id=1, source_target_pairs={{4,0},{8,4},{12,8},{16,12},{20,16},{24,20},{28,24},{5,1},{9,5},{13... | collective-permute-start | bytes 73736 | tf_op jit(solution)/shard_map/ppermute | solution.py:583
  46.5 3.2 %ghosts.1 = (f32[12,96,128]{2,1,0:T(8,128)S(1)}, f32[2,64,128]{2,1,0:T(8,128)S(1)}, f32[2,64,128]{2,1,0:T(8,128)S(1)}) custom-call(f32[48,96,128]{2,1,0:T(8,128)S(1)} %get-tuple-element.53.op_ref.ops_ref, f32[4,64,128]{2,1,0:T(8,128)S(1)} %get-tuple-element.74.zero_ref, f32[2,64,128]{2,1,0:T(8,128)S(1)} %get-tuple-element.59.a1_ref, ...), custom_call_target="tpu_custom_call" | custom-call | flops 1048576 | bytes 9600000 | tf_op jit(solution)/shard_map/ghosts/pallas_call | solution.py:753
  49.7 0.0 collective-permute-done.6
  49.7 0.0 collective-permute-done.5
  49.7 0.0 collective-permute-done.4
  49.8 0.0 collective-permute-done.2.low_ref
  49.8 0.0 collective-permute-done.3.high_ref
  49.8 6.5 %second.1 = (f32[2,64,128]{2,1,0:T(8,128)S(1)}, f32[2,64,128]{2,1,0:T(8,128)S(1)}, f32[2,64,128]{2,1,0:T(8,128)S(1)}, f32[2,64,128]{2,1,0:T(8,128)S(1)}, f32[2,6...) custom-call(s32[4,48]{1,0:T(4,128)S(1)} %bitcast.30, ...), custom_call_target="tpu_custom_call" | custom-call | flops 1048576 | bytes 22400000 | tf_op jit(solution)/shard_map/second/pallas_call | solution.py:753
  56.3 3.6 %collective-permute-start.7 = (f32[2,16,128]{2,1,0:T(8,128)S(1)}, f32[2,16,128]{2,1,0:T(8,128)S(1)}, u32[]{:S(2)}, u32[]{:S(2)}) collective-permute-start(f32[2,16,128]{2,1,0:T(8,128)S(1)} %get-tuple-element.70), channel_id=1, source_target_pairs={{0,4},{4,8},{8,12},{12,16},{16,20},{20,24},{24,28},{1,5},{5,9},{9,... | collective-permute-start | bytes 49160 | tf_op jit(solution)/shard_map/ppermute | solution.py:583
  59.9 1.9 %collective-permute-start.8 = (f32[2,16,128]{2,1,0:T(8,128)S(1)}, f32[2,16,128]{2,1,0:T(8,128)S(1)}, u32[]{:S(2)}, u32[]{:S(2)}) collective-permute-start(f32[2,16,128]{2,1,0:T(8,128)S(1)} %get-tuple-element.71), channel_id=1, source_target_pairs={{4,0},{8,4},{12,8},{16,12},{20,16},{24,20},{28,24},{5,1},{9,5},{13... | collective-permute-start | bytes 49160 | tf_op jit(solution)/shard_map/ppermute | solution.py:583
  61.8 0.0 collective-permute-done.7.low_ref
  61.8 3.4 %collective-permute-done.8.high_ref = f32[2,16,128]{2,1,0:T(8,128)S(1)} collective-permute-done((f32[2,16,128]{2,1,0:T(8,128)S(1)}, f32[2,16,128]{2,1,0:T(8,128)S(1)}, u32[]{:S(2)}, u32[]{:S(2)}) %collective-permute-start.8) | collective-permute-done | bytes 16416 | tf_op jit(solution)/shard_map/ppermute | solution.py:583
  65.3 0.8 moments.1
  66.1 0.1 collective-permute-start.9
  66.1 3.5 %target.1.refs_5_ = f32[2,64,128]{2,1,0:T(8,128)S(1)} custom-call(s32[4,48]{1,0:T(4,128)S(1)} %bitcast.31, s32[1,200]{1,0:T(1,128)S(1)} %get-tuple-element.55.list_ref, f32[48,4,96,128]{3,2,1,0:T(8,128)S(1)} %get-tuple-element.54.blocks, f32[48,96,128]{2,1,0:T(8,128)S(1)} %get-tuple-element.53.op_ref.ops_ref, f32[12,96,128]{2,1,0:T(8,128)S(1)} %get-tuple-element.60.gop_ref, ...), custom_call_target="tpu_custom_call" | custom-call | flops 1048576 | bytes 9600000 | tf_op jit(solution)/shard_map/target/pallas_call | solution.py:753
  69.7 0.0 collective-permute-done.9
  69.7 1.4 %collective-permute-start.12 = (f32[8,128]{1,0:T(8,128)S(1)}, f32[8,128]{1,0:T(8,128)S(1)}, u32[]{:S(2)}, u32[]{:S(2)}) collective-permute-start(f32[8,128]{1,0:T(8,128)S(1)} %add.22.refs_6_), channel_id=1, source_target_pairs={{0,24},{4,28},{8,16},{12,20},{16,8},{20,12},{24,0},{28,4},{1,25},{... | collective-permute-start | bytes 12296 | tf_op jit(solution)/shard_map/ppermute | solution.py:567
  71.1 1.6 %collective-permute-start.11 = (f32[8,128]{1,0:T(8,128)S(1)}, f32[8,128]{1,0:T(8,128)S(1)}, u32[]{:S(2)}, u32[]{:S(2)}) collective-permute-start(f32[8,128]{1,0:T(8,128)S(1)} %add.22.refs_6_), channel_id=1, source_target_pairs={{0,16},{4,20},{8,24},{12,28},{16,0},{20,4},{24,8},{28,12},{1,17},{... | collective-permute-start | bytes 12296 | tf_op jit(solution)/shard_map/ppermute | solution.py:567
  72.7 0.0 collective-permute-start.10
  72.7 3.7 %third.1.refs_4_ = f32[2,64,128]{2,1,0:T(8,128)S(1)} custom-call(s32[4,48]{1,0:T(4,128)S(1)} %bitcast.32, s32[1,200]{1,0:T(1,128)S(1)} %get-tuple-element.55.list_ref, f32[48,4,96,128]{3,2,1,0:T(8,128)S(1)} %get-tuple-element.54.blocks, f32[48,96,128]{2,1,0:T(8,128)S(1)} %get-tuple-element.53.op_ref.ops_ref, f32[12,96,128]{2,1,0:T(8,128)S(1)} %get-tuple-element.60.gop_ref, ...), custom_call_target="tpu_custom_call" | custom-call | flops 1048576 | bytes 12800000 | tf_op jit(solution)/shard_map/third/pallas_call | solution.py:753
  76.4 0.0 collective-permute-done.11.refs_8_
  76.4 0.0 collective-permute-done.10.refs_7_
  76.5 3.4 %fourth.1 = (f32[2,64,128]{2,1,0:T(8,128)}, f32[2,64,128]{2,1,0:T(8,128)S(1)}, f32[2,64,128]{2,1,0:T(8,128)S(1)}, f32[10,8,8,128]{3,2,1,0:T(8,128)S(1)}, f32[3,8...) custom-call(s32[4,48]{1,0:T(4,128)S(1)} %bitcast.33, s32[1,12]{1,0:T(1,128)S(1)} %copy-done.8, ...), custom_call_target="tpu_custom_call" | custom-call | flops 1048576 | bytes 9600000 | tf_op jit(solution)/shard_map/fourth/pallas_call | solution.py:753
  79.9 0.2 early.1.refs_0_
  80.1 1.3 %collective-permute-start.13 = (f32[768,128]{1,0:T(8,128)S(1)}, f32[768,128]{1,0:T(8,128)S(1)}, u32[]{:S(2)}, u32[]{:S(2)}) collective-permute-start(f32[768,128]{1,0:T(8,128)S(1)} %early.1.refs_0_), channel_id=1, source_target_pairs={{0,2},{1,3},{2,0},{3,1},{4,6},{5,7},{6,4},{7,5},{8,10},{9,11},{10,... | collective-permute-start | bytes 1179656 | tf_op jit(solution)/shard_map/ppermute | solution.py:846
  81.4 4.5 %collective-permute-start.14 = (f32[2,16,128]{2,1,0:T(8,128)S(1)}, f32[2,16,128]{2,1,0:T(8,128)S(1)}, u32[]{:S(2)}, u32[]{:S(2)}) collective-permute-start(f32[2,16,128]{2,1,0:T(8,128)S(1)} %get-tuple-element.86), channel_id=1, source_target_pairs={{0,4},{4,8},{8,12},{12,16},{16,20},{20,24},{24,28},{1,5},{5,9},{9,... | collective-permute-start | bytes 49160 | tf_op jit(solution)/shard_map/ppermute | solution.py:583
  85.9 1.9 %collective-permute-start.15 = (f32[2,16,128]{2,1,0:T(8,128)S(1)}, f32[2,16,128]{2,1,0:T(8,128)S(1)}, u32[]{:S(2)}, u32[]{:S(2)}) collective-permute-start(f32[2,16,128]{2,1,0:T(8,128)S(1)} %get-tuple-element.87), channel_id=1, source_target_pairs={{4,0},{8,4},{12,8},{16,12},{20,16},{24,20},{28,24},{5,1},{9,5},{13... | collective-permute-start | bytes 49160 | tf_op jit(solution)/shard_map/ppermute | solution.py:583
  87.8 1.5 %answer.1 = (f32[2,2,64,128]{3,2,1,0:T(8,128)S(1)}, f32[2,64,128]{2,1,0:T(8,128)S(1)}) custom-call(f32[48,96,128]{2,1,0:T(8,128)S(1)} %get-tuple-element.53.op_ref.ops_ref, f32[10,8,8,128]{3,2,1,0:T(8,128)S(1)} %get-tuple-element.84.coef_ref, f32[4,64,128]{2,1,0:T(8,128)S(1)} %get-tuple-element.74.zero_ref, f32[2,64,128]{2,1,0:T(8,128)S(1)} %get-tuple-element.75.refs_0_, ...), custom_call_target="tpu_custom_call" | custom-call | flops 1048576 | bytes 4800000 | tf_op jit(solution)/shard_map/answer/pallas_call | solution.py:753
  89.3 0.0 collective-permute-done.14.low_ref
  89.3 2.0 %collective-permute-done.15.high_ref = f32[2,16,128]{2,1,0:T(8,128)S(1)} collective-permute-done((f32[2,16,128]{2,1,0:T(8,128)S(1)}, f32[2,16,128]{2,1,0:T(8,128)S(1)}, u32[]{:S(2)}, u32[]{:S(2)}) %collective-permute-start.15) | collective-permute-done | bytes 16416 | tf_op jit(solution)/shard_map/ppermute | solution.py:583
  91.3 0.0 collective-permute-done.13.refs_1_
  91.3 7.2 %collective-permute-start.16 = (f32[768,128]{1,0:T(8,128)S(1)}, f32[768,128]{1,0:T(8,128)S(1)}, u32[]{:S(2)}, u32[]{:S(2)}) collective-permute-start(f32[768,128]{1,0:T(8,128)S(1)} %early.1.refs_0_), channel_id=1, source_target_pairs={{0,1},{1,0},{2,3},{3,2},{4,5},{5,4},{6,7},{7,6},{8,9},{9,8},{10,11... | collective-permute-start | bytes 1179656 | tf_op jit(solution)/shard_map/ppermute | solution.py:855
  98.5 0.0 collective-permute-start.17
  98.5 3.7 %fifth.1.refs_4_ = f32[192,128]{1,0:T(8,128)S(1)} custom-call(s32[4,48]{1,0:T(4,128)S(1)} %bitcast.34, s32[1,200]{1,0:T(1,128)S(1)} %get-tuple-element.55.list_ref, s32[1,12]{1,0:T(1,128)S(1)} %copy-done.8, s32[2]{0:T(128)S(1)} %add_convert_fusion.edge_ref, f32[48,4,96,128]{3,2,1,0:T(8,128)S(1)} %get-tuple-element.54.blocks, ...), custom_call_target="tpu_custom_call" | custom-call | flops 1048576 | bytes 12800000 | tf_op jit(solution)/shard_map/fifth/pallas_call | solution.py:753
  102.2 0.7 collective-permute-start.20
  102.9 1.2 %collective-permute-start.18 = (f32[192,128]{1,0:T(8,128)S(1)}, f32[192,128]{1,0:T(8,128)S(1)}, u32[]{:S(2)}, u32[]{:S(2)}) collective-permute-start(f32[192,128]{1,0:T(8,128)S(1)} %fifth.1.refs_4_), channel_id=1, source_target_pairs={{0,2},{1,3},{2,0},{3,1},{4,6},{5,7},{6,4},{7,5},{8,10},{9,11},{10,... | collective-permute-start | bytes 294920 | tf_op jit(solution)/shard_map/ppermute | solution.py:865
  104.1 0.7 reshape.36
  104.8 0.0 collective-permute-done.16.refs_2_
  104.9 0.0 collective-permute-done.17.refs_3_
  104.9 2.1 %mixed.1.refs_8_ = f32[48,128,128]{2,1,0:T(8,128)S(1)} custom-call(f32[768,128]{1,0:T(8,128)S(1)} %early.1.refs_0_, f32[768,128]{1,0:T(8,128)S(1)} %collective-permute-done.13.refs_1_, f32[768,128]{1,0:T(8,128)S(1)} %collective-permute-done.16.refs_2_, f32[768,128]{1,0:T(8,128)S(1)} %collective-permute-done.17.refs_3_), custom_call_target="tpu_custom_call" | custom-call | flops 1048576 | bytes 9600000 | tf_op jit(solution)/shard_map/mixed/pallas_call | solution.py:753
  106.9 0.4 collective-permute-done.20.refs_7_
  107.4 2.0 %collective-permute-done.18.refs_5_ = f32[192,128]{1,0:T(8,128)S(1)} collective-permute-done((f32[192,128]{1,0:T(8,128)S(1)}, f32[192,128]{1,0:T(8,128)S(1)}, u32[]{:S(2)}, u32[]{:S(2)}) %collective-permute-start.18) | collective-permute-done | bytes 98336 | tf_op jit(solution)/shard_map/ppermute | solution.py:865
  109.4 10.1 %grad.1 = f32[3456,128]{1,0:T(8,128)} custom-call(f32[768,128]{1,0:T(8,128)S(1)} %early.1.refs_0_, f32[768,128]{1,0:T(8,128)S(1)} %collective-permute-done.13.refs_1_, f32[768,128]{1,0:T(8,128)S(1)} %collective-permute-done.16.refs_2_, f32[768,128]{1,0:T(8,128)S(1)} %collective-permute-done.17.refs_3_, f32[192,128]{1,0:T(8,128)S(1)} %fifth.1.refs_4_, ...), custom_call_target="tpu_custom_call" | custom-call | flops 1048576 | bytes 32000000 | tf_op jit(solution)/shard_map/grad/pallas_call | solution.py:753
  (20 shorter events, 0.1 us)
Async XLA Ops:
  1.6 3.0 %copy-start = (f32[48,4,9216]{2,1,0:T(4,128)S(1)}, f32[48,4,9216]{2,1,0:T(4,128)}, u32[]{:S(2)}) copy-start(f32[48,4,9216]{2,1,0:T(4,128)} %param.7) | copy-start | bytes 21233668
  4.6 1.5 %copy-start.2 = (f32[48,9216]{1,0:T(8,128)S(1)}, f32[48,9216]{1,0:T(8,128)}, u32[]{:S(2)}) copy-start(f32[48,9216]{1,0:T(8,128)} %param.8) | copy-start | bytes 5308420
  6.1 0.7 copy-start.7
  6.7 9.1 %copy-start.3 = (f32[48,9216]{1,0:T(8,128)S(1)}, f32[48,9216]{1,0:T(8,128)}, u32[]{:S(2)}) copy-start(f32[48,9216]{1,0:T(8,128)} %param.8) | copy-start | bytes 5308420
  6.7 20.9 %copy-start.6 = (s32[48,4]{0,1:T(4,128)S(1)}, s32[48,4]{0,1:T(4,128)}, u32[]{:S(2)}) copy-start(s32[48,4]{0,1:T(4,128)} %param.11) | copy-start | bytes 2308
  9.0 13.4 %collective-permute-start = (f32[6,80,128]{2,1,0:T(8,128)S(1)}, f32[6,80,128]{2,1,0:T(8,128)S(1)}, u32[]{:S(2)}, u32[]{:S(2)}) collective-permute-start(f32[6,80,128]{2,1,0:T(8,128)S(1)} %get-tuple-element.51), channel_id=1, source_target_pairs={{4,0},{8,4},{12,8},{16,12},{20,16},{24,20},{28,24},{5,1},{9,5},{13... | collective-permute-start | bytes 737288 | tf_op jit(solution)/shard_map/ppermute | solution.py:583
  11.2 13.8 %collective-permute-start.1 = (f32[6,80,128]{2,1,0:T(8,128)S(1)}, f32[6,80,128]{2,1,0:T(8,128)S(1)}, u32[]{:S(2)}, u32[]{:S(2)}) collective-permute-start(f32[6,80,128]{2,1,0:T(8,128)S(1)} %get-tuple-element.50), channel_id=1, source_target_pairs={{0,4},{4,8},{8,12},{12,16},{16,20},{20,24},{24,28},{1,5},{5,9},{9,... | collective-permute-start | bytes 737288 | tf_op jit(solution)/shard_map/ppermute | solution.py:583
  20.9 1.4 %copy-start.4 = (f32[48,96,128]{2,1,0:T(8,128)}, f32[48,96,128]{2,1,0:T(8,128)S(1)}, u32[]{:S(2)}) copy-start(f32[48,96,128]{2,1,0:T(8,128)S(1)} %get-tuple-element.97.refs_9_) | copy-start | bytes 7077892
  25.0 24.8 %collective-permute-start.6 = (f32[2,128]{1,0:T(2,128)S(1)}, f32[2,128]{1,0:T(2,128)S(1)}, u32[]{:S(2)}, u32[]{:S(2)}) collective-permute-start(f32[2,128]{1,0:T(2,128)S(1)} %fusion.1), channel_id=1, source_target_pairs={{0,24},{4,28},{8,16},{12,20},{16,8},{20,12},{24,0},{28,4},{1,25},{... | collective-permute-start | bytes 3080 | tf_op jit(solution)/shard_map/ppermute | solution.py:567
  26.2 23.5 %collective-permute-start.5 = (f32[2,128]{1,0:T(2,128)S(1)}, f32[2,128]{1,0:T(2,128)S(1)}, u32[]{:S(2)}, u32[]{:S(2)}) collective-permute-start(f32[2,128]{1,0:T(2,128)S(1)} %fusion.1), channel_id=1, source_target_pairs={{0,16},{4,20},{8,24},{12,28},{16,0},{20,4},{24,8},{28,12},{1,17},{... | collective-permute-start | bytes 3080 | tf_op jit(solution)/shard_map/ppermute | solution.py:567
  27.2 22.5 %collective-permute-start.4 = (f32[2,128]{1,0:T(2,128)S(1)}, f32[2,128]{1,0:T(2,128)S(1)}, u32[]{:S(2)}, u32[]{:S(2)}) collective-permute-start(f32[2,128]{1,0:T(2,128)S(1)} %fusion.1), channel_id=1, source_target_pairs={{0,8},{4,12},{8,0},{12,4},{16,24},{20,28},{24,16},{28,20},{1,9},{5... | collective-permute-start | bytes 3080 | tf_op jit(solution)/shard_map/ppermute | solution.py:567
  27.6 3.0 %copy-start.1 = (f32[48,4,9216]{2,1,0:T(4,128)S(1)}, f32[48,4,9216]{2,1,0:T(4,128)}, u32[]{:S(2)}) copy-start(f32[48,4,9216]{2,1,0:T(4,128)} %param.7) | copy-start | bytes 21233668
  30.6 5.2 %copy-start.8 = (s32[1,12]{1,0:T(1,128)S(1)}, s32[1,12]{1,0:T(1,128)}, u32[]{:S(2)}) copy-start(s32[1,12]{1,0:T(1,128)} %send_ref.11) | copy-start | bytes 148
  41.2 8.6 %collective-permute-start.2 = (f32[2,24,128]{2,1,0:T(8,128)S(1)}, f32[2,24,128]{2,1,0:T(8,128)S(1)}, u32[]{:S(2)}, u32[]{:S(2)}) collective-permute-start(f32[2,24,128]{2,1,0:T(8,128)S(1)} %get-tuple-element.64), channel_id=1, source_target_pairs={{0,4},{4,8},{8,12},{12,16},{16,20},{20,24},{24,28},{1,5},{5,9},{9,... | collective-permute-start | bytes 73736 | tf_op jit(solution)/shard_map/ppermute | solution.py:583
  43.6 6.1 %collective-permute-start.3 = (f32[2,24,128]{2,1,0:T(8,128)S(1)}, f32[2,24,128]{2,1,0:T(8,128)S(1)}, u32[]{:S(2)}, u32[]{:S(2)}) collective-permute-start(f32[2,24,128]{2,1,0:T(8,128)S(1)} %get-tuple-element.65), channel_id=1, source_target_pairs={{4,0},{8,4},{12,8},{16,12},{20,16},{24,20},{28,24},{5,1},{9,5},{13... | collective-permute-start | bytes 73736 | tf_op jit(solution)/shard_map/ppermute | solution.py:583
  56.3 5.5 %collective-permute-start.7 = (f32[2,16,128]{2,1,0:T(8,128)S(1)}, f32[2,16,128]{2,1,0:T(8,128)S(1)}, u32[]{:S(2)}, u32[]{:S(2)}) collective-permute-start(f32[2,16,128]{2,1,0:T(8,128)S(1)} %get-tuple-element.70), channel_id=1, source_target_pairs={{0,4},{4,8},{8,12},{12,16},{16,20},{20,24},{24,28},{1,5},{5,9},{9,... | collective-permute-start | bytes 49160 | tf_op jit(solution)/shard_map/ppermute | solution.py:583
  59.9 5.4 %collective-permute-start.8 = (f32[2,16,128]{2,1,0:T(8,128)S(1)}, f32[2,16,128]{2,1,0:T(8,128)S(1)}, u32[]{:S(2)}, u32[]{:S(2)}) collective-permute-start(f32[2,16,128]{2,1,0:T(8,128)S(1)} %get-tuple-element.71), channel_id=1, source_target_pairs={{4,0},{8,4},{12,8},{16,12},{20,16},{24,20},{28,24},{5,1},{9,5},{13... | collective-permute-start | bytes 49160 | tf_op jit(solution)/shard_map/ppermute | solution.py:583
  66.1 3.6 %collective-permute-start.9 = (f32[8,128]{1,0:T(8,128)S(1)}, f32[8,128]{1,0:T(8,128)S(1)}, u32[]{:S(2)}, u32[]{:S(2)}) collective-permute-start(f32[8,128]{1,0:T(8,128)S(1)} %get-tuple-element.82), channel_id=1, source_target_pairs={{0,4},{4,0},{8,12},{12,8},{16,20},{20,16},{24,28},{28,24},{1,5},{5... | collective-permute-start | bytes 12296 | tf_op jit(solution)/shard_map/ppermute | solution.py:567
  69.7 6.7 %collective-permute-start.12 = (f32[8,128]{1,0:T(8,128)S(1)}, f32[8,128]{1,0:T(8,128)S(1)}, u32[]{:S(2)}, u32[]{:S(2)}) collective-permute-start(f32[8,128]{1,0:T(8,128)S(1)} %add.22.refs_6_), channel_id=1, source_target_pairs={{0,24},{4,28},{8,16},{12,20},{16,8},{20,12},{24,0},{28,4},{1,25},{... | collective-permute-start | bytes 12296 | tf_op jit(solution)/shard_map/ppermute | solution.py:567
  71.1 5.4 %collective-permute-start.11 = (f32[8,128]{1,0:T(8,128)S(1)}, f32[8,128]{1,0:T(8,128)S(1)}, u32[]{:S(2)}, u32[]{:S(2)}) collective-permute-start(f32[8,128]{1,0:T(8,128)S(1)} %add.22.refs_6_), channel_id=1, source_target_pairs={{0,16},{4,20},{8,24},{12,28},{16,0},{20,4},{24,8},{28,12},{1,17},{... | collective-permute-start | bytes 12296 | tf_op jit(solution)/shard_map/ppermute | solution.py:567
  72.7 3.8 %collective-permute-start.10 = (f32[8,128]{1,0:T(8,128)S(1)}, f32[8,128]{1,0:T(8,128)S(1)}, u32[]{:S(2)}, u32[]{:S(2)}) collective-permute-start(f32[8,128]{1,0:T(8,128)S(1)} %add.22.refs_6_), channel_id=1, source_target_pairs={{0,8},{4,12},{8,0},{12,4},{16,24},{20,28},{24,16},{28,20},{1,9},{5... | collective-permute-start | bytes 12296 | tf_op jit(solution)/shard_map/ppermute | solution.py:567
  80.1 11.2 %collective-permute-start.13 = (f32[768,128]{1,0:T(8,128)S(1)}, f32[768,128]{1,0:T(8,128)S(1)}, u32[]{:S(2)}, u32[]{:S(2)}) collective-permute-start(f32[768,128]{1,0:T(8,128)S(1)} %early.1.refs_0_), channel_id=1, source_target_pairs={{0,2},{1,3},{2,0},{3,1},{4,6},{5,7},{6,4},{7,5},{8,10},{9,11},{10,... | collective-permute-start | bytes 1179656 | tf_op jit(solution)/shard_map/ppermute | solution.py:846
  81.4 8.0 %collective-permute-start.14 = (f32[2,16,128]{2,1,0:T(8,128)S(1)}, f32[2,16,128]{2,1,0:T(8,128)S(1)}, u32[]{:S(2)}, u32[]{:S(2)}) collective-permute-start(f32[2,16,128]{2,1,0:T(8,128)S(1)} %get-tuple-element.86), channel_id=1, source_target_pairs={{0,4},{4,8},{8,12},{12,16},{16,20},{20,24},{24,28},{1,5},{5,9},{9,... | collective-permute-start | bytes 49160 | tf_op jit(solution)/shard_map/ppermute | solution.py:583
  85.9 5.4 %collective-permute-start.15 = (f32[2,16,128]{2,1,0:T(8,128)S(1)}, f32[2,16,128]{2,1,0:T(8,128)S(1)}, u32[]{:S(2)}, u32[]{:S(2)}) collective-permute-start(f32[2,16,128]{2,1,0:T(8,128)S(1)} %get-tuple-element.87), channel_id=1, source_target_pairs={{4,0},{8,4},{12,8},{16,12},{20,16},{24,20},{28,24},{5,1},{9,5},{13... | collective-permute-start | bytes 49160 | tf_op jit(solution)/shard_map/ppermute | solution.py:583
  91.3 13.6 %collective-permute-start.16 = (f32[768,128]{1,0:T(8,128)S(1)}, f32[768,128]{1,0:T(8,128)S(1)}, u32[]{:S(2)}, u32[]{:S(2)}) collective-permute-start(f32[768,128]{1,0:T(8,128)S(1)} %early.1.refs_0_), channel_id=1, source_target_pairs={{0,1},{1,0},{2,3},{3,2},{4,5},{5,4},{6,7},{7,6},{8,9},{9,8},{10,11... | collective-permute-start | bytes 1179656 | tf_op jit(solution)/shard_map/ppermute | solution.py:855
  98.5 6.4 %collective-permute-start.17 = (f32[768,128]{1,0:T(8,128)S(1)}, f32[768,128]{1,0:T(8,128)S(1)}, u32[]{:S(2)}, u32[]{:S(2)}) collective-permute-start(f32[768,128]{1,0:T(8,128)S(1)} %collective-permute-done.13.refs_1_), channel_id=1, source_target_pairs={{0,1},{1,0},{2,3},{3,2},{4,5},{5,4},{6,7},{7,6},{8,9},{9,8},{10,11... | collective-permute-start | bytes 1179656 | tf_op jit(solution)/shard_map/ppermute | solution.py:855
  102.2 5.2 %collective-permute-start.20 = (f32[192,128]{1,0:T(8,128)S(1)}, f32[192,128]{1,0:T(8,128)S(1)}, u32[]{:S(2)}, u32[]{:S(2)}) collective-permute-start(f32[192,128]{1,0:T(8,128)S(1)} %fifth.1.refs_4_), channel_id=1, source_target_pairs={{0,3},{1,2},{2,1},{3,0},{4,7},{5,6},{6,5},{7,4},{8,11},{9,10},{10,... | collective-permute-start | bytes 294920 | tf_op jit(solution)/shard_map/ppermute | solution.py:865
  102.9 4.4 %collective-permute-start.19 = (f32[192,128]{1,0:T(8,128)S(1)}, f32[192,128]{1,0:T(8,128)S(1)}, u32[]{:S(2)}, u32[]{:S(2)}) collective-permute-start(f32[192,128]{1,0:T(8,128)S(1)} %fifth.1.refs_4_), channel_id=1, source_target_pairs={{0,1},{1,0},{2,3},{3,2},{4,5},{5,4},{6,7},{7,6},{8,9},{9,8},{10,11... | collective-permute-start | bytes 294920 | tf_op jit(solution)/shard_map/ppermute | solution.py:865
  102.9 6.5 %collective-permute-start.18 = (f32[192,128]{1,0:T(8,128)S(1)}, f32[192,128]{1,0:T(8,128)S(1)}, u32[]{:S(2)}, u32[]{:S(2)}) collective-permute-start(f32[192,128]{1,0:T(8,128)S(1)} %fifth.1.refs_4_), channel_id=1, source_target_pairs={{0,2},{1,3},{2,0},{3,1},{4,6},{5,7},{6,4},{7,5},{8,10},{9,11},{10,... | collective-permute-start | bytes 294920 | tf_op jit(solution)/shard_map/ppermute | solution.py:865
  104.8 4.5 %copy-start.5 = (f32[48,96,128]{2,1,0:T(8,128)S(1)}, f32[48,96,128]{2,1,0:T(8,128)}, u32[]{:S(2)}) copy-start(f32[48,96,128]{2,1,0:T(8,128)} %copy-done.4) | copy-start | bytes 7077892

commit v6 on v5

--- a/solution.py
+++ b/solution.py
@@ -17,7 +17,7 @@
 EARLY = 16
 LATE = 4
 CUTS = BS * BS // 128
-PITCH = CUTS + 1
+GROUPS = 3
 LANES = 128
 OFF = 8
 ROWS = 64
@@ -84,7 +84,9 @@
 
 def scatter_apply(blocks, op_ref, x_ref, y_ref, col_ref, column_ref):
     count = x_ref.shape[0]
-    y_ref[...] = jnp.zeros_like(y_ref)
+    for k in range(1, K):
+        for r in range(count):
+            y_ref[k][r][...] = jnp.zeros_like(y_ref[k][r])
 
     def step(group, carry):
         base = pl.multiple_of(group * CHUNK, CHUNK)
@@ -98,9 +100,10 @@
                     column_ref[r] = jnp.where(lane_ids() == n + OFF, images[r], column_ref[r])
             for k in range(K):
                 block = blocks[n, k]
-                slot = col_ref[k, n] + LOW
+                slot = n + OFF if k == 0 else col_ref[k, n] + LOW
                 for r in range(count):
-                    y_ref[r, slot] = y_ref[r, slot] + fold(block * images[r])
+                    part = fold(block * images[r])
+                    y_ref[k][r][slot] = part if k == 0 else y_ref[k][r][slot] + part
         return carry
 
     lax.fori_loop(0, NBLK // CHUNK, step, 0)
@@ -133,7 +136,7 @@
             block = blocks[n, k]
             for r in range(count):
                 image = jnp.sum(block * g_ref[r, pl.ds(slot, 1), :], axis=1, keepdims=True)
-                y_ref[r, n + OFF] = y_ref[r, n + OFF] + fold(jnp.where(mask, image, 0.0))
+                y_ref[0][r][n + OFF] = y_ref[0][r][n + OFF] + fold(jnp.where(mask, image, 0.0))
         return carry
 
     lax.fori_loop(0, (list_ref[0, 0] + 3) >> 2, step, 0)
@@ -145,7 +148,13 @@
     for g in range(ROWS // 8):
         total = jnp.zeros((8, LANES), f32)
         for i in range(8):
-            line = jnp.sum(y_ref[r, g * 8 + i], axis=0, keepdims=True)
+            slot = g * 8 + i
+            line = y_ref[1][r][slot]
+            for k in range(2, K):
+                line = line + y_ref[k][r][slot]
+            if OFF <= slot < HIGH:
+                line = line + y_ref[0][r][slot]
+            line = jnp.sum(line, axis=0, keepdims=True)
             total = jnp.where(sub == i, line, total)
         groups.append(total)
     return jnp.concatenate(groups, axis=0)
@@ -211,16 +220,16 @@
         for i in range(CUTS):
             tile = raw_ref[pl.ds(pl.multiple_of(group * (8 * CUTS) + 8 * i, 8), 8), :]
             squares = squares + tile * tile
-        for i in range(0, CHUNK, 2):
-            start = (group * CHUNK + i) * (CUTS * K)
-            for q in range(0, CUTS, 8):
-                traces = traces + mask[q : q + 8] * stiff_ref[pl.ds(start + K * q, 8, stride=K), :]
         return squares, traces
 
     blank = jnp.zeros((8, LANES), f32)
     squares, traces = lax.fori_loop(0, NBLK // CHUNK, gather, (blank, blank))
+    for i in range(CHUNK):
+        for q in range(0, CUTS, 8):
+            start = i * (CUTS * K) + K * q
+            traces = traces + mask[q : q + 8] * stiff_ref[pl.ds(start, 8, stride=K), :]
     squares = jnp.sum(squares, axis=0, keepdims=True)
-    traces = 2.0 * jnp.sum(traces, axis=0, keepdims=True)
+    traces = (NBLK // CHUNK) * jnp.sum(traces, axis=0, keepdims=True)
     for part, ref in ((0, down_ref), (IF, up_ref)):
         for j in range(IF):
             n = send_ref[0, part + j]
@@ -241,33 +250,29 @@
         ref[0, CUTS + 7 : CUTS + 8, :] = traces
 
 
-def operator_kernel(raw_ref, weights_ref, ops_ref, gram_ref, turn_ref):
-    def step(group, carry):
-        for q in range(CUTS):
-            tile = raw_ref[pl.ds(pl.multiple_of(group * (8 * CUTS) + 8 * q, 8), 8), :]
-            turn_ref[pl.ds(q, 8, stride=PITCH), :] = tile
-        for i in range(CHUNK):
-            n = group * CHUNK + i
-            weights = unflatten(lambda q: turn_ref[pl.ds(PITCH * i + q, 8, stride=3), :])
-            weights_ref[n] = weights
-            ops_ref[n] = make_operator(weights, gram_ref.at[i & 1])
-        return carry
-
-    lax.fori_loop(0, NBLK // CHUNK, step, 0)
-
-
-def blocks_kernel(col_ref, stiff_ref, blocks_ref, list_ref):
-    def step(group, count):
-        for i in range(CHUNK):
-            n = group * CHUNK + i
-            for k in range(K):
-                blocks_ref[n, k] = unflatten(lambda q: stiff_ref[pl.ds(n * (CUTS * K) + 4 * q + k, 8, stride=12), :])
-                col = col_ref[k, n]
-                list_ref[0, 1 + count] = n * K + k
-                count = count + jnp.where((col < IF) | (col >= IF + NBLK), 1, 0)
-        return count
-
-    count = lax.fori_loop(0, NBLK // CHUNK, step, jnp.int32(0))
+def operator_kernel(raw_ref, weights_ref, ops_ref, gram_ref):
+    base = pl.program_id(0) * CHUNK
+    for i in range(CHUNK):
+        weights = unflatten(lambda q: raw_ref[pl.ds(8 * q + i, 8, stride=24), :])
+        weights_ref[i] = weights
+        ops_ref[base + i] = make_operator(weights, gram_ref.at[i & 1])
+
+
+def blocks_kernel(col_ref, stiff_ref, blocks_ref, list_ref, count_ref):
+    base = pl.program_id(0) * CHUNK
+
+    @pl.when(base == 0)
+    def _():
+        count_ref[0] = 0
+
+    count = count_ref[0]
+    for i in range(CHUNK):
+        for k in range(K):
+            blocks_ref[base + i, k] = unflatten(lambda q: stiff_ref[pl.ds(i * (CUTS * K) + 4 * q + k, 8, stride=12), :])
+            col = col_ref[k, base + i]
+            list_ref[0, 1 + count] = (base + i) * K + k
+            count = count + jnp.where((col < IF) | (col >= IF + NBLK), 1, 0)
+    count_ref[0] = count
     list_ref[0, 0] = count
     for u in range(4):
         list_ref[0, 1 + count + u] = 0
@@ -522,9 +527,9 @@
 
 
 def grad_kernel(*refs):
-    peers = (len(refs) - 4) // 2
-    early, late, mixed_ref, weights_ref, grad_ref, turn_ref = refs[:peers], refs[peers : 2 * peers], *refs[-4:]
-    group = pl.program_id(0)
+    peers = (len(refs) - 3) // 2
+    early, late, mixed_ref, weights_ref, grad_ref = refs[:peers], refs[peers : 2 * peers], *refs[-3:]
+    first = pl.program_id(0) * GROUPS
     upper = lax.broadcasted_iota(jnp.int32, (8, LANES), 0) < LATE
 
     def join(tiles):
@@ -534,23 +539,26 @@
             out.append(jnp.where(upper, tiles[q], other))
         return out
 
-    for i in range(CHUNK):
-        n = group * CHUNK + i
-        at = pl.multiple_of(n * EARLY, EARLY)
-        pair = pl.ds(pl.multiple_of(group * (CHUNK * LATE) + 8 * (i // 2), 8), 8)
-        resid = join([ref[pl.ds(at, 8), :] for ref in early])
-        zeta = [ref[pair, :] for ref in late]
-        zeta = join([pltpu.roll(tile, LATE, 0) for tile in zeta] if i % 2 else zeta)
-        left = jnp.concatenate(resid + zeta, axis=0)
-        right = jnp.concatenate(zeta + resid, axis=0)
-        grad = product(weights_ref[n], mixed_ref[n] + product(left, right, 0), 1)
-
-        def write(q, value):
-            turn_ref[pl.ds(PITCH * i + q, 8, stride=3), :] = value
-
-        flatten(grad, write)
-    for q in range(CUTS):
-        grad_ref[8 * q : 8 * q + 8, :] = turn_ref[pl.ds(q, 8, stride=PITCH), :]
+    def step(part, carry):
+        group = first + part
+        for i in range(CHUNK):
+            n = group * CHUNK + i
+            at = pl.multiple_of(n * EARLY, EARLY)
+            pair = pl.ds(pl.multiple_of(group * (CHUNK * LATE) + 8 * (i // 2), 8), 8)
+            resid = join([ref[pl.ds(at, 8), :] for ref in early])
+            zeta = [ref[pair, :] for ref in late]
+            zeta = join([pltpu.roll(tile, LATE, 0) for tile in zeta] if i % 2 else zeta)
+            left = jnp.concatenate(resid + zeta, axis=0)
+            right = jnp.concatenate(zeta + resid, axis=0)
+            grad = product(weights_ref[part * CHUNK + i], mixed_ref[n] + product(left, right, 0), 1)
+
+            def write(q, value):
+                grad_ref[pl.ds(part * (8 * CUTS) + 8 * q + i, 8, stride=24), :] = value
+
+            flatten(grad, write)
+        return carry
+
+    lax.fori_loop(0, GROUPS, step, 0)
 
 
 def widening(parts, axis, step, most):
@@ -749,11 +757,11 @@
     def shape(*dims):
         return jax.ShapeDtypeStruct(dims, f32)
 
-    def call(kernel, name, scalars_in, arrays_in, outs, scratch, expected, specs=None, grid=()):
+    def call(kernel, name, scalars_in, arrays_in, outs, scratch, expected, specs=None, grid=(), in_specs=None):
         return pl.pallas_call(
             kernel,
             grid=grid,
-            in_specs=[smem()] * len(scalars_in) + [vmem()] * len(arrays_in),
+            in_specs=in_specs or [smem()] * len(scalars_in) + [vmem()] * len(arrays_in),
             out_specs=specs or [vmem()] * len(outs),
             out_shape=outs,
             scratch_shapes=scratch,
@@ -766,20 +774,20 @@
     message = shape(count, 16, LANES)
     longer = shape(count, 24, LANES)
     ghost_message = shape(IF, CUTS + 8, LANES)
-    partial = lambda r: pltpu.VMEM((r, ROWS, 8, LANES), f32)
+    partial = lambda r: [[pltpu.VMEM((ROWS, 8, LANES), f32)] * r] * K
     turned = [pltpu.VMEM((count, BS, LANES), f32), pltpu.VMEM((LANES, LANES), f32)]
     held = lambda r: pltpu.VMEM((r, ROWS, LANES), f32)
     grams = pltpu.VMEM((2, BS, LANES), f32)
-    turn = pltpu.VMEM((8 * PITCH, LANES), f32)
 
     up, down = call(
-        pack_kernel, "pack", [send_rows], [weight_cuts, stiff_cuts, base], [ghost_message] * 2, [], 3
+        pack_kernel, "pack", [send_rows], [weight_cuts, lax.slice_in_dim(stiff_cuts, 0, CHUNK * CUTS * K), base], [ghost_message] * 2, [], 3
     )
     near, far = exchange(up, down)
 
     weights, ops = call(
         operator_kernel, "operators", [], [weight_cuts], [shape(NBLK, BS, LANES), shape(NBLK, BS, LANES)],
-        [grams, turn], 4,
+        [grams], 4, [pl.BlockSpec((CHUNK, BS, LANES), lambda g: (g, 0, 0)), vmem()], (NBLK // CHUNK,),
+        [pl.BlockSpec((CHUNK * CUTS, LANES), lambda g: (g, 0))],
     )
     stats, partner = up[0, CUTS + 6 :], jnp.where(sub % 2 == 0, far[0, CUTS + 6 :], near[0, CUTS + 6 :])
     if size > 1 and size & (size - 1) == 0:
@@ -792,7 +800,8 @@
     blocks, halo_list = call(
         blocks_kernel, "blocks", [columns], [stiff_cuts],
         [shape(NBLK, K, BS, LANES), jax.ShapeDtypeStruct((1, NBLK * K + 8), jnp.int32)],
-        [], 5, [vmem(), smem()],
+        [pltpu.SMEM((1,), jnp.int32)], 5, [vmem(), smem()], (NBLK // CHUNK,),
+        [smem(), pl.BlockSpec((CHUNK * CUTS * K, LANES), lambda g: (g, 0))],
     )
 
     zero, a1, a2, up, down = call(
@@ -868,8 +877,9 @@
 
     (mixed,) = call(mixed_kernel, "mixed", [], early, [shape(NBLK, LANES, LANES)], [], 3)
     (grad,) = call(
-        grad_kernel, "grad", [], [*early, *late, mixed, weights], [shape(NBLK * CUTS, LANES)],
-        [turn], 10, [pl.BlockSpec((8 * CUTS, LANES), lambda g: (g, 0))], (NBLK // 8,),
+        grad_kernel, "grad", [], [*early, *late, mixed, weights], [shape(NBLK * CUTS, LANES)], [], 10,
+        [pl.BlockSpec((GROUPS * 8 * CUTS, LANES), lambda g: (g, 0))], (NBLK // (GROUPS * CHUNK),),
+        [vmem()] * (len(early) + len(late) + 1) + [pl.BlockSpec((GROUPS * CHUNK, BS, LANES), lambda g: (g, 0, 0))],
     )
     grad = grad.reshape(NBLK // 8, CUTS, 8, LANES).transpose(0, 2, 1, 3).reshape(NBLK, BS * BS)
     return answer[:, OFF:HIGH, :BS].reshape(count, NBLK * BS), grad

time: 120 us -> 116 us (0.967)
  local copies, waits for them, and re-layouts: 10.4 us -> 6.64 us
    unnamed x18 -> x12, local copies, waits for them, and re-layouts: 9.57 us -> 4.44 us
    slice x0 -> x1, local copies, waits for them, and re-layouts: none -> 1.35 us  [shards(): lax.slice_in_dim(stiff_cuts, 0, CHUNK * CUTS * K)]
  transfers between devices with their start and end apart: 21 -> 21, of which waited for: 5 -> 5; matrix products, arithmetic and copies ran while one was open for 1% -> 1% of each run, Pallas kernels for 28% -> 29%
where the time goes in v6:
time: 116 us; the launch traced here: 115 us
  Pallas kernels  56.9 us (49%)
  starting transfers between devices  38.8 us (33%)
  waiting for transfers between devices  10.2 us (9%)
  local copies, waits for them, and re-layouts  6.64 us (6%)
  between operations  1.63 us (1%)
    pallas_call x15, Pallas kernels, call(): pl.pallas_call(kernel, grid=grid, in_specs=in_specs or [smem()] * len(sca...  56.9 us
    ppermute x8, starting transfers between devices, exchange(): return (lax.ppermute(up, 'sub', rising), lax.ppermute(down, 'sub', falling))  22.8 us
    ppermute x8, waiting for transfers between devices, exchange(): return (lax.ppermute(up, 'sub', rising), lax.ppermute(down, 'sub', falling))  7.75 us
    ppermute x2, starting transfers between devices, shards(): lax.ppermute(part, 'rhs', [(i, i ^ 1) for i in range(size)])  7.21 us
    ppermute x7, starting transfers between devices, widening(): lax.ppermute(total, axis, [(i, i ^ d * step) for i in range(size)])  5.67 us
    unnamed x12, local copies, waits for them, and re-layouts  4.44 us
    ppermute x3, waiting for transfers between devices, shards(): lax.ppermute(late, 'rhs', [(i, i ^ d) for i in range(size)])  2.44 us
  transfers between devices with their start and end apart: 21, of which 5 were waited for; matrix products, arithmetic and copies ran while one was open for 1% of the time, Pallas kernels for 29%

profile of v6, /device:TPU:13, one launch (start us, length us, event | category | flops | bytes accessed | tf_op | source)
XLA Modules:
  0.0 115.3 jit_solution(14903577397701447519)
XLA Ops:
  0.7 1.0 pad_maximum_fusion
  1.6 0.1 reshape.35
  1.7 1.4 %slice.24 = f32[8,72,4,128]{3,2,1,0:T(4,128)S(1)} slice(f32[48,72,4,128]{3,2,1,0:T(4,128)} %bitcast.25), slice={[0:8], [0:72], [0:4], [0:128]} | slice | bytes 2359296 | tf_op jit(solution)/shard_map/slice | solution.py:783
  3.1 0.0 copy-start.4
  3.1 2.3 %pack.1 = (f32[6,80,128]{2,1,0:T(8,128)S(1)}, f32[6,80,128]{2,1,0:T(8,128)S(1)}) custom-call(s32[1,12]{1,0:T(1,128)S(1)} %copy-done.5, f32[3456,128]{1,0:T(8,128)S(1)} %bitcast.27, f32[2304,128]{1,0:T(8,128)S(1)} %bitcast.29, f32[4,64,128]{2,1,0:T(8,128)S(1)} %pad.4.base_ref), custom_call_target="tpu_custom_call" | custom-call | flops 1048576 | bytes 9600000 | tf_op jit(solution)/shard_map/pack/pallas_call | solution.py:761
  5.4 2.1 %collective-permute-start = (f32[6,80,128]{2,1,0:T(8,128)S(1)}, f32[6,80,128]{2,1,0:T(8,128)S(1)}, u32[]{:S(2)}, u32[]{:S(2)}) collective-permute-start(f32[6,80,128]{2,1,0:T(8,128)S(1)} %get-tuple-element.51), channel_id=1, source_target_pairs={{4,0},{8,4},{12,8},{16,12},{20,16},{24,20},{28,24},{5,1},{9,5},{13... | collective-permute-start | bytes 737288 | tf_op jit(solution)/shard_map/ppermute | solution.py:591
  7.6 4.0 %collective-permute-start.1 = (f32[6,80,128]{2,1,0:T(8,128)S(1)}, f32[6,80,128]{2,1,0:T(8,128)S(1)}, u32[]{:S(2)}, u32[]{:S(2)}) collective-permute-start(f32[6,80,128]{2,1,0:T(8,128)S(1)} %get-tuple-element.50), channel_id=1, source_target_pairs={{0,4},{4,8},{8,12},{12,16},{16,20},{20,24},{24,28},{1,5},{5,9},{9,... | collective-permute-start | bytes 737288 | tf_op jit(solution)/shard_map/ppermute | solution.py:591
  12.3 5.0 %operators.1 = (f32[48,96,128]{2,1,0:T(8,128)S(1)}, f32[48,96,128]{2,1,0:T(8,128)S(1)}) custom-call(f32[3456,128]{1,0:T(8,128)S(1)} %bitcast.28), custom_call_target="tpu_custom_call" | custom-call | flops 1048576 | bytes 12800000 | tf_op jit(solution)/shard_map/operators/pallas_call | solution.py:761
  17.3 1.4 %copy-done.2 = f32[48,96,128]{2,1,0:T(8,128)} copy-done((f32[48,96,128]{2,1,0:T(8,128)}, f32[48,96,128]{2,1,0:T(8,128)S(1)}, u32[]{:S(2)}) %copy-start.2) | copy-done | bytes 2359320
  18.7 0.1 add_convert_fusion.edge_ref
  18.7 0.0 collective-permute-done.high_ref
  18.7 2.6 %collective-permute-done.1.low_ref = f32[6,80,128]{2,1,0:T(8,128)S(1)} collective-permute-done((f32[6,80,128]{2,1,0:T(8,128)S(1)}, f32[6,80,128]{2,1,0:T(8,128)S(1)}, u32[]{:S(2)}, u32[]{:S(2)}) %collective-permute-start.1) | collective-permute-done | bytes 245792 | tf_op jit(solution)/shard_map/ppermute | solution.py:591
  21.4 1.3 %collective-permute-start.6 = (f32[2,128]{1,0:T(2,128)S(1)}, f32[2,128]{1,0:T(2,128)S(1)}, u32[]{:S(2)}, u32[]{:S(2)}) collective-permute-start(f32[2,128]{1,0:T(2,128)S(1)} %fusion.1), channel_id=1, source_target_pairs={{0,24},{4,28},{8,16},{12,20},{16,8},{20,12},{24,0},{28,4},{1,25},{... | collective-permute-start | bytes 3080 | tf_op jit(solution)/shard_map/ppermute | solution.py:575
  22.7 1.0 collective-permute-start.5
  23.6 0.4 collective-permute-start.4
  24.0 3.0 %copy-done = f32[48,4,9216]{2,1,0:T(4,128)S(1)} copy-done((f32[48,4,9216]{2,1,0:T(4,128)S(1)}, f32[48,4,9216]{2,1,0:T(4,128)}, u32[]{:S(2)}) %copy-start) | copy-done | bytes 7077912
  27.0 4.9 %blocks.1 = (f32[48,4,96,128]{3,2,1,0:T(8,128)S(1)}, s32[1,200]{1,0:T(1,128)S(1)}) custom-call(s32[4,48]{1,0:T(4,128)S(1)} %bitcast.30, f32[13824,128]{1,0:T(8,128)S(1)} %bitcast.26), custom_call_target="tpu_custom_call" | custom-call | flops 1048576 | bytes 16000000 | tf_op jit(solution)/shard_map/blocks/pallas_call | solution.py:761
  31.9 5.4 %first.1 = (f32[4,64,128]{2,1,0:T(8,128)S(1)}, f32[2,64,128]{2,1,0:T(8,128)S(1)}, f32[2,64,128]{2,1,0:T(8,128)S(1)}, f32[2,24,128]{2,1,0:T(8,128)S(1)}, f32[2,24,128]{2,1,0:T(8,128)S(1)}) custom-call(s32[4,48]{1,0:T(4,128)S(1)} %bitcast.31, s32[1,200]{1,0:T(1,128)S(1)} %get-tuple-element.55.list_ref, s32[1,12]{1,0:T(1,128)S(1)} %copy-done.5, ...), custom_call_target="tpu_custom_call" | custom-call | flops 1048576 | bytes 19200000 | tf_op jit(solution)/shard_map/first/pallas_call | solution.py:761
  37.3 2.2 %collective-permute-start.2 = (f32[2,24,128]{2,1,0:T(8,128)S(1)}, f32[2,24,128]{2,1,0:T(8,128)S(1)}, u32[]{:S(2)}, u32[]{:S(2)}) collective-permute-start(f32[2,24,128]{2,1,0:T(8,128)S(1)} %get-tuple-element.64), channel_id=1, source_target_pairs={{0,4},{4,8},{8,12},{12,16},{16,20},{20,24},{24,28},{1,5},{5,9},{9,... | collective-permute-start | bytes 73736 | tf_op jit(solution)/shard_map/ppermute | solution.py:591
  39.5 3.1 %collective-permute-start.3 = (f32[2,24,128]{2,1,0:T(8,128)S(1)}, f32[2,24,128]{2,1,0:T(8,128)S(1)}, u32[]{:S(2)}, u32[]{:S(2)}) collective-permute-start(f32[2,24,128]{2,1,0:T(8,128)S(1)} %get-tuple-element.65), channel_id=1, source_target_pairs={{4,0},{8,4},{12,8},{16,12},{20,16},{24,20},{28,24},{5,1},{9,5},{13... | collective-permute-start | bytes 73736 | tf_op jit(solution)/shard_map/ppermute | solution.py:591
  42.6 3.2 %ghosts.1 = (f32[12,96,128]{2,1,0:T(8,128)S(1)}, f32[2,64,128]{2,1,0:T(8,128)S(1)}, f32[2,64,128]{2,1,0:T(8,128)S(1)}) custom-call(f32[48,96,128]{2,1,0:T(8,128)S(1)} %get-tuple-element.53.op_ref.ops_ref, f32[4,64,128]{2,1,0:T(8,128)S(1)} %get-tuple-element.74.zero_ref, f32[2,64,128]{2,1,0:T(8,128)S(1)} %get-tuple-element.59.a1_ref, ...), custom_call_target="tpu_custom_call" | custom-call | flops 1048576 | bytes 9600000 | tf_op jit(solution)/shard_map/ghosts/pallas_call | solution.py:761
  45.9 0.0 collective-permute-done.6
  45.9 0.0 collective-permute-done.5
  45.9 0.0 collective-permute-done.4
  45.9 0.0 collective-permute-done.2.low_ref
  45.9 0.0 collective-permute-done.3.high_ref
  45.9 6.7 %second.1 = (f32[2,64,128]{2,1,0:T(8,128)S(1)}, f32[2,64,128]{2,1,0:T(8,128)S(1)}, f32[2,64,128]{2,1,0:T(8,128)S(1)}, f32[2,64,128]{2,1,0:T(8,128)S(1)}, f32[2,6...) custom-call(s32[4,48]{1,0:T(4,128)S(1)} %bitcast.32, ...), custom_call_target="tpu_custom_call" | custom-call | flops 1048576 | bytes 22400000 | tf_op jit(solution)/shard_map/second/pallas_call | solution.py:761
  52.6 3.1 %collective-permute-start.7 = (f32[2,16,128]{2,1,0:T(8,128)S(1)}, f32[2,16,128]{2,1,0:T(8,128)S(1)}, u32[]{:S(2)}, u32[]{:S(2)}) collective-permute-start(f32[2,16,128]{2,1,0:T(8,128)S(1)} %get-tuple-element.70), channel_id=1, source_target_pairs={{0,4},{4,8},{8,12},{12,16},{16,20},{20,24},{24,28},{1,5},{5,9},{9,... | collective-permute-start | bytes 49160 | tf_op jit(solution)/shard_map/ppermute | solution.py:591
  55.7 2.2 %collective-permute-start.8 = (f32[2,16,128]{2,1,0:T(8,128)S(1)}, f32[2,16,128]{2,1,0:T(8,128)S(1)}, u32[]{:S(2)}, u32[]{:S(2)}) collective-permute-start(f32[2,16,128]{2,1,0:T(8,128)S(1)} %get-tuple-element.71), channel_id=1, source_target_pairs={{4,0},{8,4},{12,8},{16,12},{20,16},{24,20},{28,24},{5,1},{9,5},{13... | collective-permute-start | bytes 49160 | tf_op jit(solution)/shard_map/ppermute | solution.py:591
  57.9 0.0 collective-permute-done.7.low_ref
  57.9 3.2 %collective-permute-done.8.high_ref = f32[2,16,128]{2,1,0:T(8,128)S(1)} collective-permute-done((f32[2,16,128]{2,1,0:T(8,128)S(1)}, f32[2,16,128]{2,1,0:T(8,128)S(1)}, u32[]{:S(2)}, u32[]{:S(2)}) %collective-permute-start.8) | collective-permute-done | bytes 16416 | tf_op jit(solution)/shard_map/ppermute | solution.py:591
  61.1 0.8 moments.1
  61.9 0.1 collective-permute-start.9
  62.0 3.6 %target.1.refs_5_ = f32[2,64,128]{2,1,0:T(8,128)S(1)} custom-call(s32[4,48]{1,0:T(4,128)S(1)} %bitcast.33, s32[1,200]{1,0:T(1,128)S(1)} %get-tuple-element.55.list_ref, f32[48,4,96,128]{3,2,1,0:T(8,128)S(1)} %get-tuple-element.54.blocks, f32[48,96,128]{2,1,0:T(8,128)S(1)} %get-tuple-element.53.op_ref.ops_ref, f32[12,96,128]{2,1,0:T(8,128)S(1)} %get-tuple-element.60.gop_ref, ...), custom_call_target="tpu_custom_call" | custom-call | flops 1048576 | bytes 9600000 | tf_op jit(solution)/shard_map/target/pallas_call | solution.py:761
  65.6 0.0 collective-permute-done.9
  65.6 1.3 %collective-permute-start.12 = (f32[8,128]{1,0:T(8,128)S(1)}, f32[8,128]{1,0:T(8,128)S(1)}, u32[]{:S(2)}, u32[]{:S(2)}) collective-permute-start(f32[8,128]{1,0:T(8,128)S(1)} %add.22.refs_6_), channel_id=1, source_target_pairs={{0,24},{4,28},{8,16},{12,20},{16,8},{20,12},{24,0},{28,4},{1,25},{... | collective-permute-start | bytes 12296 | tf_op jit(solution)/shard_map/ppermute | solution.py:575
  67.0 1.6 %collective-permute-start.11 = (f32[8,128]{1,0:T(8,128)S(1)}, f32[8,128]{1,0:T(8,128)S(1)}, u32[]{:S(2)}, u32[]{:S(2)}) collective-permute-start(f32[8,128]{1,0:T(8,128)S(1)} %add.22.refs_6_), channel_id=1, source_target_pairs={{0,16},{4,20},{8,24},{12,28},{16,0},{20,4},{24,8},{28,12},{1,17},{... | collective-permute-start | bytes 12296 | tf_op jit(solution)/shard_map/ppermute | solution.py:575
  68.6 0.0 collective-permute-start.10
  68.6 3.8 %third.1.refs_4_ = f32[2,64,128]{2,1,0:T(8,128)S(1)} custom-call(s32[4,48]{1,0:T(4,128)S(1)} %bitcast.34, s32[1,200]{1,0:T(1,128)S(1)} %get-tuple-element.55.list_ref, f32[48,4,96,128]{3,2,1,0:T(8,128)S(1)} %get-tuple-element.54.blocks, f32[48,96,128]{2,1,0:T(8,128)S(1)} %get-tuple-element.53.op_ref.ops_ref, f32[12,96,128]{2,1,0:T(8,128)S(1)} %get-tuple-element.60.gop_ref, ...), custom_call_target="tpu_custom_call" | custom-call | flops 1048576 | bytes 12800000 | tf_op jit(solution)/shard_map/third/pallas_call | solution.py:761
  72.4 0.0 collective-permute-done.12.refs_9_
  72.4 0.0 collective-permute-done.11.refs_8_
  72.4 0.0 collective-permute-done.10.refs_7_
  72.4 3.5 %fourth.1 = (f32[2,64,128]{2,1,0:T(8,128)}, f32[2,64,128]{2,1,0:T(8,128)S(1)}, f32[2,64,128]{2,1,0:T(8,128)S(1)}, f32[10,8,8,128]{3,2,1,0:T(8,128)S(1)}, f32[3,8...) custom-call(s32[4,48]{1,0:T(4,128)S(1)} %bitcast.35, s32[1,12]{1,0:T(1,128)S(1)} %copy-done.5, ...), custom_call_target="tpu_custom_call" | custom-call | flops 1048576 | bytes 9600000 | tf_op jit(solution)/shard_map/fourth/pallas_call | solution.py:761
  75.9 0.2 early.1.refs_0_
  76.1 1.3 %collective-permute-start.13 = (f32[768,128]{1,0:T(8,128)S(1)}, f32[768,128]{1,0:T(8,128)S(1)}, u32[]{:S(2)}, u32[]{:S(2)}) collective-permute-start(f32[768,128]{1,0:T(8,128)S(1)} %early.1.refs_0_), channel_id=1, source_target_pairs={{0,2},{1,3},{2,0},{3,1},{4,6},{5,7},{6,4},{7,5},{8,10},{9,11},{10,... | collective-permute-start | bytes 1179656 | tf_op jit(solution)/shard_map/ppermute | solution.py:855
  77.4 4.1 %collective-permute-start.14 = (f32[2,16,128]{2,1,0:T(8,128)S(1)}, f32[2,16,128]{2,1,0:T(8,128)S(1)}, u32[]{:S(2)}, u32[]{:S(2)}) collective-permute-start(f32[2,16,128]{2,1,0:T(8,128)S(1)} %get-tuple-element.86), channel_id=1, source_target_pairs={{0,4},{4,8},{8,12},{12,16},{16,20},{20,24},{24,28},{1,5},{5,9},{9,... | collective-permute-start | bytes 49160 | tf_op jit(solution)/shard_map/ppermute | solution.py:591
  81.5 1.9 %collective-permute-start.15 = (f32[2,16,128]{2,1,0:T(8,128)S(1)}, f32[2,16,128]{2,1,0:T(8,128)S(1)}, u32[]{:S(2)}, u32[]{:S(2)}) collective-permute-start(f32[2,16,128]{2,1,0:T(8,128)S(1)} %get-tuple-element.87), channel_id=1, source_target_pairs={{4,0},{8,4},{12,8},{16,12},{20,16},{24,20},{28,24},{5,1},{9,5},{13... | collective-permute-start | bytes 49160 | tf_op jit(solution)/shard_map/ppermute | solution.py:591
  83.4 1.5 %answer.1 = (f32[2,2,64,128]{3,2,1,0:T(8,128)S(1)}, f32[2,64,128]{2,1,0:T(8,128)S(1)}) custom-call(f32[48,96,128]{2,1,0:T(8,128)S(1)} %get-tuple-element.53.op_ref.ops_ref, f32[10,8,8,128]{3,2,1,0:T(8,128)S(1)} %get-tuple-element.84.coef_ref, f32[4,64,128]{2,1,0:T(8,128)S(1)} %get-tuple-element.74.zero_ref, f32[2,64,128]{2,1,0:T(8,128)S(1)} %get-tuple-element.75.refs_0_, ...), custom_call_target="tpu_custom_call" | custom-call | flops 1048576 | bytes 4800000 | tf_op jit(solution)/shard_map/answer/pallas_call | solution.py:761
  84.9 0.0 collective-permute-done.14.low_ref
  84.9 2.0 %collective-permute-done.15.high_ref = f32[2,16,128]{2,1,0:T(8,128)S(1)} collective-permute-done((f32[2,16,128]{2,1,0:T(8,128)S(1)}, f32[2,16,128]{2,1,0:T(8,128)S(1)}, u32[]{:S(2)}, u32[]{:S(2)}) %collective-permute-start.15) | collective-permute-done | bytes 16416 | tf_op jit(solution)/shard_map/ppermute | solution.py:591
  86.9 0.0 collective-permute-done.13.refs_1_
  86.9 7.2 %collective-permute-start.16 = (f32[768,128]{1,0:T(8,128)S(1)}, f32[768,128]{1,0:T(8,128)S(1)}, u32[]{:S(2)}, u32[]{:S(2)}) collective-permute-start(f32[768,128]{1,0:T(8,128)S(1)} %early.1.refs_0_), channel_id=1, source_target_pairs={{0,1},{1,0},{2,3},{3,2},{4,5},{5,4},{6,7},{7,6},{8,9},{9,8},{10,11... | collective-permute-start | bytes 1179656 | tf_op jit(solution)/shard_map/ppermute | solution.py:864
  94.1 0.0 collective-permute-start.17
  94.1 3.7 %fifth.1.refs_4_ = f32[192,128]{1,0:T(8,128)S(1)} custom-call(s32[4,48]{1,0:T(4,128)S(1)} %bitcast.36, s32[1,200]{1,0:T(1,128)S(1)} %get-tuple-element.55.list_ref, s32[1,12]{1,0:T(1,128)S(1)} %copy-done.5, s32[2]{0:T(128)S(1)} %add_convert_fusion.edge_ref, f32[48,4,96,128]{3,2,1,0:T(8,128)S(1)} %get-tuple-element.54.blocks, ...), custom_call_target="tpu_custom_call" | custom-call | flops 1048576 | bytes 12800000 | tf_op jit(solution)/shard_map/fifth/pallas_call | solution.py:761
  97.9 0.7 collective-permute-start.20
  98.6 0.0 collective-permute-start.19
  98.6 1.2 %collective-permute-start.18 = (f32[192,128]{1,0:T(8,128)S(1)}, f32[192,128]{1,0:T(8,128)S(1)}, u32[]{:S(2)}, u32[]{:S(2)}) collective-permute-start(f32[192,128]{1,0:T(8,128)S(1)} %fifth.1.refs_4_), channel_id=1, source_target_pairs={{0,2},{1,3},{2,0},{3,1},{4,6},{5,7},{6,4},{7,5},{8,10},{9,11},{10,... | collective-permute-start | bytes 294920 | tf_op jit(solution)/shard_map/ppermute | solution.py:874
  99.8 0.7 reshape.37
  100.5 0.0 collective-permute-done.16.refs_2_
  100.5 0.0 collective-permute-done.17.refs_3_
  100.5 2.1 %mixed.1.refs_8_ = f32[48,128,128]{2,1,0:T(8,128)S(1)} custom-call(f32[768,128]{1,0:T(8,128)S(1)} %early.1.refs_0_, f32[768,128]{1,0:T(8,128)S(1)} %collective-permute-done.13.refs_1_, f32[768,128]{1,0:T(8,128)S(1)} %collective-permute-done.16.refs_2_, f32[768,128]{1,0:T(8,128)S(1)} %collective-permute-done.17.refs_3_), custom_call_target="tpu_custom_call" | custom-call | flops 1048576 | bytes 9600000 | tf_op jit(solution)/shard_map/mixed/pallas_call | solution.py:761
  102.6 0.4 collective-permute-done.20.refs_7_
  103.0 2.0 %collective-permute-done.18.refs_5_ = f32[192,128]{1,0:T(8,128)S(1)} collective-permute-done((f32[192,128]{1,0:T(8,128)S(1)}, f32[192,128]{1,0:T(8,128)S(1)}, u32[]{:S(2)}, u32[]{:S(2)}) %collective-permute-start.18) | collective-permute-done | bytes 98336 | tf_op jit(solution)/shard_map/ppermute | solution.py:874
  105.1 10.2 %grad.1 = f32[3456,128]{1,0:T(8,128)} custom-call(f32[768,128]{1,0:T(8,128)S(1)} %early.1.refs_0_, f32[768,128]{1,0:T(8,128)S(1)} %collective-permute-done.13.refs_1_, f32[768,128]{1,0:T(8,128)S(1)} %collective-permute-done.16.refs_2_, f32[768,128]{1,0:T(8,128)S(1)} %collective-permute-done.17.refs_3_, f32[192,128]{1,0:T(8,128)S(1)} %fifth.1.refs_4_, ...), custom_call_target="tpu_custom_call" | custom-call | flops 1048576 | bytes 32000000 | tf_op jit(solution)/shard_map/grad/pallas_call | solution.py:761
  (15 shorter events, 0.1 us)
Async XLA Ops:
  0.6 2.5 %copy-start.5 = (s32[1,12]{1,0:T(1,128)S(1)}, s32[1,12]{1,0:T(1,128)}, u32[]{:S(2)}) copy-start(s32[1,12]{1,0:T(1,128)} %send_ref.11) | copy-start | bytes 148
  0.6 2.5 %copy-start.1 = (f32[48,9216]{1,0:T(8,128)S(1)}, f32[48,9216]{1,0:T(8,128)}, u32[]{:S(2)}) copy-start(f32[48,9216]{1,0:T(8,128)} %param.8) | copy-start | bytes 5308420
  3.1 20.9 %copy-start.4 = (s32[48,4]{0,1:T(4,128)S(1)}, s32[48,4]{0,1:T(4,128)}, u32[]{:S(2)}) copy-start(s32[48,4]{0,1:T(4,128)} %param.11) | copy-start | bytes 2308
  5.4 13.3 %collective-permute-start = (f32[6,80,128]{2,1,0:T(8,128)S(1)}, f32[6,80,128]{2,1,0:T(8,128)S(1)}, u32[]{:S(2)}, u32[]{:S(2)}) collective-permute-start(f32[6,80,128]{2,1,0:T(8,128)S(1)} %get-tuple-element.51), channel_id=1, source_target_pairs={{4,0},{8,4},{12,8},{16,12},{20,16},{24,20},{28,24},{5,1},{9,5},{13... | collective-permute-start | bytes 737288 | tf_op jit(solution)/shard_map/ppermute | solution.py:591
  7.6 13.8 %collective-permute-start.1 = (f32[6,80,128]{2,1,0:T(8,128)S(1)}, f32[6,80,128]{2,1,0:T(8,128)S(1)}, u32[]{:S(2)}, u32[]{:S(2)}) collective-permute-start(f32[6,80,128]{2,1,0:T(8,128)S(1)} %get-tuple-element.50), channel_id=1, source_target_pairs={{0,4},{4,8},{8,12},{12,16},{16,20},{20,24},{24,28},{1,5},{5,9},{9,... | collective-permute-start | bytes 737288 | tf_op jit(solution)/shard_map/ppermute | solution.py:591
  17.2 1.4 %copy-start.2 = (f32[48,96,128]{2,1,0:T(8,128)}, f32[48,96,128]{2,1,0:T(8,128)S(1)}, u32[]{:S(2)}) copy-start(f32[48,96,128]{2,1,0:T(8,128)S(1)} %get-tuple-element.97.refs_9_) | copy-start | bytes 7077892
  21.4 24.5 %collective-permute-start.6 = (f32[2,128]{1,0:T(2,128)S(1)}, f32[2,128]{1,0:T(2,128)S(1)}, u32[]{:S(2)}, u32[]{:S(2)}) collective-permute-start(f32[2,128]{1,0:T(2,128)S(1)} %fusion.1), channel_id=1, source_target_pairs={{0,24},{4,28},{8,16},{12,20},{16,8},{20,12},{24,0},{28,4},{1,25},{... | collective-permute-start | bytes 3080 | tf_op jit(solution)/shard_map/ppermute | solution.py:575
  22.7 23.2 %collective-permute-start.5 = (f32[2,128]{1,0:T(2,128)S(1)}, f32[2,128]{1,0:T(2,128)S(1)}, u32[]{:S(2)}, u32[]{:S(2)}) collective-permute-start(f32[2,128]{1,0:T(2,128)S(1)} %fusion.1), channel_id=1, source_target_pairs={{0,16},{4,20},{8,24},{12,28},{16,0},{20,4},{24,8},{28,12},{1,17},{... | collective-permute-start | bytes 3080 | tf_op jit(solution)/shard_map/ppermute | solution.py:575
  23.6 22.3 %collective-permute-start.4 = (f32[2,128]{1,0:T(2,128)S(1)}, f32[2,128]{1,0:T(2,128)S(1)}, u32[]{:S(2)}, u32[]{:S(2)}) collective-permute-start(f32[2,128]{1,0:T(2,128)S(1)} %fusion.1), channel_id=1, source_target_pairs={{0,8},{4,12},{8,0},{12,4},{16,24},{20,28},{24,16},{28,20},{1,9},{5... | collective-permute-start | bytes 3080 | tf_op jit(solution)/shard_map/ppermute | solution.py:575
  24.0 3.0 %copy-start = (f32[48,4,9216]{2,1,0:T(4,128)S(1)}, f32[48,4,9216]{2,1,0:T(4,128)}, u32[]{:S(2)}) copy-start(f32[48,4,9216]{2,1,0:T(4,128)} %param.7) | copy-start | bytes 21233668
  37.3 8.6 %collective-permute-start.2 = (f32[2,24,128]{2,1,0:T(8,128)S(1)}, f32[2,24,128]{2,1,0:T(8,128)S(1)}, u32[]{:S(2)}, u32[]{:S(2)}) collective-permute-start(f32[2,24,128]{2,1,0:T(8,128)S(1)} %get-tuple-element.64), channel_id=1, source_target_pairs={{0,4},{4,8},{8,12},{12,16},{16,20},{20,24},{24,28},{1,5},{5,9},{9,... | collective-permute-start | bytes 73736 | tf_op jit(solution)/shard_map/ppermute | solution.py:591
  39.5 6.4 %collective-permute-start.3 = (f32[2,24,128]{2,1,0:T(8,128)S(1)}, f32[2,24,128]{2,1,0:T(8,128)S(1)}, u32[]{:S(2)}, u32[]{:S(2)}) collective-permute-start(f32[2,24,128]{2,1,0:T(8,128)S(1)} %get-tuple-element.65), channel_id=1, source_target_pairs={{4,0},{8,4},{12,8},{16,12},{20,16},{24,20},{28,24},{5,1},{9,5},{13... | collective-permute-start | bytes 73736 | tf_op jit(solution)/shard_map/ppermute | solution.py:591
  52.6 5.3 %collective-permute-start.7 = (f32[2,16,128]{2,1,0:T(8,128)S(1)}, f32[2,16,128]{2,1,0:T(8,128)S(1)}, u32[]{:S(2)}, u32[]{:S(2)}) collective-permute-start(f32[2,16,128]{2,1,0:T(8,128)S(1)} %get-tuple-element.70), channel_id=1, source_target_pairs={{0,4},{4,8},{8,12},{12,16},{16,20},{20,24},{24,28},{1,5},{5,9},{9,... | collective-permute-start | bytes 49160 | tf_op jit(solution)/shard_map/ppermute | solution.py:591
  55.7 5.4 %collective-permute-start.8 = (f32[2,16,128]{2,1,0:T(8,128)S(1)}, f32[2,16,128]{2,1,0:T(8,128)S(1)}, u32[]{:S(2)}, u32[]{:S(2)}) collective-permute-start(f32[2,16,128]{2,1,0:T(8,128)S(1)} %get-tuple-element.71), channel_id=1, source_target_pairs={{4,0},{8,4},{12,8},{16,12},{20,16},{24,20},{28,24},{5,1},{9,5},{13... | collective-permute-start | bytes 49160 | tf_op jit(solution)/shard_map/ppermute | solution.py:591
  61.9 3.7 %collective-permute-start.9 = (f32[8,128]{1,0:T(8,128)S(1)}, f32[8,128]{1,0:T(8,128)S(1)}, u32[]{:S(2)}, u32[]{:S(2)}) collective-permute-start(f32[8,128]{1,0:T(8,128)S(1)} %get-tuple-element.82), channel_id=1, source_target_pairs={{0,4},{4,0},{8,12},{12,8},{16,20},{20,16},{24,28},{28,24},{1,5},{5... | collective-permute-start | bytes 12296 | tf_op jit(solution)/shard_map/ppermute | solution.py:575
  65.6 6.8 %collective-permute-start.12 = (f32[8,128]{1,0:T(8,128)S(1)}, f32[8,128]{1,0:T(8,128)S(1)}, u32[]{:S(2)}, u32[]{:S(2)}) collective-permute-start(f32[8,128]{1,0:T(8,128)S(1)} %add.22.refs_6_), channel_id=1, source_target_pairs={{0,24},{4,28},{8,16},{12,20},{16,8},{20,12},{24,0},{28,4},{1,25},{... | collective-permute-start | bytes 12296 | tf_op jit(solution)/shard_map/ppermute | solution.py:575
  67.0 5.5 %collective-permute-start.11 = (f32[8,128]{1,0:T(8,128)S(1)}, f32[8,128]{1,0:T(8,128)S(1)}, u32[]{:S(2)}, u32[]{:S(2)}) collective-permute-start(f32[8,128]{1,0:T(8,128)S(1)} %add.22.refs_6_), channel_id=1, source_target_pairs={{0,16},{4,20},{8,24},{12,28},{16,0},{20,4},{24,8},{28,12},{1,17},{... | collective-permute-start | bytes 12296 | tf_op jit(solution)/shard_map/ppermute | solution.py:575
  68.6 3.9 %collective-permute-start.10 = (f32[8,128]{1,0:T(8,128)S(1)}, f32[8,128]{1,0:T(8,128)S(1)}, u32[]{:S(2)}, u32[]{:S(2)}) collective-permute-start(f32[8,128]{1,0:T(8,128)S(1)} %add.22.refs_6_), channel_id=1, source_target_pairs={{0,8},{4,12},{8,0},{12,4},{16,24},{20,28},{24,16},{28,20},{1,9},{5... | collective-permute-start | bytes 12296 | tf_op jit(solution)/shard_map/ppermute | solution.py:575
  76.1 10.8 %collective-permute-start.13 = (f32[768,128]{1,0:T(8,128)S(1)}, f32[768,128]{1,0:T(8,128)S(1)}, u32[]{:S(2)}, u32[]{:S(2)}) collective-permute-start(f32[768,128]{1,0:T(8,128)S(1)} %early.1.refs_0_), channel_id=1, source_target_pairs={{0,2},{1,3},{2,0},{3,1},{4,6},{5,7},{6,4},{7,5},{8,10},{9,11},{10,... | collective-permute-start | bytes 1179656 | tf_op jit(solution)/shard_map/ppermute | solution.py:855
  77.4 7.5 %collective-permute-start.14 = (f32[2,16,128]{2,1,0:T(8,128)S(1)}, f32[2,16,128]{2,1,0:T(8,128)S(1)}, u32[]{:S(2)}, u32[]{:S(2)}) collective-permute-start(f32[2,16,128]{2,1,0:T(8,128)S(1)} %get-tuple-element.86), channel_id=1, source_target_pairs={{0,4},{4,8},{8,12},{12,16},{16,20},{20,24},{24,28},{1,5},{5,9},{9,... | collective-permute-start | bytes 49160 | tf_op jit(solution)/shard_map/ppermute | solution.py:591
  81.5 5.4 %collective-permute-start.15 = (f32[2,16,128]{2,1,0:T(8,128)S(1)}, f32[2,16,128]{2,1,0:T(8,128)S(1)}, u32[]{:S(2)}, u32[]{:S(2)}) collective-permute-start(f32[2,16,128]{2,1,0:T(8,128)S(1)} %get-tuple-element.87), channel_id=1, source_target_pairs={{4,0},{8,4},{12,8},{16,12},{20,16},{24,20},{28,24},{5,1},{9,5},{13... | collective-permute-start | bytes 49160 | tf_op jit(solution)/shard_map/ppermute | solution.py:591
  86.9 13.6 %collective-permute-start.16 = (f32[768,128]{1,0:T(8,128)S(1)}, f32[768,128]{1,0:T(8,128)S(1)}, u32[]{:S(2)}, u32[]{:S(2)}) collective-permute-start(f32[768,128]{1,0:T(8,128)S(1)} %early.1.refs_0_), channel_id=1, source_target_pairs={{0,1},{1,0},{2,3},{3,2},{4,5},{5,4},{6,7},{7,6},{8,9},{9,8},{10,11... | collective-permute-start | bytes 1179656 | tf_op jit(solution)/shard_map/ppermute | solution.py:864
  94.1 6.4 %collective-permute-start.17 = (f32[768,128]{1,0:T(8,128)S(1)}, f32[768,128]{1,0:T(8,128)S(1)}, u32[]{:S(2)}, u32[]{:S(2)}) collective-permute-start(f32[768,128]{1,0:T(8,128)S(1)} %collective-permute-done.13.refs_1_), channel_id=1, source_target_pairs={{0,1},{1,0},{2,3},{3,2},{4,5},{5,4},{6,7},{7,6},{8,9},{9,8},{10,11... | collective-permute-start | bytes 1179656 | tf_op jit(solution)/shard_map/ppermute | solution.py:864
  97.9 5.2 %collective-permute-start.20 = (f32[192,128]{1,0:T(8,128)S(1)}, f32[192,128]{1,0:T(8,128)S(1)}, u32[]{:S(2)}, u32[]{:S(2)}) collective-permute-start(f32[192,128]{1,0:T(8,128)S(1)} %fifth.1.refs_4_), channel_id=1, source_target_pairs={{0,3},{1,2},{2,1},{3,0},{4,7},{5,6},{6,5},{7,4},{8,11},{9,10},{10,... | collective-permute-start | bytes 294920 | tf_op jit(solution)/shard_map/ppermute | solution.py:874
  98.6 4.4 %collective-permute-start.19 = (f32[192,128]{1,0:T(8,128)S(1)}, f32[192,128]{1,0:T(8,128)S(1)}, u32[]{:S(2)}, u32[]{:S(2)}) collective-permute-start(f32[192,128]{1,0:T(8,128)S(1)} %fifth.1.refs_4_), channel_id=1, source_target_pairs={{0,1},{1,0},{2,3},{3,2},{4,5},{5,4},{6,7},{7,6},{8,9},{9,8},{10,11... | collective-permute-start | bytes 294920 | tf_op jit(solution)/shard_map/ppermute | solution.py:874
  98.6 6.5 %collective-permute-start.18 = (f32[192,128]{1,0:T(8,128)S(1)}, f32[192,128]{1,0:T(8,128)S(1)}, u32[]{:S(2)}, u32[]{:S(2)}) collective-permute-start(f32[192,128]{1,0:T(8,128)S(1)} %fifth.1.refs_4_), channel_id=1, source_target_pairs={{0,2},{1,3},{2,0},{3,1},{4,6},{5,7},{6,4},{7,5},{8,10},{9,11},{10,... | collective-permute-start | bytes 294920 | tf_op jit(solution)/shard_map/ppermute | solution.py:874
  100.5 4.5 %copy-start.3 = (f32[48,96,128]{2,1,0:T(8,128)S(1)}, f32[48,96,128]{2,1,0:T(8,128)}, u32[]{:S(2)}) copy-start(f32[48,96,128]{2,1,0:T(8,128)} %copy-done.2) | copy-start | bytes 7077892

commit v7 on v6

--- a/solution.py
+++ b/solution.py
@@ -17,7 +17,8 @@
 EARLY = 16
 LATE = 4
 CUTS = BS * BS // 128
-GROUPS = 3
+SPAN = 24
+WIDE = 16
 LANES = 128
 OFF = 8
 ROWS = 64
@@ -89,10 +90,10 @@
             y_ref[k][r][...] = jnp.zeros_like(y_ref[k][r])
 
     def step(group, carry):
-        base = pl.multiple_of(group * CHUNK, CHUNK)
-        tiles = [x_ref[r, pl.ds(base + OFF, CHUNK), :] for r in range(count)]
-        for i in range(CHUNK):
-            n = group * CHUNK + i
+        base = pl.multiple_of(group * SPAN, CHUNK)
+        tiles = [x_ref[r, pl.ds(base + OFF, SPAN), :] for r in range(count)]
+        for i in range(SPAN):
+            n = group * SPAN + i
             oper = op_ref[n]
             images = [jnp.sum(oper * tiles[r][i : i + 1, :], axis=1, keepdims=True) for r in range(count)]
             if column_ref is not None:
@@ -106,7 +107,7 @@
                     y_ref[k][r][slot] = part if k == 0 else y_ref[k][r][slot] + part
         return carry
 
-    lax.fori_loop(0, NBLK // CHUNK, step, 0)
+    lax.fori_loop(0, NBLK // SPAN, step, 0)
 
 
 def ghost_images(op_ref, x_ref, g_ref):
@@ -250,12 +251,12 @@
         ref[0, CUTS + 7 : CUTS + 8, :] = traces
 
 
-def operator_kernel(raw_ref, weights_ref, ops_ref, gram_ref):
-    base = pl.program_id(0) * CHUNK
-    for i in range(CHUNK):
-        weights = unflatten(lambda q: raw_ref[pl.ds(8 * q + i, 8, stride=24), :])
-        weights_ref[i] = weights
-        ops_ref[base + i] = make_operator(weights, gram_ref.at[i & 1])
+def operator_kernel(raw_ref, ops_ref, gram_ref):
+    base = pl.program_id(0) * WIDE
+    for i in range(WIDE):
+        start = i // 8 * (8 * CUTS) + i % 8
+        weights = unflatten(lambda q: raw_ref[pl.ds(start + 8 * q, 8, stride=24), :])
+        ops_ref[base + i] = make_operator(weights, gram_ref.at[i & 3])
 
 
 def blocks_kernel(col_ref, stiff_ref, blocks_ref, list_ref, count_ref):
@@ -511,7 +512,7 @@
 
 
 def mixed_kernel(*refs):
-    early, mixed_ref = refs[:-1], refs[-1]
+    early, (raw_ref, mixed_ref, weights_ref) = refs[:-3], refs[-3:]
 
     def step(group, carry):
         for i in range(CHUNK):
@@ -521,6 +522,8 @@
             left = jnp.concatenate(resid + zeta, axis=0)
             right = jnp.concatenate(zeta + resid, axis=0)
             mixed_ref[group * CHUNK + i] = product(left, right, 0)
+            start = group * (8 * CUTS) + i
+            weights_ref[group * CHUNK + i] = unflatten(lambda q: raw_ref[pl.ds(start + 8 * q, 8, stride=24), :])
         return carry
 
     lax.fori_loop(0, NBLK // CHUNK, step, 0)
@@ -529,7 +532,7 @@
 def grad_kernel(*refs):
     peers = (len(refs) - 3) // 2
     early, late, mixed_ref, weights_ref, grad_ref = refs[:peers], refs[peers : 2 * peers], *refs[-3:]
-    first = pl.program_id(0) * GROUPS
+    first = pl.program_id(0) * WIDE
     upper = lax.broadcasted_iota(jnp.int32, (8, LANES), 0) < LATE
 
     def join(tiles):
@@ -539,26 +542,21 @@
             out.append(jnp.where(upper, tiles[q], other))
         return out
 
-    def step(part, carry):
-        group = first + part
-        for i in range(CHUNK):
-            n = group * CHUNK + i
-            at = pl.multiple_of(n * EARLY, EARLY)
-            pair = pl.ds(pl.multiple_of(group * (CHUNK * LATE) + 8 * (i // 2), 8), 8)
-            resid = join([ref[pl.ds(at, 8), :] for ref in early])
-            zeta = [ref[pair, :] for ref in late]
-            zeta = join([pltpu.roll(tile, LATE, 0) for tile in zeta] if i % 2 else zeta)
-            left = jnp.concatenate(resid + zeta, axis=0)
-            right = jnp.concatenate(zeta + resid, axis=0)
-            grad = product(weights_ref[part * CHUNK + i], mixed_ref[n] + product(left, right, 0), 1)
-
-            def write(q, value):
-                grad_ref[pl.ds(part * (8 * CUTS) + 8 * q + i, 8, stride=24), :] = value
-
-            flatten(grad, write)
-        return carry
-
-    lax.fori_loop(0, GROUPS, step, 0)
+    for i in range(WIDE):
+        n = first + i
+        at = pl.multiple_of(n * EARLY, EARLY)
+        pair = pl.ds(pl.multiple_of(first * LATE + 8 * (i // 2), 8), 8)
+        resid = join([ref[pl.ds(at, 8), :] for ref in early])
+        zeta = [ref[pair, :] for ref in late]
+        zeta = join([pltpu.roll(tile, LATE, 0) for tile in zeta] if i % 2 else zeta)
+        left = jnp.concatenate(resid + zeta, axis=0)
+        right = jnp.concatenate(zeta + resid, axis=0)
+        grad = product(weights_ref[i], mixed_ref[n] + product(left, right, 0), 1)
+
+        def write(q, value):
+            grad_ref[pl.ds(i // 8 * (8 * CUTS) + 8 * q + i % 8, 8, stride=24), :] = value
+
+        flatten(grad, write)
 
 
 def widening(parts, axis, step, most):
@@ -777,17 +775,17 @@
     partial = lambda r: [[pltpu.VMEM((ROWS, 8, LANES), f32)] * r] * K
     turned = [pltpu.VMEM((count, BS, LANES), f32), pltpu.VMEM((LANES, LANES), f32)]
     held = lambda r: pltpu.VMEM((r, ROWS, LANES), f32)
-    grams = pltpu.VMEM((2, BS, LANES), f32)
+    grams = pltpu.VMEM((4, BS, LANES), f32)
 
     up, down = call(
         pack_kernel, "pack", [send_rows], [weight_cuts, lax.slice_in_dim(stiff_cuts, 0, CHUNK * CUTS * K), base], [ghost_message] * 2, [], 3
     )
     near, far = exchange(up, down)
 
-    weights, ops = call(
-        operator_kernel, "operators", [], [weight_cuts], [shape(NBLK, BS, LANES), shape(NBLK, BS, LANES)],
-        [grams], 4, [pl.BlockSpec((CHUNK, BS, LANES), lambda g: (g, 0, 0)), vmem()], (NBLK // CHUNK,),
-        [pl.BlockSpec((CHUNK * CUTS, LANES), lambda g: (g, 0))],
+    (ops,) = call(
+        operator_kernel, "operators", [], [weight_cuts], [shape(NBLK, BS, LANES)],
+        [grams], 4, [vmem()], (NBLK // WIDE,),
+        [pl.BlockSpec((WIDE * CUTS, LANES), lambda g: (g, 0))],
     )
     stats, partner = up[0, CUTS + 6 :], jnp.where(sub % 2 == 0, far[0, CUTS + 6 :], near[0, CUTS + 6 :])
     if size > 1 and size & (size - 1) == 0:
@@ -875,11 +873,13 @@
     else:
         late = all_of(late, "rhs")
 
-    (mixed,) = call(mixed_kernel, "mixed", [], early, [shape(NBLK, LANES, LANES)], [], 3)
+    mixed, weights = call(
+        mixed_kernel, "mixed", [], [*early, weight_cuts], [shape(NBLK, LANES, LANES), shape(NBLK, BS, LANES)], [], 3
+    )
     (grad,) = call(
         grad_kernel, "grad", [], [*early, *late, mixed, weights], [shape(NBLK * CUTS, LANES)], [], 10,
-        [pl.BlockSpec((GROUPS * 8 * CUTS, LANES), lambda g: (g, 0))], (NBLK // (GROUPS * CHUNK),),
-        [vmem()] * (len(early) + len(late) + 1) + [pl.BlockSpec((GROUPS * CHUNK, BS, LANES), lambda g: (g, 0, 0))],
+        [pl.BlockSpec((WIDE * CUTS, LANES), lambda g: (g, 0))], (NBLK // WIDE,),
+        [vmem()] * (len(early) + len(late) + 1) + [pl.BlockSpec((WIDE, BS, LANES), lambda g: (g, 0, 0))],
     )
     grad = grad.reshape(NBLK // 8, CUTS, 8, LANES).transpose(0, 2, 1, 3).reshape(NBLK, BS * BS)
     return answer[:, OFF:HIGH, :BS].reshape(count, NBLK * BS), grad

time: 116 us -> 115 us (level)
  Pallas kernels: 56.9 us -> 55.5 us
    ppermute x8, waiting for transfers between devices: 7.75 us -> 9.89 us  [exchange(): return (lax.ppermute(up, 'sub', rising), lax.ppermute(down, 'sub', falling))]
    pallas_call x15, Pallas kernels: 56.9 us -> 55.5 us  [call(): pl.pallas_call(kernel, grid=grid, in_specs=in_specs or [smem()] * len(sca...]
    unnamed x12 -> x8, local copies, waits for them, and re-layouts: 4.44 us -> 3.02 us
    ppermute x3, waiting for transfers between devices: 2.44 us -> 1.1 us  [shards(): lax.ppermute(late, 'rhs', [(i, i ^ d) for i in range(size)])]
  transfers between devices with their start and end apart: 21 -> 21, of which waited for: 5 -> 4; matrix products, arithmetic and copies ran while one was open for 1% -> 2% of each run, Pallas kernels for 29% -> 28%
where the time goes in v7:
time: 115 us
  Pallas kernels  55.5 us (48%)
  starting transfers between devices  38.9 us (34%)
  waiting for transfers between devices  11 us (10%)
  local copies, waits for them, and re-layouts  6.64 us (6%)
  between operations  1.64 us (1%)
    pallas_call x15, Pallas kernels, call(): pl.pallas_call(kernel, grid=grid, in_specs=in_specs or [smem()] * len(sca...  55.5 us
    ppermute x8, starting transfers between devices, exchange(): return (lax.ppermute(up, 'sub', rising), lax.ppermute(down, 'sub', falling))  22.8 us
    ppermute x8, waiting for transfers between devices, exchange(): return (lax.ppermute(up, 'sub', rising), lax.ppermute(down, 'sub', falling))  9.89 us
    ppermute x2, starting transfers between devices, shards(): lax.ppermute(part, 'rhs', [(i, i ^ 1) for i in range(size)])  7.21 us
    ppermute x7, starting transfers between devices, widening(): lax.ppermute(total, axis, [(i, i ^ d * step) for i in range(size)])  5.66 us
    unnamed x8, local copies, waits for them, and re-layouts  3.02 us
  transfers between devices with their start and end apart: 21, of which 4 were waited for; matrix products, arithmetic and copies ran while one was open for 2% of the time, Pallas kernels for 28%

profile of v7, /device:TPU:13, one launch (start us, length us, event | category | flops | bytes accessed | tf_op | source)
XLA Modules:
  0.0 114.7 jit_solution(6155226380952938033)
XLA Ops:
  0.7 1.0 pad_maximum_fusion
  1.6 0.1 reshape.35
  1.7 1.4 %slice.24 = f32[8,72,4,128]{3,2,1,0:T(4,128)S(1)} slice(f32[48,72,4,128]{3,2,1,0:T(4,128)} %bitcast.28), slice={[0:8], [0:72], [0:4], [0:128]} | slice | bytes 2359296 | tf_op jit(solution)/shard_map/slice | solution.py:781
  3.1 2.3 %pack.1 = (f32[6,80,128]{2,1,0:T(8,128)S(1)}, f32[6,80,128]{2,1,0:T(8,128)S(1)}) custom-call(s32[1,12]{1,0:T(1,128)S(1)} %copy-done.3, f32[3456,128]{1,0:T(8,128)S(1)} %bitcast.25, f32[2304,128]{1,0:T(8,128)S(1)} %bitcast.30, f32[4,64,128]{2,1,0:T(8,128)S(1)} %pad.4.base_ref), custom_call_target="tpu_custom_call" | custom-call | flops 1048576 | bytes 9600000 | tf_op jit(solution)/shard_map/pack/pallas_call | solution.py:759
  5.4 0.0 copy-start.2
  5.4 2.1 %collective-permute-start = (f32[6,80,128]{2,1,0:T(8,128)S(1)}, f32[6,80,128]{2,1,0:T(8,128)S(1)}, u32[]{:S(2)}, u32[]{:S(2)}) collective-permute-start(f32[6,80,128]{2,1,0:T(8,128)S(1)} %get-tuple-element.51), channel_id=1, source_target_pairs={{4,0},{8,4},{12,8},{16,12},{20,16},{24,20},{28,24},{5,1},{9,5},{13... | collective-permute-start | bytes 737288 | tf_op jit(solution)/shard_map/ppermute | solution.py:589
  7.6 4.0 %collective-permute-start.1 = (f32[6,80,128]{2,1,0:T(8,128)S(1)}, f32[6,80,128]{2,1,0:T(8,128)S(1)}, u32[]{:S(2)}, u32[]{:S(2)}) collective-permute-start(f32[6,80,128]{2,1,0:T(8,128)S(1)} %get-tuple-element.50), channel_id=1, source_target_pairs={{0,4},{4,8},{8,12},{12,16},{16,20},{20,24},{24,28},{1,5},{5,9},{9,... | collective-permute-start | bytes 737288 | tf_op jit(solution)/shard_map/ppermute | solution.py:589
  12.3 4.2 %operators.1.op_ref.ops_ref = f32[48,96,128]{2,1,0:T(8,128)S(1)} custom-call(f32[3456,128]{1,0:T(8,128)S(1)} %bitcast.26), custom_call_target="tpu_custom_call" | custom-call | flops 1048576 | bytes 12800000 | tf_op jit(solution)/shard_map/operators/pallas_call | solution.py:759
  16.5 0.1 add_convert_fusion.edge_ref
  16.6 0.0 collective-permute-done.high_ref
  16.6 4.8 %collective-permute-done.1.low_ref = f32[6,80,128]{2,1,0:T(8,128)S(1)} collective-permute-done((f32[6,80,128]{2,1,0:T(8,128)S(1)}, f32[6,80,128]{2,1,0:T(8,128)S(1)}, u32[]{:S(2)}, u32[]{:S(2)}) %collective-permute-start.1) | collective-permute-done | bytes 245792 | tf_op jit(solution)/shard_map/ppermute | solution.py:589
  21.4 1.3 %collective-permute-start.6 = (f32[2,128]{1,0:T(2,128)S(1)}, f32[2,128]{1,0:T(2,128)S(1)}, u32[]{:S(2)}, u32[]{:S(2)}) collective-permute-start(f32[2,128]{1,0:T(2,128)S(1)} %fusion.1), channel_id=1, source_target_pairs={{0,24},{4,28},{8,16},{12,20},{16,8},{20,12},{24,0},{28,4},{1,25},{... | collective-permute-start | bytes 3080 | tf_op jit(solution)/shard_map/ppermute | solution.py:573
  22.7 1.0 collective-permute-start.5
  23.6 0.4 collective-permute-start.4
  24.0 3.0 %copy-done.1 = f32[48,4,9216]{2,1,0:T(4,128)S(1)} copy-done((f32[48,4,9216]{2,1,0:T(4,128)S(1)}, f32[48,4,9216]{2,1,0:T(4,128)}, u32[]{:S(2)}) %copy-start.1) | copy-done | bytes 7077912
  27.0 4.9 %blocks.1 = (f32[48,4,96,128]{3,2,1,0:T(8,128)S(1)}, s32[1,200]{1,0:T(1,128)S(1)}) custom-call(s32[4,48]{1,0:T(4,128)S(1)} %bitcast.31, f32[13824,128]{1,0:T(8,128)S(1)} %bitcast.29), custom_call_target="tpu_custom_call" | custom-call | flops 1048576 | bytes 16000000 | tf_op jit(solution)/shard_map/blocks/pallas_call | solution.py:759
  31.9 5.2 %first.1 = (f32[4,64,128]{2,1,0:T(8,128)S(1)}, f32[2,64,128]{2,1,0:T(8,128)S(1)}, f32[2,64,128]{2,1,0:T(8,128)S(1)}, f32[2,24,128]{2,1,0:T(8,128)S(1)}, f32[2,24,128]{2,1,0:T(8,128)S(1)}) custom-call(s32[4,48]{1,0:T(4,128)S(1)} %bitcast.32, s32[1,200]{1,0:T(1,128)S(1)} %get-tuple-element.54.list_ref, s32[1,12]{1,0:T(1,128)S(1)} %copy-done.3, ...), custom_call_target="tpu_custom_call" | custom-call | flops 1048576 | bytes 19200000 | tf_op jit(solution)/shard_map/first/pallas_call | solution.py:759
  37.1 2.2 %collective-permute-start.2 = (f32[2,24,128]{2,1,0:T(8,128)S(1)}, f32[2,24,128]{2,1,0:T(8,128)S(1)}, u32[]{:S(2)}, u32[]{:S(2)}) collective-permute-start(f32[2,24,128]{2,1,0:T(8,128)S(1)} %get-tuple-element.63), channel_id=1, source_target_pairs={{0,4},{4,8},{8,12},{12,16},{16,20},{20,24},{24,28},{1,5},{5,9},{9,... | collective-permute-start | bytes 73736 | tf_op jit(solution)/shard_map/ppermute | solution.py:589
  39.3 3.1 %collective-permute-start.3 = (f32[2,24,128]{2,1,0:T(8,128)S(1)}, f32[2,24,128]{2,1,0:T(8,128)S(1)}, u32[]{:S(2)}, u32[]{:S(2)}) collective-permute-start(f32[2,24,128]{2,1,0:T(8,128)S(1)} %get-tuple-element.64), channel_id=1, source_target_pairs={{4,0},{8,4},{12,8},{16,12},{20,16},{24,20},{28,24},{5,1},{9,5},{13... | collective-permute-start | bytes 73736 | tf_op jit(solution)/shard_map/ppermute | solution.py:589
  42.4 3.2 %ghosts.1 = (f32[12,96,128]{2,1,0:T(8,128)S(1)}, f32[2,64,128]{2,1,0:T(8,128)S(1)}, f32[2,64,128]{2,1,0:T(8,128)S(1)}) custom-call(f32[48,96,128]{2,1,0:T(8,128)S(1)} %operators.1.op_ref.ops_ref, f32[4,64,128]{2,1,0:T(8,128)S(1)} %get-tuple-element.73.zero_ref, f32[2,64,128]{2,1,0:T(8,128)S(1)} %get-tuple-element.58.a1_ref, ...), custom_call_target="tpu_custom_call" | custom-call | flops 1048576 | bytes 9600000 | tf_op jit(solution)/shard_map/ghosts/pallas_call | solution.py:759
  45.7 0.0 collective-permute-done.6
  45.7 0.0 collective-permute-done.5
  45.7 0.0 collective-permute-done.4
  45.7 0.0 collective-permute-done.2.low_ref
  45.7 0.0 collective-permute-done.3.high_ref
  45.7 6.6 %second.1 = (f32[2,64,128]{2,1,0:T(8,128)S(1)}, f32[2,64,128]{2,1,0:T(8,128)S(1)}, f32[2,64,128]{2,1,0:T(8,128)S(1)}, f32[2,64,128]{2,1,0:T(8,128)S(1)}, f32[2,6...) custom-call(s32[4,48]{1,0:T(4,128)S(1)} %bitcast.33, ...), custom_call_target="tpu_custom_call" | custom-call | flops 1048576 | bytes 22400000 | tf_op jit(solution)/shard_map/second/pallas_call | solution.py:759
  52.3 3.1 %collective-permute-start.7 = (f32[2,16,128]{2,1,0:T(8,128)S(1)}, f32[2,16,128]{2,1,0:T(8,128)S(1)}, u32[]{:S(2)}, u32[]{:S(2)}) collective-permute-start(f32[2,16,128]{2,1,0:T(8,128)S(1)} %get-tuple-element.69), channel_id=1, source_target_pairs={{0,4},{4,8},{8,12},{12,16},{16,20},{20,24},{24,28},{1,5},{5,9},{9,... | collective-permute-start | bytes 49160 | tf_op jit(solution)/shard_map/ppermute | solution.py:589
  55.4 2.2 %collective-permute-start.8 = (f32[2,16,128]{2,1,0:T(8,128)S(1)}, f32[2,16,128]{2,1,0:T(8,128)S(1)}, u32[]{:S(2)}, u32[]{:S(2)}) collective-permute-start(f32[2,16,128]{2,1,0:T(8,128)S(1)} %get-tuple-element.70), channel_id=1, source_target_pairs={{4,0},{8,4},{12,8},{16,12},{20,16},{24,20},{28,24},{5,1},{9,5},{13... | collective-permute-start | bytes 49160 | tf_op jit(solution)/shard_map/ppermute | solution.py:589
  57.6 0.0 collective-permute-done.7.low_ref
  57.7 3.2 %collective-permute-done.8.high_ref = f32[2,16,128]{2,1,0:T(8,128)S(1)} collective-permute-done((f32[2,16,128]{2,1,0:T(8,128)S(1)}, f32[2,16,128]{2,1,0:T(8,128)S(1)}, u32[]{:S(2)}, u32[]{:S(2)}) %collective-permute-start.8) | collective-permute-done | bytes 16416 | tf_op jit(solution)/shard_map/ppermute | solution.py:589
  60.8 0.8 moments.1
  61.6 0.1 collective-permute-start.9
  61.7 3.5 %target.1.refs_5_ = f32[2,64,128]{2,1,0:T(8,128)S(1)} custom-call(s32[4,48]{1,0:T(4,128)S(1)} %bitcast.34, s32[1,200]{1,0:T(1,128)S(1)} %get-tuple-element.54.list_ref, f32[48,4,96,128]{3,2,1,0:T(8,128)S(1)} %get-tuple-element.53.blocks, f32[48,96,128]{2,1,0:T(8,128)S(1)} %operators.1.op_ref.ops_ref, f32[12,96,128]{2,1,0:T(8,128)S(1)} %get-tuple-element.59.gop_ref, ...), custom_call_target="tpu_custom_call" | custom-call | flops 1048576 | bytes 9600000 | tf_op jit(solution)/shard_map/target/pallas_call | solution.py:759
  65.2 0.0 collective-permute-done.9
  65.2 1.4 %collective-permute-start.12 = (f32[8,128]{1,0:T(8,128)S(1)}, f32[8,128]{1,0:T(8,128)S(1)}, u32[]{:S(2)}, u32[]{:S(2)}) collective-permute-start(f32[8,128]{1,0:T(8,128)S(1)} %add.22.refs_6_), channel_id=1, source_target_pairs={{0,24},{4,28},{8,16},{12,20},{16,8},{20,12},{24,0},{28,4},{1,25},{... | collective-permute-start | bytes 12296 | tf_op jit(solution)/shard_map/ppermute | solution.py:573
  66.6 1.6 %collective-permute-start.11 = (f32[8,128]{1,0:T(8,128)S(1)}, f32[8,128]{1,0:T(8,128)S(1)}, u32[]{:S(2)}, u32[]{:S(2)}) collective-permute-start(f32[8,128]{1,0:T(8,128)S(1)} %add.22.refs_6_), channel_id=1, source_target_pairs={{0,16},{4,20},{8,24},{12,28},{16,0},{20,4},{24,8},{28,12},{1,17},{... | collective-permute-start | bytes 12296 | tf_op jit(solution)/shard_map/ppermute | solution.py:573
  68.2 0.0 collective-permute-start.10
  68.2 3.6 %third.1.refs_4_ = f32[2,64,128]{2,1,0:T(8,128)S(1)} custom-call(s32[4,48]{1,0:T(4,128)S(1)} %bitcast.35, s32[1,200]{1,0:T(1,128)S(1)} %get-tuple-element.54.list_ref, f32[48,4,96,128]{3,2,1,0:T(8,128)S(1)} %get-tuple-element.53.blocks, f32[48,96,128]{2,1,0:T(8,128)S(1)} %operators.1.op_ref.ops_ref, f32[12,96,128]{2,1,0:T(8,128)S(1)} %get-tuple-element.59.gop_ref, ...), custom_call_target="tpu_custom_call" | custom-call | flops 1048576 | bytes 12800000 | tf_op jit(solution)/shard_map/third/pallas_call | solution.py:759
  71.8 0.0 collective-permute-done.12.refs_9_
  71.8 0.0 collective-permute-done.11.refs_8_
  71.8 0.0 collective-permute-done.10.refs_7_
  71.8 3.4 %fourth.1 = (f32[2,64,128]{2,1,0:T(8,128)}, f32[2,64,128]{2,1,0:T(8,128)S(1)}, f32[2,64,128]{2,1,0:T(8,128)S(1)}, f32[10,8,8,128]{3,2,1,0:T(8,128)S(1)}, f32[3,8...) custom-call(s32[4,48]{1,0:T(4,128)S(1)} %bitcast.36, s32[1,12]{1,0:T(1,128)S(1)} %copy-done.3, ...), custom_call_target="tpu_custom_call" | custom-call | flops 1048576 | bytes 9600000 | tf_op jit(solution)/shard_map/fourth/pallas_call | solution.py:759
  75.2 0.2 early.1.refs_0_
  75.4 1.3 %collective-permute-start.13 = (f32[768,128]{1,0:T(8,128)S(1)}, f32[768,128]{1,0:T(8,128)S(1)}, u32[]{:S(2)}, u32[]{:S(2)}) collective-permute-start(f32[768,128]{1,0:T(8,128)S(1)} %early.1.refs_0_), channel_id=1, source_target_pairs={{0,2},{1,3},{2,0},{3,1},{4,6},{5,7},{6,4},{7,5},{8,10},{9,11},{10,... | collective-permute-start | bytes 1179656 | tf_op jit(solution)/shard_map/ppermute | solution.py:853
  76.6 4.1 %collective-permute-start.14 = (f32[2,16,128]{2,1,0:T(8,128)S(1)}, f32[2,16,128]{2,1,0:T(8,128)S(1)}, u32[]{:S(2)}, u32[]{:S(2)}) collective-permute-start(f32[2,16,128]{2,1,0:T(8,128)S(1)} %get-tuple-element.85), channel_id=1, source_target_pairs={{0,4},{4,8},{8,12},{12,16},{16,20},{20,24},{24,28},{1,5},{5,9},{9,... | collective-permute-start | bytes 49160 | tf_op jit(solution)/shard_map/ppermute | solution.py:589
  80.8 1.9 %collective-permute-start.15 = (f32[2,16,128]{2,1,0:T(8,128)S(1)}, f32[2,16,128]{2,1,0:T(8,128)S(1)}, u32[]{:S(2)}, u32[]{:S(2)}) collective-permute-start(f32[2,16,128]{2,1,0:T(8,128)S(1)} %get-tuple-element.86), channel_id=1, source_target_pairs={{4,0},{8,4},{12,8},{16,12},{20,16},{24,20},{28,24},{5,1},{9,5},{13... | collective-permute-start | bytes 49160 | tf_op jit(solution)/shard_map/ppermute | solution.py:589
  82.7 1.5 %answer.1 = (f32[2,2,64,128]{3,2,1,0:T(8,128)S(1)}, f32[2,64,128]{2,1,0:T(8,128)S(1)}) custom-call(f32[48,96,128]{2,1,0:T(8,128)S(1)} %operators.1.op_ref.ops_ref, f32[10,8,8,128]{3,2,1,0:T(8,128)S(1)} %get-tuple-element.83.coef_ref, f32[4,64,128]{2,1,0:T(8,128)S(1)} %get-tuple-element.73.zero_ref, f32[2,64,128]{2,1,0:T(8,128)S(1)} %get-tuple-element.74.refs_0_, ...), custom_call_target="tpu_custom_call" | custom-call | flops 1048576 | bytes 4800000 | tf_op jit(solution)/shard_map/answer/pallas_call | solution.py:759
  84.2 0.0 collective-permute-done.14.low_ref
  84.2 2.0 %collective-permute-done.15.high_ref = f32[2,16,128]{2,1,0:T(8,128)S(1)} collective-permute-done((f32[2,16,128]{2,1,0:T(8,128)S(1)}, f32[2,16,128]{2,1,0:T(8,128)S(1)}, u32[]{:S(2)}, u32[]{:S(2)}) %collective-permute-start.15) | collective-permute-done | bytes 16416 | tf_op jit(solution)/shard_map/ppermute | solution.py:589
  86.1 0.0 collective-permute-done.13.refs_1_
  86.2 7.2 %collective-permute-start.16 = (f32[768,128]{1,0:T(8,128)S(1)}, f32[768,128]{1,0:T(8,128)S(1)}, u32[]{:S(2)}, u32[]{:S(2)}) collective-permute-start(f32[768,128]{1,0:T(8,128)S(1)} %early.1.refs_0_), channel_id=1, source_target_pairs={{0,1},{1,0},{2,3},{3,2},{4,5},{5,4},{6,7},{7,6},{8,9},{9,8},{10,11... | collective-permute-start | bytes 1179656 | tf_op jit(solution)/shard_map/ppermute | solution.py:862
  93.4 0.0 collective-permute-start.17
  93.4 3.6 %fifth.1.refs_4_ = f32[192,128]{1,0:T(8,128)S(1)} custom-call(s32[4,48]{1,0:T(4,128)S(1)} %bitcast.37, s32[1,200]{1,0:T(1,128)S(1)} %get-tuple-element.54.list_ref, s32[1,12]{1,0:T(1,128)S(1)} %copy-done.3, s32[2]{0:T(128)S(1)} %add_convert_fusion.edge_ref, f32[48,4,96,128]{3,2,1,0:T(8,128)S(1)} %get-tuple-element.53.blocks, ...), custom_call_target="tpu_custom_call" | custom-call | flops 1048576 | bytes 12800000 | tf_op jit(solution)/shard_map/fifth/pallas_call | solution.py:759
  97.0 0.7 collective-permute-start.20
  97.7 0.0 collective-permute-start.19
  97.7 1.2 %collective-permute-start.18 = (f32[192,128]{1,0:T(8,128)S(1)}, f32[192,128]{1,0:T(8,128)}, u32[]{:S(2)}, u32[]{:S(2)}) collective-permute-start(f32[192,128]{1,0:T(8,128)S(1)} %fifth.1.refs_4_), channel_id=1, source_target_pairs={{0,2},{1,3},{2,0},{3,1},{4,6},{5,7},{6,4},{7,5},{8,10},{9,11},{10,... | collective-permute-start | bytes 294920 | tf_op jit(solution)/shard_map/ppermute | solution.py:872
  98.9 0.6 slice.23
  99.6 1.5 %reshape.37 = f32[2,4608]{1,0:T(2,128)} reshape(f32[2,48,96]{2,1,0:T(8,128)} %slice.23) | data formatting | bytes 73728 | tf_op jit(solution)/shard_map/reshape | solution.py:885
  101.1 0.0 collective-permute-done.16.refs_2_
  101.1 0.0 collective-permute-done.17.refs_3_
  101.1 2.1 %mixed.1 = (f32[48,128,128]{2,1,0:T(8,128)S(1)}, f32[48,96,128]{2,1,0:T(8,128)S(1)}) custom-call(f32[768,128]{1,0:T(8,128)S(1)} %early.1.refs_0_, f32[768,128]{1,0:T(8,128)S(1)} %collective-permute-done.13.refs_1_, f32[768,128]{1,0:T(8,128)S(1)} %collective-permute-done.16.refs_2_, f32[768,128]{1,0:T(8,128)S(1)} %collective-permute-done.17.refs_3_, ...), custom_call_target="tpu_custom_call" | custom-call | flops 1048576 | bytes 9600000 | tf_op jit(solution)/shard_map/mixed/pallas_call | solution.py:759
  103.2 0.0 collective-permute-done.20.refs_7_
  103.2 1.1 collective-permute-done.18.refs_5_
  104.3 10.4 %grad.1 = f32[3456,128]{1,0:T(8,128)} custom-call(f32[768,128]{1,0:T(8,128)S(1)} %early.1.refs_0_, f32[768,128]{1,0:T(8,128)S(1)} %collective-permute-done.13.refs_1_, f32[768,128]{1,0:T(8,128)S(1)} %collective-permute-done.16.refs_2_, f32[768,128]{1,0:T(8,128)S(1)} %collective-permute-done.17.refs_3_, f32[192,128]{1,0:T(8,128)S(1)} %fifth.1.refs_4_, ...), custom_call_target="tpu_custom_call" | custom-call | flops 1048576 | bytes 32000000 | tf_op jit(solution)/shard_map/grad/pallas_call | solution.py:759
  (11 shorter events, 0.0 us)
Async XLA Ops:
  0.6 2.5 %copy-start.3 = (s32[1,12]{1,0:T(1,128)S(1)}, s32[1,12]{1,0:T(1,128)}, u32[]{:S(2)}) copy-start(s32[1,12]{1,0:T(1,128)} %send_ref.11) | copy-start | bytes 148
  0.6 2.5 %copy-start = (f32[48,9216]{1,0:T(8,128)S(1)}, f32[48,9216]{1,0:T(8,128)}, u32[]{:S(2)}) copy-start(f32[48,9216]{1,0:T(8,128)} %param.8) | copy-start | bytes 5308420
  5.4 18.6 %copy-start.2 = (s32[48,4]{0,1:T(4,128)S(1)}, s32[48,4]{0,1:T(4,128)}, u32[]{:S(2)}) copy-start(s32[48,4]{0,1:T(4,128)} %param.11) | copy-start | bytes 2308
  5.4 11.2 %collective-permute-start = (f32[6,80,128]{2,1,0:T(8,128)S(1)}, f32[6,80,128]{2,1,0:T(8,128)S(1)}, u32[]{:S(2)}, u32[]{:S(2)}) collective-permute-start(f32[6,80,128]{2,1,0:T(8,128)S(1)} %get-tuple-element.51), channel_id=1, source_target_pairs={{4,0},{8,4},{12,8},{16,12},{20,16},{24,20},{28,24},{5,1},{9,5},{13... | collective-permute-start | bytes 737288 | tf_op jit(solution)/shard_map/ppermute | solution.py:589
  7.6 13.8 %collective-permute-start.1 = (f32[6,80,128]{2,1,0:T(8,128)S(1)}, f32[6,80,128]{2,1,0:T(8,128)S(1)}, u32[]{:S(2)}, u32[]{:S(2)}) collective-permute-start(f32[6,80,128]{2,1,0:T(8,128)S(1)} %get-tuple-element.50), channel_id=1, source_target_pairs={{0,4},{4,8},{8,12},{12,16},{16,20},{20,24},{24,28},{1,5},{5,9},{9,... | collective-permute-start | bytes 737288 | tf_op jit(solution)/shard_map/ppermute | solution.py:589
  21.4 24.3 %collective-permute-start.6 = (f32[2,128]{1,0:T(2,128)S(1)}, f32[2,128]{1,0:T(2,128)S(1)}, u32[]{:S(2)}, u32[]{:S(2)}) collective-permute-start(f32[2,128]{1,0:T(2,128)S(1)} %fusion.1), channel_id=1, source_target_pairs={{0,24},{4,28},{8,16},{12,20},{16,8},{20,12},{24,0},{28,4},{1,25},{... | collective-permute-start | bytes 3080 | tf_op jit(solution)/shard_map/ppermute | solution.py:573
  22.7 23.0 %collective-permute-start.5 = (f32[2,128]{1,0:T(2,128)S(1)}, f32[2,128]{1,0:T(2,128)S(1)}, u32[]{:S(2)}, u32[]{:S(2)}) collective-permute-start(f32[2,128]{1,0:T(2,128)S(1)} %fusion.1), channel_id=1, source_target_pairs={{0,16},{4,20},{8,24},{12,28},{16,0},{20,4},{24,8},{28,12},{1,17},{... | collective-permute-start | bytes 3080 | tf_op jit(solution)/shard_map/ppermute | solution.py:573
  23.6 22.1 %collective-permute-start.4 = (f32[2,128]{1,0:T(2,128)S(1)}, f32[2,128]{1,0:T(2,128)S(1)}, u32[]{:S(2)}, u32[]{:S(2)}) collective-permute-start(f32[2,128]{1,0:T(2,128)S(1)} %fusion.1), channel_id=1, source_target_pairs={{0,8},{4,12},{8,0},{12,4},{16,24},{20,28},{24,16},{28,20},{1,9},{5... | collective-permute-start | bytes 3080 | tf_op jit(solution)/shard_map/ppermute | solution.py:573
  24.0 3.0 %copy-start.1 = (f32[48,4,9216]{2,1,0:T(4,128)S(1)}, f32[48,4,9216]{2,1,0:T(4,128)}, u32[]{:S(2)}) copy-start(f32[48,4,9216]{2,1,0:T(4,128)} %param.7) | copy-start | bytes 21233668
  37.1 8.6 %collective-permute-start.2 = (f32[2,24,128]{2,1,0:T(8,128)S(1)}, f32[2,24,128]{2,1,0:T(8,128)S(1)}, u32[]{:S(2)}, u32[]{:S(2)}) collective-permute-start(f32[2,24,128]{2,1,0:T(8,128)S(1)} %get-tuple-element.63), channel_id=1, source_target_pairs={{0,4},{4,8},{8,12},{12,16},{16,20},{20,24},{24,28},{1,5},{5,9},{9,... | collective-permute-start | bytes 73736 | tf_op jit(solution)/shard_map/ppermute | solution.py:589
  39.3 6.4 %collective-permute-start.3 = (f32[2,24,128]{2,1,0:T(8,128)S(1)}, f32[2,24,128]{2,1,0:T(8,128)S(1)}, u32[]{:S(2)}, u32[]{:S(2)}) collective-permute-start(f32[2,24,128]{2,1,0:T(8,128)S(1)} %get-tuple-element.64), channel_id=1, source_target_pairs={{4,0},{8,4},{12,8},{16,12},{20,16},{24,20},{28,24},{5,1},{9,5},{13... | collective-permute-start | bytes 73736 | tf_op jit(solution)/shard_map/ppermute | solution.py:589
  52.3 5.3 %collective-permute-start.7 = (f32[2,16,128]{2,1,0:T(8,128)S(1)}, f32[2,16,128]{2,1,0:T(8,128)S(1)}, u32[]{:S(2)}, u32[]{:S(2)}) collective-permute-start(f32[2,16,128]{2,1,0:T(8,128)S(1)} %get-tuple-element.69), channel_id=1, source_target_pairs={{0,4},{4,8},{8,12},{12,16},{16,20},{20,24},{24,28},{1,5},{5,9},{9,... | collective-permute-start | bytes 49160 | tf_op jit(solution)/shard_map/ppermute | solution.py:589
  55.4 5.4 %collective-permute-start.8 = (f32[2,16,128]{2,1,0:T(8,128)S(1)}, f32[2,16,128]{2,1,0:T(8,128)S(1)}, u32[]{:S(2)}, u32[]{:S(2)}) collective-permute-start(f32[2,16,128]{2,1,0:T(8,128)S(1)} %get-tuple-element.70), channel_id=1, source_target_pairs={{4,0},{8,4},{12,8},{16,12},{20,16},{24,20},{28,24},{5,1},{9,5},{13... | collective-permute-start | bytes 49160 | tf_op jit(solution)/shard_map/ppermute | solution.py:589
  61.6 3.6 %collective-permute-start.9 = (f32[8,128]{1,0:T(8,128)S(1)}, f32[8,128]{1,0:T(8,128)S(1)}, u32[]{:S(2)}, u32[]{:S(2)}) collective-permute-start(f32[8,128]{1,0:T(8,128)S(1)} %get-tuple-element.81), channel_id=1, source_target_pairs={{0,4},{4,0},{8,12},{12,8},{16,20},{20,16},{24,28},{28,24},{1,5},{5... | collective-permute-start | bytes 12296 | tf_op jit(solution)/shard_map/ppermute | solution.py:573
  65.2 6.5 %collective-permute-start.12 = (f32[8,128]{1,0:T(8,128)S(1)}, f32[8,128]{1,0:T(8,128)S(1)}, u32[]{:S(2)}, u32[]{:S(2)}) collective-permute-start(f32[8,128]{1,0:T(8,128)S(1)} %add.22.refs_6_), channel_id=1, source_target_pairs={{0,24},{4,28},{8,16},{12,20},{16,8},{20,12},{24,0},{28,4},{1,25},{... | collective-permute-start | bytes 12296 | tf_op jit(solution)/shard_map/ppermute | solution.py:573
  66.6 5.2 %collective-permute-start.11 = (f32[8,128]{1,0:T(8,128)S(1)}, f32[8,128]{1,0:T(8,128)S(1)}, u32[]{:S(2)}, u32[]{:S(2)}) collective-permute-start(f32[8,128]{1,0:T(8,128)S(1)} %add.22.refs_6_), channel_id=1, source_target_pairs={{0,16},{4,20},{8,24},{12,28},{16,0},{20,4},{24,8},{28,12},{1,17},{... | collective-permute-start | bytes 12296 | tf_op jit(solution)/shard_map/ppermute | solution.py:573
  68.2 3.6 %collective-permute-start.10 = (f32[8,128]{1,0:T(8,128)S(1)}, f32[8,128]{1,0:T(8,128)S(1)}, u32[]{:S(2)}, u32[]{:S(2)}) collective-permute-start(f32[8,128]{1,0:T(8,128)S(1)} %add.22.refs_6_), channel_id=1, source_target_pairs={{0,8},{4,12},{8,0},{12,4},{16,24},{20,28},{24,16},{28,20},{1,9},{5... | collective-permute-start | bytes 12296 | tf_op jit(solution)/shard_map/ppermute | solution.py:573
  75.4 10.8 %collective-permute-start.13 = (f32[768,128]{1,0:T(8,128)S(1)}, f32[768,128]{1,0:T(8,128)S(1)}, u32[]{:S(2)}, u32[]{:S(2)}) collective-permute-start(f32[768,128]{1,0:T(8,128)S(1)} %early.1.refs_0_), channel_id=1, source_target_pairs={{0,2},{1,3},{2,0},{3,1},{4,6},{5,7},{6,4},{7,5},{8,10},{9,11},{10,... | collective-permute-start | bytes 1179656 | tf_op jit(solution)/shard_map/ppermute | solution.py:853
  76.6 7.5 %collective-permute-start.14 = (f32[2,16,128]{2,1,0:T(8,128)S(1)}, f32[2,16,128]{2,1,0:T(8,128)S(1)}, u32[]{:S(2)}, u32[]{:S(2)}) collective-permute-start(f32[2,16,128]{2,1,0:T(8,128)S(1)} %get-tuple-element.85), channel_id=1, source_target_pairs={{0,4},{4,8},{8,12},{12,16},{16,20},{20,24},{24,28},{1,5},{5,9},{9,... | collective-permute-start | bytes 49160 | tf_op jit(solution)/shard_map/ppermute | solution.py:589
  80.8 5.4 %collective-permute-start.15 = (f32[2,16,128]{2,1,0:T(8,128)S(1)}, f32[2,16,128]{2,1,0:T(8,128)S(1)}, u32[]{:S(2)}, u32[]{:S(2)}) collective-permute-start(f32[2,16,128]{2,1,0:T(8,128)S(1)} %get-tuple-element.86), channel_id=1, source_target_pairs={{4,0},{8,4},{12,8},{16,12},{20,16},{24,20},{28,24},{5,1},{9,5},{13... | collective-permute-start | bytes 49160 | tf_op jit(solution)/shard_map/ppermute | solution.py:589
  86.2 14.9 %collective-permute-start.16 = (f32[768,128]{1,0:T(8,128)S(1)}, f32[768,128]{1,0:T(8,128)S(1)}, u32[]{:S(2)}, u32[]{:S(2)}) collective-permute-start(f32[768,128]{1,0:T(8,128)S(1)} %early.1.refs_0_), channel_id=1, source_target_pairs={{0,1},{1,0},{2,3},{3,2},{4,5},{5,4},{6,7},{7,6},{8,9},{9,8},{10,11... | collective-permute-start | bytes 1179656 | tf_op jit(solution)/shard_map/ppermute | solution.py:862
  93.4 7.7 %collective-permute-start.17 = (f32[768,128]{1,0:T(8,128)S(1)}, f32[768,128]{1,0:T(8,128)S(1)}, u32[]{:S(2)}, u32[]{:S(2)}) collective-permute-start(f32[768,128]{1,0:T(8,128)S(1)} %collective-permute-done.13.refs_1_), channel_id=1, source_target_pairs={{0,1},{1,0},{2,3},{3,2},{4,5},{5,4},{6,7},{7,6},{8,9},{9,8},{10,11... | collective-permute-start | bytes 1179656 | tf_op jit(solution)/shard_map/ppermute | solution.py:862
  97.0 6.2 %collective-permute-start.20 = (f32[192,128]{1,0:T(8,128)S(1)}, f32[192,128]{1,0:T(8,128)S(1)}, u32[]{:S(2)}, u32[]{:S(2)}) collective-permute-start(f32[192,128]{1,0:T(8,128)S(1)} %fifth.1.refs_4_), channel_id=1, source_target_pairs={{0,3},{1,2},{2,1},{3,0},{4,7},{5,6},{6,5},{7,4},{8,11},{9,10},{10,... | collective-permute-start | bytes 294920 | tf_op jit(solution)/shard_map/ppermute | solution.py:872
  97.7 5.5 %collective-permute-start.19 = (f32[192,128]{1,0:T(8,128)S(1)}, f32[192,128]{1,0:T(8,128)}, u32[]{:S(2)}, u32[]{:S(2)}) collective-permute-start(f32[192,128]{1,0:T(8,128)S(1)} %fifth.1.refs_4_), channel_id=1, source_target_pairs={{0,1},{1,0},{2,3},{3,2},{4,5},{5,4},{6,7},{7,6},{8,9},{9,8},{10,11... | collective-permute-start | bytes 294920 | tf_op jit(solution)/shard_map/ppermute | solution.py:872
  97.7 6.6 %collective-permute-start.18 = (f32[192,128]{1,0:T(8,128)S(1)}, f32[192,128]{1,0:T(8,128)}, u32[]{:S(2)}, u32[]{:S(2)}) collective-permute-start(f32[192,128]{1,0:T(8,128)S(1)} %fifth.1.refs_4_), channel_id=1, source_target_pairs={{0,2},{1,3},{2,0},{3,1},{4,6},{5,7},{6,4},{7,5},{8,10},{9,11},{10,... | collective-permute-start | bytes 294920 | tf_op jit(solution)/shard_map/ppermute | solution.py:872

commit v8 on v7

--- a/solution.py
+++ b/solution.py
@@ -63,15 +63,17 @@
     return jnp.concatenate(out, axis=0)
 
 
-def flatten(block, write):
+def flatten(block):
     lane = lax.broadcasted_iota(jnp.int32, (8, LANES), 1)
+    out = []
     for h in range(BS // 32):
         one, two, three, four = (block[32 * h + 8 * j : 32 * h + 8 * j + 8] for j in range(4))
         two = pltpu.roll(two, 96, 1)
         three = pltpu.roll(three, 64, 1)
-        write(24 * h, jnp.where(lane < BS, one, two))
-        write(24 * h + 1, jnp.where(lane < 64, two, three))
-        write(24 * h + 2, jnp.where(lane < 32, three, pltpu.roll(four, 32, 1)))
+        out.append(jnp.where(lane < BS, one, two))
+        out.append(jnp.where(lane < 64, two, three))
+        out.append(jnp.where(lane < 32, three, pltpu.roll(four, 32, 1)))
+    return out
 
 
 def make_operator(weights, gram_ref):
@@ -530,8 +532,8 @@
 
 
 def grad_kernel(*refs):
-    peers = (len(refs) - 3) // 2
-    early, late, mixed_ref, weights_ref, grad_ref = refs[:peers], refs[peers : 2 * peers], *refs[-3:]
+    peers = (len(refs) - 4) // 2
+    early, late, mixed_ref, weights_ref, grad_ref, turn_ref = refs[:peers], refs[peers : 2 * peers], *refs[-4:]
     first = pl.program_id(0) * WIDE
     upper = lax.broadcasted_iota(jnp.int32, (8, LANES), 0) < LATE
 
@@ -552,11 +554,13 @@
         left = jnp.concatenate(resid + zeta, axis=0)
         right = jnp.concatenate(zeta + resid, axis=0)
         grad = product(weights_ref[i], mixed_ref[n] + product(left, right, 0), 1)
-
-        def write(q, value):
-            grad_ref[pl.ds(i // 8 * (8 * CUTS) + 8 * q + i % 8, 8, stride=24), :] = value
-
-        flatten(grad, write)
+        for t, tile in enumerate(flatten(grad)):
+            turn_ref[i * CUTS + 8 * t : i * CUTS + 8 * t + 8, :] = tile
+        if i % 8 == 7:
+            for q in range(CUTS):
+                start = (i - 7) * CUTS + 8 * (3 * (q // 24) + q % 3) + q % 24 // 3
+                at = i // 8 * (8 * CUTS) + 8 * q
+                grad_ref[at : at + 8, :] = turn_ref[pl.ds(start, 8, stride=CUTS), :]
 
 
 def widening(parts, axis, step, most):
@@ -792,9 +796,6 @@
         stats, waiting = [stats + partner], 2
     else:
         stats, waiting = [stats], 0
-    stats, near, far, ops = lax.optimization_barrier((stats, near, far, ops))
-    while waiting is not None and waiting < size:
-        stats, waiting = widening(stats, "sub", waiting, 4)
     blocks, halo_list = call(
         blocks_kernel, "blocks", [columns], [stiff_cuts],
         [shape(NBLK, K, BS, LANES), jax.ShapeDtypeStruct((1, NBLK * K + 8), jnp.int32)],
@@ -802,11 +803,15 @@
         [smem(), pl.BlockSpec((CHUNK * CUTS * K, LANES), lambda g: (g, 0))],
     )
 
+    near, far, blocks, stats = lax.optimization_barrier((near, far, blocks, stats))
     zero, a1, a2, up, down = call(
         first_kernel, "first", [columns, halo_list, send_rows, counts], [blocks, ops, base, near, far],
         [shape(2 * count, ROWS, LANES), rows, rows, longer, longer],
         [partial(count), held(count)], 6,
     )
+    stats, a2 = lax.optimization_barrier((stats, a2))
+    while waiting is not None and waiting < size:
+        stats, waiting = widening(stats, "sub", waiting, 4)
     low, high = exchange(up, down)
     stats = jnp.stack(stats)
 
@@ -877,7 +882,8 @@
         mixed_kernel, "mixed", [], [*early, weight_cuts], [shape(NBLK, LANES, LANES), shape(NBLK, BS, LANES)], [], 3
     )
     (grad,) = call(
-        grad_kernel, "grad", [], [*early, *late, mixed, weights], [shape(NBLK * CUTS, LANES)], [], 10,
+        grad_kernel, "grad", [], [*early, *late, mixed, weights], [shape(NBLK * CUTS, LANES)],
+        [pltpu.VMEM((WIDE * CUTS, LANES), f32)], 10,
         [pl.BlockSpec((WIDE * CUTS, LANES), lambda g: (g, 0))], (NBLK // WIDE,),
         [vmem()] * (len(early) + len(late) + 1) + [pl.BlockSpec((WIDE, BS, LANES), lambda g: (g, 0, 0))],
     )

time: 115 us -> 110 us (0.957)
  waiting for transfers between devices: 11 us -> 6.57 us
    ppermute x8, waiting for transfers between devices: 9.89 us -> 5.43 us  [exchange(): return (lax.ppermute(up, 'sub', rising), lax.ppermute(down, 'sub', falling))]
  transfers between devices with their start and end apart: 21 -> 21, of which waited for: 4 -> 3; matrix products, arithmetic and copies ran while one was open for 2% -> 2% of each run, Pallas kernels for 28% -> 24%
where the time goes in v8:
time: 110 us
  Pallas kernels  54.7 us (50%)
  starting transfers between devices  39.3 us (36%)
  local copies, waits for them, and re-layouts  6.64 us (6%)
  waiting for transfers between devices  6.57 us (6%)
  between operations  1.68 us (2%)
    pallas_call x15, Pallas kernels, call(): pl.pallas_call(kernel, grid=grid, in_specs=in_specs or [smem()] * len(sca...  54.7 us
    ppermute x8, starting transfers between devices, exchange(): return (lax.ppermute(up, 'sub', rising), lax.ppermute(down, 'sub', falling))  23.6 us
    ppermute x2, starting transfers between devices, shards(): lax.ppermute(part, 'rhs', [(i, i ^ 1) for i in range(size)])  6.9 us
    ppermute x7, starting transfers between devices, widening(): lax.ppermute(total, axis, [(i, i ^ d * step) for i in range(size)])  5.56 us
    ppermute x8, waiting for transfers between devices, exchange(): return (lax.ppermute(up, 'sub', rising), lax.ppermute(down, 'sub', falling))  5.43 us
    unnamed x8, local copies, waits for them, and re-layouts  3.02 us
  transfers between devices with their start and end apart: 21, of which 3 were waited for; matrix products, arithmetic and copies ran while one was open for 2% of the time, Pallas kernels for 24%

profile of v8, /device:TPU:13, one launch (start us, length us, event | category | flops | bytes accessed | tf_op | source)
XLA Modules:
  0.0 109.9 jit_solution(7996651333606163085)
XLA Ops:
  0.7 1.0 pad_maximum_fusion
  1.6 0.1 reshape.35
  1.7 1.4 %slice.24 = f32[8,72,4,128]{3,2,1,0:T(4,128)S(1)} slice(f32[48,72,4,128]{3,2,1,0:T(4,128)} %bitcast.28), slice={[0:8], [0:72], [0:4], [0:128]} | slice | bytes 2359296 | tf_op jit(solution)/shard_map/slice | solution.py:785
  3.1 2.3 %pack.1 = (f32[6,80,128]{2,1,0:T(8,128)S(1)}, f32[6,80,128]{2,1,0:T(8,128)S(1)}) custom-call(s32[1,12]{1,0:T(1,128)S(1)} %copy-done.3, f32[3456,128]{1,0:T(8,128)S(1)} %bitcast.25, f32[2304,128]{1,0:T(8,128)S(1)} %bitcast.30, f32[4,64,128]{2,1,0:T(8,128)S(1)} %pad.4.base_ref), custom_call_target="tpu_custom_call" | custom-call | flops 1048576 | bytes 9600000 | tf_op jit(solution)/shard_map/pack/pallas_call | solution.py:763
  5.4 0.0 copy-start.2
  5.4 2.1 %collective-permute-start.1 = (f32[6,80,128]{2,1,0:T(8,128)S(1)}, f32[6,80,128]{2,1,0:T(8,128)S(1)}, u32[]{:S(2)}, u32[]{:S(2)}) collective-permute-start(f32[6,80,128]{2,1,0:T(8,128)S(1)} %get-tuple-element.53), channel_id=1, source_target_pairs={{4,0},{8,4},{12,8},{16,12},{20,16},{24,20},{28,24},{5,1},{9,5},{13... | collective-permute-start | bytes 737288 | tf_op jit(solution)/shard_map/ppermute | solution.py:593
  7.6 4.0 %collective-permute-start = (f32[6,80,128]{2,1,0:T(8,128)S(1)}, f32[6,80,128]{2,1,0:T(8,128)S(1)}, u32[]{:S(2)}, u32[]{:S(2)}) collective-permute-start(f32[6,80,128]{2,1,0:T(8,128)S(1)} %get-tuple-element.52), channel_id=1, source_target_pairs={{0,4},{4,8},{8,12},{12,16},{16,20},{20,24},{24,28},{1,5},{5,9},{9,... | collective-permute-start | bytes 737288 | tf_op jit(solution)/shard_map/ppermute | solution.py:593
  12.3 4.2 %operators.1.op_ref.ops_ref = f32[48,96,128]{2,1,0:T(8,128)S(1)} custom-call(f32[3456,128]{1,0:T(8,128)S(1)} %bitcast.26), custom_call_target="tpu_custom_call" | custom-call | flops 1048576 | bytes 12800000 | tf_op jit(solution)/shard_map/operators/pallas_call | solution.py:763
  16.5 0.0 copy-start.1
  16.5 3.0 %copy-done.1 = f32[48,4,9216]{2,1,0:T(4,128)S(1)} copy-done((f32[48,4,9216]{2,1,0:T(4,128)S(1)}, f32[48,4,9216]{2,1,0:T(4,128)}, u32[]{:S(2)}) %copy-start.1) | copy-done | bytes 7077912
  19.5 4.9 %blocks.1 = (f32[48,4,96,128]{3,2,1,0:T(8,128)S(1)}, s32[1,200]{1,0:T(1,128)S(1)}) custom-call(s32[4,48]{1,0:T(4,128)S(1)} %bitcast.31, f32[13824,128]{1,0:T(8,128)S(1)} %bitcast.29), custom_call_target="tpu_custom_call" | custom-call | flops 1048576 | bytes 16000000 | tf_op jit(solution)/shard_map/blocks/pallas_call | solution.py:763
  24.4 0.0 collective-permute-done.1.high_ref
  24.4 0.0 collective-permute-done.low_ref
  24.4 5.0 %first.1 = (f32[4,64,128]{2,1,0:T(8,128)S(1)}, f32[2,64,128]{2,1,0:T(8,128)S(1)}, f32[2,64,128]{2,1,0:T(8,128)S(1)}, f32[2,24,128]{2,1,0:T(8,128)S(1)}, f32[2,24,128]{2,1,0:T(8,128)S(1)}) custom-call(s32[4,48]{1,0:T(4,128)S(1)} %bitcast.32, s32[1,200]{1,0:T(1,128)S(1)} %get-tuple-element.56.list_ref, s32[1,12]{1,0:T(1,128)S(1)} %copy-done.3, ...), custom_call_target="tpu_custom_call" | custom-call | flops 1048576 | bytes 19200000 | tf_op jit(solution)/shard_map/first/pallas_call | solution.py:763
  29.4 1.4 %collective-permute-start.6 = (f32[2,128]{1,0:T(2,128)S(1)}, f32[2,128]{1,0:T(2,128)S(1)}, u32[]{:S(2)}, u32[]{:S(2)}) collective-permute-start(f32[2,128]{1,0:T(2,128)S(1)} %fusion.1), channel_id=1, source_target_pairs={{0,24},{4,28},{8,16},{12,20},{16,8},{20,12},{24,0},{28,4},{1,25},{... | collective-permute-start | bytes 3080 | tf_op jit(solution)/shard_map/ppermute | solution.py:577
  30.8 1.0 collective-permute-start.5
  31.8 0.4 collective-permute-start.4
  32.2 0.1 add_convert_fusion.edge_ref
  32.2 3.0 %collective-permute-start.2 = (f32[2,24,128]{2,1,0:T(8,128)S(1)}, f32[2,24,128]{2,1,0:T(8,128)S(1)}, u32[]{:S(2)}, u32[]{:S(2)}) collective-permute-start(f32[2,24,128]{2,1,0:T(8,128)S(1)} %get-tuple-element.67), channel_id=1, source_target_pairs={{0,4},{4,8},{8,12},{12,16},{16,20},{20,24},{24,28},{1,5},{5,9},{9,... | collective-permute-start | bytes 73736 | tf_op jit(solution)/shard_map/ppermute | solution.py:593
  35.2 2.3 %collective-permute-start.3 = (f32[2,24,128]{2,1,0:T(8,128)S(1)}, f32[2,24,128]{2,1,0:T(8,128)S(1)}, u32[]{:S(2)}, u32[]{:S(2)}) collective-permute-start(f32[2,24,128]{2,1,0:T(8,128)S(1)} %get-tuple-element.68), channel_id=1, source_target_pairs={{4,0},{8,4},{12,8},{16,12},{20,16},{24,20},{28,24},{5,1},{9,5},{13... | collective-permute-start | bytes 73736 | tf_op jit(solution)/shard_map/ppermute | solution.py:593
  37.5 3.2 %ghosts.1 = (f32[12,96,128]{2,1,0:T(8,128)S(1)}, f32[2,64,128]{2,1,0:T(8,128)S(1)}, f32[2,64,128]{2,1,0:T(8,128)S(1)}) custom-call(f32[48,96,128]{2,1,0:T(8,128)S(1)} %operators.1.op_ref.ops_ref, f32[4,64,128]{2,1,0:T(8,128)S(1)} %get-tuple-element.77.zero_ref, f32[2,64,128]{2,1,0:T(8,128)S(1)} %get-tuple-element.60.a1_ref, ...), custom_call_target="tpu_custom_call" | custom-call | flops 1048576 | bytes 9600000 | tf_op jit(solution)/shard_map/ghosts/pallas_call | solution.py:763
  40.8 0.0 collective-permute-done.6
  40.8 0.0 collective-permute-done.5
  40.8 0.0 collective-permute-done.4
  40.8 0.0 collective-permute-done.2.low_ref
  40.8 0.0 collective-permute-done.3.high_ref
  40.8 6.4 %second.1 = (f32[2,64,128]{2,1,0:T(8,128)S(1)}, f32[2,64,128]{2,1,0:T(8,128)S(1)}, f32[2,64,128]{2,1,0:T(8,128)S(1)}, f32[2,64,128]{2,1,0:T(8,128)S(1)}, f32[2,6...) custom-call(s32[4,48]{1,0:T(4,128)S(1)} %bitcast.33, ...), custom_call_target="tpu_custom_call" | custom-call | flops 1048576 | bytes 22400000 | tf_op jit(solution)/shard_map/second/pallas_call | solution.py:763
  47.3 3.9 %collective-permute-start.7 = (f32[2,16,128]{2,1,0:T(8,128)S(1)}, f32[2,16,128]{2,1,0:T(8,128)S(1)}, u32[]{:S(2)}, u32[]{:S(2)}) collective-permute-start(f32[2,16,128]{2,1,0:T(8,128)S(1)} %get-tuple-element.73), channel_id=1, source_target_pairs={{0,4},{4,8},{8,12},{12,16},{16,20},{20,24},{24,28},{1,5},{5,9},{9,... | collective-permute-start | bytes 49160 | tf_op jit(solution)/shard_map/ppermute | solution.py:593
  51.2 1.9 %collective-permute-start.8 = (f32[2,16,128]{2,1,0:T(8,128)S(1)}, f32[2,16,128]{2,1,0:T(8,128)S(1)}, u32[]{:S(2)}, u32[]{:S(2)}) collective-permute-start(f32[2,16,128]{2,1,0:T(8,128)S(1)} %get-tuple-element.74), channel_id=1, source_target_pairs={{4,0},{8,4},{12,8},{16,12},{20,16},{24,20},{28,24},{5,1},{9,5},{13... | collective-permute-start | bytes 49160 | tf_op jit(solution)/shard_map/ppermute | solution.py:593
  53.1 0.0 collective-permute-done.7.low_ref
  53.1 3.4 %collective-permute-done.8.high_ref = f32[2,16,128]{2,1,0:T(8,128)S(1)} collective-permute-done((f32[2,16,128]{2,1,0:T(8,128)S(1)}, f32[2,16,128]{2,1,0:T(8,128)S(1)}, u32[]{:S(2)}, u32[]{:S(2)}) %collective-permute-start.8) | collective-permute-done | bytes 16416 | tf_op jit(solution)/shard_map/ppermute | solution.py:593
  56.5 0.8 moments.1
  57.3 0.1 collective-permute-start.9
  57.4 3.4 %target.1.refs_5_ = f32[2,64,128]{2,1,0:T(8,128)S(1)} custom-call(s32[4,48]{1,0:T(4,128)S(1)} %bitcast.34, s32[1,200]{1,0:T(1,128)S(1)} %get-tuple-element.56.list_ref, f32[48,4,96,128]{3,2,1,0:T(8,128)S(1)} %get-tuple-element.55.blocks, f32[48,96,128]{2,1,0:T(8,128)S(1)} %operators.1.op_ref.ops_ref, f32[12,96,128]{2,1,0:T(8,128)S(1)} %get-tuple-element.61.gop_ref, ...), custom_call_target="tpu_custom_call" | custom-call | flops 1048576 | bytes 9600000 | tf_op jit(solution)/shard_map/target/pallas_call | solution.py:763
  60.8 0.0 collective-permute-done.9
  60.9 1.5 %collective-permute-start.12 = (f32[8,128]{1,0:T(8,128)S(1)}, f32[8,128]{1,0:T(8,128)S(1)}, u32[]{:S(2)}, u32[]{:S(2)}) collective-permute-start(f32[8,128]{1,0:T(8,128)S(1)} %add.22.refs_6_), channel_id=1, source_target_pairs={{0,24},{4,28},{8,16},{12,20},{16,8},{20,12},{24,0},{28,4},{1,25},{... | collective-permute-start | bytes 12296 | tf_op jit(solution)/shard_map/ppermute | solution.py:577
  62.4 0.9 collective-permute-start.11
  63.3 0.3 collective-permute-start.10
  63.6 3.4 %third.1.refs_4_ = f32[2,64,128]{2,1,0:T(8,128)S(1)} custom-call(s32[4,48]{1,0:T(4,128)S(1)} %bitcast.35, s32[1,200]{1,0:T(1,128)S(1)} %get-tuple-element.56.list_ref, f32[48,4,96,128]{3,2,1,0:T(8,128)S(1)} %get-tuple-element.55.blocks, f32[48,96,128]{2,1,0:T(8,128)S(1)} %operators.1.op_ref.ops_ref, f32[12,96,128]{2,1,0:T(8,128)S(1)} %get-tuple-element.61.gop_ref, ...), custom_call_target="tpu_custom_call" | custom-call | flops 1048576 | bytes 12800000 | tf_op jit(solution)/shard_map/third/pallas_call | solution.py:763
  67.1 0.0 collective-permute-done.12.refs_9_
  67.1 0.0 collective-permute-done.11.refs_8_
  67.1 0.0 collective-permute-done.10.refs_7_
  67.1 3.3 %fourth.1 = (f32[2,64,128]{2,1,0:T(8,128)}, f32[2,64,128]{2,1,0:T(8,128)S(1)}, f32[2,64,128]{2,1,0:T(8,128)S(1)}, f32[10,8,8,128]{3,2,1,0:T(8,128)S(1)}, f32[3,8...) custom-call(s32[4,48]{1,0:T(4,128)S(1)} %bitcast.36, s32[1,12]{1,0:T(1,128)S(1)} %copy-done.3, ...), custom_call_target="tpu_custom_call" | custom-call | flops 1048576 | bytes 9600000 | tf_op jit(solution)/shard_map/fourth/pallas_call | solution.py:763
  70.4 0.2 early.1.refs_0_
  70.6 1.3 %collective-permute-start.13 = (f32[768,128]{1,0:T(8,128)S(1)}, f32[768,128]{1,0:T(8,128)S(1)}, u32[]{:S(2)}, u32[]{:S(2)}) collective-permute-start(f32[768,128]{1,0:T(8,128)S(1)} %early.1.refs_0_), channel_id=1, source_target_pairs={{0,2},{1,3},{2,0},{3,1},{4,6},{5,7},{6,4},{7,5},{8,10},{9,11},{10,... | collective-permute-start | bytes 1179656 | tf_op jit(solution)/shard_map/ppermute | solution.py:858
  71.9 4.5 %collective-permute-start.14 = (f32[2,16,128]{2,1,0:T(8,128)S(1)}, f32[2,16,128]{2,1,0:T(8,128)S(1)}, u32[]{:S(2)}, u32[]{:S(2)}) collective-permute-start(f32[2,16,128]{2,1,0:T(8,128)S(1)} %get-tuple-element.89), channel_id=1, source_target_pairs={{0,4},{4,8},{8,12},{12,16},{16,20},{20,24},{24,28},{1,5},{5,9},{9,... | collective-permute-start | bytes 49160 | tf_op jit(solution)/shard_map/ppermute | solution.py:593
  76.3 1.9 %collective-permute-start.15 = (f32[2,16,128]{2,1,0:T(8,128)S(1)}, f32[2,16,128]{2,1,0:T(8,128)S(1)}, u32[]{:S(2)}, u32[]{:S(2)}) collective-permute-start(f32[2,16,128]{2,1,0:T(8,128)S(1)} %get-tuple-element.90), channel_id=1, source_target_pairs={{4,0},{8,4},{12,8},{16,12},{20,16},{24,20},{28,24},{5,1},{9,5},{13... | collective-permute-start | bytes 49160 | tf_op jit(solution)/shard_map/ppermute | solution.py:593
  78.3 1.5 %answer.1 = (f32[2,2,64,128]{3,2,1,0:T(8,128)S(1)}, f32[2,64,128]{2,1,0:T(8,128)S(1)}) custom-call(f32[48,96,128]{2,1,0:T(8,128)S(1)} %operators.1.op_ref.ops_ref, f32[10,8,8,128]{3,2,1,0:T(8,128)S(1)} %get-tuple-element.87.coef_ref, f32[4,64,128]{2,1,0:T(8,128)S(1)} %get-tuple-element.77.zero_ref, f32[2,64,128]{2,1,0:T(8,128)S(1)} %get-tuple-element.78.refs_0_, ...), custom_call_target="tpu_custom_call" | custom-call | flops 1048576 | bytes 4800000 | tf_op jit(solution)/shard_map/answer/pallas_call | solution.py:763
  79.7 0.0 collective-permute-done.14.low_ref
  79.8 2.0 %collective-permute-done.15.high_ref = f32[2,16,128]{2,1,0:T(8,128)S(1)} collective-permute-done((f32[2,16,128]{2,1,0:T(8,128)S(1)}, f32[2,16,128]{2,1,0:T(8,128)S(1)}, u32[]{:S(2)}, u32[]{:S(2)}) %collective-permute-start.15) | collective-permute-done | bytes 16416 | tf_op jit(solution)/shard_map/ppermute | solution.py:593
  81.7 0.0 collective-permute-done.13.refs_1_
  81.7 6.9 %collective-permute-start.16 = (f32[768,128]{1,0:T(8,128)S(1)}, f32[768,128]{1,0:T(8,128)S(1)}, u32[]{:S(2)}, u32[]{:S(2)}) collective-permute-start(f32[768,128]{1,0:T(8,128)S(1)} %early.1.refs_0_), channel_id=1, source_target_pairs={{0,1},{1,0},{2,3},{3,2},{4,5},{5,4},{6,7},{7,6},{8,9},{9,8},{10,11... | collective-permute-start | bytes 1179656 | tf_op jit(solution)/shard_map/ppermute | solution.py:867
  88.6 0.0 collective-permute-start.17
  88.6 3.5 %fifth.1.refs_4_ = f32[192,128]{1,0:T(8,128)S(1)} custom-call(s32[4,48]{1,0:T(4,128)S(1)} %bitcast.37, s32[1,200]{1,0:T(1,128)S(1)} %get-tuple-element.56.list_ref, s32[1,12]{1,0:T(1,128)S(1)} %copy-done.3, s32[2]{0:T(128)S(1)} %add_convert_fusion.edge_ref, f32[48,4,96,128]{3,2,1,0:T(8,128)S(1)} %get-tuple-element.55.blocks, ...), custom_call_target="tpu_custom_call" | custom-call | flops 1048576 | bytes 12800000 | tf_op jit(solution)/shard_map/fifth/pallas_call | solution.py:763
  92.2 0.7 collective-permute-start.20
  92.9 0.0 collective-permute-start.19
  92.9 1.2 %collective-permute-start.18 = (f32[192,128]{1,0:T(8,128)S(1)}, f32[192,128]{1,0:T(8,128)}, u32[]{:S(2)}, u32[]{:S(2)}) collective-permute-start(f32[192,128]{1,0:T(8,128)S(1)} %fifth.1.refs_4_), channel_id=1, source_target_pairs={{0,2},{1,3},{2,0},{3,1},{4,6},{5,7},{6,4},{7,5},{8,10},{9,11},{10,... | collective-permute-start | bytes 294920 | tf_op jit(solution)/shard_map/ppermute | solution.py:877
  94.1 0.6 slice.23
  94.7 1.5 %reshape.37 = f32[2,4608]{1,0:T(2,128)} reshape(f32[2,48,96]{2,1,0:T(8,128)} %slice.23) | data formatting | bytes 73728 | tf_op jit(solution)/shard_map/reshape | solution.py:891
  96.2 0.0 collective-permute-done.17.refs_3_
  96.2 2.1 %mixed.1 = (f32[48,128,128]{2,1,0:T(8,128)S(1)}, f32[48,96,128]{2,1,0:T(8,128)S(1)}) custom-call(f32[768,128]{1,0:T(8,128)S(1)} %early.1.refs_0_, f32[768,128]{1,0:T(8,128)S(1)} %collective-permute-done.13.refs_1_, f32[768,128]{1,0:T(8,128)S(1)} %collective-permute-done.16.refs_2_, f32[768,128]{1,0:T(8,128)S(1)} %collective-permute-done.17.refs_3_, ...), custom_call_target="tpu_custom_call" | custom-call | flops 1048576 | bytes 9600000 | tf_op jit(solution)/shard_map/mixed/pallas_call | solution.py:763
  98.3 0.0 collective-permute-done.20.refs_7_
  98.4 1.1 collective-permute-done.18.refs_5_
  99.4 10.5 %grad.1 = f32[3456,128]{1,0:T(8,128)} custom-call(f32[768,128]{1,0:T(8,128)S(1)} %early.1.refs_0_, f32[768,128]{1,0:T(8,128)S(1)} %collective-permute-done.13.refs_1_, f32[768,128]{1,0:T(8,128)S(1)} %collective-permute-done.16.refs_2_, f32[768,128]{1,0:T(8,128)S(1)} %collective-permute-done.17.refs_3_, f32[192,128]{1,0:T(8,128)S(1)} %fifth.1.refs_4_, ...), custom_call_target="tpu_custom_call" | custom-call | flops 1048576 | bytes 32000000 | tf_op jit(solution)/shard_map/grad/pallas_call | solution.py:763
  (11 shorter events, 0.0 us)
Async XLA Ops:
  0.6 2.5 %copy-start.3 = (s32[1,12]{1,0:T(1,128)S(1)}, s32[1,12]{1,0:T(1,128)}, u32[]{:S(2)}) copy-start(s32[1,12]{1,0:T(1,128)} %send_ref.11) | copy-start | bytes 148
  0.6 2.5 %copy-start = (f32[48,9216]{1,0:T(8,128)S(1)}, f32[48,9216]{1,0:T(8,128)}, u32[]{:S(2)}) copy-start(f32[48,9216]{1,0:T(8,128)} %param.8) | copy-start | bytes 5308420
  5.4 11.1 %copy-start.2 = (s32[48,4]{0,1:T(4,128)S(1)}, s32[48,4]{0,1:T(4,128)}, u32[]{:S(2)}) copy-start(s32[48,4]{0,1:T(4,128)} %param.11) | copy-start | bytes 2308
  5.4 19.0 %collective-permute-start.1 = (f32[6,80,128]{2,1,0:T(8,128)S(1)}, f32[6,80,128]{2,1,0:T(8,128)S(1)}, u32[]{:S(2)}, u32[]{:S(2)}) collective-permute-start(f32[6,80,128]{2,1,0:T(8,128)S(1)} %get-tuple-element.53), channel_id=1, source_target_pairs={{4,0},{8,4},{12,8},{16,12},{20,16},{24,20},{28,24},{5,1},{9,5},{13... | collective-permute-start | bytes 737288 | tf_op jit(solution)/shard_map/ppermute | solution.py:593
  7.6 16.9 %collective-permute-start = (f32[6,80,128]{2,1,0:T(8,128)S(1)}, f32[6,80,128]{2,1,0:T(8,128)S(1)}, u32[]{:S(2)}, u32[]{:S(2)}) collective-permute-start(f32[6,80,128]{2,1,0:T(8,128)S(1)} %get-tuple-element.52), channel_id=1, source_target_pairs={{0,4},{4,8},{8,12},{12,16},{16,20},{20,24},{24,28},{1,5},{5,9},{9,... | collective-permute-start | bytes 737288 | tf_op jit(solution)/shard_map/ppermute | solution.py:593
  16.5 3.0 %copy-start.1 = (f32[48,4,9216]{2,1,0:T(4,128)S(1)}, f32[48,4,9216]{2,1,0:T(4,128)}, u32[]{:S(2)}) copy-start(f32[48,4,9216]{2,1,0:T(4,128)} %param.7) | copy-start | bytes 21233668
  29.4 11.3 %collective-permute-start.6 = (f32[2,128]{1,0:T(2,128)S(1)}, f32[2,128]{1,0:T(2,128)S(1)}, u32[]{:S(2)}, u32[]{:S(2)}) collective-permute-start(f32[2,128]{1,0:T(2,128)S(1)} %fusion.1), channel_id=1, source_target_pairs={{0,24},{4,28},{8,16},{12,20},{16,8},{20,12},{24,0},{28,4},{1,25},{... | collective-permute-start | bytes 3080 | tf_op jit(solution)/shard_map/ppermute | solution.py:577
  30.8 10.0 %collective-permute-start.5 = (f32[2,128]{1,0:T(2,128)S(1)}, f32[2,128]{1,0:T(2,128)S(1)}, u32[]{:S(2)}, u32[]{:S(2)}) collective-permute-start(f32[2,128]{1,0:T(2,128)S(1)} %fusion.1), channel_id=1, source_target_pairs={{0,16},{4,20},{8,24},{12,28},{16,0},{20,4},{24,8},{28,12},{1,17},{... | collective-permute-start | bytes 3080 | tf_op jit(solution)/shard_map/ppermute | solution.py:577
  31.8 9.0 %collective-permute-start.4 = (f32[2,128]{1,0:T(2,128)S(1)}, f32[2,128]{1,0:T(2,128)S(1)}, u32[]{:S(2)}, u32[]{:S(2)}) collective-permute-start(f32[2,128]{1,0:T(2,128)S(1)} %fusion.1), channel_id=1, source_target_pairs={{0,8},{4,12},{8,0},{12,4},{16,24},{20,28},{24,16},{28,20},{1,9},{5... | collective-permute-start | bytes 3080 | tf_op jit(solution)/shard_map/ppermute | solution.py:577
  32.2 8.6 %collective-permute-start.2 = (f32[2,24,128]{2,1,0:T(8,128)S(1)}, f32[2,24,128]{2,1,0:T(8,128)S(1)}, u32[]{:S(2)}, u32[]{:S(2)}) collective-permute-start(f32[2,24,128]{2,1,0:T(8,128)S(1)} %get-tuple-element.67), channel_id=1, source_target_pairs={{0,4},{4,8},{8,12},{12,16},{16,20},{20,24},{24,28},{1,5},{5,9},{9,... | collective-permute-start | bytes 73736 | tf_op jit(solution)/shard_map/ppermute | solution.py:593
  35.2 5.6 %collective-permute-start.3 = (f32[2,24,128]{2,1,0:T(8,128)S(1)}, f32[2,24,128]{2,1,0:T(8,128)S(1)}, u32[]{:S(2)}, u32[]{:S(2)}) collective-permute-start(f32[2,24,128]{2,1,0:T(8,128)S(1)} %get-tuple-element.68), channel_id=1, source_target_pairs={{4,0},{8,4},{12,8},{16,12},{20,16},{24,20},{28,24},{5,1},{9,5},{13... | collective-permute-start | bytes 73736 | tf_op jit(solution)/shard_map/ppermute | solution.py:593
  47.3 5.8 %collective-permute-start.7 = (f32[2,16,128]{2,1,0:T(8,128)S(1)}, f32[2,16,128]{2,1,0:T(8,128)S(1)}, u32[]{:S(2)}, u32[]{:S(2)}) collective-permute-start(f32[2,16,128]{2,1,0:T(8,128)S(1)} %get-tuple-element.73), channel_id=1, source_target_pairs={{0,4},{4,8},{8,12},{12,16},{16,20},{20,24},{24,28},{1,5},{5,9},{9,... | collective-permute-start | bytes 49160 | tf_op jit(solution)/shard_map/ppermute | solution.py:593
  51.2 5.4 %collective-permute-start.8 = (f32[2,16,128]{2,1,0:T(8,128)S(1)}, f32[2,16,128]{2,1,0:T(8,128)S(1)}, u32[]{:S(2)}, u32[]{:S(2)}) collective-permute-start(f32[2,16,128]{2,1,0:T(8,128)S(1)} %get-tuple-element.74), channel_id=1, source_target_pairs={{4,0},{8,4},{12,8},{16,12},{20,16},{24,20},{28,24},{5,1},{9,5},{13... | collective-permute-start | bytes 49160 | tf_op jit(solution)/shard_map/ppermute | solution.py:593
  57.3 3.5 %collective-permute-start.9 = (f32[8,128]{1,0:T(8,128)S(1)}, f32[8,128]{1,0:T(8,128)S(1)}, u32[]{:S(2)}, u32[]{:S(2)}) collective-permute-start(f32[8,128]{1,0:T(8,128)S(1)} %get-tuple-element.85), channel_id=1, source_target_pairs={{0,4},{4,0},{8,12},{12,8},{16,20},{20,16},{24,28},{28,24},{1,5},{5... | collective-permute-start | bytes 12296 | tf_op jit(solution)/shard_map/ppermute | solution.py:577
  60.9 6.2 %collective-permute-start.12 = (f32[8,128]{1,0:T(8,128)S(1)}, f32[8,128]{1,0:T(8,128)S(1)}, u32[]{:S(2)}, u32[]{:S(2)}) collective-permute-start(f32[8,128]{1,0:T(8,128)S(1)} %add.22.refs_6_), channel_id=1, source_target_pairs={{0,24},{4,28},{8,16},{12,20},{16,8},{20,12},{24,0},{28,4},{1,25},{... | collective-permute-start | bytes 12296 | tf_op jit(solution)/shard_map/ppermute | solution.py:577
  62.4 4.7 %collective-permute-start.11 = (f32[8,128]{1,0:T(8,128)S(1)}, f32[8,128]{1,0:T(8,128)S(1)}, u32[]{:S(2)}, u32[]{:S(2)}) collective-permute-start(f32[8,128]{1,0:T(8,128)S(1)} %add.22.refs_6_), channel_id=1, source_target_pairs={{0,16},{4,20},{8,24},{12,28},{16,0},{20,4},{24,8},{28,12},{1,17},{... | collective-permute-start | bytes 12296 | tf_op jit(solution)/shard_map/ppermute | solution.py:577
  63.3 3.8 %collective-permute-start.10 = (f32[8,128]{1,0:T(8,128)S(1)}, f32[8,128]{1,0:T(8,128)S(1)}, u32[]{:S(2)}, u32[]{:S(2)}) collective-permute-start(f32[8,128]{1,0:T(8,128)S(1)} %add.22.refs_6_), channel_id=1, source_target_pairs={{0,8},{4,12},{8,0},{12,4},{16,24},{20,28},{24,16},{28,20},{1,9},{5... | collective-permute-start | bytes 12296 | tf_op jit(solution)/shard_map/ppermute | solution.py:577
  70.6 11.1 %collective-permute-start.13 = (f32[768,128]{1,0:T(8,128)S(1)}, f32[768,128]{1,0:T(8,128)S(1)}, u32[]{:S(2)}, u32[]{:S(2)}) collective-permute-start(f32[768,128]{1,0:T(8,128)S(1)} %early.1.refs_0_), channel_id=1, source_target_pairs={{0,2},{1,3},{2,0},{3,1},{4,6},{5,7},{6,4},{7,5},{8,10},{9,11},{10,... | collective-permute-start | bytes 1179656 | tf_op jit(solution)/shard_map/ppermute | solution.py:858
  71.9 7.9 %collective-permute-start.14 = (f32[2,16,128]{2,1,0:T(8,128)S(1)}, f32[2,16,128]{2,1,0:T(8,128)S(1)}, u32[]{:S(2)}, u32[]{:S(2)}) collective-permute-start(f32[2,16,128]{2,1,0:T(8,128)S(1)} %get-tuple-element.89), channel_id=1, source_target_pairs={{0,4},{4,8},{8,12},{12,16},{16,20},{20,24},{24,28},{1,5},{5,9},{9,... | collective-permute-start | bytes 49160 | tf_op jit(solution)/shard_map/ppermute | solution.py:593
  76.3 5.4 %collective-permute-start.15 = (f32[2,16,128]{2,1,0:T(8,128)S(1)}, f32[2,16,128]{2,1,0:T(8,128)S(1)}, u32[]{:S(2)}, u32[]{:S(2)}) collective-permute-start(f32[2,16,128]{2,1,0:T(8,128)S(1)} %get-tuple-element.90), channel_id=1, source_target_pairs={{4,0},{8,4},{12,8},{16,12},{20,16},{24,20},{28,24},{5,1},{9,5},{13... | collective-permute-start | bytes 49160 | tf_op jit(solution)/shard_map/ppermute | solution.py:593
  81.7 14.5 %collective-permute-start.16 = (f32[768,128]{1,0:T(8,128)S(1)}, f32[768,128]{1,0:T(8,128)S(1)}, u32[]{:S(2)}, u32[]{:S(2)}) collective-permute-start(f32[768,128]{1,0:T(8,128)S(1)} %early.1.refs_0_), channel_id=1, source_target_pairs={{0,1},{1,0},{2,3},{3,2},{4,5},{5,4},{6,7},{7,6},{8,9},{9,8},{10,11... | collective-permute-start | bytes 1179656 | tf_op jit(solution)/shard_map/ppermute | solution.py:867
  88.6 7.6 %collective-permute-start.17 = (f32[768,128]{1,0:T(8,128)S(1)}, f32[768,128]{1,0:T(8,128)S(1)}, u32[]{:S(2)}, u32[]{:S(2)}) collective-permute-start(f32[768,128]{1,0:T(8,128)S(1)} %collective-permute-done.13.refs_1_), channel_id=1, source_target_pairs={{0,1},{1,0},{2,3},{3,2},{4,5},{5,4},{6,7},{7,6},{8,9},{9,8},{10,11... | collective-permute-start | bytes 1179656 | tf_op jit(solution)/shard_map/ppermute | solution.py:867
  92.2 6.2 %collective-permute-start.20 = (f32[192,128]{1,0:T(8,128)S(1)}, f32[192,128]{1,0:T(8,128)S(1)}, u32[]{:S(2)}, u32[]{:S(2)}) collective-permute-start(f32[192,128]{1,0:T(8,128)S(1)} %fifth.1.refs_4_), channel_id=1, source_target_pairs={{0,3},{1,2},{2,1},{3,0},{4,7},{5,6},{6,5},{7,4},{8,11},{9,10},{10,... | collective-permute-start | bytes 294920 | tf_op jit(solution)/shard_map/ppermute | solution.py:877
  92.9 5.5 %collective-permute-start.19 = (f32[192,128]{1,0:T(8,128)S(1)}, f32[192,128]{1,0:T(8,128)}, u32[]{:S(2)}, u32[]{:S(2)}) collective-permute-start(f32[192,128]{1,0:T(8,128)S(1)} %fifth.1.refs_4_), channel_id=1, source_target_pairs={{0,1},{1,0},{2,3},{3,2},{4,5},{5,4},{6,7},{7,6},{8,9},{9,8},{10,11... | collective-permute-start | bytes 294920 | tf_op jit(solution)/shard_map/ppermute | solution.py:877
  92.9 6.6 %collective-permute-start.18 = (f32[192,128]{1,0:T(8,128)S(1)}, f32[192,128]{1,0:T(8,128)}, u32[]{:S(2)}, u32[]{:S(2)}) collective-permute-start(f32[192,128]{1,0:T(8,128)S(1)} %fifth.1.refs_4_), channel_id=1, source_target_pairs={{0,2},{1,3},{2,0},{3,1},{4,6},{5,7},{6,4},{7,5},{8,10},{9,11},{10,... | collective-permute-start | bytes 294920 | tf_op jit(solution)/shard_map/ppermute | solution.py:877
